TPU v7x, 32 devices: a whole 2x2x4 slice. The times are simulated.
32 devices in a mesh: frames: 8 (over y, x, core), space: 4 (over z).
Axes of the slice: x: 2, y: 2, z: 4, core: 2. Of those that a mesh axis runs over, the one named last changes fastest.
Arguments:
- latents: bfloat16 [8, 1792, 1152], P('frames', 'space'), may hold values from -6 to 6
- merge_slot: int32 [8, 1792], P('frames', 'space'), may hold values from 0 to 895, as said below
- modulation: float32 [6, 1152], replicated, may hold values from -3 to 3
- spatial_qkv: bfloat16 [1152, 1728], replicated, may hold values from -0.41247896 to 0.41247896
- spatial_proj: bfloat16 [576, 1152], replicated, may hold values from -0.25 to 0.25
- temporal_qkv: bfloat16 [1152, 1728], replicated, may hold values from -0.41247896 to 0.41247896
- temporal_proj: bfloat16 [576, 1152], replicated, may hold values from -0.25 to 0.25
Outputs:
- block_out: bfloat16 [8, 1792, 1152], P('frames', 'space')
Inputs may be any that keep to these rules, and one draw needn't show every extreme that they name: `merge_slot`: within each frame, the tokens of the k-th aligned block of 448 tokens join merged tokens k * 224 to (k + 1) * 224 - 1 only, and every merged token is joined by at least one token.
All inputs are finite; a program needn't handle non-finite values.
Results may differ from a plain program's by a relative error of at most 0.0062.
Values may be sent and summed in bfloat16 or wider, within the bound.
No kernel may reach another device: no remote copies, remote signals or barrier semaphores. Data moves between devices by JAX's collectives and lax.ppermute only.
A program may use at most 128 MiB of HBM per device.

v0:
```python
import math

import jax
import jax.numpy as jnp
from jax import lax
from jax.sharding import PartitionSpec as P

HEADS = 8
HD = 72


def layer_norm(values):
    values = values.astype(jnp.float32)
    center = values - jnp.mean(values, -1, keepdims=True)
    spread = jnp.mean(center * center, -1, keepdims=True)
    return center * lax.rsqrt(spread + 1e-06)


def modulate(values, modulation, which):
    return (layer_norm(values) * (1.0 + modulation[which + 1]) + modulation[which]).astype(
        jnp.bfloat16
    )


def shards(latents, merge_slot, modulation, spatial_qkv, spatial_proj, temporal_qkv, temporal_proj):
    row_count = latents.shape[1]
    slot_count = row_count // 2
    width = latents.shape[2]
    inner = spatial_proj.shape[0]
    root_size = math.sqrt(HD)
    own_rows = latents[0]
    normed = modulate(own_rows, modulation, 0)
    local_slot = merge_slot[0] - lax.axis_index("space") * slot_count
    one_hot = (local_slot[:, None] == jnp.arange(slot_count, dtype=jnp.int32)[None, :]).astype(
        jnp.bfloat16
    )
    counts = jnp.sum(one_hot.astype(jnp.float32), 0)
    summed = lax.dot_general(
        one_hot, normed, (((0,), (0,)), ((), ())), preferred_element_type=jnp.float32
    )
    merged = (summed / counts[:, None]).astype(jnp.bfloat16)
    projected = jnp.dot(merged, spatial_qkv, preferred_element_type=jnp.float32).astype(
        jnp.bfloat16
    )
    query_rows = projected[:, :inner]
    key_rows = projected[:, inner : 2 * inner]
    value_rows = projected[:, 2 * inner :]
    head_query, head_key, head_value = (
        lax.all_to_all(query_rows, "space", split_axis=1, concat_axis=0, tiled=True),
        lax.all_to_all(key_rows, "space", split_axis=1, concat_axis=0, tiled=True),
        lax.all_to_all(value_rows, "space", split_axis=1, concat_axis=0, tiled=True),
    )
    local_heads = head_query.shape[1] // HD
    all_slots = head_query.shape[0]
    scores = (
        jnp.einsum(
            "qhd,khd->hqk",
            head_query.reshape(all_slots, local_heads, HD),
            head_key.reshape(all_slots, local_heads, HD),
            preferred_element_type=jnp.float32,
        )
        / root_size
    )
    weights = jnp.exp(scores - jnp.max(scores, -1, keepdims=True))
    row_total = jnp.sum(weights, -1)
    mixture = jnp.einsum(
        "hqk,khd->qhd",
        weights.astype(jnp.bfloat16),
        head_value.reshape(all_slots, local_heads, HD),
        preferred_element_type=jnp.float32,
    )
    head_result = (
        (mixture / row_total.T[..., None]).astype(jnp.bfloat16).reshape(all_slots, local_heads * HD)
    )
    attended = lax.all_to_all(head_result, "space", split_axis=0, concat_axis=1, tiled=True)
    spatial_out = jnp.dot(attended, spatial_proj, preferred_element_type=jnp.float32).astype(
        jnp.bfloat16
    )
    spread_back = jnp.dot(one_hot, spatial_out, preferred_element_type=jnp.float32)
    after_spatial = (own_rows.astype(jnp.float32) + modulation[2] * spread_back).astype(
        jnp.bfloat16
    )
    by_place = lax.all_to_all(
        after_spatial[None], "frames", split_axis=1, concat_axis=0, tiled=True
    )
    frame_count = by_place.shape[0]
    place_count = by_place.shape[1]
    flat = by_place.reshape(frame_count * place_count, width)
    normed_time = modulate(flat, modulation, 3)
    projected_time = jnp.dot(normed_time, temporal_qkv, preferred_element_type=jnp.float32).astype(
        jnp.bfloat16
    )
    split = projected_time.reshape(frame_count, place_count, 3, HEADS, HD)
    scores_time = (
        jnp.einsum(
            "flhd,glhd->lhfg", split[:, :, 0], split[:, :, 1], preferred_element_type=jnp.float32
        )
        / root_size
    )
    weights_time = jnp.exp(scores_time - jnp.max(scores_time, -1, keepdims=True))
    total_time = jnp.sum(weights_time, -1)
    mixture_time = (
        jnp.einsum(
            "lhfg,glhd->flhd",
            weights_time.astype(jnp.bfloat16),
            split[:, :, 2],
            preferred_element_type=jnp.float32,
        )
        / total_time.transpose(2, 0, 1)[..., None]
    )
    attended_time = mixture_time.astype(jnp.bfloat16).reshape(frame_count * place_count, inner)
    branch = jnp.dot(attended_time, temporal_proj, preferred_element_type=jnp.float32)
    finished = (
        (flat.astype(jnp.float32) + modulation[5] * branch)
        .astype(jnp.bfloat16)
        .reshape(frame_count, place_count, width)
    )
    return lax.all_to_all(finished, "frames", split_axis=0, concat_axis=1, tiled=True)


def solution(mesh):
    placed = (P("frames", "space", None), P("frames", "space"), P(), P(), P(), P(), P())
    return jax.shard_map(
        shards, mesh=mesh, in_specs=placed, out_specs=P("frames", "space", None), check_vma=False
    )
```

profile of v0, /device:TPU:0, one launch (start us, length us, event | category | flops | bytes accessed | tf_op | source)
XLA Modules:
  0.0 141.8 jit_solution(10127715478575550968)
XLA Ops:
  0.0 0.0 copy-start
  0.0 1.7 %slice_reduce_fusion.1 = (f32[1152]{0:T(1024)S(1)}, f32[1152]{0:T(1024)S(1)}, f32[1152]{0:T(1024)S(1)}, f32[1152]{0:T(1024)}, f32[1152]{0:T(1024)S(1)}, /*index=5*/f32[1152]{0:T(1024)}) fusion(f32[6,1152]{1,0:T(8,128)} %param.9), kind=kLoop, calls=%fused_computation.67 | loop fusion | flops 2304 | bytes 55296 | tf_op jit(solution)/shard_map/slice | solution.py:114
  1.7 1.4 %convert_reduce_fusion.1 = f32[448]{0:T(512)S(1)} fusion(bf16[1,448,1152]{2,1,0:T(8,128)(2,1)} %param.7), kind=kLoop, calls=%fused_computation.18 | loop fusion | flops 1031744 | bytes 1033984 | tf_op jit(solution)/shard_map/reduce_sum | solution.py:14
  3.1 1.6 %fusion.14 = f32[448]{0:T(512)S(1)} fusion(bf16[1,448,1152]{2,1,0:T(8,128)(2,1)} %param.7, f32[448]{0:T(512)S(1)} %broadcast_multiply_fusion.1), kind=kLoop, calls=%fused_computation.26 | loop fusion | flops 2063936 | bytes 1035776 | tf_op jit(solution)/shard_map/reduce_sum | solution.py:15
  4.8 0.0 copy-done.9
  4.8 0.0 copy-start.7
  4.8 0.1 convert_reduce_fusion.2
  5.0 0.4 copy-done.7
  5.4 0.0 copy-done.1
  5.4 5.0 %convolution_convert_fusion.2 = bf16[224,1728]{1,0:T(8,128)(2,1)} fusion(bf16[1152,1728]{0,1:T(8,128)(2,1)} %param.10, bf16[1,448,1152]{2,1,0:T(8,128)(2,1)S(1)} %copy-done.1, f32[1152]{0:T(1024)S(1)} %get-tuple-element.6, f32[1152]{0:T(1024)S(1)} %get-tuple-element.7, f32[448]{0:T(512)S(1)} %add_rsqrt_fusion.1, f32[448]{0:T(512)S(1)} %broadcast_multiply_fusion.1, ...), kind=kOutput, calls=%fused_computation.22 | convolution fusion | flops 1127124992 | bytes 5803136 | tf_op jit(solution)/shard_map/dot_general | solution.py:42
  10.4 1.3 fusion.60
  11.7 0.9 copy.44
  12.6 6.3 %all-to-all-start = ((bf16[224,4,144]{0,2,1:T(8,128)(2,1)}), bf16[224,4,144]{0,2,1:T(8,128)(2,1)S(1)}, u32[]{:S(2)}, u32[]{:S(2)}) async-start(bf16[224,4,144]{0,2,1:T(8,128)(2,1)} %bitcast.2), calls=%async_computation | async-start | bytes 589824 | tf_op jit(solution)/shard_map/all_to_all | solution.py:51
  18.9 0.9 copy.46
  19.8 8.8 %all-to-all-done = bf16[224,4,144]{0,2,1:T(8,128)(2,1)S(1)} async-done(((bf16[224,4,144]{0,2,1:T(8,128)(2,1)}), bf16[224,4,144]{0,2,1:T(8,128)(2,1)S(1)}, u32[]{:S(2)}, u32[]{:S(2)}) %all-to-all-start) | async-done | bytes 258080 | tf_op jit(solution)/shard_map/all_to_all | solution.py:51
  28.6 3.5 %all-to-all-start.1 = ((bf16[224,4,144]{0,2,1:T(8,128)(2,1)}), bf16[224,4,144]{0,2,1:T(8,128)(2,1)S(1)}, u32[]{:S(2)}, u32[]{:S(2)}) async-start(bf16[224,4,144]{0,2,1:T(8,128)(2,1)} %bitcast.4), calls=%async_computation.1 | async-start | bytes 589824 | tf_op jit(solution)/shard_map/all_to_all | solution.py:49
  32.0 0.9 copy.48
  32.9 7.2 %all-to-all-done.1 = bf16[224,4,144]{0,2,1:T(8,128)(2,1)S(1)} async-done(((bf16[224,4,144]{0,2,1:T(8,128)(2,1)}), bf16[224,4,144]{0,2,1:T(8,128)(2,1)S(1)}, u32[]{:S(2)}, u32[]{:S(2)}) %all-to-all-start.1) | async-done | bytes 258080 | tf_op jit(solution)/shard_map/all_to_all | solution.py:49
  40.1 3.5 %all-to-all-start.2 = ((bf16[224,4,144]{0,2,1:T(8,128)(2,1)}), bf16[224,4,144]{0,2,1:T(8,128)(2,1)S(1)}, u32[]{:S(2)}, u32[]{:S(2)}) async-start(bf16[224,4,144]{0,2,1:T(8,128)(2,1)} %bitcast.6), calls=%async_computation.2 | async-start | bytes 589824 | tf_op jit(solution)/shard_map/all_to_all | solution.py:50
  43.5 0.2 copy.45
  43.7 0.9 reshape.108
  44.6 0.2 copy.47
  44.8 0.2 reshape.109
  45.0 5.5 %all-to-all-done.2 = bf16[224,4,144]{0,2,1:T(8,128)(2,1)S(1)} async-done(((bf16[224,4,144]{0,2,1:T(8,128)(2,1)}), bf16[224,4,144]{0,2,1:T(8,128)(2,1)S(1)}, u32[]{:S(2)}, u32[]{:S(2)}) %all-to-all-start.2) | async-done | bytes 258080 | tf_op jit(solution)/shard_map/all_to_all | solution.py:50
  50.5 0.2 copy.49
  50.7 0.2 reshape.110
  50.9 1.1 multiply_reduce_fusion
  52.0 0.0 copy-start.4
  52.0 1.1 fusion
  53.1 0.0 copy-done.4
  53.1 0.0 copy-start.6
  53.1 0.0 copy-start.8
  53.1 1.2 fusion.43
  54.3 0.3 all_to_all.75
  54.6 11.1 %all_to_all.88 = bf16[4,224,144]{1,2,0:T(8,128)(2,1)S(1)} all-to-all(bf16[4,224,144]{1,2,0:T(8,128)(2,1)S(1)} %copy.51), channel_id=1, replica_groups=mesh['frames'=8,'space'=4] {'space'}, dimensions={0} | all-to-all | bytes 516096 | tf_op jit(solution)/shard_map/all_to_all | solution.py:75
  65.7 0.0 copy-done
  65.7 0.0 copy-done.6
  65.7 0.0 copy-done.8
  65.7 2.0 %fusion.8 = bf16[1,448,1152]{2,1,0:T(8,128)(2,1)} fusion(bf16[1,448,1152]{2,1,0:T(8,128)(2,1)S(1)} %copy-done.1, f32[1152]{0:T(1024)S(1)} %copy-done.6, bf16[224,576]{0,1:T(8,128)(2,1)S(1)} %bitcast.105, bf16[576,1152]{1,0:T(8,128)(2,1)S(1)} %copy-done, s32[448]{0:T(512)S(1)} %bitcast.109), kind=kOutput, calls=%fused_computation.16 | convolution fusion | flops 530905088 | bytes 3655936 | tf_op jit(solution)/shard_map/dot_general | solution.py:79
  67.7 2.8 %copy.76 = bf16[1,448,1152]{2,0,1:T(2,128)(2,1)S(1)} copy(bf16[1,448,1152]{2,1,0:T(8,128)(2,1)} %fusion.8) | data formatting | bytes 2064384 | tf_op jit(solution)/shard_map/broadcast_in_dim | solution.py:84
  70.5 0.6 broadcast.83
  71.1 7.9 %reduce.17 = bf16[448,1152]{1,0:T(8,128)(2,1)} reduce(bf16[448,1,1152]{2,1,0:T(2,128)(2,1)S(1)} %bitcast.98, bf16[]{:T(256)} %broadcast.83), dimensions={1}, to_apply=%bitcast.97.reduce_sub_computation | reduce | bytes 2064386
  79.0 2.5 %reshape.121 = bf16[8,2,32256]{2,1,0:T(2,128)(2,1)S(1)} reshape(bf16[448,1152]{1,0:T(8,128)(2,1)} %reduce.17) | data formatting | bytes 2064384
  81.5 18.8 %all_to_all.89 = bf16[8,2,32256]{2,1,0:T(2,128)(2,1)} all-to-all(bf16[8,2,32256]{2,1,0:T(2,128)(2,1)S(1)} %reshape.121), channel_id=1, replica_groups=mesh['frames'=8,'space'=4] {'frames'}, dimensions={0} | all-to-all | bytes 2064384 | tf_op jit(solution)/shard_map/all_to_all | solution.py:83
  100.3 4.2 %reshape.122 = bf16[448,1,1152]{2,1,0:T(2,128)(2,1)S(1)} reshape(bf16[8,2,32256]{2,1,0:T(2,128)(2,1)} %all_to_all.89) | data formatting | bytes 2064384
  104.5 0.0 copy-start.5
  104.5 0.0 copy-start.10
  104.5 0.2 convert_reduce_fusion
  104.8 0.4 fusion.23
  105.2 0.5 copy-done.2
  105.8 0.0 copy-done.5
  105.8 1.3 copy-done.10
  107.0 2.5 %convolution_convert_fusion = bf16[448,1728]{1,0:T(8,128)(2,1)S(1)} fusion(bf16[1152,1728]{0,1:T(8,128)(2,1)S(1)} %copy-done.10, bf16[1,448,1152]{2,1,0:T(8,128)(2,1)S(1)} %get-tuple-element.12, f32[1152]{0:T(1024)S(1)} %get-tuple-element.9, f32[1152]{0:T(1024)S(1)} %copy-done.5, f32[448]{0:T(512)S(1)} %add_rsqrt_fusion, f32[448]{0:T(512)S(1)} %broadcast_multiply_fusion), kind=kOutput, calls=%fused_computation.12 | convolution fusion | flops 1787498496 | bytes 6574592 | tf_op jit(solution)/shard_map/dot_general | solution.py:90
  109.5 4.0 %reshape.111 = bf16[8,56,3,8,72]{4,3,2,1,0:T(8,128)(2,1)} reshape(bf16[448,1728]{1,0:T(8,128)(2,1)S(1)} %convolution_convert_fusion) | data formatting | bytes 3096576 | tf_op jit(solution)/shard_map/reshape | solution.py:93
  113.5 1.9 %fusion.59 = (bf16[8,56,1,8,72]{4,3,2,1,0:T(8,128)(2,1)S(1)}, bf16[8,56,1,8,72]{4,3,2,1,0:T(8,128)(2,1)S(1)}, bf16[8,56,1,8,72]{4,3,2,1,0:T(8,128)(2,1)S(1)}) fusion(bf16[8,56,3,8,72]{4,3,2,1,0:T(8,128)(2,1)} %reshape.111), kind=kLoop, calls=%fused_computation.78 | loop fusion | bytes 3096576 | tf_op jit(solution)/shard_map/slice | solution.py:106
  115.4 1.5 %multiply_reduce_fusion.1 = (f32[56,8,8]{2,1,0:T(8,128)S(1)}, f32[56,8,8,8]{2,3,1,0:T(8,128)S(1)}) fusion(bf16[8,56,1,8,72]{4,3,2,1,0:T(8,128)(2,1)S(1)} %get-tuple-element.15, bf16[8,56,1,8,72]{4,3,2,1,0:T(8,128)(2,1)S(1)} %get-tuple-element.14), kind=kOutput, calls=%fused_computation.39 | convolution fusion | flops 4182528 | bytes 1161216 | tf_op jit(solution)/shard_map/flhd,glhd->lhfg/dot_general | solution.py:95
  116.9 0.8 fusion.25
  117.7 1.3 fusion.24
  119.0 0.0 copy-start.3
  119.1 0.1 copy.58
  119.2 1.5 %reshape.112 = bf16[448,576]{1,0:T(8,128)(2,1)} reshape(bf16[8,56,8,72]{3,2,1,0:T(8,128)(2,1)S(1)} %copy.58) | data formatting | bytes 1032192 | tf_op jit(solution)/shard_map/reshape | solution.py:111
  120.7 2.5 %fusion.6 = bf16[448,1152]{1,0:T(8,128)(2,1)S(1)} fusion(bf16[448,576]{1,0:T(8,128)(2,1)} %reshape.112, bf16[576,1152]{1,0:T(8,128)(2,1)} %param.13, bf16[1,448,1152]{2,1,0:T(8,128)(2,1)S(1)} %copy-done.3, f32[1152]{0:T(1024)S(1)} %get-tuple-element.5), kind=kOutput, calls=%fused_computation.13 | convolution fusion | flops 596606976 | bytes 3912192 | tf_op jit(solution)/shard_map/dot_general | solution.py:112
  123.2 17.6 %all_to_all.90 = bf16[8,56,1152]{2,1,0:T(8,128)(2,1)S(1)} all-to-all(bf16[8,56,1152]{2,1,0:T(8,128)(2,1)S(1)} %bitcast.104), channel_id=1, replica_groups=mesh['frames'=8,'space'=4] {'frames'}, dimensions={0} | all-to-all | bytes 2064384 | tf_op jit(solution)/shard_map/all_to_all | solution.py:118
  140.8 1.0 copy.78
  (10 shorter events, 0.1 us)
Async XLA Ops:
  0.0 65.7 %copy-start = (bf16[576,1152]{1,0:T(8,128)(2,1)S(1)}, bf16[576,1152]{1,0:T(8,128)(2,1)}, u32[]{:S(2)}) copy-start(bf16[576,1152]{1,0:T(8,128)(2,1)} %param.11) | copy-start | bytes 3981316
  0.0 5.4 %copy-start.1 = (bf16[1,448,1152]{2,1,0:T(8,128)(2,1)S(1)}, bf16[1,448,1152]{2,1,0:T(8,128)(2,1)}, u32[]{:S(2)}) copy-start(bf16[1,448,1152]{2,1,0:T(8,128)(2,1)} %param.7) | copy-start | bytes 3096580
  0.0 4.8 %copy-start.9 = (s32[1,448]{1,0:T(1,128)S(1)}, s32[1,448]{1,0:T(1,128)}, u32[]{:S(2)}) copy-start(s32[1,448]{1,0:T(1,128)} %param.8) | copy-start | bytes 5380
  4.8 0.6 copy-start.7
  12.6 15.9 %all-to-all-start = ((bf16[224,4,144]{0,2,1:T(8,128)(2,1)}), bf16[224,4,144]{0,2,1:T(8,128)(2,1)S(1)}, u32[]{:S(2)}, u32[]{:S(2)}) async-start(bf16[224,4,144]{0,2,1:T(8,128)(2,1)} %bitcast.2), calls=%async_computation | async-start | bytes 589824 | tf_op jit(solution)/shard_map/all_to_all | solution.py:51
  28.6 11.5 %all-to-all-start.1 = ((bf16[224,4,144]{0,2,1:T(8,128)(2,1)}), bf16[224,4,144]{0,2,1:T(8,128)(2,1)S(1)}, u32[]{:S(2)}, u32[]{:S(2)}) async-start(bf16[224,4,144]{0,2,1:T(8,128)(2,1)} %bitcast.4), calls=%async_computation.1 | async-start | bytes 589824 | tf_op jit(solution)/shard_map/all_to_all | solution.py:49
  40.1 10.5 %all-to-all-start.2 = ((bf16[224,4,144]{0,2,1:T(8,128)(2,1)}), bf16[224,4,144]{0,2,1:T(8,128)(2,1)S(1)}, u32[]{:S(2)}, u32[]{:S(2)}) async-start(bf16[224,4,144]{0,2,1:T(8,128)(2,1)} %bitcast.6), calls=%async_computation.2 | async-start | bytes 589824 | tf_op jit(solution)/shard_map/all_to_all | solution.py:50
  52.0 1.1 copy-start.4
  53.1 12.6 %copy-start.6 = (f32[1152]{0:T(1024)S(1)}, f32[1152]{0:T(1024)}, u32[]{:S(2)}) copy-start(f32[1152]{0:T(1024)} %get-tuple-element.8) | copy-start | bytes 13828
  53.1 12.6 %copy-start.8 = (s32[1,448]{1,0:T(1,128)S(1)}, s32[1,448]{1,0:T(1,128)}, u32[]{:S(2)}) copy-start(s32[1,448]{1,0:T(1,128)} %copy-done.7) | copy-start | bytes 5380
  104.5 1.2 copy-start.5
  104.5 2.5 %copy-start.10 = (bf16[1152,1728]{0,1:T(8,128)(2,1)S(1)}, bf16[1152,1728]{0,1:T(8,128)(2,1)}, u32[]{:S(2)}) copy-start(bf16[1152,1728]{0,1:T(8,128)(2,1)} %param.12) | copy-start | bytes 11943940
  104.8 1.0 copy-start.2
  119.0 1.7 %copy-start.3 = (bf16[1,448,1152]{2,1,0:T(8,128)(2,1)S(1)}, bf16[1,448,1152]{2,1,0:T(8,128)(2,1)}, u32[]{:S(2)}) copy-start(bf16[1,448,1152]{2,1,0:T(8,128)(2,1)} %copy-done.2) | copy-start | bytes 3096580
where the time goes:
time: 143 us; the launch traced here: 142 us
  blocking collectives  47.5 us (33%)
  local copies, waits for them, and re-layouts  26.9 us (19%)
  waiting for transfers between devices  21.5 us (15%)
  matrix products  17 us (12%)
  other arithmetic  15.4 us (11%)
  starting transfers between devices  13.2 us (9%)
    all_to_all x1, blocking collectives, shards(): lax.all_to_all(after_spatial[None], 'frames', split_axis=1, concat_axis=0...  18.8 us
    all_to_all x1, blocking collectives, shards(): lax.all_to_all(finished, 'frames', split_axis=0, concat_axis=1, tiled=True)  17.6 us
    all_to_all x1, blocking collectives, shards(): lax.all_to_all(head_result, 'space', split_axis=0, concat_axis=1, tiled=T...  11.1 us
    unnamed x26, local copies, waits for them, and re-layouts  10.5 us
    all_to_all x1, waiting for transfers between devices, shards(): lax.all_to_all(value_rows, 'space', split_axis=1, concat_axis=0, tiled=True)  8.75 us
    unnamed x1, other arithmetic  7.93 us
    all_to_all x1, waiting for transfers between devices, shards(): lax.all_to_all(query_rows, 'space', split_axis=1, concat_axis=0, tiled=True)  7.19 us
    all_to_all x1, starting transfers between devices, shards(): lax.all_to_all(value_rows, 'space', split_axis=1, concat_axis=0, tiled=True)  6.33 us
  transfers between devices with their start and end apart: 3, of which 3 were waited for; matrix products, arithmetic and copies ran while one was open for 2% of the time, Pallas kernels for 0%

commit v1 on v0

--- a/solution.py
+++ b/solution.py
@@ -1,35 +1,333 @@
+import functools
 import math
 
 import jax
 import jax.numpy as jnp
 from jax import lax
+from jax.experimental import pallas as pl
+from jax.experimental.pallas import tpu as pltpu
 from jax.sharding import PartitionSpec as P
 
-HEADS = 8
 HD = 72
+LANES = 128
+SUB = 16
+F32 = jnp.float32
+BF16 = jnp.bfloat16
+VMEM = pl.BlockSpec(memory_space=pltpu.VMEM)
+ANY = pl.BlockSpec(memory_space=pl.ANY)
+MIB = 1 << 20
+
+
+def struct(*shape):
+    return jax.ShapeDtypeStruct(shape, BF16)
+
+
+def params(mib):
+    return pltpu.CompilerParams(vmem_limit_bytes=mib * MIB)
 
 
 def layer_norm(values):
-    values = values.astype(jnp.float32)
     center = values - jnp.mean(values, -1, keepdims=True)
     spread = jnp.mean(center * center, -1, keepdims=True)
     return center * lax.rsqrt(spread + 1e-06)
 
 
-def modulate(values, modulation, which):
-    return (layer_norm(values) * (1.0 + modulation[which + 1]) + modulation[which]).astype(
-        jnp.bfloat16
-    )
-
-
-def shards(latents, merge_slot, modulation, spatial_qkv, spatial_proj, temporal_qkv, temporal_proj):
+def dot(left, right):
+    return jnp.dot(left, right, preferred_element_type=F32)
+
+
+def packing(rows, width):
+    full, rest = divmod(width, LANES)
+    groups = 1
+    if rest:
+        units = rows // SUB
+        groups = max([g for g in range(1, units + 1) if units % g == 0 and g * rest <= LANES and rows % SUB == 0] or [1])
+    return full, rest, groups
+
+
+def packed_rows(rows, width):
+    full, rest, groups = packing(rows, width)
+    return full * rows + (rows // groups if rest else 0)
+
+
+def pack(block):
+    rows, width = block.shape
+    full, rest, groups = packing(rows, width)
+    parts = [block[:, j * LANES : (j + 1) * LANES] for j in range(full)]
+    if rest:
+        high = rows // groups
+        tail = block[:, full * LANES :]
+        pieces = [tail[i * high : (i + 1) * high] for i in range(groups)]
+        if groups * rest < LANES:
+            pieces.append(jnp.zeros((high, LANES - groups * rest), block.dtype))
+        parts.append(jnp.concatenate(pieces, 1))
+    return jnp.concatenate(parts, 0)
+
+
+def unpack(packed, rows, width):
+    full, rest, groups = packing(rows, width)
+    parts = [packed[j * rows : (j + 1) * rows] for j in range(full)]
+    if rest:
+        high = rows // groups
+        tail = packed[full * rows : full * rows + high]
+        pieces = [tail[:, i * rest : (i + 1) * rest] for i in range(groups)]
+        parts.append(jnp.concatenate(pieces, 0))
+    return jnp.concatenate(parts, 1)
+
+
+def merge_kernel(n_space, latents, slot, modulation, weights, *refs):
+    outs, (held, arrived, sem) = refs[:n_space], refs[n_space:]
+    copy = pltpu.make_async_copy(weights, arrived, sem)
+    copy.start()
+    me = lax.axis_index("space")
+    rows, slots = latents.shape[0], latents.shape[0] // 2
+    inner = weights.shape[1] // 3
+    wide = inner // n_space
+    values = layer_norm(latents[...].astype(F32))
+    normed = (values * (1.0 + modulation[1:2]) + modulation[0:1]).astype(BF16)
+    local = slot[...] - me * slots
+    chosen = lax.broadcasted_iota(jnp.int32, (slots, rows), 0) == local
+    counts = jnp.sum(chosen.astype(F32), 1, keepdims=True)
+    merged = (dot(chosen.astype(BF16), normed) / counts).astype(BF16)
+    copy.wait()
+    projected = dot(merged, arrived[...]).astype(BF16)
+    for d in range(n_space):
+        held[d] = pack(
+            jnp.concatenate([projected[:, j * inner + d * wide : j * inner + (d + 1) * wide] for j in range(3)], 1)
+        )
+    for s in range(n_space):
+        outs[s][...] = held[me ^ s]
+
+
+def attention_kernel(n_space, slots, wide, *refs):
+    ins, outs = refs[:n_space], refs[n_space:]
+    blocks = [unpack(r[...], slots, 3 * wide) for r in ins]
+    results = [[] for _ in range(n_space)]
+    for h in range(wide // HD):
+        keys = jnp.concatenate([b[:, wide + h * HD : wide + (h + 1) * HD] for b in blocks], 0)
+        vals = jnp.concatenate([b[:, 2 * wide + h * HD : 2 * wide + (h + 1) * HD] for b in blocks], 0)
+        vals = jnp.concatenate([vals, jnp.ones((vals.shape[0], LANES - HD), BF16)], 1)
+        for s in range(n_space):
+            query = blocks[s][:, h * HD : (h + 1) * HD]
+            scores = lax.dot_general(query, keys, (((1,), (1,)), ((), ())), preferred_element_type=F32)
+            top = jnp.max(scores, -1, keepdims=True)
+            weights = jnp.exp((scores - top) * (1.0 / math.sqrt(HD)))
+            mixed = dot(weights.astype(BF16), vals)
+            results[s].append((mixed[:, :HD] / mixed[:, HD : HD + 1]).astype(BF16))
+    for s in range(n_space):
+        outs[s][...] = pack(jnp.concatenate(results[s], 1))
+
+
+def expand_kernel(n_space, n_pair, slots, wide, slot, *refs):
+    ins, (keep, give, attended, held, spread) = refs[:n_space], refs[n_space:]
+    me, frame = lax.axis_index("space"), lax.axis_index("frames")
+    for s in range(n_space):
+        held[me ^ s] = unpack(ins[s][...], slots, wide)
+    whole = jnp.concatenate([held[d] for d in range(n_space)], 1)
+    attended[...] = whole
+    local = slot[...] - me * slots
+    rows = slot.shape[0]
+    chosen = (lax.broadcasted_iota(jnp.int32, (rows, slots), 1) == local).astype(BF16)
+    wanted = dot(chosen, whole)
+    places = keep.shape[1]
+    for f in range(2 * n_pair):
+        spread[f] = wanted[f * places : (f + 1) * places].astype(BF16)
+    for s in range(n_pair):
+        keep[s] = spread[frame ^ (2 * s)]
+        give[s] = spread[frame ^ (2 * s + 1)]
+
+
+def share_kernel(n_pair, latents, keep, give):
+    frame = lax.axis_index("frames")
+    for s in range(n_pair):
+        keep[s] = latents[frame ^ (2 * s)]
+        give[s] = latents[frame ^ (2 * s + 1)]
+
+
+def residual_kernel(attended, slot, latents, modulation, proj, after):
+    me = lax.axis_index("space")
+    slots, rows = attended.shape[0], slot.shape[0]
+    places = latents.shape[1]
+    out = dot(attended[...], proj[...]).astype(BF16)
+    local = slot[...] - me * slots
+    chosen = (lax.broadcasted_iota(jnp.int32, (rows, slots), 1) == local).astype(BF16)
+    spread = modulation[2:3] * dot(chosen, out)
+    for f in range(latents.shape[0]):
+        after[f] = (latents[f].astype(F32) + spread[f * places : (f + 1) * places]).astype(BF16)
+
+
+def gather_blocks(parts, places):
+    groups = -(-places // SUB)
+    blocks = []
+    for ref in parts:
+        for t in range(ref.shape[0]):
+            value = ref[t].astype(F32)
+            if groups * SUB > places:
+                value = jnp.concatenate([value, jnp.zeros((groups * SUB - places, value.shape[1]), F32)], 0)
+            blocks.append(value)
+    return jnp.concatenate([b[g * SUB : (g + 1) * SUB] for g in range(groups) for b in blocks], 0)
+
+
+def temporal_kernel(n_pair, places, modulation, proj, weights, *refs):
+    tokens, results = refs[:n_pair], refs[n_pair : 2 * n_pair]
+    keep, give, held = refs[2 * n_pair :]
+    n_frames = 2 * n_pair
+    groups = -(-places // SUB)
+    inner = proj.shape[0]
+    attended = gather_blocks(results, places).astype(BF16)
+    spatial = dot(attended, proj[...]).astype(BF16)
+    after = (gather_blocks(tokens, places) + modulation[2:3] * spatial.astype(F32)).astype(BF16)
+    normed = (layer_norm(after.astype(F32)) * (1.0 + modulation[4:5]) + modulation[3:4]).astype(BF16)
+    projected = dot(normed, weights[...]).astype(BF16)
+    size = n_frames * SUB
+    row = lax.broadcasted_iota(jnp.int32, (size, size), 0)
+    col = lax.broadcasted_iota(jnp.int32, (size, size), 1)
+    same = (row & (SUB - 1)) == (col & (SUB - 1))
+    ones = jnp.ones((size, LANES - HD), BF16)
+    for g in range(groups):
+        block = projected[g * size : (g + 1) * size]
+        mixtures = []
+        for h in range(inner // HD):
+            query, key, val = (block[:, j * inner + h * HD : j * inner + (h + 1) * HD] for j in range(3))
+            scores = lax.dot_general(query, key, (((1,), (1,)), ((), ())), preferred_element_type=F32)
+            scores = jnp.where(same, scores, -jnp.inf)
+            top = jnp.max(scores, -1, keepdims=True)
+            mix = jnp.exp((scores - top) * (1.0 / math.sqrt(HD)))
+            mixed = dot(mix.astype(BF16), jnp.concatenate([val, ones], 1))
+            mixtures.append((mixed[:, :HD] / mixed[:, HD : HD + 1]).astype(BF16))
+        whole = jnp.concatenate(mixtures, 1)
+        for f in range(n_frames):
+            held[f, g * SUB : (g + 1) * SUB] = whole[f * SUB : (f + 1) * SUB]
+    for s in range(n_pair):
+        keep[s] = held[2 * s][:places]
+        give[s] = held[2 * s + 1][:places]
+
+
+def finish_kernel(n_pair, places, modulation, proj, after, *refs):
+    parts, out = refs[:n_pair], refs[n_pair]
+    frame = lax.axis_index("frames")
+    pad = -(-places // SUB) * SUB
+    blocks = []
+    for ref in parts:
+        for t in range(ref.shape[0]):
+            value = ref[t].astype(F32)
+            if pad > places:
+                value = jnp.concatenate([value, jnp.zeros((pad - places, value.shape[1]), F32)], 0)
+            blocks.append(value.astype(BF16))
+    branch = modulation[5:6] * dot(jnp.concatenate(blocks, 0), proj[...])
+    for k in range(2 * n_pair):
+        at = frame ^ k
+        out[at] = (after[at].astype(F32) + branch[k * pad : k * pad + places]).astype(BF16)
+
+
+def swap(block, axis, size, mask):
+    return lax.ppermute(block, axis, [(i, i ^ mask) for i in range(size)])
+
+
+def exchange(keep, give, size):
+    got = swap(give, "frames", size, 1)
+    both = jnp.stack([keep, got], 1)
+    others = [swap(both[s], "frames", size, 2 * s) for s in range(1, size // 2)]
+    return [both[0]] + others
+
+
+def shards(n_frames, n_space, latents, merge_slot, modulation, spatial_qkv, spatial_proj, temporal_qkv, temporal_proj):
+    rows, width = latents.shape[1:]
+    slots, places = rows // 2, rows // n_frames
+    inner = spatial_proj.shape[0]
+    wide = inner // n_space
+    n_pair = n_frames // 2
+    own = latents[0]
+    blocks = latents.reshape(n_frames, places, width)
+    slot_column = merge_slot.reshape(rows, 1)
+    sent = packed_rows(slots, 3 * wide)
+    queries = pl.pallas_call(
+        functools.partial(merge_kernel, n_space),
+        out_shape=[struct(sent, LANES)] * n_space,
+        in_specs=[VMEM, VMEM, VMEM, ANY],
+        out_specs=[VMEM] * n_space,
+        scratch_shapes=[
+            pltpu.VMEM((n_space, sent, LANES), BF16),
+            pltpu.VMEM(spatial_qkv.shape, BF16),
+            pltpu.SemaphoreType.DMA,
+        ],
+        compiler_params=params(32),
+        name="merge",
+    )(own, merge_slot, modulation, spatial_qkv)
+    held = [queries[0]] + [swap(queries[s], "space", n_space, s) for s in range(1, n_space)]
+    returned = packed_rows(slots, wide)
+    results = pl.pallas_call(
+        functools.partial(attention_kernel, n_space, slots, wide),
+        out_shape=[struct(returned, LANES)] * n_space,
+        in_specs=[VMEM] * n_space,
+        out_specs=[VMEM] * n_space,
+        compiler_params=params(32),
+        name="attend",
+    )(*held)
+    mine = [results[0]] + [swap(results[s], "space", n_space, s) for s in range(1, n_space)]
+    keep, give, attended = pl.pallas_call(
+        functools.partial(expand_kernel, n_space, n_pair, slots, wide),
+        out_shape=[struct(n_pair, places, inner), struct(n_pair, places, inner), struct(slots, inner)],
+        in_specs=[VMEM] * (n_space + 1),
+        out_specs=[VMEM] * 3,
+        scratch_shapes=[pltpu.VMEM((n_space, slots, wide), BF16), pltpu.VMEM((n_frames, places, inner), BF16)],
+        compiler_params=params(32),
+        name="expand",
+    )(slot_column, *mine)
+    blocks_late, _ = lax.optimization_barrier((blocks, queries[0]))
+    token_keep, token_give = pl.pallas_call(
+        functools.partial(share_kernel, n_pair),
+        out_shape=[struct(n_pair, places, width)] * 2,
+        in_specs=[VMEM],
+        out_specs=[VMEM] * 2,
+        compiler_params=params(32),
+        name="share",
+    )(blocks_late)
+    tokens = exchange(token_keep, token_give, n_frames)
+    attended_parts = exchange(keep, give, n_frames)
+    after = pl.pallas_call(
+        residual_kernel,
+        out_shape=struct(n_frames, places, width),
+        in_specs=[VMEM] * 5,
+        out_specs=VMEM,
+        compiler_params=params(32),
+        name="residual",
+    )(attended, slot_column, blocks, modulation, spatial_proj)
+    pad = -(-places // SUB) * SUB
+    mixed_keep, mixed_give = pl.pallas_call(
+        functools.partial(temporal_kernel, n_pair, places),
+        out_shape=[struct(n_pair, places, inner)] * 2,
+        in_specs=[VMEM] * (3 + 2 * n_pair),
+        out_specs=[VMEM] * 2,
+        scratch_shapes=[pltpu.VMEM((n_frames, pad, inner), BF16)],
+        compiler_params=params(48),
+        name="temporal",
+    )(modulation, spatial_proj, temporal_qkv, *tokens, *attended_parts)
+    parts = exchange(mixed_keep, mixed_give, n_frames)
+    out = pl.pallas_call(
+        functools.partial(finish_kernel, n_pair, places),
+        out_shape=struct(n_frames, places, width),
+        in_specs=[VMEM] * (3 + n_pair),
+        out_specs=VMEM,
+        compiler_params=params(32),
+        name="finish",
+    )(modulation, temporal_proj, after, *parts)
+    return out.reshape(1, rows, width)
+
+
+def plain_modulate(values, modulation, which):
+    normed = layer_norm(values.astype(F32))
+    return (normed * (1.0 + modulation[which + 1]) + modulation[which]).astype(BF16)
+
+
+def plain_shards(latents, merge_slot, modulation, spatial_qkv, spatial_proj, temporal_qkv, temporal_proj):
     row_count = latents.shape[1]
     slot_count = row_count // 2
     width = latents.shape[2]
     inner = spatial_proj.shape[0]
     root_size = math.sqrt(HD)
     own_rows = latents[0]
-    normed = modulate(own_rows, modulation, 0)
+    normed = plain_modulate(own_rows, modulation, 0)
     local_slot = merge_slot[0] - lax.axis_index("space") * slot_count
     one_hot = (local_slot[:, None] == jnp.arange(slot_count, dtype=jnp.int32)[None, :]).astype(
         jnp.bfloat16
@@ -86,11 +384,11 @@
     frame_count = by_place.shape[0]
     place_count = by_place.shape[1]
     flat = by_place.reshape(frame_count * place_count, width)
-    normed_time = modulate(flat, modulation, 3)
+    normed_time = plain_modulate(flat, modulation, 3)
     projected_time = jnp.dot(normed_time, temporal_qkv, preferred_element_type=jnp.float32).astype(
         jnp.bfloat16
     )
-    split = projected_time.reshape(frame_count, place_count, 3, HEADS, HD)
+    split = projected_time.reshape(frame_count, place_count, 3, inner // HD, HD)
     scores_time = (
         jnp.einsum(
             "flhd,glhd->lhfg", split[:, :, 0], split[:, :, 1], preferred_element_type=jnp.float32
@@ -119,7 +417,12 @@
 
 
 def solution(mesh):
+    n_frames, n_space = mesh.shape["frames"], mesh.shape["space"]
     placed = (P("frames", "space", None), P("frames", "space"), P(), P(), P(), P(), P())
-    return jax.shard_map(
-        shards, mesh=mesh, in_specs=placed, out_specs=P("frames", "space", None), check_vma=False
-    )
+
+    def local(latents, *rest):
+        fits = latents.shape[1] % (8 * n_frames) == 0 and n_frames & (n_frames - 1) == 0 and n_space & (n_space - 1) == 0
+        body = functools.partial(shards, n_frames, n_space) if fits else plain_shards
+        return body(latents, *rest)
+
+    return jax.shard_map(local, mesh=mesh, in_specs=placed, out_specs=P("frames", "space", None), check_vma=False)

time: 143 us -> 103 us (0.72)
  blocking collectives: 47.5 us -> 0 us
  Pallas kernels: 0 us -> 25.7 us
  matrix products: 17 us -> 0 us
  other arithmetic: 15.4 us -> 2.89 us
  waiting for transfers between devices: 21.5 us -> 33.5 us
  starting transfers between devices: 13.2 us -> 25.1 us
  local copies, waits for them, and re-layouts: 26.9 us -> 15.3 us
    all_to_all x3 -> x0, blocking collectives: 47.5 us -> none  [the longest x1 18.8 us: shards(): lax.all_to_all(after_spatial[None], 'frames', split_axis=1, concat_axis=0...]
    ppermute x0 -> x18, waiting for transfers between devices: none -> 33.5 us  [swap(): return lax.ppermute(block, axis, [(i, i ^ mask) for i in range(size)])]
    pallas_call x0 -> x7, Pallas kernels: none -> 25.7 us  [the longest x1 14.5 us: shards(): pl.pallas_call(functools.partial(temporal_kernel, n_pair, places), out_sh...]
    ppermute x0 -> x18, starting transfers between devices: none -> 25.1 us  [swap(): return lax.ppermute(block, axis, [(i, i ^ mask) for i in range(size)])]
    all_to_all x3 -> x0, waiting for transfers between devices: 21.5 us -> none  [the longest x1 8.75 us: shards(): lax.all_to_all(value_rows, 'space', split_axis=1, concat_axis=0, tiled=True)]
    dot_general x8 -> x0, matrix products: 17 us -> none  [the longest x1 4.99 us: shards(): jnp.dot(merged, spatial_qkv, preferred_element_type=jnp.float32)]
    all_to_all x3 -> x0, starting transfers between devices: 13.2 us -> none  [the longest x1 6.33 us: shards(): lax.all_to_all(value_rows, 'space', split_axis=1, concat_axis=0, tiled=True)]
    unnamed x1 -> x0, other arithmetic: 7.93 us -> none
  transfers between devices with their start and end apart: 3 -> 18, of which waited for: 3 -> 8; matrix products, arithmetic and copies ran while one was open for 2% -> 8% of each run, Pallas kernels for 0% -> 6%
where the time goes in v1:
time: 103 us
  waiting for transfers between devices  33.5 us (33%)
  Pallas kernels  25.7 us (25%)
  starting transfers between devices  25.1 us (24%)
  local copies, waits for them, and re-layouts  15.3 us (15%)
  other arithmetic  2.89 us (3%)
    ppermute x18, waiting for transfers between devices, swap(): return lax.ppermute(block, axis, [(i, i ^ mask) for i in range(size)])  33.5 us
    ppermute x18, starting transfers between devices, swap(): return lax.ppermute(block, axis, [(i, i ^ mask) for i in range(size)])  25.1 us
    unnamed x14, local copies, waits for them, and re-layouts  15.2 us
    pallas_call x1, Pallas kernels, shards(): pl.pallas_call(functools.partial(temporal_kernel, n_pair, places), out_sh...  14.5 us
    pallas_call x1, Pallas kernels, shards(): pl.pallas_call(functools.partial(attention_kernel, n_space, slots, wide),...  4.12 us
    pallas_call x1, Pallas kernels, shards(): pl.pallas_call(functools.partial(merge_kernel, n_space), out_shape=[struc...  3.19 us
    squeeze x3, other arithmetic, exchange(): others = [swap(both[s], 'frames', size, 2 * s) for s in range(1, size // 2)]  2.89 us
    pallas_call x1, Pallas kernels, shards(): pl.pallas_call(functools.partial(finish_kernel, n_pair, places), out_shap...  2.19 us
  transfers between devices with their start and end apart: 18, of which 8 were waited for; matrix products, arithmetic and copies ran while one was open for 8% of the time, Pallas kernels for 6%

profile of v1, /device:TPU:0, one launch (start us, length us, event | category | flops | bytes accessed | tf_op | source)
XLA Modules:
  0.0 102.6 jit_solution(13169989032226444849)
XLA Ops:
  0.0 0.0 copy-start.1
  0.0 0.0 copy-start.5
  0.0 0.0 copy-start.4
  0.0 6.5 %copy.10.weights = bf16[1152,1728]{1,0:T(8,128)(2,1)} copy(bf16[1152,1728]{0,1:T(8,128)(2,1)} %param.10) | data formatting | bytes 7962624 | tf_op args[3]
  6.6 0.0 copy-done.1
  6.6 0.0 copy-done.5
  6.6 0.0 copy-done.4
  6.6 0.0 copy-start
  6.6 2.2 %copy-done = bf16[1152,1728]{1,0:T(8,128)(2,1)S(1)} copy-done((bf16[1152,1728]{1,0:T(8,128)(2,1)S(1)}, bf16[1152,1728]{1,0:T(8,128)(2,1)}, u32[]{:S(2)}) %copy-start) | copy-done | bytes 3981336
  8.7 3.2 %merge.1 = (bf16[784,128]{1,0:T(8,128)(2,1)S(1)}, bf16[784,128]{1,0:T(8,128)(2,1)S(1)}, bf16[784,128]{1,0:T(8,128)(2,1)S(1)}, bf16[784,128]{1,0:T(8,128)(2,1)S(1)}) custom-call(bf16[448,1152]{1,0:T(8,128)(2,1)S(1)} %bitcast.34, s32[1,448]{1,0:T(1,128)S(1)} %copy-done.5, f32[6,1152]{1,0:T(8,128)S(1)} %copy-done.4, bf16[1152,1728]{1,0:T(8,128)(2,1)S(1)} %copy-done), custom_call_target="tpu_custom_call" | custom-call | tf_op jit(solution)/shard_map/merge/pallas_call | solution.py:244
  11.9 0.1 share.1
  12.0 0.5 collective-permute-start.6
  12.6 2.7 %collective-permute-start = (bf16[784,128]{1,0:T(8,128)(2,1)S(1)}, bf16[784,128]{1,0:T(8,128)(2,1)S(1)}, u32[]{:S(2)}, u32[]{:S(2)}) collective-permute-start(bf16[784,128]{1,0:T(8,128)(2,1)S(1)} %get-tuple-element.22), channel_id=1, source_target_pairs={{0,1},{1,0},{2,3},{3,2},{4,5},{5,4},{6,7},{7,6},{8,9},{9,8},{10,11... | collective-permute-start | bytes 602120 | tf_op jit(solution)/shard_map/ppermute | solution.py:224
  15.2 2.6 %collective-permute-start.1 = (bf16[784,128]{1,0:T(8,128)(2,1)S(1)}, bf16[784,128]{1,0:T(8,128)(2,1)S(1)}, u32[]{:S(2)}, u32[]{:S(2)}) collective-permute-start(bf16[784,128]{1,0:T(8,128)(2,1)S(1)} %get-tuple-element.23), channel_id=1, source_target_pairs={{0,2},{1,3},{2,0},{3,1},{4,6},{5,7},{6,4},{7,5},{8,10},{9,11},{10,... | collective-permute-start | bytes 602120 | tf_op jit(solution)/shard_map/ppermute | solution.py:224
  17.8 0.0 collective-permute-start.2
  17.8 6.8 %collective-permute-done.refs_1_ = bf16[784,128]{1,0:T(8,128)(2,1)S(1)} collective-permute-done((bf16[784,128]{1,0:T(8,128)(2,1)S(1)}, bf16[784,128]{1,0:T(8,128)(2,1)S(1)}, u32[]{:S(2)}, u32[]{:S(2)}) %collective-permute-start) | collective-permute-done | bytes 200736 | tf_op jit(solution)/shard_map/ppermute | solution.py:224
  24.6 7.9 %collective-permute-done.1.refs_2_ = bf16[784,128]{1,0:T(8,128)(2,1)S(1)} collective-permute-done((bf16[784,128]{1,0:T(8,128)(2,1)S(1)}, bf16[784,128]{1,0:T(8,128)(2,1)S(1)}, u32[]{:S(2)}, u32[]{:S(2)}) %collective-permute-start.1) | collective-permute-done | bytes 200736 | tf_op jit(solution)/shard_map/ppermute | solution.py:224
  32.6 0.0 collective-permute-done.2.refs_3_
  32.6 4.1 %attend.1 = (bf16[256,128]{1,0:T(8,128)(2,1)S(1)}, bf16[256,128]{1,0:T(8,128)(2,1)S(1)}, bf16[256,128]{1,0:T(8,128)(2,1)S(1)}, bf16[256,128]{1,0:T(8,128)(2,1)S(1)}) custom-call(bf16[784,128]{1,0:T(8,128)(2,1)S(1)} %get-tuple-element.21.refs_0_, bf16[784,128]{1,0:T(8,128)(2,1)S(1)} %collective-permute-done.refs_1_, ...), custom_call_target="tpu_custom_call" | custom-call | tf_op jit(solution)/shard_map/attend/pallas_call | solution.py:259
  36.7 4.1 %collective-permute-start.3 = (bf16[256,128]{1,0:T(8,128)(2,1)S(1)}, bf16[256,128]{1,0:T(8,128)(2,1)S(1)}, u32[]{:S(2)}, u32[]{:S(2)}) collective-permute-start(bf16[256,128]{1,0:T(8,128)(2,1)S(1)} %get-tuple-element.26), channel_id=1, source_target_pairs={{0,1},{1,0},{2,3},{3,2},{4,5},{5,4},{6,7},{7,6},{8,9},{9,8},{10,11... | collective-permute-start | bytes 196616 | tf_op jit(solution)/shard_map/ppermute | solution.py:224
  40.9 1.1 %collective-permute-start.4 = (bf16[256,128]{1,0:T(8,128)(2,1)S(1)}, bf16[256,128]{1,0:T(8,128)(2,1)S(1)}, u32[]{:S(2)}, u32[]{:S(2)}) collective-permute-start(bf16[256,128]{1,0:T(8,128)(2,1)S(1)} %get-tuple-element.27), channel_id=1, source_target_pairs={{0,2},{1,3},{2,0},{3,1},{4,6},{5,7},{6,4},{7,5},{8,10},{9,11},{10,... | collective-permute-start | bytes 196616 | tf_op jit(solution)/shard_map/ppermute | solution.py:224
  41.9 1.4 %collective-permute-start.5 = (bf16[256,128]{1,0:T(8,128)(2,1)S(1)}, bf16[256,128]{1,0:T(8,128)(2,1)S(1)}, u32[]{:S(2)}, u32[]{:S(2)}) collective-permute-start(bf16[256,128]{1,0:T(8,128)(2,1)S(1)} %get-tuple-element.28), channel_id=1, source_target_pairs={{0,3},{1,2},{2,1},{3,0},{4,7},{5,6},{6,5},{7,4},{8,11},{9,10},{10,... | collective-permute-start | bytes 196616 | tf_op jit(solution)/shard_map/ppermute | solution.py:224
  43.3 0.1 copy.11.slot
  43.5 0.0 collective-permute-done.3.refs_1_
  43.5 4.8 %collective-permute-done.4.refs_2_ = bf16[256,128]{1,0:T(8,128)(2,1)S(1)} collective-permute-done((bf16[256,128]{1,0:T(8,128)(2,1)S(1)}, bf16[256,128]{1,0:T(8,128)(2,1)S(1)}, u32[]{:S(2)}, u32[]{:S(2)}) %collective-permute-start.4) | collective-permute-done | bytes 65568 | tf_op jit(solution)/shard_map/ppermute | solution.py:224
  48.3 0.0 collective-permute-done.5.refs_3_
  48.3 0.6 expand.1
  49.0 0.1 collective-permute-start.10
  49.1 0.0 collective-permute-done.6
  49.1 2.0 %fusion.6 = (bf16[2,56,1152]{2,1,0:T(8,128)(2,1)}, bf16[2,56,1152]{2,1,0:T(8,128)(2,1)S(1)}, bf16[2,56,1152]{2,1,0:T(8,128)(2,1)}, bf16[2,56,1152]{2,1,0:T(8,128)(2,1)}) fusion(bf16[4,1,56,1152]{3,2,1,0:T(8,128)(2,1)} %bitcast.4, bf16[4,1,56,1152]{3,2,1,0:T(8,128)(2,1)S(1)} %bitcast.37), kind=kLoop, calls=%fused_computation.25 | loop fusion | flops 516096 | bytes 2064384 | tf_op jit(solution)/shard_map/squeeze | solution.py:230
  51.1 0.0 collective-permute-done.10
  51.1 0.8 fusion.20
  51.9 1.5 %collective-permute-start.11 = (bf16[2,56,576]{2,1,0:T(8,128)(2,1)S(1)}, bf16[2,56,576]{2,1,0:T(8,128)(2,1)S(1)}, u32[]{:S(2)}, u32[]{:S(2)}) collective-permute-start(bf16[2,56,576]{2,1,0:T(8,128)(2,1)S(1)} %get-tuple-element.47), channel_id=1, source_target_pairs={{0,8},{4,12},{8,0},{12,4},{16,24},{20,28},{24,16},{28,20},{1,9},{5... | collective-permute-start | bytes 387080 | tf_op jit(solution)/shard_map/ppermute | solution.py:224
  53.4 0.5 collective-permute-start.7
  53.9 1.5 %collective-permute-start.8 = (bf16[2,56,1152]{2,1,0:T(8,128)(2,1)}, bf16[2,56,1152]{2,1,0:T(8,128)(2,1)}, u32[]{:S(2)}, u32[]{:S(2)}) collective-permute-start(bf16[2,56,1152]{2,1,0:T(8,128)(2,1)} %get-tuple-element.40), channel_id=1, source_target_pairs={{0,16},{4,20},{8,24},{12,28},{16,0},{20,4},{24,8},{28,12},{1,17},{... | collective-permute-start | bytes 774152 | tf_op jit(solution)/shard_map/ppermute | solution.py:224
  55.4 1.4 %collective-permute-start.9 = (bf16[2,56,1152]{2,1,0:T(8,128)(2,1)}, bf16[2,56,1152]{2,1,0:T(8,128)(2,1)}, u32[]{:S(2)}, u32[]{:S(2)}) collective-permute-start(bf16[2,56,1152]{2,1,0:T(8,128)(2,1)} %get-tuple-element.37), channel_id=1, source_target_pairs={{0,24},{4,28},{8,16},{12,20},{16,8},{20,12},{24,0},{28,4},{1,25},{... | collective-permute-start | bytes 774152 | tf_op jit(solution)/shard_map/ppermute | solution.py:224
  56.8 1.5 %collective-permute-start.12 = (bf16[2,56,576]{2,1,0:T(8,128)(2,1)}, bf16[2,56,576]{2,1,0:T(8,128)(2,1)}, u32[]{:S(2)}, u32[]{:S(2)}) collective-permute-start(bf16[2,56,576]{2,1,0:T(8,128)(2,1)} %get-tuple-element.48), channel_id=1, source_target_pairs={{0,16},{4,20},{8,24},{12,28},{16,0},{20,4},{24,8},{28,12},{1,17},{... | collective-permute-start | bytes 387080 | tf_op jit(solution)/shard_map/ppermute | solution.py:224
  58.4 0.1 collective-permute-done.11.refs_5_
  58.4 0.0 copy-start.2
  58.4 2.4 %collective-permute-start.13 = (bf16[2,56,576]{2,1,0:T(8,128)(2,1)}, bf16[2,56,576]{2,1,0:T(8,128)(2,1)}, u32[]{:S(2)}, u32[]{:S(2)}) collective-permute-start(bf16[2,56,576]{2,1,0:T(8,128)(2,1)} %get-tuple-element.45), channel_id=1, source_target_pairs={{0,24},{4,28},{8,16},{12,20},{16,8},{20,12},{24,0},{28,4},{1,25},{... | collective-permute-start | bytes 387080 | tf_op jit(solution)/shard_map/ppermute | solution.py:224
  60.9 6.5 %copy.13.weights = bf16[1152,1728]{1,0:T(8,128)(2,1)} copy(bf16[1152,1728]{0,1:T(8,128)(2,1)} %param.12) | data formatting | bytes 7962624 | tf_op args[5]
  67.3 6.6 %collective-permute-done.12.refs_6_ = bf16[2,56,576]{2,1,0:T(8,128)(2,1)} collective-permute-done((bf16[2,56,576]{2,1,0:T(8,128)(2,1)}, bf16[2,56,576]{2,1,0:T(8,128)(2,1)}, u32[]{:S(2)}, u32[]{:S(2)}) %collective-permute-start.12) | collective-permute-done | bytes 129056 | tf_op jit(solution)/shard_map/ppermute | solution.py:224
  73.9 0.0 collective-permute-done.13.refs_7_
  73.9 0.0 collective-permute-done.7.refs_1_
  73.9 0.0 collective-permute-done.8.refs_2_
  73.9 0.0 collective-permute-done.9.refs_3_
  74.0 0.0 copy-done.2
  74.0 14.5 %temporal.1 = (bf16[4,56,576]{2,1,0:T(8,128)(2,1)S(1)}, bf16[4,56,576]{2,1,0:T(8,128)(2,1)S(1)}) custom-call(f32[6,1152]{1,0:T(8,128)S(1)} %copy-done.4, bf16[576,1152]{1,0:T(8,128)(2,1)S(1)} %copy-done.2, bf16[1152,1728]{1,0:T(8,128)(2,1)} %copy.13.weights, bf16[2,56,1152]{2,1,0:T(8,128)(2,1)S(1)} %get-tuple-element.38.refs_0_, ...), custom_call_target="tpu_custom_call" | custom-call | tf_op jit(solution)/shard_map/temporal/pallas_call | solution.py:297
  88.5 0.0 copy-start.3
  88.5 0.1 collective-permute-start.14
  88.6 1.6 %collective-permute-done.14 = bf16[4,56,576]{2,1,0:T(8,128)(2,1)S(1)} collective-permute-done((bf16[4,56,576]{2,1,0:T(8,128)(2,1)S(1)}, bf16[4,56,576]{2,1,0:T(8,128)(2,1)S(1)}, u32[]{:S(2)}, u32[]{:S(2)}) %collective-permute-start.14) | collective-permute-done | bytes 258080 | tf_op jit(solution)/shard_map/ppermute | solution.py:224
  90.1 0.1 fusion.19
  90.2 1.6 %collective-permute-start.15 = (bf16[2,56,576]{2,1,0:T(8,128)(2,1)S(1)}, bf16[2,56,576]{2,1,0:T(8,128)(2,1)S(1)}, u32[]{:S(2)}, u32[]{:S(2)}) collective-permute-start(bf16[2,56,576]{2,1,0:T(8,128)(2,1)S(1)} %get-tuple-element.43), channel_id=1, source_target_pairs={{0,8},{4,12},{8,0},{12,4},{16,24},{20,28},{24,16},{28,20},{1,9},{5... | collective-permute-start | bytes 387080 | tf_op jit(solution)/shard_map/ppermute | solution.py:224
  91.8 1.5 %collective-permute-start.16 = (bf16[2,56,576]{2,1,0:T(8,128)(2,1)S(1)}, bf16[2,56,576]{2,1,0:T(8,128)(2,1)S(1)}, u32[]{:S(2)}, u32[]{:S(2)}) collective-permute-start(bf16[2,56,576]{2,1,0:T(8,128)(2,1)S(1)} %get-tuple-element.44), channel_id=1, source_target_pairs={{0,16},{4,20},{8,24},{12,28},{16,0},{20,4},{24,8},{28,12},{1,17},{... | collective-permute-start | bytes 387080 | tf_op jit(solution)/shard_map/ppermute | solution.py:224
  93.3 0.5 collective-permute-start.17
  93.8 0.9 residual.1.after
  94.7 2.0 %collective-permute-done.15.refs_1_ = bf16[2,56,576]{2,1,0:T(8,128)(2,1)S(1)} collective-permute-done((bf16[2,56,576]{2,1,0:T(8,128)(2,1)S(1)}, bf16[2,56,576]{2,1,0:T(8,128)(2,1)S(1)}, u32[]{:S(2)}, u32[]{:S(2)}) %collective-permute-start.15) | collective-permute-done | bytes 129056 | tf_op jit(solution)/shard_map/ppermute | solution.py:224
  96.7 3.7 %collective-permute-done.16.refs_2_ = bf16[2,56,576]{2,1,0:T(8,128)(2,1)S(1)} collective-permute-done((bf16[2,56,576]{2,1,0:T(8,128)(2,1)S(1)}, bf16[2,56,576]{2,1,0:T(8,128)(2,1)S(1)}, u32[]{:S(2)}, u32[]{:S(2)}) %collective-permute-start.16) | collective-permute-done | bytes 129056 | tf_op jit(solution)/shard_map/ppermute | solution.py:224
  100.4 0.0 collective-permute-done.17.refs_3_
  100.4 0.0 copy-done.3
  100.4 2.2 %finish.1 = bf16[8,56,1152]{2,1,0:T(8,128)(2,1)} custom-call(f32[6,1152]{1,0:T(8,128)S(1)} %copy-done.4, bf16[576,1152]{1,0:T(8,128)(2,1)S(1)} %copy-done.3, bf16[8,56,1152]{2,1,0:T(8,128)(2,1)S(1)} %residual.1.after, bf16[2,56,576]{2,1,0:T(8,128)(2,1)S(1)} %get-tuple-element.42.refs_0_, bf16[2,56,576]{2,1,0:T(8,128)(2,1)S(1)} %collective-permute-done.15.refs_1_, ...), custom_call_target="tpu_custom_call" | custom-call | tf_op jit(solution)/shard_map/finish/pallas_call | solution.py:307
Async XLA Ops:
  0.0 6.6 %copy-start.1 = (bf16[1,448,1152]{2,1,0:T(8,128)(2,1)S(1)}, bf16[1,448,1152]{2,1,0:T(8,128)(2,1)}, u32[]{:S(2)}) copy-start(bf16[1,448,1152]{2,1,0:T(8,128)(2,1)} %param.7) | copy-start | bytes 3096580
  0.0 6.6 %copy-start.5 = (s32[1,448]{1,0:T(1,128)S(1)}, s32[1,448]{1,0:T(1,128)}, u32[]{:S(2)}) copy-start(s32[1,448]{1,0:T(1,128)} %slot.1) | copy-start | bytes 5380
  0.0 6.6 %copy-start.4 = (f32[6,1152]{1,0:T(8,128)S(1)}, f32[6,1152]{1,0:T(8,128)}, u32[]{:S(2)}) copy-start(f32[6,1152]{1,0:T(8,128)} %modulation.7) | copy-start | bytes 82948
  6.6 2.2 %copy-start = (bf16[1152,1728]{1,0:T(8,128)(2,1)S(1)}, bf16[1152,1728]{1,0:T(8,128)(2,1)}, u32[]{:S(2)}) copy-start(bf16[1152,1728]{1,0:T(8,128)(2,1)} %copy.10.weights) | copy-start | bytes 11943940
  12.0 37.0 %collective-permute-start.6 = (bf16[4,56,1152]{2,1,0:T(8,128)(2,1)S(1)}, bf16[4,56,1152]{2,1,0:T(8,128)(2,1)}, u32[]{:S(2)}, u32[]{:S(2)}) collective-permute-start(bf16[4,56,1152]{2,1,0:T(8,128)(2,1)S(1)} %get-tuple-element.32), channel_id=1, source_target_pairs={{0,4},{4,0},{8,12},{12,8},{16,20},{20,16},{24,28},{28,24},{1,5},{5... | collective-permute-start | bytes 1548296 | tf_op jit(solution)/shard_map/ppermute | solution.py:224
  12.6 12.1 %collective-permute-start = (bf16[784,128]{1,0:T(8,128)(2,1)S(1)}, bf16[784,128]{1,0:T(8,128)(2,1)S(1)}, u32[]{:S(2)}, u32[]{:S(2)}) collective-permute-start(bf16[784,128]{1,0:T(8,128)(2,1)S(1)} %get-tuple-element.22), channel_id=1, source_target_pairs={{0,1},{1,0},{2,3},{3,2},{4,5},{5,4},{6,7},{7,6},{8,9},{9,8},{10,11... | collective-permute-start | bytes 602120 | tf_op jit(solution)/shard_map/ppermute | solution.py:224
  15.2 17.4 %collective-permute-start.1 = (bf16[784,128]{1,0:T(8,128)(2,1)S(1)}, bf16[784,128]{1,0:T(8,128)(2,1)S(1)}, u32[]{:S(2)}, u32[]{:S(2)}) collective-permute-start(bf16[784,128]{1,0:T(8,128)(2,1)S(1)} %get-tuple-element.23), channel_id=1, source_target_pairs={{0,2},{1,3},{2,0},{3,1},{4,6},{5,7},{6,4},{7,5},{8,10},{9,11},{10,... | collective-permute-start | bytes 602120 | tf_op jit(solution)/shard_map/ppermute | solution.py:224
  17.8 14.8 %collective-permute-start.2 = (bf16[784,128]{1,0:T(8,128)(2,1)S(1)}, bf16[784,128]{1,0:T(8,128)(2,1)S(1)}, u32[]{:S(2)}, u32[]{:S(2)}) collective-permute-start(bf16[784,128]{1,0:T(8,128)(2,1)S(1)} %get-tuple-element.24), channel_id=1, source_target_pairs={{0,3},{1,2},{2,1},{3,0},{4,7},{5,6},{6,5},{7,4},{8,11},{9,10},{10,... | collective-permute-start | bytes 602120 | tf_op jit(solution)/shard_map/ppermute | solution.py:224
  36.7 6.8 %collective-permute-start.3 = (bf16[256,128]{1,0:T(8,128)(2,1)S(1)}, bf16[256,128]{1,0:T(8,128)(2,1)S(1)}, u32[]{:S(2)}, u32[]{:S(2)}) collective-permute-start(bf16[256,128]{1,0:T(8,128)(2,1)S(1)} %get-tuple-element.26), channel_id=1, source_target_pairs={{0,1},{1,0},{2,3},{3,2},{4,5},{5,4},{6,7},{7,6},{8,9},{9,8},{10,11... | collective-permute-start | bytes 196616 | tf_op jit(solution)/shard_map/ppermute | solution.py:224
  40.9 7.5 %collective-permute-start.4 = (bf16[256,128]{1,0:T(8,128)(2,1)S(1)}, bf16[256,128]{1,0:T(8,128)(2,1)S(1)}, u32[]{:S(2)}, u32[]{:S(2)}) collective-permute-start(bf16[256,128]{1,0:T(8,128)(2,1)S(1)} %get-tuple-element.27), channel_id=1, source_target_pairs={{0,2},{1,3},{2,0},{3,1},{4,6},{5,7},{6,4},{7,5},{8,10},{9,11},{10,... | collective-permute-start | bytes 196616 | tf_op jit(solution)/shard_map/ppermute | solution.py:224
  41.9 6.4 %collective-permute-start.5 = (bf16[256,128]{1,0:T(8,128)(2,1)S(1)}, bf16[256,128]{1,0:T(8,128)(2,1)S(1)}, u32[]{:S(2)}, u32[]{:S(2)}) collective-permute-start(bf16[256,128]{1,0:T(8,128)(2,1)S(1)} %get-tuple-element.28), channel_id=1, source_target_pairs={{0,3},{1,2},{2,1},{3,0},{4,7},{5,6},{6,5},{7,4},{8,11},{9,10},{10,... | collective-permute-start | bytes 196616 | tf_op jit(solution)/shard_map/ppermute | solution.py:224
  49.0 2.1 %collective-permute-start.10 = (bf16[4,56,576]{2,1,0:T(8,128)(2,1)S(1)}, bf16[4,56,576]{2,1,0:T(8,128)(2,1)S(1)}, u32[]{:S(2)}, u32[]{:S(2)}) collective-permute-start(bf16[4,56,576]{2,1,0:T(8,128)(2,1)S(1)} %get-tuple-element.34), channel_id=1, source_target_pairs={{0,4},{4,0},{8,12},{12,8},{16,20},{20,16},{24,28},{28,24},{1,5},{5... | collective-permute-start | bytes 774152 | tf_op jit(solution)/shard_map/ppermute | solution.py:224
  51.9 6.6 %collective-permute-start.11 = (bf16[2,56,576]{2,1,0:T(8,128)(2,1)S(1)}, bf16[2,56,576]{2,1,0:T(8,128)(2,1)S(1)}, u32[]{:S(2)}, u32[]{:S(2)}) collective-permute-start(bf16[2,56,576]{2,1,0:T(8,128)(2,1)S(1)} %get-tuple-element.47), channel_id=1, source_target_pairs={{0,8},{4,12},{8,0},{12,4},{16,24},{20,28},{24,16},{28,20},{1,9},{5... | collective-permute-start | bytes 387080 | tf_op jit(solution)/shard_map/ppermute | solution.py:224
  53.4 20.6 %collective-permute-start.7 = (bf16[2,56,1152]{2,1,0:T(8,128)(2,1)}, bf16[2,56,1152]{2,1,0:T(8,128)(2,1)}, u32[]{:S(2)}, u32[]{:S(2)}) collective-permute-start(bf16[2,56,1152]{2,1,0:T(8,128)(2,1)} %get-tuple-element.39), channel_id=1, source_target_pairs={{0,8},{4,12},{8,0},{12,4},{16,24},{20,28},{24,16},{28,20},{1,9},{5... | collective-permute-start | bytes 774152 | tf_op jit(solution)/shard_map/ppermute | solution.py:224
  53.9 20.0 %collective-permute-start.8 = (bf16[2,56,1152]{2,1,0:T(8,128)(2,1)}, bf16[2,56,1152]{2,1,0:T(8,128)(2,1)}, u32[]{:S(2)}, u32[]{:S(2)}) collective-permute-start(bf16[2,56,1152]{2,1,0:T(8,128)(2,1)} %get-tuple-element.40), channel_id=1, source_target_pairs={{0,16},{4,20},{8,24},{12,28},{16,0},{20,4},{24,8},{28,12},{1,17},{... | collective-permute-start | bytes 774152 | tf_op jit(solution)/shard_map/ppermute | solution.py:224
  55.4 18.5 %collective-permute-start.9 = (bf16[2,56,1152]{2,1,0:T(8,128)(2,1)}, bf16[2,56,1152]{2,1,0:T(8,128)(2,1)}, u32[]{:S(2)}, u32[]{:S(2)}) collective-permute-start(bf16[2,56,1152]{2,1,0:T(8,128)(2,1)} %get-tuple-element.37), channel_id=1, source_target_pairs={{0,24},{4,28},{8,16},{12,20},{16,8},{20,12},{24,0},{28,4},{1,25},{... | collective-permute-start | bytes 774152 | tf_op jit(solution)/shard_map/ppermute | solution.py:224
  56.8 17.1 %collective-permute-start.12 = (bf16[2,56,576]{2,1,0:T(8,128)(2,1)}, bf16[2,56,576]{2,1,0:T(8,128)(2,1)}, u32[]{:S(2)}, u32[]{:S(2)}) collective-permute-start(bf16[2,56,576]{2,1,0:T(8,128)(2,1)} %get-tuple-element.48), channel_id=1, source_target_pairs={{0,16},{4,20},{8,24},{12,28},{16,0},{20,4},{24,8},{28,12},{1,17},{... | collective-permute-start | bytes 387080 | tf_op jit(solution)/shard_map/ppermute | solution.py:224
  58.4 15.5 %copy-start.2 = (bf16[576,1152]{1,0:T(8,128)(2,1)S(1)}, bf16[576,1152]{1,0:T(8,128)(2,1)}, u32[]{:S(2)}) copy-start(bf16[576,1152]{1,0:T(8,128)(2,1)} %proj.4) | copy-start | bytes 3981316
  58.4 15.5 %collective-permute-start.13 = (bf16[2,56,576]{2,1,0:T(8,128)(2,1)}, bf16[2,56,576]{2,1,0:T(8,128)(2,1)}, u32[]{:S(2)}, u32[]{:S(2)}) collective-permute-start(bf16[2,56,576]{2,1,0:T(8,128)(2,1)} %get-tuple-element.45), channel_id=1, source_target_pairs={{0,24},{4,28},{8,16},{12,20},{16,8},{20,12},{24,0},{28,4},{1,25},{... | collective-permute-start | bytes 387080 | tf_op jit(solution)/shard_map/ppermute | solution.py:224
  88.5 11.9 %copy-start.3 = (bf16[576,1152]{1,0:T(8,128)(2,1)S(1)}, bf16[576,1152]{1,0:T(8,128)(2,1)}, u32[]{:S(2)}) copy-start(bf16[576,1152]{1,0:T(8,128)(2,1)} %proj.5) | copy-start | bytes 3981316
  88.5 1.6 %collective-permute-start.14 = (bf16[4,56,576]{2,1,0:T(8,128)(2,1)S(1)}, bf16[4,56,576]{2,1,0:T(8,128)(2,1)S(1)}, u32[]{:S(2)}, u32[]{:S(2)}) collective-permute-start(bf16[4,56,576]{2,1,0:T(8,128)(2,1)S(1)} %get-tuple-element.36), channel_id=1, source_target_pairs={{0,4},{4,0},{8,12},{12,8},{16,20},{20,16},{24,28},{28,24},{1,5},{5... | collective-permute-start | bytes 774152 | tf_op jit(solution)/shard_map/ppermute | solution.py:224
  90.2 6.5 %collective-permute-start.15 = (bf16[2,56,576]{2,1,0:T(8,128)(2,1)S(1)}, bf16[2,56,576]{2,1,0:T(8,128)(2,1)S(1)}, u32[]{:S(2)}, u32[]{:S(2)}) collective-permute-start(bf16[2,56,576]{2,1,0:T(8,128)(2,1)S(1)} %get-tuple-element.43), channel_id=1, source_target_pairs={{0,8},{4,12},{8,0},{12,4},{16,24},{20,28},{24,16},{28,20},{1,9},{5... | collective-permute-start | bytes 387080 | tf_op jit(solution)/shard_map/ppermute | solution.py:224
  91.8 8.6 %collective-permute-start.16 = (bf16[2,56,576]{2,1,0:T(8,128)(2,1)S(1)}, bf16[2,56,576]{2,1,0:T(8,128)(2,1)S(1)}, u32[]{:S(2)}, u32[]{:S(2)}) collective-permute-start(bf16[2,56,576]{2,1,0:T(8,128)(2,1)S(1)} %get-tuple-element.44), channel_id=1, source_target_pairs={{0,16},{4,20},{8,24},{12,28},{16,0},{20,4},{24,8},{28,12},{1,17},{... | collective-permute-start | bytes 387080 | tf_op jit(solution)/shard_map/ppermute | solution.py:224
  93.3 7.1 %collective-permute-start.17 = (bf16[2,56,576]{2,1,0:T(8,128)(2,1)S(1)}, bf16[2,56,576]{2,1,0:T(8,128)(2,1)S(1)}, u32[]{:S(2)}, u32[]{:S(2)}) collective-permute-start(bf16[2,56,576]{2,1,0:T(8,128)(2,1)S(1)} %get-tuple-element.41), channel_id=1, source_target_pairs={{0,24},{4,28},{8,16},{12,20},{16,8},{20,12},{24,0},{28,4},{1,25},{... | collective-permute-start | bytes 387080 | tf_op jit(solution)/shard_map/ppermute | solution.py:224

commit v2 on v1

--- a/solution.py
+++ b/solution.py
@@ -14,8 +14,9 @@
 F32 = jnp.float32
 BF16 = jnp.bfloat16
 VMEM = pl.BlockSpec(memory_space=pltpu.VMEM)
-ANY = pl.BlockSpec(memory_space=pl.ANY)
+HBM = pl.BlockSpec(memory_space=pltpu.HBM)
 MIB = 1 << 20
+SCALE = math.log2(math.e) / math.sqrt(HD)
 
 
 def struct(*shape):
@@ -34,6 +35,10 @@
 
 def dot(left, right):
     return jnp.dot(left, right, preferred_element_type=F32)
+
+
+def dot_t(left, right):
+    return lax.dot_general(left, right, (((1,), (1,)), ((), ())), preferred_element_type=F32)
 
 
 def packing(rows, width):
@@ -75,54 +80,69 @@
     return jnp.concatenate(parts, 1)
 
 
-def merge_kernel(n_space, latents, slot, modulation, weights, *refs):
-    outs, (held, arrived, sem) = refs[:n_space], refs[n_space:]
-    copy = pltpu.make_async_copy(weights, arrived, sem)
-    copy.start()
-    me = lax.axis_index("space")
-    rows, slots = latents.shape[0], latents.shape[0] // 2
-    inner = weights.shape[1] // 3
+def merge_kernel(n_space, n_pair, latents, slot, modulation, weights, *refs):
+    outs, (keep, give, held, tokens, slots_in, mods, arrived, sems) = refs[:n_space], refs[n_space:]
+    pairs = ((latents, tokens), (slot, slots_in), (modulation, mods), (weights, arrived))
+    copies = [pltpu.make_async_copy(there, here, sems.at[i]) for i, (there, here) in enumerate(pairs)]
+    for copy in copies:
+        copy.start()
+    me, frame = lax.axis_index("space"), lax.axis_index("frames")
+    places, width = latents.shape[1:]
+    rows = 2 * n_pair * places
+    slots = rows // 2
+    inner = weights.shape[0] // 3
     wide = inner // n_space
-    values = layer_norm(latents[...].astype(F32))
-    normed = (values * (1.0 + modulation[1:2]) + modulation[0:1]).astype(BF16)
-    local = slot[...] - me * slots
+    for copy in copies[:3]:
+        copy.wait()
+    shift, scale = mods[0:1], 1.0 + mods[1:2]
+    normed = jnp.concatenate(
+        [layer_norm(tokens[f].astype(F32)) * scale + shift for f in range(2 * n_pair)], 0
+    ).astype(BF16)
+    local = slots_in[...] - me * slots
     chosen = lax.broadcasted_iota(jnp.int32, (slots, rows), 0) == local
     counts = jnp.sum(chosen.astype(F32), 1, keepdims=True)
     merged = (dot(chosen.astype(BF16), normed) / counts).astype(BF16)
-    copy.wait()
-    projected = dot(merged, arrived[...]).astype(BF16)
+    for s in range(n_pair):
+        keep[s] = tokens[frame ^ (2 * s)]
+        give[s] = tokens[frame ^ (2 * s + 1)]
+    copies[3].wait()
+    projected = dot_t(merged, arrived[...])
+    queries = (projected[:, :inner] * SCALE).astype(BF16)
+    others = projected[:, inner:].astype(BF16)
     for d in range(n_space):
+        at = d * wide
         held[d] = pack(
-            jnp.concatenate([projected[:, j * inner + d * wide : j * inner + (d + 1) * wide] for j in range(3)], 1)
+            jnp.concatenate(
+                [queries[:, at : at + wide], others[:, at : at + wide], others[:, inner + at : inner + at + wide]], 1
+            )
         )
     for s in range(n_space):
         outs[s][...] = held[me ^ s]
 
 
-def attention_kernel(n_space, slots, wide, *refs):
+def attention_kernel(n_space, slots, wide, asked, *refs):
     ins, outs = refs[:n_space], refs[n_space:]
-    blocks = [unpack(r[...], slots, 3 * wide) for r in ins]
+    blocks = [unpack(r[...], slots, 3 * wide) for r in reversed(ins)]
     results = [[] for _ in range(n_space)]
     for h in range(wide // HD):
         keys = jnp.concatenate([b[:, wide + h * HD : wide + (h + 1) * HD] for b in blocks], 0)
         vals = jnp.concatenate([b[:, 2 * wide + h * HD : 2 * wide + (h + 1) * HD] for b in blocks], 0)
         vals = jnp.concatenate([vals, jnp.ones((vals.shape[0], LANES - HD), BF16)], 1)
-        for s in range(n_space):
+        for s in asked:
             query = blocks[s][:, h * HD : (h + 1) * HD]
-            scores = lax.dot_general(query, keys, (((1,), (1,)), ((), ())), preferred_element_type=F32)
+            scores = dot_t(query, keys)
             top = jnp.max(scores, -1, keepdims=True)
-            weights = jnp.exp((scores - top) * (1.0 / math.sqrt(HD)))
-            mixed = dot(weights.astype(BF16), vals)
+            mixed = dot(jnp.exp2(scores - top).astype(BF16), vals)
             results[s].append((mixed[:, :HD] / mixed[:, HD : HD + 1]).astype(BF16))
-    for s in range(n_space):
-        outs[s][...] = pack(jnp.concatenate(results[s], 1))
+    for out, s in zip(outs, asked):
+        out[...] = pack(jnp.concatenate(results[s], 1))
 
 
 def expand_kernel(n_space, n_pair, slots, wide, slot, *refs):
     ins, (keep, give, attended, held, spread) = refs[:n_space], refs[n_space:]
     me, frame = lax.axis_index("space"), lax.axis_index("frames")
     for s in range(n_space):
-        held[me ^ s] = unpack(ins[s][...], slots, wide)
+        held[me ^ s] = unpack(ins[n_space - 1 - s][...], slots, wide)
     whole = jnp.concatenate([held[d] for d in range(n_space)], 1)
     attended[...] = whole
     local = slot[...] - me * slots
@@ -137,11 +157,8 @@
         give[s] = spread[frame ^ (2 * s + 1)]
 
 
-def share_kernel(n_pair, latents, keep, give):
-    frame = lax.axis_index("frames")
-    for s in range(n_pair):
-        keep[s] = latents[frame ^ (2 * s)]
-        give[s] = latents[frame ^ (2 * s + 1)]
+def cost(flops):
+    return pl.CostEstimate(flops=flops, bytes_accessed=flops // 100, transcendentals=0)
 
 
 def residual_kernel(attended, slot, latents, modulation, proj, after):
@@ -156,79 +173,86 @@
         after[f] = (latents[f].astype(F32) + spread[f * places : (f + 1) * places]).astype(BF16)
 
 
-def gather_blocks(parts, places):
-    groups = -(-places // SUB)
-    blocks = []
-    for ref in parts:
-        for t in range(ref.shape[0]):
-            value = ref[t].astype(F32)
-            if groups * SUB > places:
-                value = jnp.concatenate([value, jnp.zeros((groups * SUB - places, value.shape[1]), F32)], 0)
-            blocks.append(value)
-    return jnp.concatenate([b[g * SUB : (g + 1) * SUB] for g in range(groups) for b in blocks], 0)
-
-
-def temporal_kernel(n_pair, places, modulation, proj, weights, *refs):
-    tokens, results = refs[:n_pair], refs[n_pair : 2 * n_pair]
-    keep, give, held = refs[2 * n_pair :]
+def project_blocks(places, modulation, proj, weights, tokens, results, normed):
+    frames = [(s, t) for s in range(len(tokens)) for t in range(2)]
+    attended = jnp.concatenate([results[s][t].astype(F32) for s, t in frames], 0).astype(BF16)
+    spatial = dot(attended, proj[...])
+    gate, shift, scale = modulation[2:3], modulation[3:4], 1.0 + modulation[4:5]
+    for f, (s, t) in enumerate(frames):
+        at = slice(f * places, (f + 1) * places)
+        normed[at] = layer_norm(tokens[s][t].astype(F32) + gate * spatial[at]) * scale + shift
+    projected = dot_t(normed[...].astype(BF16), weights[...])
+    space = jnp.zeros((-places % SUB, projected.shape[1]), F32)
+    return [
+        jnp.concatenate([projected[f * places : (f + 1) * places], space], 0).astype(BF16)
+        for f in range(len(frames))
+    ]
+
+
+def project_kernel(places, n_parts, modulation, proj, weights, *refs):
+    out, normed = refs[2 * n_parts :]
+    blocks = project_blocks(places, modulation, proj, weights, refs[:n_parts], refs[n_parts : 2 * n_parts], normed)
+    for f, block in enumerate(blocks):
+        out[f] = block
+
+
+def temporal_kernel(n_pair, places, n_parts, order, modulation, proj, weights, *refs):
+    tokens, results, before = refs[:n_parts], refs[n_parts : 2 * n_parts], refs[2 * n_parts : n_pair + n_parts]
+    keep, give, normed, held = refs[n_pair + n_parts :]
     n_frames = 2 * n_pair
     groups = -(-places // SUB)
     inner = proj.shape[0]
-    attended = gather_blocks(results, places).astype(BF16)
-    spatial = dot(attended, proj[...]).astype(BF16)
-    after = (gather_blocks(tokens, places) + modulation[2:3] * spatial.astype(F32)).astype(BF16)
-    normed = (layer_norm(after.astype(F32)) * (1.0 + modulation[4:5]) + modulation[3:4]).astype(BF16)
-    projected = dot(normed, weights[...]).astype(BF16)
+    heads = inner // HD
+    by_frame = [ref[t] for ref in before for t in range(2)]
+    by_frame += project_blocks(places, modulation, proj, weights, tokens, results, normed)
     size = n_frames * SUB
     row = lax.broadcasted_iota(jnp.int32, (size, size), 0)
     col = lax.broadcasted_iota(jnp.int32, (size, size), 1)
-    same = (row & (SUB - 1)) == (col & (SUB - 1))
+    same = ((row & (SUB - 1)) == (col & (SUB - 1)))[None]
     ones = jnp.ones((size, LANES - HD), BF16)
     for g in range(groups):
-        block = projected[g * size : (g + 1) * size]
-        mixtures = []
-        for h in range(inner // HD):
-            query, key, val = (block[:, j * inner + h * HD : j * inner + (h + 1) * HD] for j in range(3))
-            scores = lax.dot_general(query, key, (((1,), (1,)), ((), ())), preferred_element_type=F32)
-            scores = jnp.where(same, scores, -jnp.inf)
-            top = jnp.max(scores, -1, keepdims=True)
-            mix = jnp.exp((scores - top) * (1.0 / math.sqrt(HD)))
-            mixed = dot(mix.astype(BF16), jnp.concatenate([val, ones], 1))
-            mixtures.append((mixed[:, :HD] / mixed[:, HD : HD + 1]).astype(BF16))
-        whole = jnp.concatenate(mixtures, 1)
+        block = jnp.concatenate([b[g * SUB : (g + 1) * SUB] for b in by_frame], 0)
+
+        def part(j, h):
+            return block[:, j * inner + h * HD : j * inner + (h + 1) * HD]
+
+        scores = jnp.concatenate([dot_t(part(0, h), part(1, h)) for h in range(heads)], 0)
+        scores = jnp.where(same, scores.reshape(heads, size, size), -jnp.inf)
+        mix = jnp.exp2((scores - jnp.max(scores, -1, keepdims=True)) * SCALE).astype(BF16)
+        mixed = [dot(mix[h], jnp.concatenate([part(2, h), ones], 1)) for h in range(heads)]
+        whole = jnp.concatenate([(m[:, :HD] / m[:, HD : HD + 1]).astype(BF16) for m in mixed], 1)
         for f in range(n_frames):
             held[f, g * SUB : (g + 1) * SUB] = whole[f * SUB : (f + 1) * SUB]
-    for s in range(n_pair):
-        keep[s] = held[2 * s][:places]
-        give[s] = held[2 * s + 1][:places]
+    for i, s in enumerate(order):
+        keep[s] = held[2 * i][:places]
+        give[s] = held[2 * i + 1][:places]
 
 
 def finish_kernel(n_pair, places, modulation, proj, after, *refs):
     parts, out = refs[:n_pair], refs[n_pair]
     frame = lax.axis_index("frames")
-    pad = -(-places // SUB) * SUB
-    blocks = []
-    for ref in parts:
-        for t in range(ref.shape[0]):
-            value = ref[t].astype(F32)
-            if pad > places:
-                value = jnp.concatenate([value, jnp.zeros((pad - places, value.shape[1]), F32)], 0)
-            blocks.append(value.astype(BF16))
-    branch = modulation[5:6] * dot(jnp.concatenate(blocks, 0), proj[...])
+    frames = [(s, t) for s in range(n_pair) for t in range(2)]
+    mixed = jnp.concatenate([parts[s][t].astype(F32) for s, t in frames], 0).astype(BF16)
+    branch = dot(mixed, proj[...])
+    gate = modulation[5:6]
     for k in range(2 * n_pair):
         at = frame ^ k
-        out[at] = (after[at].astype(F32) + branch[k * pad : k * pad + places]).astype(BF16)
+        out[at] = (after[at].astype(F32) + gate * branch[k * places : (k + 1) * places]).astype(BF16)
 
 
 def swap(block, axis, size, mask):
     return lax.ppermute(block, axis, [(i, i ^ mask) for i in range(size)])
+
+
+def swaps(blocks, axis, size, step=1):
+    moved = {s: swap(blocks[s], axis, size, s * step) for s in range(len(blocks) - 1, 0, -1)}
+    return [blocks[0]] + [moved[s] for s in range(1, len(blocks))]
 
 
 def exchange(keep, give, size):
     got = swap(give, "frames", size, 1)
     both = jnp.stack([keep, got], 1)
-    others = [swap(both[s], "frames", size, 2 * s) for s in range(1, size // 2)]
-    return [both[0]] + others
+    return swaps([both[s] for s in range(size // 2)], "frames", size, 2)
 
 
 def shards(n_frames, n_space, latents, merge_slot, modulation, spatial_qkv, spatial_proj, temporal_qkv, temporal_proj):
@@ -237,79 +261,115 @@
     inner = spatial_proj.shape[0]
     wide = inner // n_space
     n_pair = n_frames // 2
-    own = latents[0]
+    spatial_qkv, temporal_qkv = spatial_qkv.T, temporal_qkv.T
     blocks = latents.reshape(n_frames, places, width)
     slot_column = merge_slot.reshape(rows, 1)
     sent = packed_rows(slots, 3 * wide)
-    queries = pl.pallas_call(
-        functools.partial(merge_kernel, n_space),
-        out_shape=[struct(sent, LANES)] * n_space,
-        in_specs=[VMEM, VMEM, VMEM, ANY],
-        out_specs=[VMEM] * n_space,
+    *queries, token_keep, token_give = pl.pallas_call(
+        functools.partial(merge_kernel, n_space, n_pair),
+        out_shape=[struct(sent, LANES)] * n_space + [struct(n_pair, places, width)] * 2,
+        in_specs=[HBM] * 4,
+        out_specs=[VMEM] * (n_space + 2),
         scratch_shapes=[
             pltpu.VMEM((n_space, sent, LANES), BF16),
+            pltpu.VMEM(blocks.shape, BF16),
+            pltpu.VMEM(merge_slot.shape, jnp.int32),
+            pltpu.VMEM(modulation.shape, F32),
             pltpu.VMEM(spatial_qkv.shape, BF16),
-            pltpu.SemaphoreType.DMA,
+            pltpu.SemaphoreType.DMA((4,)),
         ],
-        compiler_params=params(32),
+        compiler_params=params(57),
         name="merge",
-    )(own, merge_slot, modulation, spatial_qkv)
-    held = [queries[0]] + [swap(queries[s], "space", n_space, s) for s in range(1, n_space)]
+    )(blocks, merge_slot, modulation, spatial_qkv)
+    held = swaps(queries, "space", n_space)
+    tokens = exchange(token_keep, token_give, n_frames)
+    held = lax.optimization_barrier(held[::-1])
     returned = packed_rows(slots, wide)
-    results = pl.pallas_call(
-        functools.partial(attention_kernel, n_space, slots, wide),
-        out_shape=[struct(returned, LANES)] * n_space,
-        in_specs=[VMEM] * n_space,
-        out_specs=[VMEM] * n_space,
-        compiler_params=params(32),
-        name="attend",
-    )(*held)
-    mine = [results[0]] + [swap(results[s], "space", n_space, s) for s in range(1, n_space)]
+    results = {}
+    for name, asked in (("others", range(1, n_space)), ("own", range(1))):
+        if name == "own":
+            held, tokens = lax.optimization_barrier((held, tokens))
+        done = pl.pallas_call(
+            functools.partial(attention_kernel, n_space, slots, wide, asked),
+            out_shape=[struct(returned, LANES)] * len(asked),
+            in_specs=[VMEM] * n_space,
+            out_specs=[VMEM] * len(asked),
+            compiler_params=params(20),
+            cost_estimate=cost(4 * slots * slots * n_space * n_space * wide),
+            name="attend_" + name,
+        )(*held)
+        results.update(zip(asked, done))
+    mine = swaps(results, "space", n_space)
     keep, give, attended = pl.pallas_call(
         functools.partial(expand_kernel, n_space, n_pair, slots, wide),
         out_shape=[struct(n_pair, places, inner), struct(n_pair, places, inner), struct(slots, inner)],
         in_specs=[VMEM] * (n_space + 1),
         out_specs=[VMEM] * 3,
         scratch_shapes=[pltpu.VMEM((n_space, slots, wide), BF16), pltpu.VMEM((n_frames, places, inner), BF16)],
-        compiler_params=params(32),
+        compiler_params=params(20),
         name="expand",
-    )(slot_column, *mine)
-    blocks_late, _ = lax.optimization_barrier((blocks, queries[0]))
-    token_keep, token_give = pl.pallas_call(
-        functools.partial(share_kernel, n_pair),
-        out_shape=[struct(n_pair, places, width)] * 2,
-        in_specs=[VMEM],
-        out_specs=[VMEM] * 2,
-        compiler_params=params(32),
-        name="share",
-    )(blocks_late)
-    tokens = exchange(token_keep, token_give, n_frames)
+    )(slot_column, *reversed(mine))
     attended_parts = exchange(keep, give, n_frames)
     after = pl.pallas_call(
         residual_kernel,
         out_shape=struct(n_frames, places, width),
         in_specs=[VMEM] * 5,
         out_specs=VMEM,
-        compiler_params=params(32),
+        compiler_params=params(20),
+        cost_estimate=cost(4 * slots * inner * width),
         name="residual",
     )(attended, slot_column, blocks, modulation, spatial_proj)
     pad = -(-places // SUB) * SUB
-    mixed_keep, mixed_give = pl.pallas_call(
-        functools.partial(temporal_kernel, n_pair, places),
+    order = [0] + list(range(n_pair - 1, 0, -1))
+    steps = [order[:1], order[1:2]] if n_pair > 2 else [order[:1]]
+    last = order[len(steps) :]
+    before = []
+    for i, step in enumerate(steps):
+        before += [
+            pl.pallas_call(
+                functools.partial(project_kernel, places, len(step)),
+                out_shape=struct(2 * len(step), pad, 3 * inner),
+                in_specs=[VMEM] * (3 + 2 * len(step)),
+                out_specs=VMEM,
+                scratch_shapes=[pltpu.VMEM((2 * len(step) * places, width), F32)],
+                compiler_params=params(16),
+                cost_estimate=cost(2 * 2 * places * len(step) * 3 * inner * width),
+                name="project_%d" % i,
+            )(
+                modulation,
+                spatial_proj,
+                temporal_qkv,
+                *[tokens[s] for s in step],
+                *[attended_parts[s] for s in step],
+            )
+        ]
+    mixed = pl.pallas_call(
+        functools.partial(temporal_kernel, n_pair, places, len(last), order),
         out_shape=[struct(n_pair, places, inner)] * 2,
-        in_specs=[VMEM] * (3 + 2 * n_pair),
+        in_specs=[VMEM] * (3 + len(last) + n_pair),
         out_specs=[VMEM] * 2,
-        scratch_shapes=[pltpu.VMEM((n_frames, pad, inner), BF16)],
-        compiler_params=params(48),
+        scratch_shapes=[
+            pltpu.VMEM((2 * len(last) * places, width), F32),
+            pltpu.VMEM((n_frames, pad, inner), BF16),
+        ],
+        compiler_params=params(20),
         name="temporal",
-    )(modulation, spatial_proj, temporal_qkv, *tokens, *attended_parts)
+    )(
+        modulation,
+        spatial_proj,
+        temporal_qkv,
+        *[tokens[s] for s in last],
+        *[attended_parts[s] for s in last],
+        *before,
+    )
+    mixed_keep, mixed_give = mixed
     parts = exchange(mixed_keep, mixed_give, n_frames)
     out = pl.pallas_call(
         functools.partial(finish_kernel, n_pair, places),
         out_shape=struct(n_frames, places, width),
         in_specs=[VMEM] * (3 + n_pair),
         out_specs=VMEM,
-        compiler_params=params(32),
+        compiler_params=params(20),
         name="finish",
     )(modulation, temporal_proj, after, *parts)
     return out.reshape(1, rows, width)

time: 103 us -> 73.7 us (0.72)
  waiting for transfers between devices: 33.5 us -> 19.2 us
  local copies, waits for them, and re-layouts: 15.3 us -> 4.91 us
  Pallas kernels: 25.7 us -> 23.5 us
  starting transfers between devices: 25.1 us -> 23.5 us
    ppermute x18, waiting for transfers between devices: 33.5 us -> 19.2 us  [swap(): return lax.ppermute(block, axis, [(i, i ^ mask) for i in range(size)])]
    unnamed x14 -> x20, local copies, waits for them, and re-layouts: 15.2 us -> 4.09 us
    pallas_call x4 -> x6, Pallas kernels: 21.9 us -> 19.9 us  [the longest x1 5.7 us: shards(): pl.pallas_call(functools.partial(temporal_kernel, n_pair, places, len(las...]
    ppermute x18, starting transfers between devices: 25.1 us -> 23.5 us  [swap(): return lax.ppermute(block, axis, [(i, i ^ mask) for i in range(size)])]
  transfers between devices with their start and end apart: 18 -> 18, of which waited for: 8 -> 8; matrix products, arithmetic and copies ran while one was open for 8% -> 4% of each run, Pallas kernels for 6% -> 13%
where the time goes in v2:
time: 73.7 us; the launch traced here: 73.5 us
  Pallas kernels  23.5 us (32%)
  starting transfers between devices  23.5 us (32%)
  waiting for transfers between devices  19.2 us (26%)
  local copies, waits for them, and re-layouts  4.91 us (7%)
  other arithmetic  2.17 us (3%)
    ppermute x18, starting transfers between devices, swap(): return lax.ppermute(block, axis, [(i, i ^ mask) for i in range(size)])  23.5 us
    ppermute x18, waiting for transfers between devices, swap(): return lax.ppermute(block, axis, [(i, i ^ mask) for i in range(size)])  19.2 us
    pallas_call x1, Pallas kernels, shards(): pl.pallas_call(functools.partial(temporal_kernel, n_pair, places, len(las...  5.7 us
    pallas_call x2, Pallas kernels, shards(): pl.pallas_call(functools.partial(attention_kernel, n_space, slots, wide,...  5.25 us
    pallas_call x1, Pallas kernels, shards(): pl.pallas_call(functools.partial(merge_kernel, n_space, n_pair), out_shap...  5.21 us
    unnamed x20, local copies, waits for them, and re-layouts  4.09 us
    pallas_call x2, Pallas kernels, shards(): pl.pallas_call(functools.partial(project_kernel, places, len(step)), out_...  3.72 us
    squeeze x3, other arithmetic, exchange(): return swaps([both[s] for s in range(size // 2)], 'frames', size, 2)  2.17 us
  transfers between devices with their start and end apart: 18, of which 8 were waited for; matrix products, arithmetic and copies ran while one was open for 4% of the time, Pallas kernels for 13%

profile of v2, /device:TPU:0, one launch (start us, length us, event | category | flops | bytes accessed | tf_op | source)
XLA Modules:
  0.0 73.5 jit_solution(1354374521236505773)
XLA Ops:
  0.0 5.2 %merge.1 = (bf16[784,128]{1,0:T(8,128)(2,1)}, bf16[784,128]{1,0:T(8,128)(2,1)}, bf16[784,128]{1,0:T(8,128)(2,1)}, bf16[784,128]{1,0:T(8,128)(2,1)}, bf16[4,56,11...) custom-call(bf16[8,56,1152]{2,1,0:T(8,128)(2,1)} %bitcast.38, s32[1,448]{1,0:T(1,128)} %slot.1, f32[6,1152]{1,0:T(8,128)} %modulation.11, ...), custom_call_target="tpu_custom_call" | custom-call | tf_op jit(solution)/shard_map/merge/pallas_call | solution.py:268
  5.2 0.0 copy-start.7
  5.2 0.0 copy-start.2
  5.2 0.0 copy-start.5
  5.2 0.5 collective-permute-start.6
  5.8 4.7 %collective-permute-start = (bf16[784,128]{1,0:T(8,128)(2,1)}, bf16[784,128]{1,0:T(8,128)(2,1)S(1)}, u32[]{:S(2)}, u32[]{:S(2)}) collective-permute-start(bf16[784,128]{1,0:T(8,128)(2,1)} %get-tuple-element.31), channel_id=1, source_target_pairs={{0,3},{1,2},{2,1},{3,0},{4,7},{5,6},{6,5},{7,4},{8,11},{9,10},{10,... | collective-permute-start | bytes 602120 | tf_op jit(solution)/shard_map/ppermute | solution.py:244
  10.5 0.0 collective-permute-done.6
  10.5 2.0 %fusion.6 = (bf16[2,56,1152]{2,1,0:T(8,128)(2,1)}, bf16[2,56,1152]{2,1,0:T(8,128)(2,1)S(1)}, bf16[2,56,1152]{2,1,0:T(8,128)(2,1)S(1)}, bf16[2,56,1152]{2,1,0:T(8,128)(2,1)}) fusion(bf16[4,1,56,1152]{3,2,1,0:T(8,128)(2,1)S(1)} %bitcast.44, bf16[4,1,56,1152]{3,2,1,0:T(8,128)(2,1)} %bitcast.43), kind=kLoop, calls=%fused_computation.25 | loop fusion | flops 516096 | bytes 2064384 | tf_op jit(solution)/shard_map/squeeze | solution.py:255
  12.5 1.5 %collective-permute-start.7 = (bf16[2,56,1152]{2,1,0:T(8,128)(2,1)S(1)}, bf16[2,56,1152]{2,1,0:T(8,128)(2,1)S(1)}, u32[]{:S(2)}, u32[]{:S(2)}) collective-permute-start(bf16[2,56,1152]{2,1,0:T(8,128)(2,1)S(1)} %get-tuple-element.59), channel_id=1, source_target_pairs={{0,8},{4,12},{8,0},{12,4},{16,24},{20,28},{24,16},{28,20},{1,9},{5... | collective-permute-start | bytes 774152 | tf_op jit(solution)/shard_map/ppermute | solution.py:244
  14.0 1.0 %collective-permute-start.1 = (bf16[784,128]{1,0:T(8,128)(2,1)}, bf16[784,128]{1,0:T(8,128)(2,1)S(1)}, u32[]{:S(2)}, u32[]{:S(2)}) collective-permute-start(bf16[784,128]{1,0:T(8,128)(2,1)} %get-tuple-element.32), channel_id=1, source_target_pairs={{0,2},{1,3},{2,0},{3,1},{4,6},{5,7},{6,4},{7,5},{8,10},{9,11},{10,... | collective-permute-start | bytes 602120 | tf_op jit(solution)/shard_map/ppermute | solution.py:244
  15.0 1.6 %collective-permute-start.2 = (bf16[784,128]{1,0:T(8,128)(2,1)}, bf16[784,128]{1,0:T(8,128)(2,1)S(1)}, u32[]{:S(2)}, u32[]{:S(2)}) collective-permute-start(bf16[784,128]{1,0:T(8,128)(2,1)} %get-tuple-element.33), channel_id=1, source_target_pairs={{0,1},{1,0},{2,3},{3,2},{4,5},{5,4},{6,7},{7,6},{8,9},{9,8},{10,11... | collective-permute-start | bytes 602120 | tf_op jit(solution)/shard_map/ppermute | solution.py:244
  16.6 1.5 %collective-permute-start.8 = (bf16[2,56,1152]{2,1,0:T(8,128)(2,1)}, bf16[2,56,1152]{2,1,0:T(8,128)(2,1)S(1)}, u32[]{:S(2)}, u32[]{:S(2)}) collective-permute-start(bf16[2,56,1152]{2,1,0:T(8,128)(2,1)} %get-tuple-element.60), channel_id=1, source_target_pairs={{0,16},{4,20},{8,24},{12,28},{16,0},{20,4},{24,8},{28,12},{1,17},{... | collective-permute-start | bytes 774152 | tf_op jit(solution)/shard_map/ppermute | solution.py:244
  18.1 0.0 collective-permute-done.refs_0_
  18.1 1.0 %collective-permute-start.9 = (bf16[2,56,1152]{2,1,0:T(8,128)(2,1)}, bf16[2,56,1152]{2,1,0:T(8,128)(2,1)S(1)}, u32[]{:S(2)}, u32[]{:S(2)}) collective-permute-start(bf16[2,56,1152]{2,1,0:T(8,128)(2,1)} %get-tuple-element.57), channel_id=1, source_target_pairs={{0,24},{4,28},{8,16},{12,20},{16,8},{20,12},{24,0},{28,4},{1,25},{... | collective-permute-start | bytes 774152 | tf_op jit(solution)/shard_map/ppermute | solution.py:244
  19.1 9.2 %collective-permute-done.1.refs_1_ = bf16[784,128]{1,0:T(8,128)(2,1)S(1)} collective-permute-done((bf16[784,128]{1,0:T(8,128)(2,1)}, bf16[784,128]{1,0:T(8,128)(2,1)S(1)}, u32[]{:S(2)}, u32[]{:S(2)}) %collective-permute-start.1) | collective-permute-done | bytes 200736 | tf_op jit(solution)/shard_map/ppermute | solution.py:244
  28.3 0.0 collective-permute-done.2.refs_2_
  28.3 1.0 %copy-done.6 = bf16[784,128]{1,0:T(8,128)(2,1)S(1)} copy-done((bf16[784,128]{1,0:T(8,128)(2,1)S(1)}, bf16[784,128]{1,0:T(8,128)(2,1)}, u32[]{:S(2)}) %copy-start.6) | copy-done | bytes 200728
  29.3 3.7 %attend_others.1 = (bf16[256,128]{1,0:T(8,128)(2,1)S(1)}, bf16[256,128]{1,0:T(8,128)(2,1)S(1)}, bf16[256,128]{1,0:T(8,128)(2,1)}) custom-call(bf16[784,128]{1,0:T(8,128)(2,1)S(1)} %collective-permute-done.refs_0_, bf16[784,128]{1,0:T(8,128)(2,1)S(1)} %collective-permute-done.1.refs_1_, bf16[784,128]{1,0:T(8,128)(2,1)S(1)} %collective-permute-done.2.refs_2_, ...), custom_call_target="tpu_custom_call" | custom-call | flops 462422016 | bytes 4624220 | tf_op jit(solution)/shard_map/attend_others/pallas_call | solution.py:292
  33.0 2.5 %collective-permute-start.3 = (bf16[256,128]{1,0:T(8,128)(2,1)}, bf16[256,128]{1,0:T(8,128)(2,1)S(1)}, u32[]{:S(2)}, u32[]{:S(2)}) collective-permute-start(bf16[256,128]{1,0:T(8,128)(2,1)} %get-tuple-element.39), channel_id=1, source_target_pairs={{0,3},{1,2},{2,1},{3,0},{4,7},{5,6},{6,5},{7,4},{8,11},{9,10},{10,... | collective-permute-start | bytes 196616 | tf_op jit(solution)/shard_map/ppermute | solution.py:244
  35.5 0.0 collective-permute-start.4
  35.5 0.0 collective-permute-done.7.refs_1_
  35.5 1.9 %collective-permute-start.5 = (bf16[256,128]{1,0:T(8,128)(2,1)S(1)}, bf16[256,128]{1,0:T(8,128)(2,1)S(1)}, u32[]{:S(2)}, u32[]{:S(2)}) collective-permute-start(bf16[256,128]{1,0:T(8,128)(2,1)S(1)} %get-tuple-element.41), channel_id=1, source_target_pairs={{0,1},{1,0},{2,3},{3,2},{4,5},{5,4},{6,7},{7,6},{8,9},{9,8},{10,11... | collective-permute-start | bytes 196616 | tf_op jit(solution)/shard_map/ppermute | solution.py:244
  37.4 0.0 copy-done.8
  37.4 0.8 %copy.8.slot = s32[448,1]{1,0:T(8,128)S(1)} copy(s32[448,1]{0,1:T(1,128)} %bitcast.47) | data formatting | bytes 3584 | tf_op jit(solution)/shard_map/reshape | solution.py:266
  38.2 0.0 collective-permute-done.8.refs_0_
  38.2 0.0 collective-permute-done.9.refs_0_
  38.2 0.0 copy-done.7
  38.2 0.0 copy-start.9
  38.2 0.9 %copy-done.9 = bf16[784,128]{1,0:T(8,128)(2,1)S(1)} copy-done((bf16[784,128]{1,0:T(8,128)(2,1)S(1)}, bf16[784,128]{1,0:T(8,128)(2,1)}, u32[]{:S(2)}) %copy-start.9) | copy-done | bytes 200728
  39.2 1.6 %attend_own.1.refs_3_ = bf16[256,128]{1,0:T(8,128)(2,1)S(1)} custom-call(bf16[784,128]{1,0:T(8,128)(2,1)S(1)} %collective-permute-done.refs_0_, bf16[784,128]{1,0:T(8,128)(2,1)S(1)} %collective-permute-done.1.refs_1_, bf16[784,128]{1,0:T(8,128)(2,1)S(1)} %copy-done.9, bf16[784,128]{1,0:T(8,128)(2,1)S(1)} %copy-done.7), custom_call_target="tpu_custom_call" | custom-call | flops 462422016 | bytes 4624220 | tf_op jit(solution)/shard_map/attend_own/pallas_call | solution.py:292
  40.8 0.0 collective-permute-done.3.refs_0_
  40.8 0.7 collective-permute-done.4.refs_1_
  41.5 0.0 collective-permute-done.5.refs_2_
  41.5 0.6 expand.1
  42.1 0.1 collective-permute-start.10
  42.2 1.6 %collective-permute-done.10 = bf16[4,56,576]{2,1,0:T(8,128)(2,1)S(1)} collective-permute-done((bf16[4,56,576]{2,1,0:T(8,128)(2,1)S(1)}, bf16[4,56,576]{2,1,0:T(8,128)(2,1)S(1)}, u32[]{:S(2)}, u32[]{:S(2)}) %collective-permute-start.10) | collective-permute-done | bytes 258080 | tf_op jit(solution)/shard_map/ppermute | solution.py:244
  43.8 0.1 fusion.20
  43.9 2.5 %collective-permute-start.13 = (bf16[2,56,576]{2,1,0:T(8,128)(2,1)S(1)}, bf16[2,56,576]{2,1,0:T(8,128)(2,1)S(1)}, u32[]{:S(2)}, u32[]{:S(2)}) collective-permute-start(bf16[2,56,576]{2,1,0:T(8,128)(2,1)S(1)} %get-tuple-element.65), channel_id=1, source_target_pairs={{0,24},{4,28},{8,16},{12,20},{16,8},{20,12},{24,0},{28,4},{1,25},{... | collective-permute-start | bytes 387080 | tf_op jit(solution)/shard_map/ppermute | solution.py:244
  46.4 0.5 collective-permute-start.11
  46.9 0.5 collective-permute-start.12
  47.4 0.0 copy-done.2
  47.4 0.0 copy-done.5
  47.4 2.1 %copy-done = bf16[1152,1728]{0,1:T(8,128)(2,1)S(1)} copy-done((bf16[1152,1728]{0,1:T(8,128)(2,1)S(1)}, bf16[1152,1728]{0,1:T(8,128)(2,1)}, u32[]{:S(2)}) %copy-start) | copy-done | bytes 3981336
  49.5 1.9 %project_0.1.refs_4_ = bf16[2,64,1728]{2,1,0:T(8,128)(2,1)S(1)} custom-call(f32[6,1152]{1,0:T(8,128)S(1)} %copy-done.5, bf16[576,1152]{1,0:T(8,128)(2,1)S(1)} %copy-done.2, bf16[1728,1152]{1,0:T(8,128)(2,1)S(1)} %bitcast.35, bf16[2,56,1152]{2,1,0:T(8,128)(2,1)S(1)} %get-tuple-element.53.refs_0_, bf16[2,56,576]{2,1,0:T(8,128)(2,1)S(1)} %get-tuple-element.68.refs_1_), custom_call_target="tpu_custom_call" | custom-call | flops 445906944 | bytes 4459069 | tf_op jit(solution)/shard_map/project_0/pallas_call | solution.py:329
  51.4 0.0 copy-start.1
  51.4 0.0 collective-permute-done.13.refs_1_
  51.4 1.9 %project_1.1.refs_5_ = bf16[2,64,1728]{2,1,0:T(8,128)(2,1)S(1)} custom-call(f32[6,1152]{1,0:T(8,128)S(1)} %copy-done.5, bf16[576,1152]{1,0:T(8,128)(2,1)S(1)} %copy-done.2, bf16[1728,1152]{1,0:T(8,128)(2,1)S(1)} %bitcast.36, bf16[2,56,1152]{2,1,0:T(8,128)(2,1)S(1)} %collective-permute-done.9.refs_0_, bf16[2,56,576]{2,1,0:T(8,128)(2,1)S(1)} %collective-permute-done.13.refs_1_), custom_call_target="tpu_custom_call" | custom-call | flops 445906944 | bytes 4459069 | tf_op jit(solution)/shard_map/project_1/pallas_call | solution.py:329
  53.3 0.0 copy-start.3
  53.3 0.4 collective-permute-done.11.refs_2_
  53.7 0.1 collective-permute-done.12.refs_3_
  53.8 0.0 copy-done.1
  53.8 5.7 %temporal.1 = (bf16[4,56,576]{2,1,0:T(8,128)(2,1)S(1)}, bf16[4,56,576]{2,1,0:T(8,128)(2,1)S(1)}) custom-call(f32[6,1152]{1,0:T(8,128)S(1)} %copy-done.5, bf16[576,1152]{1,0:T(8,128)(2,1)S(1)} %copy-done.2, bf16[1728,1152]{1,0:T(8,128)(2,1)S(1)} %bitcast.37, bf16[2,56,1152]{2,1,0:T(8,128)(2,1)S(1)} %collective-permute-done.8.refs_0_, ...), custom_call_target="tpu_custom_call" | custom-call | tf_op jit(solution)/shard_map/temporal/pallas_call | solution.py:346
  59.5 0.0 copy-start.4
  59.5 0.1 collective-permute-start.14
  59.6 1.6 %collective-permute-done.14 = bf16[4,56,576]{2,1,0:T(8,128)(2,1)S(1)} collective-permute-done((bf16[4,56,576]{2,1,0:T(8,128)(2,1)S(1)}, bf16[4,56,576]{2,1,0:T(8,128)(2,1)S(1)}, u32[]{:S(2)}, u32[]{:S(2)}) %collective-permute-start.14) | collective-permute-done | bytes 258080 | tf_op jit(solution)/shard_map/ppermute | solution.py:244
  61.1 0.1 fusion.19
  61.2 1.6 %collective-permute-start.15 = (bf16[2,56,576]{2,1,0:T(8,128)(2,1)S(1)}, bf16[2,56,576]{2,1,0:T(8,128)(2,1)S(1)}, u32[]{:S(2)}, u32[]{:S(2)}) collective-permute-start(bf16[2,56,576]{2,1,0:T(8,128)(2,1)S(1)} %get-tuple-element.63), channel_id=1, source_target_pairs={{0,8},{4,12},{8,0},{12,4},{16,24},{20,28},{24,16},{28,20},{1,9},{5... | collective-permute-start | bytes 387080 | tf_op jit(solution)/shard_map/ppermute | solution.py:244
  62.8 1.3 %collective-permute-start.16 = (bf16[2,56,576]{2,1,0:T(8,128)(2,1)S(1)}, bf16[2,56,576]{2,1,0:T(8,128)(2,1)S(1)}, u32[]{:S(2)}, u32[]{:S(2)}) collective-permute-start(bf16[2,56,576]{2,1,0:T(8,128)(2,1)S(1)} %get-tuple-element.64), channel_id=1, source_target_pairs={{0,16},{4,20},{8,24},{12,28},{16,0},{20,4},{24,8},{28,12},{1,17},{... | collective-permute-start | bytes 387080 | tf_op jit(solution)/shard_map/ppermute | solution.py:244
  64.1 0.7 collective-permute-start.17
  64.8 0.9 %residual.1.after = bf16[8,56,1152]{2,1,0:T(8,128)(2,1)S(1)} custom-call(bf16[224,576]{1,0:T(8,128)(2,1)S(1)} %get-tuple-element.48.attended, s32[448,1]{1,0:T(8,128)S(1)} %copy.8.slot, bf16[8,56,1152]{2,1,0:T(8,128)(2,1)S(1)} %bitcast.39, f32[6,1152]{1,0:T(8,128)S(1)} %copy-done.5, bf16[576,1152]{1,0:T(8,128)(2,1)S(1)} %copy-done.2), custom_call_target="tpu_custom_call" | custom-call | flops 594542592 | bytes 5945425 | tf_op jit(solution)/shard_map/residual/pallas_call | solution.py:313
  65.7 2.0 %collective-permute-done.15.refs_1_ = bf16[2,56,576]{2,1,0:T(8,128)(2,1)S(1)} collective-permute-done((bf16[2,56,576]{2,1,0:T(8,128)(2,1)S(1)}, bf16[2,56,576]{2,1,0:T(8,128)(2,1)S(1)}, u32[]{:S(2)}, u32[]{:S(2)}) %collective-permute-start.15) | collective-permute-done | bytes 129056 | tf_op jit(solution)/shard_map/ppermute | solution.py:244
  67.7 3.7 %collective-permute-done.16.refs_2_ = bf16[2,56,576]{2,1,0:T(8,128)(2,1)S(1)} collective-permute-done((bf16[2,56,576]{2,1,0:T(8,128)(2,1)S(1)}, bf16[2,56,576]{2,1,0:T(8,128)(2,1)S(1)}, u32[]{:S(2)}, u32[]{:S(2)}) %collective-permute-start.16) | collective-permute-done | bytes 129056 | tf_op jit(solution)/shard_map/ppermute | solution.py:244
  71.4 0.0 collective-permute-done.17.refs_3_
  71.4 2.1 %finish.1 = bf16[8,56,1152]{2,1,0:T(8,128)(2,1)} custom-call(f32[6,1152]{1,0:T(8,128)S(1)} %copy-done.5, bf16[576,1152]{1,0:T(8,128)(2,1)S(1)} %copy-done.4, bf16[8,56,1152]{2,1,0:T(8,128)(2,1)S(1)} %residual.1.after, bf16[2,56,576]{2,1,0:T(8,128)(2,1)S(1)} %get-tuple-element.62.refs_0_, bf16[2,56,576]{2,1,0:T(8,128)(2,1)S(1)} %collective-permute-done.15.refs_1_, ...), custom_call_target="tpu_custom_call" | custom-call | tf_op jit(solution)/shard_map/finish/pallas_call | solution.py:367
  (5 shorter events, 0.0 us)
Async XLA Ops:
  5.2 33.0 %copy-start.7 = (bf16[784,128]{1,0:T(8,128)(2,1)S(1)}, bf16[784,128]{1,0:T(8,128)(2,1)}, u32[]{:S(2)}) copy-start(bf16[784,128]{1,0:T(8,128)(2,1)} %get-tuple-element.47.refs_3_) | copy-start | bytes 602116
  5.2 42.2 %copy-start.2 = (bf16[576,1152]{1,0:T(8,128)(2,1)S(1)}, bf16[576,1152]{1,0:T(8,128)(2,1)}, u32[]{:S(2)}) copy-start(bf16[576,1152]{1,0:T(8,128)(2,1)} %proj.8) | copy-start | bytes 3981316
  5.2 42.2 %copy-start.5 = (f32[6,1152]{1,0:T(8,128)S(1)}, f32[6,1152]{1,0:T(8,128)}, u32[]{:S(2)}) copy-start(f32[6,1152]{1,0:T(8,128)} %modulation.11) | copy-start | bytes 82948
  5.2 5.2 %collective-permute-start.6 = (bf16[4,56,1152]{2,1,0:T(8,128)(2,1)}, bf16[4,56,1152]{2,1,0:T(8,128)(2,1)S(1)}, u32[]{:S(2)}, u32[]{:S(2)}) collective-permute-start(bf16[4,56,1152]{2,1,0:T(8,128)(2,1)} %get-tuple-element.43), channel_id=1, source_target_pairs={{0,4},{4,0},{8,12},{12,8},{16,20},{20,16},{24,28},{28,24},{1,5},{5... | collective-permute-start | bytes 1548296 | tf_op jit(solution)/shard_map/ppermute | solution.py:244
  5.8 12.3 %collective-permute-start = (bf16[784,128]{1,0:T(8,128)(2,1)}, bf16[784,128]{1,0:T(8,128)(2,1)S(1)}, u32[]{:S(2)}, u32[]{:S(2)}) collective-permute-start(bf16[784,128]{1,0:T(8,128)(2,1)} %get-tuple-element.31), channel_id=1, source_target_pairs={{0,3},{1,2},{2,1},{3,0},{4,7},{5,6},{6,5},{7,4},{8,11},{9,10},{10,... | collective-permute-start | bytes 602120 | tf_op jit(solution)/shard_map/ppermute | solution.py:244
  12.5 23.0 %collective-permute-start.7 = (bf16[2,56,1152]{2,1,0:T(8,128)(2,1)S(1)}, bf16[2,56,1152]{2,1,0:T(8,128)(2,1)S(1)}, u32[]{:S(2)}, u32[]{:S(2)}) collective-permute-start(bf16[2,56,1152]{2,1,0:T(8,128)(2,1)S(1)} %get-tuple-element.59), channel_id=1, source_target_pairs={{0,8},{4,12},{8,0},{12,4},{16,24},{20,28},{24,16},{28,20},{1,9},{5... | collective-permute-start | bytes 774152 | tf_op jit(solution)/shard_map/ppermute | solution.py:244
  14.0 14.3 %collective-permute-start.1 = (bf16[784,128]{1,0:T(8,128)(2,1)}, bf16[784,128]{1,0:T(8,128)(2,1)S(1)}, u32[]{:S(2)}, u32[]{:S(2)}) collective-permute-start(bf16[784,128]{1,0:T(8,128)(2,1)} %get-tuple-element.32), channel_id=1, source_target_pairs={{0,2},{1,3},{2,0},{3,1},{4,6},{5,7},{6,4},{7,5},{8,10},{9,11},{10,... | collective-permute-start | bytes 602120 | tf_op jit(solution)/shard_map/ppermute | solution.py:244
  15.0 13.4 %collective-permute-start.2 = (bf16[784,128]{1,0:T(8,128)(2,1)}, bf16[784,128]{1,0:T(8,128)(2,1)S(1)}, u32[]{:S(2)}, u32[]{:S(2)}) collective-permute-start(bf16[784,128]{1,0:T(8,128)(2,1)} %get-tuple-element.33), channel_id=1, source_target_pairs={{0,1},{1,0},{2,3},{3,2},{4,5},{5,4},{6,7},{7,6},{8,9},{9,8},{10,11... | collective-permute-start | bytes 602120 | tf_op jit(solution)/shard_map/ppermute | solution.py:244
  16.6 21.7 %collective-permute-start.8 = (bf16[2,56,1152]{2,1,0:T(8,128)(2,1)}, bf16[2,56,1152]{2,1,0:T(8,128)(2,1)S(1)}, u32[]{:S(2)}, u32[]{:S(2)}) collective-permute-start(bf16[2,56,1152]{2,1,0:T(8,128)(2,1)} %get-tuple-element.60), channel_id=1, source_target_pairs={{0,16},{4,20},{8,24},{12,28},{16,0},{20,4},{24,8},{28,12},{1,17},{... | collective-permute-start | bytes 774152 | tf_op jit(solution)/shard_map/ppermute | solution.py:244
  18.1 20.1 %collective-permute-start.9 = (bf16[2,56,1152]{2,1,0:T(8,128)(2,1)}, bf16[2,56,1152]{2,1,0:T(8,128)(2,1)S(1)}, u32[]{:S(2)}, u32[]{:S(2)}) collective-permute-start(bf16[2,56,1152]{2,1,0:T(8,128)(2,1)} %get-tuple-element.57), channel_id=1, source_target_pairs={{0,24},{4,28},{8,16},{12,20},{16,8},{20,12},{24,0},{28,4},{1,25},{... | collective-permute-start | bytes 774152 | tf_op jit(solution)/shard_map/ppermute | solution.py:244
  28.3 9.1 %copy-start.8 = (bf16[784,128]{1,0:T(8,128)(2,1)}, bf16[784,128]{1,0:T(8,128)(2,1)S(1)}, u32[]{:S(2)}) copy-start(bf16[784,128]{1,0:T(8,128)(2,1)S(1)} %collective-permute-done.2.refs_2_) | copy-start | bytes 602116
  28.3 1.0 %copy-start.6 = (bf16[784,128]{1,0:T(8,128)(2,1)S(1)}, bf16[784,128]{1,0:T(8,128)(2,1)}, u32[]{:S(2)}) copy-start(bf16[784,128]{1,0:T(8,128)(2,1)} %get-tuple-element.47.refs_3_) | copy-start | bytes 602116
  33.0 7.8 %collective-permute-start.3 = (bf16[256,128]{1,0:T(8,128)(2,1)}, bf16[256,128]{1,0:T(8,128)(2,1)S(1)}, u32[]{:S(2)}, u32[]{:S(2)}) collective-permute-start(bf16[256,128]{1,0:T(8,128)(2,1)} %get-tuple-element.39), channel_id=1, source_target_pairs={{0,3},{1,2},{2,1},{3,0},{4,7},{5,6},{6,5},{7,4},{8,11},{9,10},{10,... | collective-permute-start | bytes 196616 | tf_op jit(solution)/shard_map/ppermute | solution.py:244
  35.5 6.0 %collective-permute-start.4 = (bf16[256,128]{1,0:T(8,128)(2,1)S(1)}, bf16[256,128]{1,0:T(8,128)(2,1)S(1)}, u32[]{:S(2)}, u32[]{:S(2)}) collective-permute-start(bf16[256,128]{1,0:T(8,128)(2,1)S(1)} %get-tuple-element.40), channel_id=1, source_target_pairs={{0,2},{1,3},{2,0},{3,1},{4,6},{5,7},{6,4},{7,5},{8,10},{9,11},{10,... | collective-permute-start | bytes 196616 | tf_op jit(solution)/shard_map/ppermute | solution.py:244
  35.5 6.0 %collective-permute-start.5 = (bf16[256,128]{1,0:T(8,128)(2,1)S(1)}, bf16[256,128]{1,0:T(8,128)(2,1)S(1)}, u32[]{:S(2)}, u32[]{:S(2)}) collective-permute-start(bf16[256,128]{1,0:T(8,128)(2,1)S(1)} %get-tuple-element.41), channel_id=1, source_target_pairs={{0,1},{1,0},{2,3},{3,2},{4,5},{5,4},{6,7},{7,6},{8,9},{9,8},{10,11... | collective-permute-start | bytes 196616 | tf_op jit(solution)/shard_map/ppermute | solution.py:244
  38.2 0.9 %copy-start.9 = (bf16[784,128]{1,0:T(8,128)(2,1)S(1)}, bf16[784,128]{1,0:T(8,128)(2,1)}, u32[]{:S(2)}) copy-start(bf16[784,128]{1,0:T(8,128)(2,1)} %copy-done.8) | copy-start | bytes 602116
  42.1 1.6 %collective-permute-start.10 = (bf16[4,56,576]{2,1,0:T(8,128)(2,1)S(1)}, bf16[4,56,576]{2,1,0:T(8,128)(2,1)S(1)}, u32[]{:S(2)}, u32[]{:S(2)}) collective-permute-start(bf16[4,56,576]{2,1,0:T(8,128)(2,1)S(1)} %get-tuple-element.52), channel_id=1, source_target_pairs={{0,4},{4,0},{8,12},{12,8},{16,20},{20,16},{24,28},{28,24},{1,5},{5... | collective-permute-start | bytes 774152 | tf_op jit(solution)/shard_map/ppermute | solution.py:244
  43.9 7.6 %collective-permute-start.13 = (bf16[2,56,576]{2,1,0:T(8,128)(2,1)S(1)}, bf16[2,56,576]{2,1,0:T(8,128)(2,1)S(1)}, u32[]{:S(2)}, u32[]{:S(2)}) collective-permute-start(bf16[2,56,576]{2,1,0:T(8,128)(2,1)S(1)} %get-tuple-element.65), channel_id=1, source_target_pairs={{0,24},{4,28},{8,16},{12,20},{16,8},{20,12},{24,0},{28,4},{1,25},{... | collective-permute-start | bytes 387080 | tf_op jit(solution)/shard_map/ppermute | solution.py:244
  46.4 7.3 %collective-permute-start.11 = (bf16[2,56,576]{2,1,0:T(8,128)(2,1)S(1)}, bf16[2,56,576]{2,1,0:T(8,128)(2,1)S(1)}, u32[]{:S(2)}, u32[]{:S(2)}) collective-permute-start(bf16[2,56,576]{2,1,0:T(8,128)(2,1)S(1)} %get-tuple-element.66), channel_id=1, source_target_pairs={{0,16},{4,20},{8,24},{12,28},{16,0},{20,4},{24,8},{28,12},{1,17},{... | collective-permute-start | bytes 387080 | tf_op jit(solution)/shard_map/ppermute | solution.py:244
  46.9 6.9 %collective-permute-start.12 = (bf16[2,56,576]{2,1,0:T(8,128)(2,1)S(1)}, bf16[2,56,576]{2,1,0:T(8,128)(2,1)S(1)}, u32[]{:S(2)}, u32[]{:S(2)}) collective-permute-start(bf16[2,56,576]{2,1,0:T(8,128)(2,1)S(1)} %get-tuple-element.67), channel_id=1, source_target_pairs={{0,8},{4,12},{8,0},{12,4},{16,24},{20,28},{24,16},{28,20},{1,9},{5... | collective-permute-start | bytes 387080 | tf_op jit(solution)/shard_map/ppermute | solution.py:244
  47.4 2.1 %copy-start = (bf16[1152,1728]{0,1:T(8,128)(2,1)S(1)}, bf16[1152,1728]{0,1:T(8,128)(2,1)}, u32[]{:S(2)}) copy-start(bf16[1152,1728]{0,1:T(8,128)(2,1)} %param.12) | copy-start | bytes 11943940
  51.4 2.4 %copy-start.1 = (bf16[1152,1728]{0,1:T(8,128)(2,1)S(1)}, bf16[1152,1728]{0,1:T(8,128)(2,1)}, u32[]{:S(2)}) copy-start(bf16[1152,1728]{0,1:T(8,128)(2,1)} %param.12) | copy-start | bytes 11943940
  53.3 11.5 %copy-start.3 = (bf16[1,448,1152]{2,1,0:T(8,128)(2,1)S(1)}, bf16[1,448,1152]{2,1,0:T(8,128)(2,1)}, u32[]{:S(2)}) copy-start(bf16[1,448,1152]{2,1,0:T(8,128)(2,1)} %param.7) | copy-start | bytes 3096580
  59.5 11.9 %copy-start.4 = (bf16[576,1152]{1,0:T(8,128)(2,1)S(1)}, bf16[576,1152]{1,0:T(8,128)(2,1)}, u32[]{:S(2)}) copy-start(bf16[576,1152]{1,0:T(8,128)(2,1)} %proj.9) | copy-start | bytes 3981316
  59.5 1.6 %collective-permute-start.14 = (bf16[4,56,576]{2,1,0:T(8,128)(2,1)S(1)}, bf16[4,56,576]{2,1,0:T(8,128)(2,1)S(1)}, u32[]{:S(2)}, u32[]{:S(2)}) collective-permute-start(bf16[4,56,576]{2,1,0:T(8,128)(2,1)S(1)} %get-tuple-element.56), channel_id=1, source_target_pairs={{0,4},{4,0},{8,12},{12,8},{16,20},{20,16},{24,28},{28,24},{1,5},{5... | collective-permute-start | bytes 774152 | tf_op jit(solution)/shard_map/ppermute | solution.py:244
  61.2 6.5 %collective-permute-start.15 = (bf16[2,56,576]{2,1,0:T(8,128)(2,1)S(1)}, bf16[2,56,576]{2,1,0:T(8,128)(2,1)S(1)}, u32[]{:S(2)}, u32[]{:S(2)}) collective-permute-start(bf16[2,56,576]{2,1,0:T(8,128)(2,1)S(1)} %get-tuple-element.63), channel_id=1, source_target_pairs={{0,8},{4,12},{8,0},{12,4},{16,24},{20,28},{24,16},{28,20},{1,9},{5... | collective-permute-start | bytes 387080 | tf_op jit(solution)/shard_map/ppermute | solution.py:244
  62.8 8.6 %collective-permute-start.16 = (bf16[2,56,576]{2,1,0:T(8,128)(2,1)S(1)}, bf16[2,56,576]{2,1,0:T(8,128)(2,1)S(1)}, u32[]{:S(2)}, u32[]{:S(2)}) collective-permute-start(bf16[2,56,576]{2,1,0:T(8,128)(2,1)S(1)} %get-tuple-element.64), channel_id=1, source_target_pairs={{0,16},{4,20},{8,24},{12,28},{16,0},{20,4},{24,8},{28,12},{1,17},{... | collective-permute-start | bytes 387080 | tf_op jit(solution)/shard_map/ppermute | solution.py:244
  64.1 7.3 %collective-permute-start.17 = (bf16[2,56,576]{2,1,0:T(8,128)(2,1)S(1)}, bf16[2,56,576]{2,1,0:T(8,128)(2,1)S(1)}, u32[]{:S(2)}, u32[]{:S(2)}) collective-permute-start(bf16[2,56,576]{2,1,0:T(8,128)(2,1)S(1)} %get-tuple-element.61), channel_id=1, source_target_pairs={{0,24},{4,28},{8,16},{12,20},{16,8},{20,12},{24,0},{28,4},{1,25},{... | collective-permute-start | bytes 387080 | tf_op jit(solution)/shard_map/ppermute | solution.py:244

commit v3 on v2

--- a/solution.py
+++ b/solution.py
@@ -43,112 +43,158 @@
 
 def packing(rows, width):
     full, rest = divmod(width, LANES)
-    groups = 1
-    if rest:
-        units = rows // SUB
-        groups = max([g for g in range(1, units + 1) if units % g == 0 and g * rest <= LANES and rows % SUB == 0] or [1])
-    return full, rest, groups
+    free = LANES - rest
+    parts = rest // free + 1 if rest and rest % free == 0 else 1
+    high = -(-rows // (8 * parts)) * 8
+    if rows - high * (parts - 1) <= 0 or parts == 1:
+        parts, high = 1, rows
+    return full, rest, parts, high
 
 
 def packed_rows(rows, width):
-    full, rest, groups = packing(rows, width)
-    return full * rows + (rows // groups if rest else 0)
+    full, rest, parts, high = packing(rows, width)
+    return -(-(full * rows + (max(parts - 1, 1) * high if rest else 0)) // SUB) * SUB
 
 
 def pack(block):
     rows, width = block.shape
-    full, rest, groups = packing(rows, width)
-    parts = [block[:, j * LANES : (j + 1) * LANES] for j in range(full)]
+    full, rest, parts, high = packing(rows, width)
+    pieces = [block[:, j * LANES : (j + 1) * LANES] for j in range(full)]
     if rest:
-        high = rows // groups
-        tail = block[:, full * LANES :]
-        pieces = [tail[i * high : (i + 1) * high] for i in range(groups)]
-        if groups * rest < LANES:
-            pieces.append(jnp.zeros((high, LANES - groups * rest), block.dtype))
-        parts.append(jnp.concatenate(pieces, 1))
-    return jnp.concatenate(parts, 0)
+        tail, free = block[:, full * LANES :], LANES - rest
+        if parts == 1:
+            pieces.append(jnp.concatenate([tail, jnp.zeros((rows, free), block.dtype)], 1))
+        else:
+            last = tail[(parts - 1) * high :]
+            if last.shape[0] < high:
+                last = jnp.concatenate([last, jnp.zeros((high - last.shape[0], rest), block.dtype)], 0)
+            for i in range(parts - 1):
+                side = last[:, i * free : (i + 1) * free]
+                pieces.append(jnp.concatenate([tail[i * high : (i + 1) * high], side], 1))
+    here = sum(p.shape[0] for p in pieces)
+    if here % SUB:
+        pieces.append(jnp.zeros((-here % SUB, LANES), block.dtype))
+    return jnp.concatenate(pieces, 0)
 
 
 def unpack(packed, rows, width):
-    full, rest, groups = packing(rows, width)
-    parts = [packed[j * rows : (j + 1) * rows] for j in range(full)]
+    full, rest, parts, high = packing(rows, width)
+    pieces = [packed[j * rows : (j + 1) * rows] for j in range(full)]
     if rest:
-        high = rows // groups
-        tail = packed[full * rows : full * rows + high]
-        pieces = [tail[:, i * rest : (i + 1) * rest] for i in range(groups)]
-        parts.append(jnp.concatenate(pieces, 0))
-    return jnp.concatenate(parts, 1)
-
-
-def merge_kernel(n_space, n_pair, latents, slot, modulation, weights, *refs):
-    outs, (keep, give, held, tokens, slots_in, mods, arrived, sems) = refs[:n_space], refs[n_space:]
-    pairs = ((latents, tokens), (slot, slots_in), (modulation, mods), (weights, arrived))
+        tail = packed[full * rows :]
+        if parts == 1:
+            pieces.append(tail[:rows, :rest])
+        else:
+            tiles = [tail[i * high : (i + 1) * high] for i in range(parts - 1)]
+            last = jnp.concatenate([t[:, rest:] for t in tiles], 1)[: rows - (parts - 1) * high]
+            pieces.append(jnp.concatenate([t[:, :rest] for t in tiles] + [last], 0))
+    return jnp.concatenate(pieces, 1)
+
+
+def merge_kernel(n_space, latents, slot, modulation, weights, out, merged, tokens, slots_in, mods, arrived, sems):
+    me = lax.axis_index("space")
+    inner = weights.shape[0] // 3
+    wide = inner // n_space
+    theirs = pl.multiple_of((me ^ (n_space - 1)) * wide, SUB)
+    pairs = [(latents, tokens), (slot, slots_in), (modulation, mods)]
+    pairs += [(weights.at[pl.ds(j * inner + theirs, wide)], arrived.at[pl.ds(j * wide, wide)]) for j in range(3)]
     copies = [pltpu.make_async_copy(there, here, sems.at[i]) for i, (there, here) in enumerate(pairs)]
     for copy in copies:
         copy.start()
-    me, frame = lax.axis_index("space"), lax.axis_index("frames")
-    places, width = latents.shape[1:]
-    rows = 2 * n_pair * places
+    n_frames, places = latents.shape[:2]
+    rows = n_frames * places
     slots = rows // 2
-    inner = weights.shape[0] // 3
-    wide = inner // n_space
     for copy in copies[:3]:
         copy.wait()
     shift, scale = mods[0:1], 1.0 + mods[1:2]
     normed = jnp.concatenate(
-        [layer_norm(tokens[f].astype(F32)) * scale + shift for f in range(2 * n_pair)], 0
+        [layer_norm(tokens[f].astype(F32)) * scale + shift for f in range(n_frames)], 0
     ).astype(BF16)
     local = slots_in[...] - me * slots
     chosen = lax.broadcasted_iota(jnp.int32, (slots, rows), 0) == local
     counts = jnp.sum(chosen.astype(F32), 1, keepdims=True)
-    merged = (dot(chosen.astype(BF16), normed) / counts).astype(BF16)
+    held = (dot(chosen.astype(BF16), normed) / counts).astype(BF16)
+    merged[...] = held
+    for copy in copies[3:]:
+        copy.wait()
+    projected = dot_t(arrived[...], held)
+    out[...] = pack(jnp.concatenate([projected[:wide] * SCALE, projected[wide:]], 0)).astype(BF16)
+
+
+def spread_kernel(n_space, merged, weights, *refs):
+    outs, (held, arrived, sem) = refs[: n_space - 1], refs[n_space - 1 :]
+    copy = pltpu.make_async_copy(weights, arrived, sem)
+    copy.start()
+    me = lax.axis_index("space")
+    inner = weights.shape[0] // 3
+    wide = inner // n_space
+    copy.wait()
+    projected = dot_t(arrived[...], merged[...])
+    for j in range(3):
+        for d in range(n_space):
+            part = projected[j * inner + d * wide : j * inner + (d + 1) * wide]
+            held[d, j * wide : (j + 1) * wide] = part * SCALE if j == 0 else part
+    for s in range(n_space - 1):
+        outs[s][...] = pack(held[me ^ s]).astype(BF16)
+
+
+def share_kernel(n_pair, latents, keep, give):
+    frame = lax.axis_index("frames")
     for s in range(n_pair):
-        keep[s] = tokens[frame ^ (2 * s)]
-        give[s] = tokens[frame ^ (2 * s + 1)]
-    copies[3].wait()
-    projected = dot_t(merged, arrived[...])
-    queries = (projected[:, :inner] * SCALE).astype(BF16)
-    others = projected[:, inner:].astype(BF16)
-    for d in range(n_space):
-        at = d * wide
-        held[d] = pack(
-            jnp.concatenate(
-                [queries[:, at : at + wide], others[:, at : at + wide], others[:, inner + at : inner + at + wide]], 1
-            )
-        )
-    for s in range(n_space):
-        outs[s][...] = held[me ^ s]
-
-
-def attention_kernel(n_space, slots, wide, asked, *refs):
-    ins, outs = refs[:n_space], refs[n_space:]
-    blocks = [unpack(r[...], slots, 3 * wide) for r in reversed(ins)]
-    results = [[] for _ in range(n_space)]
-    for h in range(wide // HD):
-        keys = jnp.concatenate([b[:, wide + h * HD : wide + (h + 1) * HD] for b in blocks], 0)
-        vals = jnp.concatenate([b[:, 2 * wide + h * HD : 2 * wide + (h + 1) * HD] for b in blocks], 0)
-        vals = jnp.concatenate([vals, jnp.ones((vals.shape[0], LANES - HD), BF16)], 1)
-        for s in asked:
-            query = blocks[s][:, h * HD : (h + 1) * HD]
-            scores = dot_t(query, keys)
-            top = jnp.max(scores, -1, keepdims=True)
-            mixed = dot(jnp.exp2(scores - top).astype(BF16), vals)
-            results[s].append((mixed[:, :HD] / mixed[:, HD : HD + 1]).astype(BF16))
-    for out, s in zip(outs, asked):
-        out[...] = pack(jnp.concatenate(results[s], 1))
-
-
-def expand_kernel(n_space, n_pair, slots, wide, slot, *refs):
+        keep[s] = latents[frame ^ (2 * s)]
+        give[s] = latents[frame ^ (2 * s + 1)]
+
+
+def prepare_kernel(wide, packed, slot, keys, others, chosen):
+    slots, rows = keys.shape[0], slot.shape[1]
+    local = slot[...] - lax.axis_index("space") * slots
+    joined = (lax.broadcasted_iota(jnp.int32, (slots, rows), 0) == local).astype(F32)
+    chosen[...] = joined.T.astype(BF16)
+    block = unpack(packed[...].astype(F32), 3 * wide, slots)
+    keys[...] = block[wide : 2 * wide].T.astype(BF16)
+    others[...] = jnp.concatenate([block[:wide], block[2 * wide :]], 0).astype(BF16)
+
+
+def attend(queries, keys, vals):
+    ones = jnp.ones((8, vals.shape[1]), F32)
+    results = []
+    for h in range(vals.shape[0] // HD):
+        at = slice(h * HD, (h + 1) * HD)
+        scores = dot(keys[:, at], queries[at].astype(BF16))
+        weights = jnp.exp2(scores - jnp.max(scores, 0, keepdims=True)).astype(BF16)
+        mixed = dot(jnp.concatenate([vals[at], ones], 0).astype(BF16), weights)
+        results.append(mixed[:HD] / mixed[HD : HD + 1])
+    return jnp.concatenate(results, 0)
+
+
+def others_kernel(n_space, slots, wide, far_keys, far_others, *refs):
+    ins, outs, (own_queries, all_keys, all_vals) = refs[: n_space - 1], refs[n_space - 1 : -3], refs[-3:]
+    blocks = [unpack(r[...].astype(F32), 3 * wide, slots) for r in reversed(ins)]
+    others = far_others[...].astype(F32)
+    queries = jnp.concatenate([b[:wide] for b in blocks[1:]] + [others[:wide]], 1)
+    vals = jnp.concatenate([b[2 * wide :] for b in blocks] + [others[wide:]], 1)
+    keys = jnp.concatenate([b[wide : 2 * wide].T.astype(BF16) for b in blocks] + [far_keys[...]], 0)
+    own_queries[...] = blocks[0][:wide].astype(BF16)
+    all_keys[...] = keys
+    all_vals[...] = vals.astype(BF16)
+    whole = attend(queries, keys, vals)
+    for i, out in enumerate(outs):
+        out[...] = pack(whole[:, i * slots : (i + 1) * slots]).astype(BF16)
+
+
+def own_kernel(queries, keys, vals, out):
+    out[...] = attend(queries[...].astype(F32), keys[...], vals[...].astype(F32)).astype(BF16)
+
+
+def expand_kernel(n_space, n_pair, slots, wide, chosen, *refs):
     ins, (keep, give, attended, held, spread) = refs[:n_space], refs[n_space:]
     me, frame = lax.axis_index("space"), lax.axis_index("frames")
-    for s in range(n_space):
-        held[me ^ s] = unpack(ins[n_space - 1 - s][...], slots, wide)
-    whole = jnp.concatenate([held[d] for d in range(n_space)], 1)
+    held[me] = ins[n_space - 1][...].astype(F32)
+    for s in range(1, n_space):
+        held[me ^ s] = unpack(ins[n_space - 1 - s][...].astype(F32), wide, slots)
+    whole = jnp.concatenate([held[d] for d in range(n_space)], 0).astype(BF16)
     attended[...] = whole
-    local = slot[...] - me * slots
-    rows = slot.shape[0]
-    chosen = (lax.broadcasted_iota(jnp.int32, (rows, slots), 1) == local).astype(BF16)
-    wanted = dot(chosen, whole)
+    wanted = dot_t(chosen[...], whole)
     places = keep.shape[1]
     for f in range(2 * n_pair):
         spread[f] = wanted[f * places : (f + 1) * places].astype(BF16)
@@ -161,16 +207,18 @@
     return pl.CostEstimate(flops=flops, bytes_accessed=flops // 100, transcendentals=0)
 
 
-def residual_kernel(attended, slot, latents, modulation, proj, after):
-    me = lax.axis_index("space")
-    slots, rows = attended.shape[0], slot.shape[0]
+def residual_kernel(attended, chosen, latents, modulation, proj, after):
     places = latents.shape[1]
-    out = dot(attended[...], proj[...]).astype(BF16)
-    local = slot[...] - me * slots
-    chosen = (lax.broadcasted_iota(jnp.int32, (rows, slots), 1) == local).astype(BF16)
-    spread = modulation[2:3] * dot(chosen, out)
+    out = dot(attended[...].astype(F32).T.astype(BF16), proj[...]).astype(BF16)
+    spread = modulation[2:3] * dot(chosen[...], out)
     for f in range(latents.shape[0]):
         after[f] = (latents[f].astype(F32) + spread[f * places : (f + 1) * places]).astype(BF16)
+
+
+def pair_kernel(keep, got, *outs):
+    for s, out in enumerate(outs):
+        out[0] = keep[s]
+        out[1] = got[s]
 
 
 def project_blocks(places, modulation, proj, weights, tokens, results, normed):
@@ -208,19 +256,25 @@
     size = n_frames * SUB
     row = lax.broadcasted_iota(jnp.int32, (size, size), 0)
     col = lax.broadcasted_iota(jnp.int32, (size, size), 1)
-    same = ((row & (SUB - 1)) == (col & (SUB - 1)))[None]
-    ones = jnp.ones((size, LANES - HD), BF16)
+    same = jnp.concatenate([(row & (SUB - 1)) == (col & (SUB - 1))] * heads, 1)
     for g in range(groups):
         block = jnp.concatenate([b[g * SUB : (g + 1) * SUB] for b in by_frame], 0)
 
         def part(j, h):
             return block[:, j * inner + h * HD : j * inner + (h + 1) * HD]
 
-        scores = jnp.concatenate([dot_t(part(0, h), part(1, h)) for h in range(heads)], 0)
-        scores = jnp.where(same, scores.reshape(heads, size, size), -jnp.inf)
-        mix = jnp.exp2((scores - jnp.max(scores, -1, keepdims=True)) * SCALE).astype(BF16)
-        mixed = [dot(mix[h], jnp.concatenate([part(2, h), ones], 1)) for h in range(heads)]
-        whole = jnp.concatenate([(m[:, :HD] / m[:, HD : HD + 1]).astype(BF16) for m in mixed], 1)
+        scores = jnp.concatenate([dot_t(part(1, h), part(0, h)) for h in range(heads)], 1)
+        scores = jnp.where(same, scores, -jnp.inf)
+        mix = jnp.exp2((scores - jnp.max(scores, 0, keepdims=True)) * SCALE)
+        total = jnp.sum(mix, 0, keepdims=True)
+        mix = mix.astype(BF16)
+        vals = block[:, 2 * inner :].astype(F32).T
+        mixed = [
+            dot(vals[h * HD : (h + 1) * HD].astype(BF16), mix[:, h * size : (h + 1) * size])
+            / total[:, h * size : (h + 1) * size]
+            for h in range(heads)
+        ]
+        whole = jnp.concatenate(mixed, 0).T.astype(BF16)
         for f in range(n_frames):
             held[f, g * SUB : (g + 1) * SUB] = whole[f * SUB : (f + 1) * SUB]
     for i, s in enumerate(order):
@@ -228,15 +282,15 @@
         give[s] = held[2 * i + 1][:places]
 
 
-def finish_kernel(n_pair, places, modulation, proj, after, *refs):
-    parts, out = refs[:n_pair], refs[n_pair]
+def finish_kernel(taken, places, modulation, proj, after, *refs):
+    parts, out = refs[: len(taken)], refs[-1]
     frame = lax.axis_index("frames")
-    frames = [(s, t) for s in range(n_pair) for t in range(2)]
+    frames = [(s, t) for s in range(len(taken)) for t in range(2)]
     mixed = jnp.concatenate([parts[s][t].astype(F32) for s, t in frames], 0).astype(BF16)
     branch = dot(mixed, proj[...])
     gate = modulation[5:6]
-    for k in range(2 * n_pair):
-        at = frame ^ k
+    for k, (s, t) in enumerate(frames):
+        at = frame ^ (2 * taken[s] + t)
         out[at] = (after[at].astype(F32) + gate * branch[k * places : (k + 1) * places]).astype(BF16)
 
 
@@ -251,8 +305,15 @@
 
 def exchange(keep, give, size):
     got = swap(give, "frames", size, 1)
-    both = jnp.stack([keep, got], 1)
-    return swaps([both[s] for s in range(size // 2)], "frames", size, 2)
+    both = pl.pallas_call(
+        pair_kernel,
+        out_shape=[struct(2, *keep.shape[1:])] * (size // 2),
+        in_specs=[VMEM] * 2,
+        out_specs=[VMEM] * (size // 2),
+        compiler_params=params(4),
+        name="pair",
+    )(keep, got)
+    return swaps(both, "frames", size, 2)
 
 
 def shards(n_frames, n_space, latents, merge_slot, modulation, spatial_qkv, spatial_proj, temporal_qkv, temporal_proj):
@@ -263,62 +324,100 @@
     n_pair = n_frames // 2
     spatial_qkv, temporal_qkv = spatial_qkv.T, temporal_qkv.T
     blocks = latents.reshape(n_frames, places, width)
-    slot_column = merge_slot.reshape(rows, 1)
-    sent = packed_rows(slots, 3 * wide)
-    *queries, token_keep, token_give = pl.pallas_call(
-        functools.partial(merge_kernel, n_space, n_pair),
-        out_shape=[struct(sent, LANES)] * n_space + [struct(n_pair, places, width)] * 2,
+    sent = packed_rows(3 * wide, slots)
+    far, merged = pl.pallas_call(
+        functools.partial(merge_kernel, n_space),
+        out_shape=[struct(sent, LANES), struct(slots, width)],
         in_specs=[HBM] * 4,
-        out_specs=[VMEM] * (n_space + 2),
+        out_specs=[VMEM] * 2,
         scratch_shapes=[
-            pltpu.VMEM((n_space, sent, LANES), BF16),
             pltpu.VMEM(blocks.shape, BF16),
             pltpu.VMEM(merge_slot.shape, jnp.int32),
             pltpu.VMEM(modulation.shape, F32),
-            pltpu.VMEM(spatial_qkv.shape, BF16),
-            pltpu.SemaphoreType.DMA((4,)),
+            pltpu.VMEM((3 * wide, width), BF16),
+            pltpu.SemaphoreType.DMA((6,)),
         ],
         compiler_params=params(57),
         name="merge",
     )(blocks, merge_slot, modulation, spatial_qkv)
+    queries = pl.pallas_call(
+        functools.partial(spread_kernel, n_space),
+        out_shape=[struct(sent, LANES)] * (n_space - 1),
+        in_specs=[VMEM, HBM],
+        out_specs=[VMEM] * (n_space - 1),
+        scratch_shapes=[
+            pltpu.VMEM((n_space, 3 * wide, slots), F32),
+            pltpu.VMEM(spatial_qkv.shape, BF16),
+            pltpu.SemaphoreType.DMA,
+        ],
+        compiler_params=params(20),
+        cost_estimate=cost(2 * slots * 3 * inner * width),
+        name="spread",
+    )(merged, spatial_qkv)
+    shared, merged = lax.optimization_barrier((blocks, merged))
+    token_keep, token_give = pl.pallas_call(
+        functools.partial(share_kernel, n_pair),
+        out_shape=[struct(n_pair, places, width)] * 2,
+        in_specs=[VMEM],
+        out_specs=[VMEM] * 2,
+        compiler_params=params(6),
+        name="share",
+    )(shared)
+    queries = list(queries)
+    queries.append(far)
     held = swaps(queries, "space", n_space)
     tokens = exchange(token_keep, token_give, n_frames)
-    held = lax.optimization_barrier(held[::-1])
-    returned = packed_rows(slots, wide)
-    results = {}
-    for name, asked in (("others", range(1, n_space)), ("own", range(1))):
-        if name == "own":
-            held, tokens = lax.optimization_barrier((held, tokens))
-        done = pl.pallas_call(
-            functools.partial(attention_kernel, n_space, slots, wide, asked),
-            out_shape=[struct(returned, LANES)] * len(asked),
-            in_specs=[VMEM] * n_space,
-            out_specs=[VMEM] * len(asked),
-            compiler_params=params(20),
-            cost_estimate=cost(4 * slots * slots * n_space * n_space * wide),
-            name="attend_" + name,
-        )(*held)
-        results.update(zip(asked, done))
-    mine = swaps(results, "space", n_space)
+    far_keys, far_others, chosen = pl.pallas_call(
+        functools.partial(prepare_kernel, wide),
+        out_shape=[struct(slots, wide), struct(2 * wide, slots), struct(rows, slots)],
+        in_specs=[VMEM] * 2,
+        out_specs=[VMEM] * 3,
+        compiler_params=params(4),
+        cost_estimate=cost(4 * slots * slots * n_space * n_space * wide),
+        name="prepare",
+    )(held[-1], merge_slot)
+    held = lax.optimization_barrier([far_keys, far_others] + held[-2::-1])
+    returned = packed_rows(wide, slots)
+    *results, own_queries, all_keys, all_vals = pl.pallas_call(
+        functools.partial(others_kernel, n_space, slots, wide),
+        out_shape=[struct(returned, LANES)] * (n_space - 1)
+        + [struct(wide, slots), struct(n_space * slots, wide), struct(wide, n_space * slots)],
+        in_specs=[VMEM] * (n_space + 1),
+        out_specs=[VMEM] * (n_space + 2),
+        compiler_params=params(12),
+        cost_estimate=cost(4 * slots * slots * n_space * (n_space - 1) * wide),
+        name="attend_others",
+    )(*held)
+    own_queries, tokens = lax.optimization_barrier((own_queries, tokens))
+    own = pl.pallas_call(
+        own_kernel,
+        out_shape=struct(wide, slots),
+        in_specs=[VMEM] * 3,
+        out_specs=VMEM,
+        compiler_params=params(8),
+        cost_estimate=cost(4 * slots * slots * n_space * wide),
+        name="attend_own",
+    )(own_queries, all_keys, all_vals)
+    mine = swaps([own] + results, "space", n_space)
     keep, give, attended = pl.pallas_call(
         functools.partial(expand_kernel, n_space, n_pair, slots, wide),
-        out_shape=[struct(n_pair, places, inner), struct(n_pair, places, inner), struct(slots, inner)],
+        out_shape=[struct(n_pair, places, inner), struct(n_pair, places, inner), struct(inner, slots)],
         in_specs=[VMEM] * (n_space + 1),
         out_specs=[VMEM] * 3,
-        scratch_shapes=[pltpu.VMEM((n_space, slots, wide), BF16), pltpu.VMEM((n_frames, places, inner), BF16)],
-        compiler_params=params(20),
+        scratch_shapes=[pltpu.VMEM((n_space, wide, slots), F32), pltpu.VMEM((n_frames, places, inner), BF16)],
+        compiler_params=params(8),
         name="expand",
-    )(slot_column, *reversed(mine))
+    )(chosen, *reversed(mine))
     attended_parts = exchange(keep, give, n_frames)
     after = pl.pallas_call(
         residual_kernel,
         out_shape=struct(n_frames, places, width),
         in_specs=[VMEM] * 5,
         out_specs=VMEM,
-        compiler_params=params(20),
+        compiler_params=params(10),
         cost_estimate=cost(4 * slots * inner * width),
         name="residual",
-    )(attended, slot_column, blocks, modulation, spatial_proj)
+    )(attended, chosen, blocks, modulation, spatial_proj)
     pad = -(-places // SUB) * SUB
     order = [0] + list(range(n_pair - 1, 0, -1))
     steps = [order[:1], order[1:2]] if n_pair > 2 else [order[:1]]
@@ -332,7 +431,7 @@
                 in_specs=[VMEM] * (3 + 2 * len(step)),
                 out_specs=VMEM,
                 scratch_shapes=[pltpu.VMEM((2 * len(step) * places, width), F32)],
-                compiler_params=params(16),
+                compiler_params=params(10),
                 cost_estimate=cost(2 * 2 * places * len(step) * 3 * inner * width),
                 name="project_%d" % i,
             )(
@@ -352,7 +451,7 @@
             pltpu.VMEM((2 * len(last) * places, width), F32),
             pltpu.VMEM((n_frames, pad, inner), BF16),
         ],
-        compiler_params=params(20),
+        compiler_params=params(16),
         name="temporal",
     )(
         modulation,
@@ -365,11 +464,11 @@
     mixed_keep, mixed_give = mixed
     parts = exchange(mixed_keep, mixed_give, n_frames)
     out = pl.pallas_call(
-        functools.partial(finish_kernel, n_pair, places),
+        functools.partial(finish_kernel, list(range(n_pair)), places),
         out_shape=struct(n_frames, places, width),
         in_specs=[VMEM] * (3 + n_pair),
         out_specs=VMEM,
-        compiler_params=params(20),
+        compiler_params=params(10),
         name="finish",
     )(modulation, temporal_proj, after, *parts)
     return out.reshape(1, rows, width)

time: 73.7 us -> 67.7 us (0.919)
  local copies, waits for them, and re-layouts: 4.91 us -> 1.09 us
  waiting for transfers between devices: 19.2 us -> 22.1 us
  Pallas kernels: 23.5 us -> 21 us
  other arithmetic: 2.17 us -> 0 us
    unnamed x20 -> x16, local copies, waits for them, and re-layouts: 4.09 us -> 1.09 us
    ppermute x18, waiting for transfers between devices: 19.2 us -> 22.1 us  [swap(): return lax.ppermute(block, axis, [(i, i ^ mask) for i in range(size)])]
    squeeze x3 -> x0, other arithmetic: 2.17 us -> none  [exchange(): return swaps([both[s] for s in range(size // 2)], 'frames', size, 2)]
    pallas_call x1, Pallas kernels: 5.7 us -> 3.93 us  [shards(): pl.pallas_call(functools.partial(temporal_kernel, n_pair, places, len(las...]
    reshape x1 -> x0, local copies, waits for them, and re-layouts: 0.81 us -> none  [shards(): slot_column = merge_slot.reshape(rows, 1)]
    pallas_call x4 -> x10, Pallas kernels: 12.5 us -> 11.8 us  [the longest x1 3.74 us: shards(): pl.pallas_call(functools.partial(merge_kernel, n_space), out_shape=[struc...]
  transfers between devices with their start and end apart: 18 -> 18, of which waited for: 8 -> 10; matrix products, arithmetic and copies ran while one was open for 4% -> 0% of each run, Pallas kernels for 13% -> 16%
where the time goes in v3:
time: 67.7 us; the launch traced here: 67.5 us
  starting transfers between devices  23.2 us (34%)
  waiting for transfers between devices  22.1 us (33%)
  Pallas kernels  21 us (31%)
  local copies, waits for them, and re-layouts  1.09 us (2%)
    ppermute x18, starting transfers between devices, swap(): return lax.ppermute(block, axis, [(i, i ^ mask) for i in range(size)])  23.2 us
    ppermute x18, waiting for transfers between devices, swap(): return lax.ppermute(block, axis, [(i, i ^ mask) for i in range(size)])  22.1 us
    pallas_call x1, Pallas kernels, shards(): pl.pallas_call(functools.partial(temporal_kernel, n_pair, places, len(las...  3.93 us
    pallas_call x1, Pallas kernels, shards(): pl.pallas_call(functools.partial(merge_kernel, n_space), out_shape=[struc...  3.74 us
    pallas_call x2, Pallas kernels, shards(): pl.pallas_call(functools.partial(project_kernel, places, len(step)), out_...  3.74 us
    pallas_call x1, Pallas kernels, shards(): pl.pallas_call(functools.partial(others_kernel, n_space, slots, wide), ou...  2.32 us
    pallas_call x1, Pallas kernels, shards(): pl.pallas_call(functools.partial(finish_kernel, list(range(n_pair)), plac...  2.08 us
    pallas_call x1, Pallas kernels, shards(): pl.pallas_call(functools.partial(spread_kernel, n_space), out_shape=[stru...  1.85 us
  transfers between devices with their start and end apart: 18, of which 10 were waited for; matrix products, arithmetic and copies ran while one was open for 0% of the time, Pallas kernels for 16%

profile of v3, /device:TPU:0, one launch (start us, length us, event | category | flops | bytes accessed | tf_op | source)
XLA Modules:
  0.0 67.5 jit_solution(12205686958455058043)
XLA Ops:
  0.0 0.0 copy-start.2
  0.0 0.0 copy-start.3
  0.0 3.7 %merge.1 = (bf16[768,128]{1,0:T(8,128)(2,1)}, bf16[224,1152]{1,0:T(8,128)(2,1)}) custom-call(bf16[8,56,1152]{2,1,0:T(8,128)(2,1)} %bitcast.9, s32[1,448]{1,0:T(1,128)} %slot.3, f32[6,1152]{1,0:T(8,128)} %modulation.11, bf16[1728,1152]{1,0:T(8,128)(2,1)} %bitcast.7), custom_call_target="tpu_custom_call" | custom-call | tf_op jit(solution)/shard_map/merge/pallas_call | solution.py:328
  3.8 0.0 copy-start.7
  3.8 0.0 copy-done.3
  3.8 0.1 share.1
  3.9 0.5 collective-permute-start.6
  4.4 4.7 %collective-permute-start = (bf16[768,128]{1,0:T(8,128)(2,1)}, bf16[768,128]{1,0:T(8,128)(2,1)S(1)}, u32[]{:S(2)}, u32[]{:S(2)}) collective-permute-start(bf16[768,128]{1,0:T(8,128)(2,1)} %get-tuple-element.49), channel_id=1, source_target_pairs={{0,3},{1,2},{2,1},{3,0},{4,7},{5,6},{6,5},{7,4},{8,11},{9,10},{10,... | collective-permute-start | bytes 589832 | tf_op jit(solution)/shard_map/ppermute | solution.py:298
  9.1 0.0 collective-permute-done.6.got
  9.1 0.1 pair.3
  9.1 0.0 copy-start
  9.2 0.0 copy-start.1
  9.2 0.0 copy-start.5
  9.2 1.6 %collective-permute-start.7 = (bf16[2,56,1152]{2,1,0:T(8,128)(2,1)S(1)}, bf16[2,56,1152]{2,1,0:T(8,128)(2,1)S(1)}, u32[]{:S(2)}, u32[]{:S(2)}) collective-permute-start(bf16[2,56,1152]{2,1,0:T(8,128)(2,1)S(1)} %get-tuple-element.70), channel_id=1, source_target_pairs={{0,8},{4,12},{8,0},{12,4},{16,24},{20,28},{24,16},{28,20},{1,9},{5... | collective-permute-start | bytes 774152 | tf_op jit(solution)/shard_map/ppermute | solution.py:298
  10.7 0.0 copy-done.2
  10.7 0.0 copy-start.6
  10.7 1.0 %copy-done.6 = bf16[224,1152]{1,0:T(8,128)(2,1)S(1)} copy-done((bf16[224,1152]{1,0:T(8,128)(2,1)S(1)}, bf16[224,1152]{1,0:T(8,128)(2,1)}, u32[]{:S(2)}) %copy-start.6) | copy-done | bytes 516120
  11.8 1.9 %spread.1 = (bf16[768,128]{1,0:T(8,128)(2,1)S(1)}, bf16[768,128]{1,0:T(8,128)(2,1)S(1)}, bf16[768,128]{1,0:T(8,128)(2,1)S(1)}) custom-call(bf16[224,1152]{1,0:T(8,128)(2,1)S(1)} %copy-done.6, bf16[1728,1152]{1,0:T(8,128)(2,1)S(1)} %bitcast.8), custom_call_target="tpu_custom_call" | custom-call | flops 891813888 | bytes 8918138 | tf_op jit(solution)/shard_map/spread/pallas_call | solution.py:343
  13.7 0.9 %collective-permute-start.1 = (bf16[768,128]{1,0:T(8,128)(2,1)S(1)}, bf16[768,128]{1,0:T(8,128)(2,1)S(1)}, u32[]{:S(2)}, u32[]{:S(2)}) collective-permute-start(bf16[768,128]{1,0:T(8,128)(2,1)S(1)} %get-tuple-element.54), channel_id=1, source_target_pairs={{0,2},{1,3},{2,0},{3,1},{4,6},{5,7},{6,4},{7,5},{8,10},{9,11},{10,... | collective-permute-start | bytes 589832 | tf_op jit(solution)/shard_map/ppermute | solution.py:298
  14.5 1.6 %collective-permute-start.2 = (bf16[768,128]{1,0:T(8,128)(2,1)S(1)}, bf16[768,128]{1,0:T(8,128)(2,1)S(1)}, u32[]{:S(2)}, u32[]{:S(2)}) collective-permute-start(bf16[768,128]{1,0:T(8,128)(2,1)S(1)} %get-tuple-element.55), channel_id=1, source_target_pairs={{0,1},{1,0},{2,3},{3,2},{4,5},{5,4},{6,7},{7,6},{8,9},{9,8},{10,11... | collective-permute-start | bytes 589832 | tf_op jit(solution)/shard_map/ppermute | solution.py:298
  16.1 1.5 %collective-permute-start.8 = (bf16[2,56,1152]{2,1,0:T(8,128)(2,1)S(1)}, bf16[2,56,1152]{2,1,0:T(8,128)(2,1)S(1)}, u32[]{:S(2)}, u32[]{:S(2)}) collective-permute-start(bf16[2,56,1152]{2,1,0:T(8,128)(2,1)S(1)} %get-tuple-element.71), channel_id=1, source_target_pairs={{0,16},{4,20},{8,24},{12,28},{16,0},{20,4},{24,8},{28,12},{1,17},{... | collective-permute-start | bytes 774152 | tf_op jit(solution)/shard_map/ppermute | solution.py:298
  17.6 0.0 collective-permute-done.packed
  17.6 0.8 %collective-permute-start.9 = (bf16[2,56,1152]{2,1,0:T(8,128)(2,1)S(1)}, bf16[2,56,1152]{2,1,0:T(8,128)(2,1)S(1)}, u32[]{:S(2)}, u32[]{:S(2)}) collective-permute-start(bf16[2,56,1152]{2,1,0:T(8,128)(2,1)S(1)} %get-tuple-element.72), channel_id=1, source_target_pairs={{0,24},{4,28},{8,16},{12,20},{16,8},{20,12},{24,0},{28,4},{1,25},{... | collective-permute-start | bytes 774152 | tf_op jit(solution)/shard_map/ppermute | solution.py:298
  18.4 0.0 copy-done.7
  18.4 0.3 prepare.1
  18.7 7.9 %collective-permute-done.1.refs_0_ = bf16[768,128]{1,0:T(8,128)(2,1)S(1)} collective-permute-done((bf16[768,128]{1,0:T(8,128)(2,1)S(1)}, bf16[768,128]{1,0:T(8,128)(2,1)S(1)}, u32[]{:S(2)}, u32[]{:S(2)}) %collective-permute-start.1) | collective-permute-done | bytes 196640 | tf_op jit(solution)/shard_map/ppermute | solution.py:298
  26.6 0.0 collective-permute-done.2.refs_1_
  26.6 2.3 %attend_others.1 = (bf16[272,128]{1,0:T(8,128)(2,1)S(1)}, bf16[272,128]{1,0:T(8,128)(2,1)S(1)}, bf16[272,128]{1,0:T(8,128)(2,1)S(1)}, bf16[144,224]{1,0:T(8,128)...) custom-call(bf16[224,144]{1,0:T(8,128)(2,1)S(1)} %get-tuple-element.57.far_keys, ...), custom_call_target="tpu_custom_call" | custom-call | flops 346816512 | bytes 3468165 | tf_op jit(solution)/shard_map/attend_others/pallas_call | solution.py:381
  28.9 2.5 %collective-permute-start.3 = (bf16[272,128]{1,0:T(8,128)(2,1)S(1)}, bf16[272,128]{1,0:T(8,128)(2,1)S(1)}, u32[]{:S(2)}, u32[]{:S(2)}) collective-permute-start(bf16[272,128]{1,0:T(8,128)(2,1)S(1)} %get-tuple-element.62), channel_id=1, source_target_pairs={{0,3},{1,2},{2,1},{3,0},{4,7},{5,6},{6,5},{7,4},{8,11},{9,10},{10,... | collective-permute-start | bytes 208904 | tf_op jit(solution)/shard_map/ppermute | solution.py:298
  31.4 0.0 collective-permute-start.4
  31.4 0.0 collective-permute-done.7.refs_1_
  31.5 1.9 %collective-permute-start.5 = (bf16[272,128]{1,0:T(8,128)(2,1)S(1)}, bf16[272,128]{1,0:T(8,128)(2,1)S(1)}, u32[]{:S(2)}, u32[]{:S(2)}) collective-permute-start(bf16[272,128]{1,0:T(8,128)(2,1)S(1)} %get-tuple-element.64), channel_id=1, source_target_pairs={{0,1},{1,0},{2,3},{3,2},{4,5},{5,4},{6,7},{7,6},{8,9},{9,8},{10,11... | collective-permute-start | bytes 208904 | tf_op jit(solution)/shard_map/ppermute | solution.py:298
  33.4 0.0 collective-permute-done.8.refs_0_
  33.4 0.0 collective-permute-done.9.refs_0_
  33.4 1.3 %attend_own.1.refs_3_ = bf16[144,224]{1,0:T(8,128)(2,1)S(1)} custom-call(bf16[144,224]{1,0:T(8,128)(2,1)S(1)} %get-tuple-element.73.queries, bf16[896,144]{1,0:T(8,128)(2,1)S(1)} %get-tuple-element.74.keys, bf16[144,896]{1,0:T(8,128)(2,1)S(1)} %get-tuple-element.75.vals), custom_call_target="tpu_custom_call" | custom-call | flops 115605504 | bytes 1156055 | tf_op jit(solution)/shard_map/attend_own/pallas_call | solution.py:392
  34.7 0.7 %collective-permute-done.3.refs_0_ = bf16[272,128]{1,0:T(8,128)(2,1)S(1)} collective-permute-done((bf16[272,128]{1,0:T(8,128)(2,1)S(1)}, bf16[272,128]{1,0:T(8,128)(2,1)S(1)}, u32[]{:S(2)}, u32[]{:S(2)}) %collective-permute-start.3) | collective-permute-done | bytes 69664 | tf_op jit(solution)/shard_map/ppermute | solution.py:298
  35.4 2.1 %collective-permute-done.4.refs_1_ = bf16[272,128]{1,0:T(8,128)(2,1)S(1)} collective-permute-done((bf16[272,128]{1,0:T(8,128)(2,1)S(1)}, bf16[272,128]{1,0:T(8,128)(2,1)S(1)}, u32[]{:S(2)}, u32[]{:S(2)}) %collective-permute-start.4) | collective-permute-done | bytes 69664 | tf_op jit(solution)/shard_map/ppermute | solution.py:298
  37.5 0.0 collective-permute-done.5.refs_2_
  37.5 0.5 expand.1
  38.0 0.1 collective-permute-start.10
  38.1 1.6 %collective-permute-done.10.got = bf16[4,56,576]{2,1,0:T(8,128)(2,1)S(1)} collective-permute-done((bf16[4,56,576]{2,1,0:T(8,128)(2,1)S(1)}, bf16[4,56,576]{2,1,0:T(8,128)(2,1)S(1)}, u32[]{:S(2)}, u32[]{:S(2)}) %collective-permute-start.10) | collective-permute-done | bytes 258080 | tf_op jit(solution)/shard_map/ppermute | solution.py:298
  39.7 2.5 %collective-permute-start.13 = (bf16[2,56,576]{2,1,0:T(8,128)(2,1)S(1)}, bf16[2,56,576]{2,1,0:T(8,128)(2,1)S(1)}, u32[]{:S(2)}, u32[]{:S(2)}) collective-permute-start(bf16[2,56,576]{2,1,0:T(8,128)(2,1)S(1)} %get-tuple-element.86), channel_id=1, source_target_pairs={{0,24},{4,28},{8,16},{12,20},{16,8},{20,12},{24,0},{28,4},{1,25},{... | collective-permute-start | bytes 387080 | tf_op jit(solution)/shard_map/ppermute | solution.py:298
  42.2 0.5 collective-permute-start.11
  42.7 0.5 collective-permute-start.12
  43.3 0.0 copy-done
  43.3 0.0 copy-done.1
  43.3 0.0 copy-done.5
  43.3 1.9 %project_0.1.refs_4_ = bf16[2,64,1728]{2,1,0:T(8,128)(2,1)S(1)} custom-call(f32[6,1152]{1,0:T(8,128)S(1)} %copy-done.5, bf16[576,1152]{1,0:T(8,128)(2,1)S(1)} %copy-done.1, bf16[1728,1152]{1,0:T(8,128)(2,1)S(1)} %bitcast.4, bf16[2,56,1152]{2,1,0:T(8,128)(2,1)S(1)} %get-tuple-element.83.refs_0_, bf16[2,56,576]{2,1,0:T(8,128)(2,1)S(1)} %get-tuple-element.84.refs_1_), custom_call_target="tpu_custom_call" | custom-call | flops 445906944 | bytes 4459069 | tf_op jit(solution)/shard_map/project_0/pallas_call | solution.py:428
  45.2 1.9 %collective-permute-done.13.refs_1_ = bf16[2,56,576]{2,1,0:T(8,128)(2,1)S(1)} collective-permute-done((bf16[2,56,576]{2,1,0:T(8,128)(2,1)S(1)}, bf16[2,56,576]{2,1,0:T(8,128)(2,1)S(1)}, u32[]{:S(2)}, u32[]{:S(2)}) %collective-permute-start.13) | collective-permute-done | bytes 129056 | tf_op jit(solution)/shard_map/ppermute | solution.py:298
  47.0 1.9 %project_1.1.refs_5_ = bf16[2,64,1728]{2,1,0:T(8,128)(2,1)S(1)} custom-call(f32[6,1152]{1,0:T(8,128)S(1)} %copy-done.5, bf16[576,1152]{1,0:T(8,128)(2,1)S(1)} %copy-done.1, bf16[1728,1152]{1,0:T(8,128)(2,1)S(1)} %bitcast.5, bf16[2,56,1152]{2,1,0:T(8,128)(2,1)S(1)} %collective-permute-done.9.refs_0_, bf16[2,56,576]{2,1,0:T(8,128)(2,1)S(1)} %collective-permute-done.13.refs_1_), custom_call_target="tpu_custom_call" | custom-call | flops 445906944 | bytes 4459069 | tf_op jit(solution)/shard_map/project_1/pallas_call | solution.py:428
  48.9 0.6 collective-permute-done.11.refs_2_
  49.6 0.1 collective-permute-done.12.refs_3_
  49.7 3.9 %temporal.1 = (bf16[4,56,576]{2,1,0:T(8,128)(2,1)S(1)}, bf16[4,56,576]{2,1,0:T(8,128)(2,1)S(1)}) custom-call(f32[6,1152]{1,0:T(8,128)S(1)} %copy-done.5, bf16[576,1152]{1,0:T(8,128)(2,1)S(1)} %copy-done.1, bf16[1728,1152]{1,0:T(8,128)(2,1)S(1)} %bitcast.6, bf16[2,56,1152]{2,1,0:T(8,128)(2,1)S(1)} %collective-permute-done.8.refs_0_, ...), custom_call_target="tpu_custom_call" | custom-call | tf_op jit(solution)/shard_map/temporal/pallas_call | solution.py:445
  53.6 0.1 collective-permute-start.14
  53.7 1.6 %collective-permute-done.14.got = bf16[4,56,576]{2,1,0:T(8,128)(2,1)S(1)} collective-permute-done((bf16[4,56,576]{2,1,0:T(8,128)(2,1)S(1)}, bf16[4,56,576]{2,1,0:T(8,128)(2,1)S(1)}, u32[]{:S(2)}, u32[]{:S(2)}) %collective-permute-start.14) | collective-permute-done | bytes 258080 | tf_op jit(solution)/shard_map/ppermute | solution.py:298
  55.3 1.6 %collective-permute-start.15 = (bf16[2,56,576]{2,1,0:T(8,128)(2,1)S(1)}, bf16[2,56,576]{2,1,0:T(8,128)(2,1)S(1)}, u32[]{:S(2)}, u32[]{:S(2)}) collective-permute-start(bf16[2,56,576]{2,1,0:T(8,128)(2,1)S(1)} %get-tuple-element.90), channel_id=1, source_target_pairs={{0,8},{4,12},{8,0},{12,4},{16,24},{20,28},{24,16},{28,20},{1,9},{5... | collective-permute-start | bytes 387080 | tf_op jit(solution)/shard_map/ppermute | solution.py:298
  56.8 1.1 %collective-permute-start.16 = (bf16[2,56,576]{2,1,0:T(8,128)(2,1)S(1)}, bf16[2,56,576]{2,1,0:T(8,128)(2,1)S(1)}, u32[]{:S(2)}, u32[]{:S(2)}) collective-permute-start(bf16[2,56,576]{2,1,0:T(8,128)(2,1)S(1)} %get-tuple-element.91), channel_id=1, source_target_pairs={{0,16},{4,20},{8,24},{12,28},{16,0},{20,4},{24,8},{28,12},{1,17},{... | collective-permute-start | bytes 387080 | tf_op jit(solution)/shard_map/ppermute | solution.py:298
  57.9 0.9 %collective-permute-start.17 = (bf16[2,56,576]{2,1,0:T(8,128)(2,1)S(1)}, bf16[2,56,576]{2,1,0:T(8,128)(2,1)S(1)}, u32[]{:S(2)}, u32[]{:S(2)}) collective-permute-start(bf16[2,56,576]{2,1,0:T(8,128)(2,1)S(1)} %get-tuple-element.92), channel_id=1, source_target_pairs={{0,24},{4,28},{8,16},{12,20},{16,8},{20,12},{24,0},{28,4},{1,25},{... | collective-permute-start | bytes 387080 | tf_op jit(solution)/shard_map/ppermute | solution.py:298
  58.8 1.0 %residual.1.after = bf16[8,56,1152]{2,1,0:T(8,128)(2,1)S(1)} custom-call(bf16[576,224]{1,0:T(8,128)(2,1)S(1)} %get-tuple-element.76.attended, bf16[448,224]{1,0:T(8,128)(2,1)S(1)} %get-tuple-element.50.chosen, bf16[8,56,1152]{2,1,0:T(8,128)(2,1)S(1)} %bitcast.11, f32[6,1152]{1,0:T(8,128)S(1)} %copy-done.5, bf16[576,1152]{1,0:T(8,128)(2,1)S(1)} %copy-done.1), custom_call_target="tpu_custom_call" | custom-call | flops 594542592 | bytes 5945425 | tf_op jit(solution)/shard_map/residual/pallas_call | solution.py:412
  59.8 1.9 %collective-permute-done.15.refs_1_ = bf16[2,56,576]{2,1,0:T(8,128)(2,1)S(1)} collective-permute-done((bf16[2,56,576]{2,1,0:T(8,128)(2,1)S(1)}, bf16[2,56,576]{2,1,0:T(8,128)(2,1)S(1)}, u32[]{:S(2)}, u32[]{:S(2)}) %collective-permute-start.15) | collective-permute-done | bytes 129056 | tf_op jit(solution)/shard_map/ppermute | solution.py:298
  61.8 3.7 %collective-permute-done.16.refs_2_ = bf16[2,56,576]{2,1,0:T(8,128)(2,1)S(1)} collective-permute-done((bf16[2,56,576]{2,1,0:T(8,128)(2,1)S(1)}, bf16[2,56,576]{2,1,0:T(8,128)(2,1)S(1)}, u32[]{:S(2)}, u32[]{:S(2)}) %collective-permute-start.16) | collective-permute-done | bytes 129056 | tf_op jit(solution)/shard_map/ppermute | solution.py:298
  65.4 0.0 collective-permute-done.17.refs_3_
  65.4 0.0 copy-done.4
  65.4 2.1 %finish.1 = bf16[8,56,1152]{2,1,0:T(8,128)(2,1)} custom-call(f32[6,1152]{1,0:T(8,128)S(1)} %copy-done.5, bf16[576,1152]{1,0:T(8,128)(2,1)S(1)} %copy-done.4, bf16[8,56,1152]{2,1,0:T(8,128)(2,1)S(1)} %residual.1.after, bf16[2,56,576]{2,1,0:T(8,128)(2,1)S(1)} %get-tuple-element.89.refs_0_, bf16[2,56,576]{2,1,0:T(8,128)(2,1)S(1)} %collective-permute-done.15.refs_1_, ...), custom_call_target="tpu_custom_call" | custom-call | tf_op jit(solution)/shard_map/finish/pallas_call | solution.py:466
  (3 shorter events, 0.1 us)
Async XLA Ops:
  0.0 10.7 %copy-start.2 = (bf16[1152,1728]{0,1:T(8,128)(2,1)S(1)}, bf16[1152,1728]{0,1:T(8,128)(2,1)}, u32[]{:S(2)}) copy-start(bf16[1152,1728]{0,1:T(8,128)(2,1)} %param.10) | copy-start | bytes 11943940
  0.0 3.8 %copy-start.3 = (bf16[1,448,1152]{2,1,0:T(8,128)(2,1)S(1)}, bf16[1,448,1152]{2,1,0:T(8,128)(2,1)}, u32[]{:S(2)}) copy-start(bf16[1,448,1152]{2,1,0:T(8,128)(2,1)} %param.7) | copy-start | bytes 3096580
  3.8 14.7 %copy-start.7 = (s32[1,448]{1,0:T(1,128)S(1)}, s32[1,448]{1,0:T(1,128)}, u32[]{:S(2)}) copy-start(s32[1,448]{1,0:T(1,128)} %slot.3) | copy-start | bytes 5380
  3.9 5.2 %collective-permute-start.6 = (bf16[4,56,1152]{2,1,0:T(8,128)(2,1)S(1)}, bf16[4,56,1152]{2,1,0:T(8,128)(2,1)S(1)}, u32[]{:S(2)}, u32[]{:S(2)}) collective-permute-start(bf16[4,56,1152]{2,1,0:T(8,128)(2,1)S(1)} %get-tuple-element.68), channel_id=1, source_target_pairs={{0,4},{4,0},{8,12},{12,8},{16,20},{20,16},{24,28},{28,24},{1,5},{5... | collective-permute-start | bytes 1548296 | tf_op jit(solution)/shard_map/ppermute | solution.py:298
  4.4 13.2 %collective-permute-start = (bf16[768,128]{1,0:T(8,128)(2,1)}, bf16[768,128]{1,0:T(8,128)(2,1)S(1)}, u32[]{:S(2)}, u32[]{:S(2)}) collective-permute-start(bf16[768,128]{1,0:T(8,128)(2,1)} %get-tuple-element.49), channel_id=1, source_target_pairs={{0,3},{1,2},{2,1},{3,0},{4,7},{5,6},{6,5},{7,4},{8,11},{9,10},{10,... | collective-permute-start | bytes 589832 | tf_op jit(solution)/shard_map/ppermute | solution.py:298
  9.1 34.1 %copy-start = (bf16[1152,1728]{0,1:T(8,128)(2,1)S(1)}, bf16[1152,1728]{0,1:T(8,128)(2,1)}, u32[]{:S(2)}) copy-start(bf16[1152,1728]{0,1:T(8,128)(2,1)} %param.12) | copy-start | bytes 11943940
  9.2 34.1 %copy-start.1 = (bf16[576,1152]{1,0:T(8,128)(2,1)S(1)}, bf16[576,1152]{1,0:T(8,128)(2,1)}, u32[]{:S(2)}) copy-start(bf16[576,1152]{1,0:T(8,128)(2,1)} %proj.8) | copy-start | bytes 3981316
  9.2 34.1 %copy-start.5 = (f32[6,1152]{1,0:T(8,128)S(1)}, f32[6,1152]{1,0:T(8,128)}, u32[]{:S(2)}) copy-start(f32[6,1152]{1,0:T(8,128)} %modulation.11) | copy-start | bytes 82948
  9.2 22.3 %collective-permute-start.7 = (bf16[2,56,1152]{2,1,0:T(8,128)(2,1)S(1)}, bf16[2,56,1152]{2,1,0:T(8,128)(2,1)S(1)}, u32[]{:S(2)}, u32[]{:S(2)}) collective-permute-start(bf16[2,56,1152]{2,1,0:T(8,128)(2,1)S(1)} %get-tuple-element.70), channel_id=1, source_target_pairs={{0,8},{4,12},{8,0},{12,4},{16,24},{20,28},{24,16},{28,20},{1,9},{5... | collective-permute-start | bytes 774152 | tf_op jit(solution)/shard_map/ppermute | solution.py:298
  10.7 1.1 %copy-start.6 = (bf16[224,1152]{1,0:T(8,128)(2,1)S(1)}, bf16[224,1152]{1,0:T(8,128)(2,1)}, u32[]{:S(2)}) copy-start(bf16[224,1152]{1,0:T(8,128)(2,1)} %get-tuple-element.53.merged) | copy-start | bytes 1548292
  13.7 12.9 %collective-permute-start.1 = (bf16[768,128]{1,0:T(8,128)(2,1)S(1)}, bf16[768,128]{1,0:T(8,128)(2,1)S(1)}, u32[]{:S(2)}, u32[]{:S(2)}) collective-permute-start(bf16[768,128]{1,0:T(8,128)(2,1)S(1)} %get-tuple-element.54), channel_id=1, source_target_pairs={{0,2},{1,3},{2,0},{3,1},{4,6},{5,7},{6,4},{7,5},{8,10},{9,11},{10,... | collective-permute-start | bytes 589832 | tf_op jit(solution)/shard_map/ppermute | solution.py:298
  14.5 12.1 %collective-permute-start.2 = (bf16[768,128]{1,0:T(8,128)(2,1)S(1)}, bf16[768,128]{1,0:T(8,128)(2,1)S(1)}, u32[]{:S(2)}, u32[]{:S(2)}) collective-permute-start(bf16[768,128]{1,0:T(8,128)(2,1)S(1)} %get-tuple-element.55), channel_id=1, source_target_pairs={{0,1},{1,0},{2,3},{3,2},{4,5},{5,4},{6,7},{7,6},{8,9},{9,8},{10,11... | collective-permute-start | bytes 589832 | tf_op jit(solution)/shard_map/ppermute | solution.py:298
  16.1 17.3 %collective-permute-start.8 = (bf16[2,56,1152]{2,1,0:T(8,128)(2,1)S(1)}, bf16[2,56,1152]{2,1,0:T(8,128)(2,1)S(1)}, u32[]{:S(2)}, u32[]{:S(2)}) collective-permute-start(bf16[2,56,1152]{2,1,0:T(8,128)(2,1)S(1)} %get-tuple-element.71), channel_id=1, source_target_pairs={{0,16},{4,20},{8,24},{12,28},{16,0},{20,4},{24,8},{28,12},{1,17},{... | collective-permute-start | bytes 774152 | tf_op jit(solution)/shard_map/ppermute | solution.py:298
  17.6 15.7 %collective-permute-start.9 = (bf16[2,56,1152]{2,1,0:T(8,128)(2,1)S(1)}, bf16[2,56,1152]{2,1,0:T(8,128)(2,1)S(1)}, u32[]{:S(2)}, u32[]{:S(2)}) collective-permute-start(bf16[2,56,1152]{2,1,0:T(8,128)(2,1)S(1)} %get-tuple-element.72), channel_id=1, source_target_pairs={{0,24},{4,28},{8,16},{12,20},{16,8},{20,12},{24,0},{28,4},{1,25},{... | collective-permute-start | bytes 774152 | tf_op jit(solution)/shard_map/ppermute | solution.py:298
  28.9 6.5 %collective-permute-start.3 = (bf16[272,128]{1,0:T(8,128)(2,1)S(1)}, bf16[272,128]{1,0:T(8,128)(2,1)S(1)}, u32[]{:S(2)}, u32[]{:S(2)}) collective-permute-start(bf16[272,128]{1,0:T(8,128)(2,1)S(1)} %get-tuple-element.62), channel_id=1, source_target_pairs={{0,3},{1,2},{2,1},{3,0},{4,7},{5,6},{6,5},{7,4},{8,11},{9,10},{10,... | collective-permute-start | bytes 208904 | tf_op jit(solution)/shard_map/ppermute | solution.py:298
  31.4 6.1 %collective-permute-start.4 = (bf16[272,128]{1,0:T(8,128)(2,1)S(1)}, bf16[272,128]{1,0:T(8,128)(2,1)S(1)}, u32[]{:S(2)}, u32[]{:S(2)}) collective-permute-start(bf16[272,128]{1,0:T(8,128)(2,1)S(1)} %get-tuple-element.63), channel_id=1, source_target_pairs={{0,2},{1,3},{2,0},{3,1},{4,6},{5,7},{6,4},{7,5},{8,10},{9,11},{10,... | collective-permute-start | bytes 208904 | tf_op jit(solution)/shard_map/ppermute | solution.py:298
  31.5 6.0 %collective-permute-start.5 = (bf16[272,128]{1,0:T(8,128)(2,1)S(1)}, bf16[272,128]{1,0:T(8,128)(2,1)S(1)}, u32[]{:S(2)}, u32[]{:S(2)}) collective-permute-start(bf16[272,128]{1,0:T(8,128)(2,1)S(1)} %get-tuple-element.64), channel_id=1, source_target_pairs={{0,1},{1,0},{2,3},{3,2},{4,5},{5,4},{6,7},{7,6},{8,9},{9,8},{10,11... | collective-permute-start | bytes 208904 | tf_op jit(solution)/shard_map/ppermute | solution.py:298
  38.0 1.6 %collective-permute-start.10 = (bf16[4,56,576]{2,1,0:T(8,128)(2,1)S(1)}, bf16[4,56,576]{2,1,0:T(8,128)(2,1)S(1)}, u32[]{:S(2)}, u32[]{:S(2)}) collective-permute-start(bf16[4,56,576]{2,1,0:T(8,128)(2,1)S(1)} %get-tuple-element.80), channel_id=1, source_target_pairs={{0,4},{4,0},{8,12},{12,8},{16,20},{20,16},{24,28},{28,24},{1,5},{5... | collective-permute-start | bytes 774152 | tf_op jit(solution)/shard_map/ppermute | solution.py:298
  39.7 7.3 %collective-permute-start.13 = (bf16[2,56,576]{2,1,0:T(8,128)(2,1)S(1)}, bf16[2,56,576]{2,1,0:T(8,128)(2,1)S(1)}, u32[]{:S(2)}, u32[]{:S(2)}) collective-permute-start(bf16[2,56,576]{2,1,0:T(8,128)(2,1)S(1)} %get-tuple-element.86), channel_id=1, source_target_pairs={{0,24},{4,28},{8,16},{12,20},{16,8},{20,12},{24,0},{28,4},{1,25},{... | collective-permute-start | bytes 387080 | tf_op jit(solution)/shard_map/ppermute | solution.py:298
  42.2 7.3 %collective-permute-start.11 = (bf16[2,56,576]{2,1,0:T(8,128)(2,1)S(1)}, bf16[2,56,576]{2,1,0:T(8,128)(2,1)S(1)}, u32[]{:S(2)}, u32[]{:S(2)}) collective-permute-start(bf16[2,56,576]{2,1,0:T(8,128)(2,1)S(1)} %get-tuple-element.81), channel_id=1, source_target_pairs={{0,16},{4,20},{8,24},{12,28},{16,0},{20,4},{24,8},{28,12},{1,17},{... | collective-permute-start | bytes 387080 | tf_op jit(solution)/shard_map/ppermute | solution.py:298
  42.7 6.9 %collective-permute-start.12 = (bf16[2,56,576]{2,1,0:T(8,128)(2,1)S(1)}, bf16[2,56,576]{2,1,0:T(8,128)(2,1)S(1)}, u32[]{:S(2)}, u32[]{:S(2)}) collective-permute-start(bf16[2,56,576]{2,1,0:T(8,128)(2,1)S(1)} %get-tuple-element.82), channel_id=1, source_target_pairs={{0,8},{4,12},{8,0},{12,4},{16,24},{20,28},{24,16},{28,20},{1,9},{5... | collective-permute-start | bytes 387080 | tf_op jit(solution)/shard_map/ppermute | solution.py:298
  53.6 11.8 %copy-start.4 = (bf16[576,1152]{1,0:T(8,128)(2,1)S(1)}, bf16[576,1152]{1,0:T(8,128)(2,1)}, u32[]{:S(2)}) copy-start(bf16[576,1152]{1,0:T(8,128)(2,1)} %proj.9) | copy-start | bytes 3981316
  53.6 1.6 %collective-permute-start.14 = (bf16[4,56,576]{2,1,0:T(8,128)(2,1)S(1)}, bf16[4,56,576]{2,1,0:T(8,128)(2,1)S(1)}, u32[]{:S(2)}, u32[]{:S(2)}) collective-permute-start(bf16[4,56,576]{2,1,0:T(8,128)(2,1)S(1)} %get-tuple-element.88), channel_id=1, source_target_pairs={{0,4},{4,0},{8,12},{12,8},{16,20},{20,16},{24,28},{28,24},{1,5},{5... | collective-permute-start | bytes 774152 | tf_op jit(solution)/shard_map/ppermute | solution.py:298
  55.3 6.5 %collective-permute-start.15 = (bf16[2,56,576]{2,1,0:T(8,128)(2,1)S(1)}, bf16[2,56,576]{2,1,0:T(8,128)(2,1)S(1)}, u32[]{:S(2)}, u32[]{:S(2)}) collective-permute-start(bf16[2,56,576]{2,1,0:T(8,128)(2,1)S(1)} %get-tuple-element.90), channel_id=1, source_target_pairs={{0,8},{4,12},{8,0},{12,4},{16,24},{20,28},{24,16},{28,20},{1,9},{5... | collective-permute-start | bytes 387080 | tf_op jit(solution)/shard_map/ppermute | solution.py:298
  56.8 8.6 %collective-permute-start.16 = (bf16[2,56,576]{2,1,0:T(8,128)(2,1)S(1)}, bf16[2,56,576]{2,1,0:T(8,128)(2,1)S(1)}, u32[]{:S(2)}, u32[]{:S(2)}) collective-permute-start(bf16[2,56,576]{2,1,0:T(8,128)(2,1)S(1)} %get-tuple-element.91), channel_id=1, source_target_pairs={{0,16},{4,20},{8,24},{12,28},{16,0},{20,4},{24,8},{28,12},{1,17},{... | collective-permute-start | bytes 387080 | tf_op jit(solution)/shard_map/ppermute | solution.py:298
  57.9 7.5 %collective-permute-start.17 = (bf16[2,56,576]{2,1,0:T(8,128)(2,1)S(1)}, bf16[2,56,576]{2,1,0:T(8,128)(2,1)S(1)}, u32[]{:S(2)}, u32[]{:S(2)}) collective-permute-start(bf16[2,56,576]{2,1,0:T(8,128)(2,1)S(1)} %get-tuple-element.92), channel_id=1, source_target_pairs={{0,24},{4,28},{8,16},{12,20},{16,8},{20,12},{24,0},{28,4},{1,25},{... | collective-permute-start | bytes 387080 | tf_op jit(solution)/shard_map/ppermute | solution.py:298

commit v4 on v3

--- a/solution.py
+++ b/solution.py
@@ -195,9 +195,9 @@
     whole = jnp.concatenate([held[d] for d in range(n_space)], 0).astype(BF16)
     attended[...] = whole
     wanted = dot_t(chosen[...], whole)
-    places = keep.shape[1]
+    places = wanted.shape[0] // (2 * n_pair)
     for f in range(2 * n_pair):
-        spread[f] = wanted[f * places : (f + 1) * places].astype(BF16)
+        spread[f] = pack(wanted[f * places : (f + 1) * places]).astype(BF16)
     for s in range(n_pair):
         keep[s] = spread[frame ^ (2 * s)]
         give[s] = spread[frame ^ (2 * s + 1)]
@@ -223,7 +223,9 @@
 
 def project_blocks(places, modulation, proj, weights, tokens, results, normed):
     frames = [(s, t) for s in range(len(tokens)) for t in range(2)]
-    attended = jnp.concatenate([results[s][t].astype(F32) for s, t in frames], 0).astype(BF16)
+    inner = proj.shape[0]
+    attended = [unpack(results[s][t].astype(F32), places, inner) for s, t in frames]
+    attended = jnp.concatenate(attended, 0).astype(BF16)
     spatial = dot(attended, proj[...])
     gate, shift, scale = modulation[2:3], modulation[3:4], 1.0 + modulation[4:5]
     for f, (s, t) in enumerate(frames):
@@ -278,20 +280,26 @@
         for f in range(n_frames):
             held[f, g * SUB : (g + 1) * SUB] = whole[f * SUB : (f + 1) * SUB]
     for i, s in enumerate(order):
-        keep[s] = held[2 * i][:places]
-        give[s] = held[2 * i + 1][:places]
+        keep[s] = pack(held[2 * i].astype(F32)[:places]).astype(BF16)
+        give[s] = pack(held[2 * i + 1].astype(F32)[:places]).astype(BF16)
 
 
 def finish_kernel(taken, places, modulation, proj, after, *refs):
-    parts, out = refs[: len(taken)], refs[-1]
+    parts, (out, held, sems) = refs[: len(taken)], refs[-3:]
     frame = lax.axis_index("frames")
     frames = [(s, t) for s in range(len(taken)) for t in range(2)]
-    mixed = jnp.concatenate([parts[s][t].astype(F32) for s, t in frames], 0).astype(BF16)
+    mixed = [unpack(parts[s][t].astype(F32), places, proj.shape[0]) for s, t in frames]
+    mixed = jnp.concatenate(mixed, 0).astype(BF16)
     branch = dot(mixed, proj[...])
     gate = modulation[5:6]
+    copies = []
     for k, (s, t) in enumerate(frames):
         at = frame ^ (2 * taken[s] + t)
-        out[at] = (after[at].astype(F32) + gate * branch[k * places : (k + 1) * places]).astype(BF16)
+        held[k] = (after[at].astype(F32) + gate * branch[k * places : (k + 1) * places]).astype(BF16)
+        copies.append(pltpu.make_async_copy(held.at[k], out.at[at], sems.at[k]))
+        copies[-1].start()
+    for copy in copies:
+        copy.wait()
 
 
 def swap(block, axis, size, mask):
@@ -378,6 +386,7 @@
     )(held[-1], merge_slot)
     held = lax.optimization_barrier([far_keys, far_others] + held[-2::-1])
     returned = packed_rows(wide, slots)
+    moved = packed_rows(places, inner)
     *results, own_queries, all_keys, all_vals = pl.pallas_call(
         functools.partial(others_kernel, n_space, slots, wide),
         out_shape=[struct(returned, LANES)] * (n_space - 1)
@@ -401,10 +410,10 @@
     mine = swaps([own] + results, "space", n_space)
     keep, give, attended = pl.pallas_call(
         functools.partial(expand_kernel, n_space, n_pair, slots, wide),
-        out_shape=[struct(n_pair, places, inner), struct(n_pair, places, inner), struct(inner, slots)],
+        out_shape=[struct(n_pair, moved, LANES), struct(n_pair, moved, LANES), struct(inner, slots)],
         in_specs=[VMEM] * (n_space + 1),
         out_specs=[VMEM] * 3,
-        scratch_shapes=[pltpu.VMEM((n_space, wide, slots), F32), pltpu.VMEM((n_frames, places, inner), BF16)],
+        scratch_shapes=[pltpu.VMEM((n_space, wide, slots), F32), pltpu.VMEM((n_frames, moved, LANES), BF16)],
         compiler_params=params(8),
         name="expand",
     )(chosen, *reversed(mine))
@@ -444,7 +453,7 @@
         ]
     mixed = pl.pallas_call(
         functools.partial(temporal_kernel, n_pair, places, len(last), order),
-        out_shape=[struct(n_pair, places, inner)] * 2,
+        out_shape=[struct(n_pair, moved, LANES)] * 2,
         in_specs=[VMEM] * (3 + len(last) + n_pair),
         out_specs=[VMEM] * 2,
         scratch_shapes=[
@@ -463,14 +472,23 @@
     )
     mixed_keep, mixed_give = mixed
     parts = exchange(mixed_keep, mixed_give, n_frames)
-    out = pl.pallas_call(
-        functools.partial(finish_kernel, list(range(n_pair)), places),
-        out_shape=struct(n_frames, places, width),
-        in_specs=[VMEM] * (3 + n_pair),
-        out_specs=VMEM,
-        compiler_params=params(10),
-        name="finish",
-    )(modulation, temporal_proj, after, *parts)
+    out = None
+    for i, step in enumerate(([0, n_pair - 1], list(range(n_pair - 2, 0, -1)))):
+        if step:
+            out = pl.pallas_call(
+                functools.partial(finish_kernel, step, places),
+                out_shape=struct(n_frames, places, width),
+                in_specs=[VMEM] * (3 + len(step)) + ([HBM] if i else []),
+                out_specs=HBM,
+                scratch_shapes=[
+                    pltpu.VMEM((2 * len(step), places, width), BF16),
+                    pltpu.SemaphoreType.DMA((2 * len(step),)),
+                ],
+                input_output_aliases={3 + len(step): 0} if i else {},
+                compiler_params=params(10),
+                cost_estimate=cost(2 * 2 * places * len(step) * inner * width),
+                name="finish_%d" % i,
+            )(modulation, temporal_proj, after, *[parts[s] for s in step], *([out] if i else []))
     return out.reshape(1, rows, width)
 
 

time: 67.7 us -> 65.7 us (0.970)
  waiting for transfers between devices: 22.1 us -> 19.1 us
  Pallas kernels: 21 us -> 21.9 us
    ppermute x18, waiting for transfers between devices: 22.1 us -> 19.1 us  [swap(): return lax.ppermute(block, axis, [(i, i ^ mask) for i in range(size)])]
    pallas_call x1 -> x2, Pallas kernels: 2.08 us -> 2.85 us  [shards(): pl.pallas_call(functools.partial(finish_kernel, step, places), out_shape=...]
  transfers between devices with their start and end apart: 18 -> 18, of which waited for: 10 -> 10; matrix products, arithmetic and copies ran while one was open for 0% -> 0% of each run, Pallas kernels for 16% -> 18%
where the time goes in v4:
time: 65.7 us; the launch traced here: 65.5 us
  starting transfers between devices  23.2 us (35%)
  Pallas kernels  21.9 us (33%)
  waiting for transfers between devices  19.1 us (29%)
  local copies, waits for them, and re-layouts  1.09 us (2%)
    ppermute x18, starting transfers between devices, swap(): return lax.ppermute(block, axis, [(i, i ^ mask) for i in range(size)])  23.2 us
    ppermute x18, waiting for transfers between devices, swap(): return lax.ppermute(block, axis, [(i, i ^ mask) for i in range(size)])  19.1 us
    pallas_call x1, Pallas kernels, shards(): pl.pallas_call(functools.partial(temporal_kernel, n_pair, places, len(las...  3.97 us
    pallas_call x2, Pallas kernels, shards(): pl.pallas_call(functools.partial(project_kernel, places, len(step)), out_...  3.81 us
    pallas_call x1, Pallas kernels, shards(): pl.pallas_call(functools.partial(merge_kernel, n_space), out_shape=[struc...  3.74 us
    pallas_call x2, Pallas kernels, shards(): pl.pallas_call(functools.partial(finish_kernel, step, places), out_shape=...  2.85 us
    pallas_call x1, Pallas kernels, shards(): pl.pallas_call(functools.partial(others_kernel, n_space, slots, wide), ou...  2.32 us
    pallas_call x1, Pallas kernels, shards(): pl.pallas_call(functools.partial(spread_kernel, n_space), out_shape=[stru...  1.85 us
  transfers between devices with their start and end apart: 18, of which 10 were waited for; matrix products, arithmetic and copies ran while one was open for 0% of the time, Pallas kernels for 18%

profile of v4, /device:TPU:0, one launch (start us, length us, event | category | flops | bytes accessed | tf_op | source)
XLA Modules:
  0.0 65.5 jit_solution(788015034088014232)
XLA Ops:
  0.0 0.0 copy-start.2
  0.0 3.7 %merge.1 = (bf16[768,128]{1,0:T(8,128)(2,1)}, bf16[224,1152]{1,0:T(8,128)(2,1)}) custom-call(bf16[8,56,1152]{2,1,0:T(8,128)(2,1)} %bitcast.9, s32[1,448]{1,0:T(1,128)} %slot.3, f32[6,1152]{1,0:T(8,128)} %modulation.13, bf16[1728,1152]{1,0:T(8,128)(2,1)} %bitcast.7), custom_call_target="tpu_custom_call" | custom-call | tf_op jit(solution)/shard_map/merge/pallas_call | solution.py:336
  3.8 0.0 copy-start.7
  3.8 0.0 copy-done.3
  3.8 0.1 share.1
  3.9 0.5 collective-permute-start.6
  4.4 4.7 %collective-permute-start = (bf16[768,128]{1,0:T(8,128)(2,1)}, bf16[768,128]{1,0:T(8,128)(2,1)S(1)}, u32[]{:S(2)}, u32[]{:S(2)}) collective-permute-start(bf16[768,128]{1,0:T(8,128)(2,1)} %get-tuple-element.49), channel_id=1, source_target_pairs={{0,3},{1,2},{2,1},{3,0},{4,7},{5,6},{6,5},{7,4},{8,11},{9,10},{10,... | collective-permute-start | bytes 589832 | tf_op jit(solution)/shard_map/ppermute | solution.py:306
  9.1 0.0 collective-permute-done.6.got
  9.1 0.1 pair.3
  9.1 0.0 copy-start
  9.2 0.0 copy-start.1
  9.2 0.0 copy-start.5
  9.2 1.6 %collective-permute-start.7 = (bf16[2,56,1152]{2,1,0:T(8,128)(2,1)S(1)}, bf16[2,56,1152]{2,1,0:T(8,128)(2,1)S(1)}, u32[]{:S(2)}, u32[]{:S(2)}) collective-permute-start(bf16[2,56,1152]{2,1,0:T(8,128)(2,1)S(1)} %get-tuple-element.70), channel_id=1, source_target_pairs={{0,8},{4,12},{8,0},{12,4},{16,24},{20,28},{24,16},{28,20},{1,9},{5... | collective-permute-start | bytes 774152 | tf_op jit(solution)/shard_map/ppermute | solution.py:306
  10.7 0.0 copy-done.2
  10.7 1.0 %copy-done.6 = bf16[224,1152]{1,0:T(8,128)(2,1)S(1)} copy-done((bf16[224,1152]{1,0:T(8,128)(2,1)S(1)}, bf16[224,1152]{1,0:T(8,128)(2,1)}, u32[]{:S(2)}) %copy-start.6) | copy-done | bytes 516120
  11.8 1.9 %spread.1 = (bf16[768,128]{1,0:T(8,128)(2,1)S(1)}, bf16[768,128]{1,0:T(8,128)(2,1)S(1)}, bf16[768,128]{1,0:T(8,128)(2,1)S(1)}) custom-call(bf16[224,1152]{1,0:T(8,128)(2,1)S(1)} %copy-done.6, bf16[1728,1152]{1,0:T(8,128)(2,1)S(1)} %bitcast.8), custom_call_target="tpu_custom_call" | custom-call | flops 891813888 | bytes 8918138 | tf_op jit(solution)/shard_map/spread/pallas_call | solution.py:351
  13.7 0.9 %collective-permute-start.1 = (bf16[768,128]{1,0:T(8,128)(2,1)S(1)}, bf16[768,128]{1,0:T(8,128)(2,1)S(1)}, u32[]{:S(2)}, u32[]{:S(2)}) collective-permute-start(bf16[768,128]{1,0:T(8,128)(2,1)S(1)} %get-tuple-element.54), channel_id=1, source_target_pairs={{0,2},{1,3},{2,0},{3,1},{4,6},{5,7},{6,4},{7,5},{8,10},{9,11},{10,... | collective-permute-start | bytes 589832 | tf_op jit(solution)/shard_map/ppermute | solution.py:306
  14.5 1.6 %collective-permute-start.2 = (bf16[768,128]{1,0:T(8,128)(2,1)S(1)}, bf16[768,128]{1,0:T(8,128)(2,1)S(1)}, u32[]{:S(2)}, u32[]{:S(2)}) collective-permute-start(bf16[768,128]{1,0:T(8,128)(2,1)S(1)} %get-tuple-element.55), channel_id=1, source_target_pairs={{0,1},{1,0},{2,3},{3,2},{4,5},{5,4},{6,7},{7,6},{8,9},{9,8},{10,11... | collective-permute-start | bytes 589832 | tf_op jit(solution)/shard_map/ppermute | solution.py:306
  16.1 1.5 %collective-permute-start.8 = (bf16[2,56,1152]{2,1,0:T(8,128)(2,1)S(1)}, bf16[2,56,1152]{2,1,0:T(8,128)(2,1)S(1)}, u32[]{:S(2)}, u32[]{:S(2)}) collective-permute-start(bf16[2,56,1152]{2,1,0:T(8,128)(2,1)S(1)} %get-tuple-element.71), channel_id=1, source_target_pairs={{0,16},{4,20},{8,24},{12,28},{16,0},{20,4},{24,8},{28,12},{1,17},{... | collective-permute-start | bytes 774152 | tf_op jit(solution)/shard_map/ppermute | solution.py:306
  17.6 0.0 collective-permute-done.packed
  17.6 0.8 %collective-permute-start.9 = (bf16[2,56,1152]{2,1,0:T(8,128)(2,1)S(1)}, bf16[2,56,1152]{2,1,0:T(8,128)(2,1)S(1)}, u32[]{:S(2)}, u32[]{:S(2)}) collective-permute-start(bf16[2,56,1152]{2,1,0:T(8,128)(2,1)S(1)} %get-tuple-element.72), channel_id=1, source_target_pairs={{0,24},{4,28},{8,16},{12,20},{16,8},{20,12},{24,0},{28,4},{1,25},{... | collective-permute-start | bytes 774152 | tf_op jit(solution)/shard_map/ppermute | solution.py:306
  18.4 0.0 copy-done.7
  18.4 0.3 prepare.1
  18.7 7.9 %collective-permute-done.1.refs_0_ = bf16[768,128]{1,0:T(8,128)(2,1)S(1)} collective-permute-done((bf16[768,128]{1,0:T(8,128)(2,1)S(1)}, bf16[768,128]{1,0:T(8,128)(2,1)S(1)}, u32[]{:S(2)}, u32[]{:S(2)}) %collective-permute-start.1) | collective-permute-done | bytes 196640 | tf_op jit(solution)/shard_map/ppermute | solution.py:306
  26.6 0.0 collective-permute-done.2.refs_1_
  26.6 2.3 %attend_others.1 = (bf16[272,128]{1,0:T(8,128)(2,1)S(1)}, bf16[272,128]{1,0:T(8,128)(2,1)S(1)}, bf16[272,128]{1,0:T(8,128)(2,1)S(1)}, bf16[144,224]{1,0:T(8,128)...) custom-call(bf16[224,144]{1,0:T(8,128)(2,1)S(1)} %get-tuple-element.57.far_keys, ...), custom_call_target="tpu_custom_call" | custom-call | flops 346816512 | bytes 3468165 | tf_op jit(solution)/shard_map/attend_others/pallas_call | solution.py:390
  28.9 2.5 %collective-permute-start.3 = (bf16[272,128]{1,0:T(8,128)(2,1)S(1)}, bf16[272,128]{1,0:T(8,128)(2,1)S(1)}, u32[]{:S(2)}, u32[]{:S(2)}) collective-permute-start(bf16[272,128]{1,0:T(8,128)(2,1)S(1)} %get-tuple-element.62), channel_id=1, source_target_pairs={{0,3},{1,2},{2,1},{3,0},{4,7},{5,6},{6,5},{7,4},{8,11},{9,10},{10,... | collective-permute-start | bytes 208904 | tf_op jit(solution)/shard_map/ppermute | solution.py:306
  31.4 0.0 collective-permute-start.4
  31.4 0.0 collective-permute-done.7.refs_1_
  31.5 1.9 %collective-permute-start.5 = (bf16[272,128]{1,0:T(8,128)(2,1)S(1)}, bf16[272,128]{1,0:T(8,128)(2,1)S(1)}, u32[]{:S(2)}, u32[]{:S(2)}) collective-permute-start(bf16[272,128]{1,0:T(8,128)(2,1)S(1)} %get-tuple-element.64), channel_id=1, source_target_pairs={{0,1},{1,0},{2,3},{3,2},{4,5},{5,4},{6,7},{7,6},{8,9},{9,8},{10,11... | collective-permute-start | bytes 208904 | tf_op jit(solution)/shard_map/ppermute | solution.py:306
  33.4 0.0 collective-permute-done.8.refs_0_
  33.4 0.0 collective-permute-done.9.refs_0_
  33.4 1.3 %attend_own.1.refs_3_ = bf16[144,224]{1,0:T(8,128)(2,1)S(1)} custom-call(bf16[144,224]{1,0:T(8,128)(2,1)S(1)} %get-tuple-element.73.queries, bf16[896,144]{1,0:T(8,128)(2,1)S(1)} %get-tuple-element.74.keys, bf16[144,896]{1,0:T(8,128)(2,1)S(1)} %get-tuple-element.75.vals), custom_call_target="tpu_custom_call" | custom-call | flops 115605504 | bytes 1156055 | tf_op jit(solution)/shard_map/attend_own/pallas_call | solution.py:401
  34.7 0.7 %collective-permute-done.3.refs_0_ = bf16[272,128]{1,0:T(8,128)(2,1)S(1)} collective-permute-done((bf16[272,128]{1,0:T(8,128)(2,1)S(1)}, bf16[272,128]{1,0:T(8,128)(2,1)S(1)}, u32[]{:S(2)}, u32[]{:S(2)}) %collective-permute-start.3) | collective-permute-done | bytes 69664 | tf_op jit(solution)/shard_map/ppermute | solution.py:306
  35.4 2.1 %collective-permute-done.4.refs_1_ = bf16[272,128]{1,0:T(8,128)(2,1)S(1)} collective-permute-done((bf16[272,128]{1,0:T(8,128)(2,1)S(1)}, bf16[272,128]{1,0:T(8,128)(2,1)S(1)}, u32[]{:S(2)}, u32[]{:S(2)}) %collective-permute-start.4) | collective-permute-done | bytes 69664 | tf_op jit(solution)/shard_map/ppermute | solution.py:306
  37.5 0.0 collective-permute-done.5.refs_2_
  37.5 0.6 expand.1
  38.1 0.1 collective-permute-start.10
  38.2 1.5 %collective-permute-done.10.got = bf16[4,256,128]{2,1,0:T(8,128)(2,1)S(1)} collective-permute-done((bf16[4,256,128]{2,1,0:T(8,128)(2,1)S(1)}, bf16[4,256,128]{2,1,0:T(8,128)(2,1)S(1)}, u32[]{:S(2)}, u32[]{:S(2)}) %collective-permute-start.10) | collective-permute-done | bytes 262176 | tf_op jit(solution)/shard_map/ppermute | solution.py:306
  39.7 2.5 %collective-permute-start.13 = (bf16[2,256,128]{2,1,0:T(8,128)(2,1)S(1)}, bf16[2,256,128]{2,1,0:T(8,128)(2,1)S(1)}, u32[]{:S(2)}, u32[]{:S(2)}) collective-permute-start(bf16[2,256,128]{2,1,0:T(8,128)(2,1)S(1)} %get-tuple-element.86), channel_id=1, source_target_pairs={{0,24},{4,28},{8,16},{12,20},{16,8},{20,12},{24,0},{28,4},{1,25},{... | collective-permute-start | bytes 393224 | tf_op jit(solution)/shard_map/ppermute | solution.py:306
  42.2 0.5 collective-permute-start.11
  42.8 0.5 collective-permute-start.12
  43.3 0.0 copy-done
  43.3 0.0 copy-done.1
  43.3 0.0 copy-done.5
  43.3 1.9 %project_0.1.refs_4_ = bf16[2,64,1728]{2,1,0:T(8,128)(2,1)S(1)} custom-call(f32[6,1152]{1,0:T(8,128)S(1)} %copy-done.5, bf16[576,1152]{1,0:T(8,128)(2,1)S(1)} %copy-done.1, bf16[1728,1152]{1,0:T(8,128)(2,1)S(1)} %bitcast.4, bf16[2,56,1152]{2,1,0:T(8,128)(2,1)S(1)} %get-tuple-element.83.refs_0_, bf16[2,256,128]{2,1,0:T(8,128)(2,1)S(1)} %get-tuple-element.84.refs_1_), custom_call_target="tpu_custom_call" | custom-call | flops 445906944 | bytes 4459069 | tf_op jit(solution)/shard_map/project_0/pallas_call | solution.py:437
  45.2 1.3 %collective-permute-done.13.refs_1_ = bf16[2,256,128]{2,1,0:T(8,128)(2,1)S(1)} collective-permute-done((bf16[2,256,128]{2,1,0:T(8,128)(2,1)S(1)}, bf16[2,256,128]{2,1,0:T(8,128)(2,1)S(1)}, u32[]{:S(2)}, u32[]{:S(2)}) %collective-permute-start.13) | collective-permute-done | bytes 131104 | tf_op jit(solution)/shard_map/ppermute | solution.py:306
  46.5 1.9 %project_1.1.refs_5_ = bf16[2,64,1728]{2,1,0:T(8,128)(2,1)S(1)} custom-call(f32[6,1152]{1,0:T(8,128)S(1)} %copy-done.5, bf16[576,1152]{1,0:T(8,128)(2,1)S(1)} %copy-done.1, bf16[1728,1152]{1,0:T(8,128)(2,1)S(1)} %bitcast.5, bf16[2,56,1152]{2,1,0:T(8,128)(2,1)S(1)} %collective-permute-done.9.refs_0_, bf16[2,256,128]{2,1,0:T(8,128)(2,1)S(1)} %collective-permute-done.13.refs_1_), custom_call_target="tpu_custom_call" | custom-call | flops 445906944 | bytes 4459069 | tf_op jit(solution)/shard_map/project_1/pallas_call | solution.py:437
  48.5 0.6 collective-permute-done.11.refs_2_
  49.1 0.1 collective-permute-done.12.refs_3_
  49.1 4.0 %temporal.1 = (bf16[4,256,128]{2,1,0:T(8,128)(2,1)S(1)}, bf16[4,256,128]{2,1,0:T(8,128)(2,1)S(1)}) custom-call(f32[6,1152]{1,0:T(8,128)S(1)} %copy-done.5, bf16[576,1152]{1,0:T(8,128)(2,1)S(1)} %copy-done.1, bf16[1728,1152]{1,0:T(8,128)(2,1)S(1)} %bitcast.6, bf16[2,56,1152]{2,1,0:T(8,128)(2,1)S(1)} %collective-permute-done.8.refs_0_, ...), custom_call_target="tpu_custom_call" | custom-call | tf_op jit(solution)/shard_map/temporal/pallas_call | solution.py:454
  53.1 0.0 copy-start.4
  53.1 0.1 collective-permute-start.14
  53.2 1.5 %collective-permute-done.14.got = bf16[4,256,128]{2,1,0:T(8,128)(2,1)S(1)} collective-permute-done((bf16[4,256,128]{2,1,0:T(8,128)(2,1)S(1)}, bf16[4,256,128]{2,1,0:T(8,128)(2,1)S(1)}, u32[]{:S(2)}, u32[]{:S(2)}) %collective-permute-start.14) | collective-permute-done | bytes 262176 | tf_op jit(solution)/shard_map/ppermute | solution.py:306
  54.8 2.4 %collective-permute-start.17 = (bf16[2,256,128]{2,1,0:T(8,128)(2,1)S(1)}, bf16[2,256,128]{2,1,0:T(8,128)(2,1)S(1)}, u32[]{:S(2)}, u32[]{:S(2)}) collective-permute-start(bf16[2,256,128]{2,1,0:T(8,128)(2,1)S(1)} %get-tuple-element.92), channel_id=1, source_target_pairs={{0,24},{4,28},{8,16},{12,20},{16,8},{20,12},{24,0},{28,4},{1,25},{... | collective-permute-start | bytes 393224 | tf_op jit(solution)/shard_map/ppermute | solution.py:306
  57.2 0.6 collective-permute-start.15
  57.8 0.5 collective-permute-start.16
  58.3 1.0 %residual.1.after = bf16[8,56,1152]{2,1,0:T(8,128)(2,1)S(1)} custom-call(bf16[576,224]{1,0:T(8,128)(2,1)S(1)} %get-tuple-element.76.attended, bf16[448,224]{1,0:T(8,128)(2,1)S(1)} %get-tuple-element.50.chosen, bf16[8,56,1152]{2,1,0:T(8,128)(2,1)S(1)} %bitcast.11, f32[6,1152]{1,0:T(8,128)S(1)} %copy-done.5, bf16[576,1152]{1,0:T(8,128)(2,1)S(1)} %copy-done.1), custom_call_target="tpu_custom_call" | custom-call | flops 594542592 | bytes 5945425 | tf_op jit(solution)/shard_map/residual/pallas_call | solution.py:421
  59.3 2.4 %collective-permute-done.17.refs_1_ = bf16[2,256,128]{2,1,0:T(8,128)(2,1)S(1)} collective-permute-done((bf16[2,256,128]{2,1,0:T(8,128)(2,1)S(1)}, bf16[2,256,128]{2,1,0:T(8,128)(2,1)S(1)}, u32[]{:S(2)}, u32[]{:S(2)}) %collective-permute-start.17) | collective-permute-done | bytes 131104 | tf_op jit(solution)/shard_map/ppermute | solution.py:306
  61.7 0.0 copy-done.4
  61.7 1.4 %finish_0.1.refs_2_ = bf16[8,56,1152]{2,1,0:T(8,128)(2,1)} custom-call(f32[6,1152]{1,0:T(8,128)S(1)} %copy-done.5, bf16[576,1152]{1,0:T(8,128)(2,1)S(1)} %copy-done.4, bf16[8,56,1152]{2,1,0:T(8,128)(2,1)S(1)} %residual.1.after, bf16[2,256,128]{2,1,0:T(8,128)(2,1)S(1)} %get-tuple-element.91.refs_0_, bf16[2,256,128]{2,1,0:T(8,128)(2,1)S(1)} %collective-permute-done.17.refs_1_), custom_call_target="tpu_custom_call" | custom-call | flops 297271296 | bytes 2972712 | tf_op jit(solution)/shard_map/finish_0/pallas_call | solution.py:478
  63.1 1.0 %collective-permute-done.15.refs_0_ = bf16[2,256,128]{2,1,0:T(8,128)(2,1)S(1)} collective-permute-done((bf16[2,256,128]{2,1,0:T(8,128)(2,1)S(1)}, bf16[2,256,128]{2,1,0:T(8,128)(2,1)S(1)}, u32[]{:S(2)}, u32[]{:S(2)}) %collective-permute-start.15) | collective-permute-done | bytes 131104 | tf_op jit(solution)/shard_map/ppermute | solution.py:306
  64.1 0.0 collective-permute-done.16.refs_1_
  64.1 1.4 %finish_1.1 = bf16[8,56,1152]{2,1,0:T(8,128)(2,1)} custom-call(f32[6,1152]{1,0:T(8,128)S(1)} %copy-done.5, bf16[576,1152]{1,0:T(8,128)(2,1)S(1)} %copy-done.4, bf16[8,56,1152]{2,1,0:T(8,128)(2,1)S(1)} %residual.1.after, bf16[2,256,128]{2,1,0:T(8,128)(2,1)S(1)} %collective-permute-done.15.refs_0_, ...), custom_call_target="tpu_custom_call", output_to_operand_aliasing={{}: (5, {})} | custom-call | flops 297271296 | bytes 2972712 | tf_op jit(solution)/shard_map/finish_1/pallas_call | solution.py:478
  (4 shorter events, 0.1 us)
Async XLA Ops:
  0.0 10.7 %copy-start.2 = (bf16[1152,1728]{0,1:T(8,128)(2,1)S(1)}, bf16[1152,1728]{0,1:T(8,128)(2,1)}, u32[]{:S(2)}) copy-start(bf16[1152,1728]{0,1:T(8,128)(2,1)} %param.10) | copy-start | bytes 11943940
  0.0 3.8 %copy-start.3 = (bf16[1,448,1152]{2,1,0:T(8,128)(2,1)S(1)}, bf16[1,448,1152]{2,1,0:T(8,128)(2,1)}, u32[]{:S(2)}) copy-start(bf16[1,448,1152]{2,1,0:T(8,128)(2,1)} %param.7) | copy-start | bytes 3096580
  3.8 14.7 %copy-start.7 = (s32[1,448]{1,0:T(1,128)S(1)}, s32[1,448]{1,0:T(1,128)}, u32[]{:S(2)}) copy-start(s32[1,448]{1,0:T(1,128)} %slot.3) | copy-start | bytes 5380
  3.9 5.2 %collective-permute-start.6 = (bf16[4,56,1152]{2,1,0:T(8,128)(2,1)S(1)}, bf16[4,56,1152]{2,1,0:T(8,128)(2,1)S(1)}, u32[]{:S(2)}, u32[]{:S(2)}) collective-permute-start(bf16[4,56,1152]{2,1,0:T(8,128)(2,1)S(1)} %get-tuple-element.68), channel_id=1, source_target_pairs={{0,4},{4,0},{8,12},{12,8},{16,20},{20,16},{24,28},{28,24},{1,5},{5... | collective-permute-start | bytes 1548296 | tf_op jit(solution)/shard_map/ppermute | solution.py:306
  4.4 13.2 %collective-permute-start = (bf16[768,128]{1,0:T(8,128)(2,1)}, bf16[768,128]{1,0:T(8,128)(2,1)S(1)}, u32[]{:S(2)}, u32[]{:S(2)}) collective-permute-start(bf16[768,128]{1,0:T(8,128)(2,1)} %get-tuple-element.49), channel_id=1, source_target_pairs={{0,3},{1,2},{2,1},{3,0},{4,7},{5,6},{6,5},{7,4},{8,11},{9,10},{10,... | collective-permute-start | bytes 589832 | tf_op jit(solution)/shard_map/ppermute | solution.py:306
  9.1 34.2 %copy-start = (bf16[1152,1728]{0,1:T(8,128)(2,1)S(1)}, bf16[1152,1728]{0,1:T(8,128)(2,1)}, u32[]{:S(2)}) copy-start(bf16[1152,1728]{0,1:T(8,128)(2,1)} %param.12) | copy-start | bytes 11943940
  9.2 34.1 %copy-start.1 = (bf16[576,1152]{1,0:T(8,128)(2,1)S(1)}, bf16[576,1152]{1,0:T(8,128)(2,1)}, u32[]{:S(2)}) copy-start(bf16[576,1152]{1,0:T(8,128)(2,1)} %proj.9) | copy-start | bytes 3981316
  9.2 34.1 %copy-start.5 = (f32[6,1152]{1,0:T(8,128)S(1)}, f32[6,1152]{1,0:T(8,128)}, u32[]{:S(2)}) copy-start(f32[6,1152]{1,0:T(8,128)} %modulation.13) | copy-start | bytes 82948
  9.2 22.3 %collective-permute-start.7 = (bf16[2,56,1152]{2,1,0:T(8,128)(2,1)S(1)}, bf16[2,56,1152]{2,1,0:T(8,128)(2,1)S(1)}, u32[]{:S(2)}, u32[]{:S(2)}) collective-permute-start(bf16[2,56,1152]{2,1,0:T(8,128)(2,1)S(1)} %get-tuple-element.70), channel_id=1, source_target_pairs={{0,8},{4,12},{8,0},{12,4},{16,24},{20,28},{24,16},{28,20},{1,9},{5... | collective-permute-start | bytes 774152 | tf_op jit(solution)/shard_map/ppermute | solution.py:306
  10.7 1.1 %copy-start.6 = (bf16[224,1152]{1,0:T(8,128)(2,1)S(1)}, bf16[224,1152]{1,0:T(8,128)(2,1)}, u32[]{:S(2)}) copy-start(bf16[224,1152]{1,0:T(8,128)(2,1)} %get-tuple-element.53.merged) | copy-start | bytes 1548292
  13.7 12.9 %collective-permute-start.1 = (bf16[768,128]{1,0:T(8,128)(2,1)S(1)}, bf16[768,128]{1,0:T(8,128)(2,1)S(1)}, u32[]{:S(2)}, u32[]{:S(2)}) collective-permute-start(bf16[768,128]{1,0:T(8,128)(2,1)S(1)} %get-tuple-element.54), channel_id=1, source_target_pairs={{0,2},{1,3},{2,0},{3,1},{4,6},{5,7},{6,4},{7,5},{8,10},{9,11},{10,... | collective-permute-start | bytes 589832 | tf_op jit(solution)/shard_map/ppermute | solution.py:306
  14.5 12.1 %collective-permute-start.2 = (bf16[768,128]{1,0:T(8,128)(2,1)S(1)}, bf16[768,128]{1,0:T(8,128)(2,1)S(1)}, u32[]{:S(2)}, u32[]{:S(2)}) collective-permute-start(bf16[768,128]{1,0:T(8,128)(2,1)S(1)} %get-tuple-element.55), channel_id=1, source_target_pairs={{0,1},{1,0},{2,3},{3,2},{4,5},{5,4},{6,7},{7,6},{8,9},{9,8},{10,11... | collective-permute-start | bytes 589832 | tf_op jit(solution)/shard_map/ppermute | solution.py:306
  16.1 17.3 %collective-permute-start.8 = (bf16[2,56,1152]{2,1,0:T(8,128)(2,1)S(1)}, bf16[2,56,1152]{2,1,0:T(8,128)(2,1)S(1)}, u32[]{:S(2)}, u32[]{:S(2)}) collective-permute-start(bf16[2,56,1152]{2,1,0:T(8,128)(2,1)S(1)} %get-tuple-element.71), channel_id=1, source_target_pairs={{0,16},{4,20},{8,24},{12,28},{16,0},{20,4},{24,8},{28,12},{1,17},{... | collective-permute-start | bytes 774152 | tf_op jit(solution)/shard_map/ppermute | solution.py:306
  17.6 15.7 %collective-permute-start.9 = (bf16[2,56,1152]{2,1,0:T(8,128)(2,1)S(1)}, bf16[2,56,1152]{2,1,0:T(8,128)(2,1)S(1)}, u32[]{:S(2)}, u32[]{:S(2)}) collective-permute-start(bf16[2,56,1152]{2,1,0:T(8,128)(2,1)S(1)} %get-tuple-element.72), channel_id=1, source_target_pairs={{0,24},{4,28},{8,16},{12,20},{16,8},{20,12},{24,0},{28,4},{1,25},{... | collective-permute-start | bytes 774152 | tf_op jit(solution)/shard_map/ppermute | solution.py:306
  28.9 6.5 %collective-permute-start.3 = (bf16[272,128]{1,0:T(8,128)(2,1)S(1)}, bf16[272,128]{1,0:T(8,128)(2,1)S(1)}, u32[]{:S(2)}, u32[]{:S(2)}) collective-permute-start(bf16[272,128]{1,0:T(8,128)(2,1)S(1)} %get-tuple-element.62), channel_id=1, source_target_pairs={{0,3},{1,2},{2,1},{3,0},{4,7},{5,6},{6,5},{7,4},{8,11},{9,10},{10,... | collective-permute-start | bytes 208904 | tf_op jit(solution)/shard_map/ppermute | solution.py:306
  31.4 6.1 %collective-permute-start.4 = (bf16[272,128]{1,0:T(8,128)(2,1)S(1)}, bf16[272,128]{1,0:T(8,128)(2,1)S(1)}, u32[]{:S(2)}, u32[]{:S(2)}) collective-permute-start(bf16[272,128]{1,0:T(8,128)(2,1)S(1)} %get-tuple-element.63), channel_id=1, source_target_pairs={{0,2},{1,3},{2,0},{3,1},{4,6},{5,7},{6,4},{7,5},{8,10},{9,11},{10,... | collective-permute-start | bytes 208904 | tf_op jit(solution)/shard_map/ppermute | solution.py:306
  31.5 6.0 %collective-permute-start.5 = (bf16[272,128]{1,0:T(8,128)(2,1)S(1)}, bf16[272,128]{1,0:T(8,128)(2,1)S(1)}, u32[]{:S(2)}, u32[]{:S(2)}) collective-permute-start(bf16[272,128]{1,0:T(8,128)(2,1)S(1)} %get-tuple-element.64), channel_id=1, source_target_pairs={{0,1},{1,0},{2,3},{3,2},{4,5},{5,4},{6,7},{7,6},{8,9},{9,8},{10,11... | collective-permute-start | bytes 208904 | tf_op jit(solution)/shard_map/ppermute | solution.py:306
  38.1 1.6 %collective-permute-start.10 = (bf16[4,256,128]{2,1,0:T(8,128)(2,1)S(1)}, bf16[4,256,128]{2,1,0:T(8,128)(2,1)S(1)}, u32[]{:S(2)}, u32[]{:S(2)}) collective-permute-start(bf16[4,256,128]{2,1,0:T(8,128)(2,1)S(1)} %get-tuple-element.80), channel_id=1, source_target_pairs={{0,4},{4,0},{8,12},{12,8},{16,20},{20,16},{24,28},{28,24},{1,5},{5... | collective-permute-start | bytes 786440 | tf_op jit(solution)/shard_map/ppermute | solution.py:306
  39.7 6.8 %collective-permute-start.13 = (bf16[2,256,128]{2,1,0:T(8,128)(2,1)S(1)}, bf16[2,256,128]{2,1,0:T(8,128)(2,1)S(1)}, u32[]{:S(2)}, u32[]{:S(2)}) collective-permute-start(bf16[2,256,128]{2,1,0:T(8,128)(2,1)S(1)} %get-tuple-element.86), channel_id=1, source_target_pairs={{0,24},{4,28},{8,16},{12,20},{16,8},{20,12},{24,0},{28,4},{1,25},{... | collective-permute-start | bytes 393224 | tf_op jit(solution)/shard_map/ppermute | solution.py:306
  42.2 6.8 %collective-permute-start.11 = (bf16[2,256,128]{2,1,0:T(8,128)(2,1)S(1)}, bf16[2,256,128]{2,1,0:T(8,128)(2,1)S(1)}, u32[]{:S(2)}, u32[]{:S(2)}) collective-permute-start(bf16[2,256,128]{2,1,0:T(8,128)(2,1)S(1)} %get-tuple-element.81), channel_id=1, source_target_pairs={{0,16},{4,20},{8,24},{12,28},{16,0},{20,4},{24,8},{28,12},{1,17},{... | collective-permute-start | bytes 393224 | tf_op jit(solution)/shard_map/ppermute | solution.py:306
  42.8 6.4 %collective-permute-start.12 = (bf16[2,256,128]{2,1,0:T(8,128)(2,1)S(1)}, bf16[2,256,128]{2,1,0:T(8,128)(2,1)S(1)}, u32[]{:S(2)}, u32[]{:S(2)}) collective-permute-start(bf16[2,256,128]{2,1,0:T(8,128)(2,1)S(1)} %get-tuple-element.82), channel_id=1, source_target_pairs={{0,8},{4,12},{8,0},{12,4},{16,24},{20,28},{24,16},{28,20},{1,9},{5... | collective-permute-start | bytes 393224 | tf_op jit(solution)/shard_map/ppermute | solution.py:306
  53.1 8.6 %copy-start.4 = (bf16[576,1152]{1,0:T(8,128)(2,1)S(1)}, bf16[576,1152]{1,0:T(8,128)(2,1)}, u32[]{:S(2)}) copy-start(bf16[576,1152]{1,0:T(8,128)(2,1)} %proj.11) | copy-start | bytes 3981316
  53.1 1.6 %collective-permute-start.14 = (bf16[4,256,128]{2,1,0:T(8,128)(2,1)S(1)}, bf16[4,256,128]{2,1,0:T(8,128)(2,1)S(1)}, u32[]{:S(2)}, u32[]{:S(2)}) collective-permute-start(bf16[4,256,128]{2,1,0:T(8,128)(2,1)S(1)} %get-tuple-element.88), channel_id=1, source_target_pairs={{0,4},{4,0},{8,12},{12,8},{16,20},{20,16},{24,28},{28,24},{1,5},{5... | collective-permute-start | bytes 786440 | tf_op jit(solution)/shard_map/ppermute | solution.py:306
  54.8 6.9 %collective-permute-start.17 = (bf16[2,256,128]{2,1,0:T(8,128)(2,1)S(1)}, bf16[2,256,128]{2,1,0:T(8,128)(2,1)S(1)}, u32[]{:S(2)}, u32[]{:S(2)}) collective-permute-start(bf16[2,256,128]{2,1,0:T(8,128)(2,1)S(1)} %get-tuple-element.92), channel_id=1, source_target_pairs={{0,24},{4,28},{8,16},{12,20},{16,8},{20,12},{24,0},{28,4},{1,25},{... | collective-permute-start | bytes 393224 | tf_op jit(solution)/shard_map/ppermute | solution.py:306
  57.2 6.9 %collective-permute-start.15 = (bf16[2,256,128]{2,1,0:T(8,128)(2,1)S(1)}, bf16[2,256,128]{2,1,0:T(8,128)(2,1)S(1)}, u32[]{:S(2)}, u32[]{:S(2)}) collective-permute-start(bf16[2,256,128]{2,1,0:T(8,128)(2,1)S(1)} %get-tuple-element.89), channel_id=1, source_target_pairs={{0,16},{4,20},{8,24},{12,28},{16,0},{20,4},{24,8},{28,12},{1,17},{... | collective-permute-start | bytes 393224 | tf_op jit(solution)/shard_map/ppermute | solution.py:306
  57.8 6.3 %collective-permute-start.16 = (bf16[2,256,128]{2,1,0:T(8,128)(2,1)S(1)}, bf16[2,256,128]{2,1,0:T(8,128)(2,1)S(1)}, u32[]{:S(2)}, u32[]{:S(2)}) collective-permute-start(bf16[2,256,128]{2,1,0:T(8,128)(2,1)S(1)} %get-tuple-element.90), channel_id=1, source_target_pairs={{0,8},{4,12},{8,0},{12,4},{16,24},{20,28},{24,16},{28,20},{1,9},{5... | collective-permute-start | bytes 393224 | tf_op jit(solution)/shard_map/ppermute | solution.py:306

commit v5 on v4

--- a/solution.py
+++ b/solution.py
@@ -53,7 +53,7 @@
 
 def packed_rows(rows, width):
     full, rest, parts, high = packing(rows, width)
-    return -(-(full * rows + (max(parts - 1, 1) * high if rest else 0)) // SUB) * SUB
+    return -(-(full * rows + (max(parts - 1, 1) * high if rest else 0)) // 8) * 8
 
 
 def pack(block):
@@ -72,8 +72,8 @@
                 side = last[:, i * free : (i + 1) * free]
                 pieces.append(jnp.concatenate([tail[i * high : (i + 1) * high], side], 1))
     here = sum(p.shape[0] for p in pieces)
-    if here % SUB:
-        pieces.append(jnp.zeros((-here % SUB, LANES), block.dtype))
+    if here % 8:
+        pieces.append(jnp.zeros((-here % 8, LANES), block.dtype))
     return jnp.concatenate(pieces, 0)
 
 
@@ -258,27 +258,30 @@
     size = n_frames * SUB
     row = lax.broadcasted_iota(jnp.int32, (size, size), 0)
     col = lax.broadcasted_iota(jnp.int32, (size, size), 1)
-    same = jnp.concatenate([(row & (SUB - 1)) == (col & (SUB - 1))] * heads, 1)
+    same = jnp.concatenate([(row & (SUB - 1)) == (col & (SUB - 1))] * (heads * groups), 1)
+    blocks = [jnp.concatenate([b[g * SUB : (g + 1) * SUB] for b in by_frame], 0) for g in range(groups)]
+    scores = [
+        dot_t(block[:, inner + h * HD : inner + (h + 1) * HD], block[:, h * HD : (h + 1) * HD])
+        for block in blocks
+        for h in range(heads)
+    ]
+    scores = jnp.where(same, jnp.concatenate(scores, 1), -jnp.inf)
+    mix = jnp.exp2((scores - jnp.max(scores, 0, keepdims=True)) * SCALE)
+    total = jnp.sum(mix, 0, keepdims=True)
+    mix = mix.astype(BF16)
+    mixed = []
+    for g, block in enumerate(blocks):
+        vals = block[:, 2 * inner :].astype(F32).T
+        parts = []
+        for h in range(heads):
+            at = slice((g * heads + h) * size, (g * heads + h + 1) * size)
+            parts.append(dot(vals[h * HD : (h + 1) * HD].astype(BF16), mix[:, at]) / total[:, at])
+        mixed.append(jnp.concatenate(parts, 0))
+    whole = jnp.concatenate(mixed, 1).T.astype(BF16)
     for g in range(groups):
-        block = jnp.concatenate([b[g * SUB : (g + 1) * SUB] for b in by_frame], 0)
-
-        def part(j, h):
-            return block[:, j * inner + h * HD : j * inner + (h + 1) * HD]
-
-        scores = jnp.concatenate([dot_t(part(1, h), part(0, h)) for h in range(heads)], 1)
-        scores = jnp.where(same, scores, -jnp.inf)
-        mix = jnp.exp2((scores - jnp.max(scores, 0, keepdims=True)) * SCALE)
-        total = jnp.sum(mix, 0, keepdims=True)
-        mix = mix.astype(BF16)
-        vals = block[:, 2 * inner :].astype(F32).T
-        mixed = [
-            dot(vals[h * HD : (h + 1) * HD].astype(BF16), mix[:, h * size : (h + 1) * size])
-            / total[:, h * size : (h + 1) * size]
-            for h in range(heads)
-        ]
-        whole = jnp.concatenate(mixed, 0).T.astype(BF16)
         for f in range(n_frames):
-            held[f, g * SUB : (g + 1) * SUB] = whole[f * SUB : (f + 1) * SUB]
+            at = g * size + f * SUB
+            held[f, g * SUB : (g + 1) * SUB] = whole[at : at + SUB]
     for i, s in enumerate(order):
         keep[s] = pack(held[2 * i].astype(F32)[:places]).astype(BF16)
         give[s] = pack(held[2 * i + 1].astype(F32)[:places]).astype(BF16)

time: 65.7 us -> 65.3 us (level)
  no operation moved by 1% of the time
where the time goes in v5:
time: 65.3 us; the launch traced here: 65.2 us
  starting transfers between devices  23.2 us (36%)
  Pallas kernels  21.7 us (33%)
  waiting for transfers between devices  19 us (29%)
  local copies, waits for them, and re-layouts  1.09 us (2%)
    ppermute x18, starting transfers between devices, swap(): return lax.ppermute(block, axis, [(i, i ^ mask) for i in range(size)])  23.2 us
    ppermute x18, waiting for transfers between devices, swap(): return lax.ppermute(block, axis, [(i, i ^ mask) for i in range(size)])  19 us
    pallas_call x2, Pallas kernels, shards(): pl.pallas_call(functools.partial(project_kernel, places, len(step)), out_...  3.81 us
    pallas_call x1, Pallas kernels, shards(): pl.pallas_call(functools.partial(temporal_kernel, n_pair, places, len(las...  3.76 us
    pallas_call x1, Pallas kernels, shards(): pl.pallas_call(functools.partial(merge_kernel, n_space), out_shape=[struc...  3.74 us
    pallas_call x2, Pallas kernels, shards(): pl.pallas_call(functools.partial(finish_kernel, step, places), out_shape=...  2.84 us
    pallas_call x1, Pallas kernels, shards(): pl.pallas_call(functools.partial(others_kernel, n_space, slots, wide), ou...  2.31 us
    pallas_call x1, Pallas kernels, shards(): pl.pallas_call(functools.partial(spread_kernel, n_space), out_shape=[stru...  1.85 us
  transfers between devices with their start and end apart: 18, of which 10 were waited for; matrix products, arithmetic and copies ran while one was open for 0% of the time, Pallas kernels for 18%

profile of v5, /device:TPU:0, one launch (start us, length us, event | category | flops | bytes accessed | tf_op | source)
XLA Modules:
  0.0 65.2 jit_solution(5616257589252578186)
XLA Ops:
  0.0 0.0 copy-start.2
  0.0 3.7 %merge.1 = (bf16[768,128]{1,0:T(8,128)(2,1)}, bf16[224,1152]{1,0:T(8,128)(2,1)}) custom-call(bf16[8,56,1152]{2,1,0:T(8,128)(2,1)} %bitcast.9, s32[1,448]{1,0:T(1,128)} %slot.3, f32[6,1152]{1,0:T(8,128)} %modulation.13, bf16[1728,1152]{1,0:T(8,128)(2,1)} %bitcast.7), custom_call_target="tpu_custom_call" | custom-call | tf_op jit(solution)/shard_map/merge/pallas_call | solution.py:339
  3.8 0.0 copy-start.7
  3.8 0.0 copy-done.3
  3.8 0.1 share.1
  3.9 0.5 collective-permute-start.6
  4.4 4.7 %collective-permute-start = (bf16[768,128]{1,0:T(8,128)(2,1)}, bf16[768,128]{1,0:T(8,128)(2,1)S(1)}, u32[]{:S(2)}, u32[]{:S(2)}) collective-permute-start(bf16[768,128]{1,0:T(8,128)(2,1)} %get-tuple-element.49), channel_id=1, source_target_pairs={{0,3},{1,2},{2,1},{3,0},{4,7},{5,6},{6,5},{7,4},{8,11},{9,10},{10,... | collective-permute-start | bytes 589832 | tf_op jit(solution)/shard_map/ppermute | solution.py:309
  9.1 0.0 collective-permute-done.6.got
  9.1 0.1 pair.3
  9.1 0.0 copy-start
  9.2 0.0 copy-start.1
  9.2 0.0 copy-start.5
  9.2 1.6 %collective-permute-start.7 = (bf16[2,56,1152]{2,1,0:T(8,128)(2,1)S(1)}, bf16[2,56,1152]{2,1,0:T(8,128)(2,1)S(1)}, u32[]{:S(2)}, u32[]{:S(2)}) collective-permute-start(bf16[2,56,1152]{2,1,0:T(8,128)(2,1)S(1)} %get-tuple-element.70), channel_id=1, source_target_pairs={{0,8},{4,12},{8,0},{12,4},{16,24},{20,28},{24,16},{28,20},{1,9},{5... | collective-permute-start | bytes 774152 | tf_op jit(solution)/shard_map/ppermute | solution.py:309
  10.7 0.0 copy-done.2
  10.7 1.0 %copy-done.6 = bf16[224,1152]{1,0:T(8,128)(2,1)S(1)} copy-done((bf16[224,1152]{1,0:T(8,128)(2,1)S(1)}, bf16[224,1152]{1,0:T(8,128)(2,1)}, u32[]{:S(2)}) %copy-start.6) | copy-done | bytes 516120
  11.8 1.9 %spread.1 = (bf16[768,128]{1,0:T(8,128)(2,1)S(1)}, bf16[768,128]{1,0:T(8,128)(2,1)S(1)}, bf16[768,128]{1,0:T(8,128)(2,1)S(1)}) custom-call(bf16[224,1152]{1,0:T(8,128)(2,1)S(1)} %copy-done.6, bf16[1728,1152]{1,0:T(8,128)(2,1)S(1)} %bitcast.8), custom_call_target="tpu_custom_call" | custom-call | flops 891813888 | bytes 8918138 | tf_op jit(solution)/shard_map/spread/pallas_call | solution.py:354
  13.7 0.9 %collective-permute-start.1 = (bf16[768,128]{1,0:T(8,128)(2,1)S(1)}, bf16[768,128]{1,0:T(8,128)(2,1)S(1)}, u32[]{:S(2)}, u32[]{:S(2)}) collective-permute-start(bf16[768,128]{1,0:T(8,128)(2,1)S(1)} %get-tuple-element.54), channel_id=1, source_target_pairs={{0,2},{1,3},{2,0},{3,1},{4,6},{5,7},{6,4},{7,5},{8,10},{9,11},{10,... | collective-permute-start | bytes 589832 | tf_op jit(solution)/shard_map/ppermute | solution.py:309
  14.5 1.6 %collective-permute-start.2 = (bf16[768,128]{1,0:T(8,128)(2,1)S(1)}, bf16[768,128]{1,0:T(8,128)(2,1)S(1)}, u32[]{:S(2)}, u32[]{:S(2)}) collective-permute-start(bf16[768,128]{1,0:T(8,128)(2,1)S(1)} %get-tuple-element.55), channel_id=1, source_target_pairs={{0,1},{1,0},{2,3},{3,2},{4,5},{5,4},{6,7},{7,6},{8,9},{9,8},{10,11... | collective-permute-start | bytes 589832 | tf_op jit(solution)/shard_map/ppermute | solution.py:309
  16.1 1.5 %collective-permute-start.8 = (bf16[2,56,1152]{2,1,0:T(8,128)(2,1)S(1)}, bf16[2,56,1152]{2,1,0:T(8,128)(2,1)S(1)}, u32[]{:S(2)}, u32[]{:S(2)}) collective-permute-start(bf16[2,56,1152]{2,1,0:T(8,128)(2,1)S(1)} %get-tuple-element.71), channel_id=1, source_target_pairs={{0,16},{4,20},{8,24},{12,28},{16,0},{20,4},{24,8},{28,12},{1,17},{... | collective-permute-start | bytes 774152 | tf_op jit(solution)/shard_map/ppermute | solution.py:309
  17.6 0.0 collective-permute-done.packed
  17.6 0.8 %collective-permute-start.9 = (bf16[2,56,1152]{2,1,0:T(8,128)(2,1)S(1)}, bf16[2,56,1152]{2,1,0:T(8,128)(2,1)S(1)}, u32[]{:S(2)}, u32[]{:S(2)}) collective-permute-start(bf16[2,56,1152]{2,1,0:T(8,128)(2,1)S(1)} %get-tuple-element.72), channel_id=1, source_target_pairs={{0,24},{4,28},{8,16},{12,20},{16,8},{20,12},{24,0},{28,4},{1,25},{... | collective-permute-start | bytes 774152 | tf_op jit(solution)/shard_map/ppermute | solution.py:309
  18.4 0.0 copy-done.7
  18.4 0.3 prepare.1
  18.7 7.9 %collective-permute-done.1.refs_0_ = bf16[768,128]{1,0:T(8,128)(2,1)S(1)} collective-permute-done((bf16[768,128]{1,0:T(8,128)(2,1)S(1)}, bf16[768,128]{1,0:T(8,128)(2,1)S(1)}, u32[]{:S(2)}, u32[]{:S(2)}) %collective-permute-start.1) | collective-permute-done | bytes 196640 | tf_op jit(solution)/shard_map/ppermute | solution.py:309
  26.6 0.0 collective-permute-done.2.refs_1_
  26.6 2.3 %attend_others.1 = (bf16[264,128]{1,0:T(8,128)(2,1)S(1)}, bf16[264,128]{1,0:T(8,128)(2,1)S(1)}, bf16[264,128]{1,0:T(8,128)(2,1)S(1)}, bf16[144,224]{1,0:T(8,128)...) custom-call(bf16[224,144]{1,0:T(8,128)(2,1)S(1)} %get-tuple-element.57.far_keys, ...), custom_call_target="tpu_custom_call" | custom-call | flops 346816512 | bytes 3468165 | tf_op jit(solution)/shard_map/attend_others/pallas_call | solution.py:393
  28.9 2.5 %collective-permute-start.3 = (bf16[264,128]{1,0:T(8,128)(2,1)S(1)}, bf16[264,128]{1,0:T(8,128)(2,1)S(1)}, u32[]{:S(2)}, u32[]{:S(2)}) collective-permute-start(bf16[264,128]{1,0:T(8,128)(2,1)S(1)} %get-tuple-element.62), channel_id=1, source_target_pairs={{0,3},{1,2},{2,1},{3,0},{4,7},{5,6},{6,5},{7,4},{8,11},{9,10},{10,... | collective-permute-start | bytes 202760 | tf_op jit(solution)/shard_map/ppermute | solution.py:309
  31.4 0.0 collective-permute-start.4
  31.4 0.0 collective-permute-done.7.refs_1_
  31.4 1.9 %collective-permute-start.5 = (bf16[264,128]{1,0:T(8,128)(2,1)S(1)}, bf16[264,128]{1,0:T(8,128)(2,1)S(1)}, u32[]{:S(2)}, u32[]{:S(2)}) collective-permute-start(bf16[264,128]{1,0:T(8,128)(2,1)S(1)} %get-tuple-element.64), channel_id=1, source_target_pairs={{0,1},{1,0},{2,3},{3,2},{4,5},{5,4},{6,7},{7,6},{8,9},{9,8},{10,11... | collective-permute-start | bytes 202760 | tf_op jit(solution)/shard_map/ppermute | solution.py:309
  33.4 0.0 collective-permute-done.8.refs_0_
  33.4 0.0 collective-permute-done.9.refs_0_
  33.4 1.3 %attend_own.1.refs_3_ = bf16[144,224]{1,0:T(8,128)(2,1)S(1)} custom-call(bf16[144,224]{1,0:T(8,128)(2,1)S(1)} %get-tuple-element.73.queries, bf16[896,144]{1,0:T(8,128)(2,1)S(1)} %get-tuple-element.74.keys, bf16[144,896]{1,0:T(8,128)(2,1)S(1)} %get-tuple-element.75.vals), custom_call_target="tpu_custom_call" | custom-call | flops 115605504 | bytes 1156055 | tf_op jit(solution)/shard_map/attend_own/pallas_call | solution.py:404
  34.7 0.6 collective-permute-done.3.refs_0_
  35.3 2.1 %collective-permute-done.4.refs_1_ = bf16[264,128]{1,0:T(8,128)(2,1)S(1)} collective-permute-done((bf16[264,128]{1,0:T(8,128)(2,1)S(1)}, bf16[264,128]{1,0:T(8,128)(2,1)S(1)}, u32[]{:S(2)}, u32[]{:S(2)}) %collective-permute-start.4) | collective-permute-done | bytes 67616 | tf_op jit(solution)/shard_map/ppermute | solution.py:309
  37.4 0.0 collective-permute-done.5.refs_2_
  37.4 0.6 expand.1
  38.0 0.1 collective-permute-start.10
  38.0 1.5 %collective-permute-done.10.got = bf16[4,256,128]{2,1,0:T(8,128)(2,1)S(1)} collective-permute-done((bf16[4,256,128]{2,1,0:T(8,128)(2,1)S(1)}, bf16[4,256,128]{2,1,0:T(8,128)(2,1)S(1)}, u32[]{:S(2)}, u32[]{:S(2)}) %collective-permute-start.10) | collective-permute-done | bytes 262176 | tf_op jit(solution)/shard_map/ppermute | solution.py:309
  39.6 2.5 %collective-permute-start.13 = (bf16[2,256,128]{2,1,0:T(8,128)(2,1)S(1)}, bf16[2,256,128]{2,1,0:T(8,128)(2,1)S(1)}, u32[]{:S(2)}, u32[]{:S(2)}) collective-permute-start(bf16[2,256,128]{2,1,0:T(8,128)(2,1)S(1)} %get-tuple-element.86), channel_id=1, source_target_pairs={{0,24},{4,28},{8,16},{12,20},{16,8},{20,12},{24,0},{28,4},{1,25},{... | collective-permute-start | bytes 393224 | tf_op jit(solution)/shard_map/ppermute | solution.py:309
  42.1 0.5 collective-permute-start.11
  42.6 0.5 collective-permute-start.12
  43.2 0.0 copy-done
  43.2 0.0 copy-done.1
  43.2 0.0 copy-done.5
  43.2 1.9 %project_0.1.refs_4_ = bf16[2,64,1728]{2,1,0:T(8,128)(2,1)S(1)} custom-call(f32[6,1152]{1,0:T(8,128)S(1)} %copy-done.5, bf16[576,1152]{1,0:T(8,128)(2,1)S(1)} %copy-done.1, bf16[1728,1152]{1,0:T(8,128)(2,1)S(1)} %bitcast.4, bf16[2,56,1152]{2,1,0:T(8,128)(2,1)S(1)} %get-tuple-element.83.refs_0_, bf16[2,256,128]{2,1,0:T(8,128)(2,1)S(1)} %get-tuple-element.84.refs_1_), custom_call_target="tpu_custom_call" | custom-call | flops 445906944 | bytes 4459069 | tf_op jit(solution)/shard_map/project_0/pallas_call | solution.py:440
  45.1 1.3 %collective-permute-done.13.refs_1_ = bf16[2,256,128]{2,1,0:T(8,128)(2,1)S(1)} collective-permute-done((bf16[2,256,128]{2,1,0:T(8,128)(2,1)S(1)}, bf16[2,256,128]{2,1,0:T(8,128)(2,1)S(1)}, u32[]{:S(2)}, u32[]{:S(2)}) %collective-permute-start.13) | collective-permute-done | bytes 131104 | tf_op jit(solution)/shard_map/ppermute | solution.py:309
  46.4 1.9 %project_1.1.refs_5_ = bf16[2,64,1728]{2,1,0:T(8,128)(2,1)S(1)} custom-call(f32[6,1152]{1,0:T(8,128)S(1)} %copy-done.5, bf16[576,1152]{1,0:T(8,128)(2,1)S(1)} %copy-done.1, bf16[1728,1152]{1,0:T(8,128)(2,1)S(1)} %bitcast.5, bf16[2,56,1152]{2,1,0:T(8,128)(2,1)S(1)} %collective-permute-done.9.refs_0_, bf16[2,256,128]{2,1,0:T(8,128)(2,1)S(1)} %collective-permute-done.13.refs_1_), custom_call_target="tpu_custom_call" | custom-call | flops 445906944 | bytes 4459069 | tf_op jit(solution)/shard_map/project_1/pallas_call | solution.py:440
  48.3 0.6 collective-permute-done.11.refs_2_
  48.9 0.1 collective-permute-done.12.refs_3_
  49.0 3.8 %temporal.1 = (bf16[4,256,128]{2,1,0:T(8,128)(2,1)S(1)}, bf16[4,256,128]{2,1,0:T(8,128)(2,1)S(1)}) custom-call(f32[6,1152]{1,0:T(8,128)S(1)} %copy-done.5, bf16[576,1152]{1,0:T(8,128)(2,1)S(1)} %copy-done.1, bf16[1728,1152]{1,0:T(8,128)(2,1)S(1)} %bitcast.6, bf16[2,56,1152]{2,1,0:T(8,128)(2,1)S(1)} %collective-permute-done.8.refs_0_, ...), custom_call_target="tpu_custom_call" | custom-call | tf_op jit(solution)/shard_map/temporal/pallas_call | solution.py:457
  52.8 0.0 copy-start.4
  52.8 0.1 collective-permute-start.14
  52.9 1.5 %collective-permute-done.14.got = bf16[4,256,128]{2,1,0:T(8,128)(2,1)S(1)} collective-permute-done((bf16[4,256,128]{2,1,0:T(8,128)(2,1)S(1)}, bf16[4,256,128]{2,1,0:T(8,128)(2,1)S(1)}, u32[]{:S(2)}, u32[]{:S(2)}) %collective-permute-start.14) | collective-permute-done | bytes 262176 | tf_op jit(solution)/shard_map/ppermute | solution.py:309
  54.4 2.4 %collective-permute-start.17 = (bf16[2,256,128]{2,1,0:T(8,128)(2,1)S(1)}, bf16[2,256,128]{2,1,0:T(8,128)(2,1)S(1)}, u32[]{:S(2)}, u32[]{:S(2)}) collective-permute-start(bf16[2,256,128]{2,1,0:T(8,128)(2,1)S(1)} %get-tuple-element.92), channel_id=1, source_target_pairs={{0,24},{4,28},{8,16},{12,20},{16,8},{20,12},{24,0},{28,4},{1,25},{... | collective-permute-start | bytes 393224 | tf_op jit(solution)/shard_map/ppermute | solution.py:309
  56.8 0.6 collective-permute-start.15
  57.5 0.5 collective-permute-start.16
  58.0 1.0 %residual.1.after = bf16[8,56,1152]{2,1,0:T(8,128)(2,1)S(1)} custom-call(bf16[576,224]{1,0:T(8,128)(2,1)S(1)} %get-tuple-element.76.attended, bf16[448,224]{1,0:T(8,128)(2,1)S(1)} %get-tuple-element.50.chosen, bf16[8,56,1152]{2,1,0:T(8,128)(2,1)S(1)} %bitcast.11, f32[6,1152]{1,0:T(8,128)S(1)} %copy-done.5, bf16[576,1152]{1,0:T(8,128)(2,1)S(1)} %copy-done.1), custom_call_target="tpu_custom_call" | custom-call | flops 594542592 | bytes 5945425 | tf_op jit(solution)/shard_map/residual/pallas_call | solution.py:424
  59.0 2.3 %collective-permute-done.17.refs_1_ = bf16[2,256,128]{2,1,0:T(8,128)(2,1)S(1)} collective-permute-done((bf16[2,256,128]{2,1,0:T(8,128)(2,1)S(1)}, bf16[2,256,128]{2,1,0:T(8,128)(2,1)S(1)}, u32[]{:S(2)}, u32[]{:S(2)}) %collective-permute-start.17) | collective-permute-done | bytes 131104 | tf_op jit(solution)/shard_map/ppermute | solution.py:309
  61.3 0.0 copy-done.4
  61.3 1.4 %finish_0.1.refs_2_ = bf16[8,56,1152]{2,1,0:T(8,128)(2,1)} custom-call(f32[6,1152]{1,0:T(8,128)S(1)} %copy-done.5, bf16[576,1152]{1,0:T(8,128)(2,1)S(1)} %copy-done.4, bf16[8,56,1152]{2,1,0:T(8,128)(2,1)S(1)} %residual.1.after, bf16[2,256,128]{2,1,0:T(8,128)(2,1)S(1)} %get-tuple-element.91.refs_0_, bf16[2,256,128]{2,1,0:T(8,128)(2,1)S(1)} %collective-permute-done.17.refs_1_), custom_call_target="tpu_custom_call" | custom-call | flops 297271296 | bytes 2972712 | tf_op jit(solution)/shard_map/finish_0/pallas_call | solution.py:481
  62.7 1.0 %collective-permute-done.15.refs_0_ = bf16[2,256,128]{2,1,0:T(8,128)(2,1)S(1)} collective-permute-done((bf16[2,256,128]{2,1,0:T(8,128)(2,1)S(1)}, bf16[2,256,128]{2,1,0:T(8,128)(2,1)S(1)}, u32[]{:S(2)}, u32[]{:S(2)}) %collective-permute-start.15) | collective-permute-done | bytes 131104 | tf_op jit(solution)/shard_map/ppermute | solution.py:309
  63.7 0.0 collective-permute-done.16.refs_1_
  63.7 1.4 %finish_1.1 = bf16[8,56,1152]{2,1,0:T(8,128)(2,1)} custom-call(f32[6,1152]{1,0:T(8,128)S(1)} %copy-done.5, bf16[576,1152]{1,0:T(8,128)(2,1)S(1)} %copy-done.4, bf16[8,56,1152]{2,1,0:T(8,128)(2,1)S(1)} %residual.1.after, bf16[2,256,128]{2,1,0:T(8,128)(2,1)S(1)} %collective-permute-done.15.refs_0_, ...), custom_call_target="tpu_custom_call", output_to_operand_aliasing={{}: (5, {})} | custom-call | flops 297271296 | bytes 2972712 | tf_op jit(solution)/shard_map/finish_1/pallas_call | solution.py:481
  (4 shorter events, 0.1 us)
Async XLA Ops:
  0.0 10.7 %copy-start.2 = (bf16[1152,1728]{0,1:T(8,128)(2,1)S(1)}, bf16[1152,1728]{0,1:T(8,128)(2,1)}, u32[]{:S(2)}) copy-start(bf16[1152,1728]{0,1:T(8,128)(2,1)} %param.10) | copy-start | bytes 11943940
  0.0 3.8 %copy-start.3 = (bf16[1,448,1152]{2,1,0:T(8,128)(2,1)S(1)}, bf16[1,448,1152]{2,1,0:T(8,128)(2,1)}, u32[]{:S(2)}) copy-start(bf16[1,448,1152]{2,1,0:T(8,128)(2,1)} %param.7) | copy-start | bytes 3096580
  3.8 14.7 %copy-start.7 = (s32[1,448]{1,0:T(1,128)S(1)}, s32[1,448]{1,0:T(1,128)}, u32[]{:S(2)}) copy-start(s32[1,448]{1,0:T(1,128)} %slot.3) | copy-start | bytes 5380
  3.9 5.2 %collective-permute-start.6 = (bf16[4,56,1152]{2,1,0:T(8,128)(2,1)S(1)}, bf16[4,56,1152]{2,1,0:T(8,128)(2,1)S(1)}, u32[]{:S(2)}, u32[]{:S(2)}) collective-permute-start(bf16[4,56,1152]{2,1,0:T(8,128)(2,1)S(1)} %get-tuple-element.68), channel_id=1, source_target_pairs={{0,4},{4,0},{8,12},{12,8},{16,20},{20,16},{24,28},{28,24},{1,5},{5... | collective-permute-start | bytes 1548296 | tf_op jit(solution)/shard_map/ppermute | solution.py:309
  4.4 13.2 %collective-permute-start = (bf16[768,128]{1,0:T(8,128)(2,1)}, bf16[768,128]{1,0:T(8,128)(2,1)S(1)}, u32[]{:S(2)}, u32[]{:S(2)}) collective-permute-start(bf16[768,128]{1,0:T(8,128)(2,1)} %get-tuple-element.49), channel_id=1, source_target_pairs={{0,3},{1,2},{2,1},{3,0},{4,7},{5,6},{6,5},{7,4},{8,11},{9,10},{10,... | collective-permute-start | bytes 589832 | tf_op jit(solution)/shard_map/ppermute | solution.py:309
  9.1 34.0 %copy-start = (bf16[1152,1728]{0,1:T(8,128)(2,1)S(1)}, bf16[1152,1728]{0,1:T(8,128)(2,1)}, u32[]{:S(2)}) copy-start(bf16[1152,1728]{0,1:T(8,128)(2,1)} %param.12) | copy-start | bytes 11943940
  9.2 34.0 %copy-start.1 = (bf16[576,1152]{1,0:T(8,128)(2,1)S(1)}, bf16[576,1152]{1,0:T(8,128)(2,1)}, u32[]{:S(2)}) copy-start(bf16[576,1152]{1,0:T(8,128)(2,1)} %proj.9) | copy-start | bytes 3981316
  9.2 34.0 %copy-start.5 = (f32[6,1152]{1,0:T(8,128)S(1)}, f32[6,1152]{1,0:T(8,128)}, u32[]{:S(2)}) copy-start(f32[6,1152]{1,0:T(8,128)} %modulation.13) | copy-start | bytes 82948
  9.2 22.3 %collective-permute-start.7 = (bf16[2,56,1152]{2,1,0:T(8,128)(2,1)S(1)}, bf16[2,56,1152]{2,1,0:T(8,128)(2,1)S(1)}, u32[]{:S(2)}, u32[]{:S(2)}) collective-permute-start(bf16[2,56,1152]{2,1,0:T(8,128)(2,1)S(1)} %get-tuple-element.70), channel_id=1, source_target_pairs={{0,8},{4,12},{8,0},{12,4},{16,24},{20,28},{24,16},{28,20},{1,9},{5... | collective-permute-start | bytes 774152 | tf_op jit(solution)/shard_map/ppermute | solution.py:309
  10.7 1.1 %copy-start.6 = (bf16[224,1152]{1,0:T(8,128)(2,1)S(1)}, bf16[224,1152]{1,0:T(8,128)(2,1)}, u32[]{:S(2)}) copy-start(bf16[224,1152]{1,0:T(8,128)(2,1)} %get-tuple-element.53.merged) | copy-start | bytes 1548292
  13.7 12.9 %collective-permute-start.1 = (bf16[768,128]{1,0:T(8,128)(2,1)S(1)}, bf16[768,128]{1,0:T(8,128)(2,1)S(1)}, u32[]{:S(2)}, u32[]{:S(2)}) collective-permute-start(bf16[768,128]{1,0:T(8,128)(2,1)S(1)} %get-tuple-element.54), channel_id=1, source_target_pairs={{0,2},{1,3},{2,0},{3,1},{4,6},{5,7},{6,4},{7,5},{8,10},{9,11},{10,... | collective-permute-start | bytes 589832 | tf_op jit(solution)/shard_map/ppermute | solution.py:309
  14.5 12.1 %collective-permute-start.2 = (bf16[768,128]{1,0:T(8,128)(2,1)S(1)}, bf16[768,128]{1,0:T(8,128)(2,1)S(1)}, u32[]{:S(2)}, u32[]{:S(2)}) collective-permute-start(bf16[768,128]{1,0:T(8,128)(2,1)S(1)} %get-tuple-element.55), channel_id=1, source_target_pairs={{0,1},{1,0},{2,3},{3,2},{4,5},{5,4},{6,7},{7,6},{8,9},{9,8},{10,11... | collective-permute-start | bytes 589832 | tf_op jit(solution)/shard_map/ppermute | solution.py:309
  16.1 17.2 %collective-permute-start.8 = (bf16[2,56,1152]{2,1,0:T(8,128)(2,1)S(1)}, bf16[2,56,1152]{2,1,0:T(8,128)(2,1)S(1)}, u32[]{:S(2)}, u32[]{:S(2)}) collective-permute-start(bf16[2,56,1152]{2,1,0:T(8,128)(2,1)S(1)} %get-tuple-element.71), channel_id=1, source_target_pairs={{0,16},{4,20},{8,24},{12,28},{16,0},{20,4},{24,8},{28,12},{1,17},{... | collective-permute-start | bytes 774152 | tf_op jit(solution)/shard_map/ppermute | solution.py:309
  17.6 15.7 %collective-permute-start.9 = (bf16[2,56,1152]{2,1,0:T(8,128)(2,1)S(1)}, bf16[2,56,1152]{2,1,0:T(8,128)(2,1)S(1)}, u32[]{:S(2)}, u32[]{:S(2)}) collective-permute-start(bf16[2,56,1152]{2,1,0:T(8,128)(2,1)S(1)} %get-tuple-element.72), channel_id=1, source_target_pairs={{0,24},{4,28},{8,16},{12,20},{16,8},{20,12},{24,0},{28,4},{1,25},{... | collective-permute-start | bytes 774152 | tf_op jit(solution)/shard_map/ppermute | solution.py:309
  28.9 6.4 %collective-permute-start.3 = (bf16[264,128]{1,0:T(8,128)(2,1)S(1)}, bf16[264,128]{1,0:T(8,128)(2,1)S(1)}, u32[]{:S(2)}, u32[]{:S(2)}) collective-permute-start(bf16[264,128]{1,0:T(8,128)(2,1)S(1)} %get-tuple-element.62), channel_id=1, source_target_pairs={{0,3},{1,2},{2,1},{3,0},{4,7},{5,6},{6,5},{7,4},{8,11},{9,10},{10,... | collective-permute-start | bytes 202760 | tf_op jit(solution)/shard_map/ppermute | solution.py:309
  31.4 5.9 %collective-permute-start.4 = (bf16[264,128]{1,0:T(8,128)(2,1)S(1)}, bf16[264,128]{1,0:T(8,128)(2,1)S(1)}, u32[]{:S(2)}, u32[]{:S(2)}) collective-permute-start(bf16[264,128]{1,0:T(8,128)(2,1)S(1)} %get-tuple-element.63), channel_id=1, source_target_pairs={{0,2},{1,3},{2,0},{3,1},{4,6},{5,7},{6,4},{7,5},{8,10},{9,11},{10,... | collective-permute-start | bytes 202760 | tf_op jit(solution)/shard_map/ppermute | solution.py:309
  31.4 5.9 %collective-permute-start.5 = (bf16[264,128]{1,0:T(8,128)(2,1)S(1)}, bf16[264,128]{1,0:T(8,128)(2,1)S(1)}, u32[]{:S(2)}, u32[]{:S(2)}) collective-permute-start(bf16[264,128]{1,0:T(8,128)(2,1)S(1)} %get-tuple-element.64), channel_id=1, source_target_pairs={{0,1},{1,0},{2,3},{3,2},{4,5},{5,4},{6,7},{7,6},{8,9},{9,8},{10,11... | collective-permute-start | bytes 202760 | tf_op jit(solution)/shard_map/ppermute | solution.py:309
  38.0 1.6 %collective-permute-start.10 = (bf16[4,256,128]{2,1,0:T(8,128)(2,1)S(1)}, bf16[4,256,128]{2,1,0:T(8,128)(2,1)S(1)}, u32[]{:S(2)}, u32[]{:S(2)}) collective-permute-start(bf16[4,256,128]{2,1,0:T(8,128)(2,1)S(1)} %get-tuple-element.80), channel_id=1, source_target_pairs={{0,4},{4,0},{8,12},{12,8},{16,20},{20,16},{24,28},{28,24},{1,5},{5... | collective-permute-start | bytes 786440 | tf_op jit(solution)/shard_map/ppermute | solution.py:309
  39.6 6.8 %collective-permute-start.13 = (bf16[2,256,128]{2,1,0:T(8,128)(2,1)S(1)}, bf16[2,256,128]{2,1,0:T(8,128)(2,1)S(1)}, u32[]{:S(2)}, u32[]{:S(2)}) collective-permute-start(bf16[2,256,128]{2,1,0:T(8,128)(2,1)S(1)} %get-tuple-element.86), channel_id=1, source_target_pairs={{0,24},{4,28},{8,16},{12,20},{16,8},{20,12},{24,0},{28,4},{1,25},{... | collective-permute-start | bytes 393224 | tf_op jit(solution)/shard_map/ppermute | solution.py:309
  42.1 6.8 %collective-permute-start.11 = (bf16[2,256,128]{2,1,0:T(8,128)(2,1)S(1)}, bf16[2,256,128]{2,1,0:T(8,128)(2,1)S(1)}, u32[]{:S(2)}, u32[]{:S(2)}) collective-permute-start(bf16[2,256,128]{2,1,0:T(8,128)(2,1)S(1)} %get-tuple-element.81), channel_id=1, source_target_pairs={{0,16},{4,20},{8,24},{12,28},{16,0},{20,4},{24,8},{28,12},{1,17},{... | collective-permute-start | bytes 393224 | tf_op jit(solution)/shard_map/ppermute | solution.py:309
  42.6 6.4 %collective-permute-start.12 = (bf16[2,256,128]{2,1,0:T(8,128)(2,1)S(1)}, bf16[2,256,128]{2,1,0:T(8,128)(2,1)S(1)}, u32[]{:S(2)}, u32[]{:S(2)}) collective-permute-start(bf16[2,256,128]{2,1,0:T(8,128)(2,1)S(1)} %get-tuple-element.82), channel_id=1, source_target_pairs={{0,8},{4,12},{8,0},{12,4},{16,24},{20,28},{24,16},{28,20},{1,9},{5... | collective-permute-start | bytes 393224 | tf_op jit(solution)/shard_map/ppermute | solution.py:309
  52.8 8.6 %copy-start.4 = (bf16[576,1152]{1,0:T(8,128)(2,1)S(1)}, bf16[576,1152]{1,0:T(8,128)(2,1)}, u32[]{:S(2)}) copy-start(bf16[576,1152]{1,0:T(8,128)(2,1)} %proj.11) | copy-start | bytes 3981316
  52.8 1.6 %collective-permute-start.14 = (bf16[4,256,128]{2,1,0:T(8,128)(2,1)S(1)}, bf16[4,256,128]{2,1,0:T(8,128)(2,1)S(1)}, u32[]{:S(2)}, u32[]{:S(2)}) collective-permute-start(bf16[4,256,128]{2,1,0:T(8,128)(2,1)S(1)} %get-tuple-element.88), channel_id=1, source_target_pairs={{0,4},{4,0},{8,12},{12,8},{16,20},{20,16},{24,28},{28,24},{1,5},{5... | collective-permute-start | bytes 786440 | tf_op jit(solution)/shard_map/ppermute | solution.py:309
  54.4 6.9 %collective-permute-start.17 = (bf16[2,256,128]{2,1,0:T(8,128)(2,1)S(1)}, bf16[2,256,128]{2,1,0:T(8,128)(2,1)S(1)}, u32[]{:S(2)}, u32[]{:S(2)}) collective-permute-start(bf16[2,256,128]{2,1,0:T(8,128)(2,1)S(1)} %get-tuple-element.92), channel_id=1, source_target_pairs={{0,24},{4,28},{8,16},{12,20},{16,8},{20,12},{24,0},{28,4},{1,25},{... | collective-permute-start | bytes 393224 | tf_op jit(solution)/shard_map/ppermute | solution.py:309
  56.8 6.9 %collective-permute-start.15 = (bf16[2,256,128]{2,1,0:T(8,128)(2,1)S(1)}, bf16[2,256,128]{2,1,0:T(8,128)(2,1)S(1)}, u32[]{:S(2)}, u32[]{:S(2)}) collective-permute-start(bf16[2,256,128]{2,1,0:T(8,128)(2,1)S(1)} %get-tuple-element.89), channel_id=1, source_target_pairs={{0,16},{4,20},{8,24},{12,28},{16,0},{20,4},{24,8},{28,12},{1,17},{... | collective-permute-start | bytes 393224 | tf_op jit(solution)/shard_map/ppermute | solution.py:309
  57.5 6.3 %collective-permute-start.16 = (bf16[2,256,128]{2,1,0:T(8,128)(2,1)S(1)}, bf16[2,256,128]{2,1,0:T(8,128)(2,1)S(1)}, u32[]{:S(2)}, u32[]{:S(2)}) collective-permute-start(bf16[2,256,128]{2,1,0:T(8,128)(2,1)S(1)} %get-tuple-element.90), channel_id=1, source_target_pairs={{0,8},{4,12},{8,0},{12,4},{16,24},{20,28},{24,16},{28,20},{1,9},{5... | collective-permute-start | bytes 393224 | tf_op jit(solution)/shard_map/ppermute | solution.py:309

commit v6 on v5

--- a/solution.py
+++ b/solution.py
@@ -148,8 +148,10 @@
 def prepare_kernel(wide, packed, slot, keys, others, chosen):
     slots, rows = keys.shape[0], slot.shape[1]
     local = slot[...] - lax.axis_index("space") * slots
-    joined = (lax.broadcasted_iota(jnp.int32, (slots, rows), 0) == local).astype(F32)
-    chosen[...] = joined.T.astype(BF16)
+    joined = (lax.broadcasted_iota(jnp.int32, (slots, rows), 0) == local).astype(F32).T
+    n_frames, places = chosen.shape[:2]
+    for f in range(n_frames):
+        chosen[lax.axis_index("frames") ^ f] = joined[f * places : (f + 1) * places]
     block = unpack(packed[...].astype(F32), 3 * wide, slots)
     keys[...] = block[wide : 2 * wide].T.astype(BF16)
     others[...] = jnp.concatenate([block[:wide], block[2 * wide :]], 0).astype(BF16)
@@ -187,20 +189,19 @@
 
 
 def expand_kernel(n_space, n_pair, slots, wide, chosen, *refs):
-    ins, (keep, give, attended, held, spread) = refs[:n_space], refs[n_space:]
-    me, frame = lax.axis_index("space"), lax.axis_index("frames")
+    ins, (keep, give, attended, held) = refs[:n_space], refs[n_space:]
+    me = lax.axis_index("space")
     held[me] = ins[n_space - 1][...].astype(F32)
     for s in range(1, n_space):
         held[me ^ s] = unpack(ins[n_space - 1 - s][...].astype(F32), wide, slots)
     whole = jnp.concatenate([held[d] for d in range(n_space)], 0).astype(BF16)
     attended[...] = whole
-    wanted = dot_t(chosen[...], whole)
-    places = wanted.shape[0] // (2 * n_pair)
-    for f in range(2 * n_pair):
-        spread[f] = pack(wanted[f * places : (f + 1) * places]).astype(BF16)
+    places = chosen.shape[1]
+    wanted = dot_t(jnp.concatenate([chosen[r] for r in range(2 * n_pair)], 0).astype(BF16), whole)
     for s in range(n_pair):
-        keep[s] = spread[frame ^ (2 * s)]
-        give[s] = spread[frame ^ (2 * s + 1)]
+        for t, out in enumerate((keep, give)):
+            at = (2 * s + t) * places
+            out[s] = pack(wanted[at : at + places]).astype(BF16)
 
 
 def cost(flops):
@@ -210,9 +211,12 @@
 def residual_kernel(attended, chosen, latents, modulation, proj, after):
     places = latents.shape[1]
     out = dot(attended[...].astype(F32).T.astype(BF16), proj[...]).astype(BF16)
-    spread = modulation[2:3] * dot(chosen[...], out)
-    for f in range(latents.shape[0]):
-        after[f] = (latents[f].astype(F32) + spread[f * places : (f + 1) * places]).astype(BF16)
+    n_frames = latents.shape[0]
+    picked = jnp.concatenate([chosen[r] for r in range(n_frames)], 0).astype(BF16)
+    spread = modulation[2:3] * dot(picked, out)
+    for r in range(n_frames):
+        f = lax.axis_index("frames") ^ r
+        after[f] = (latents[f].astype(F32) + spread[r * places : (r + 1) * places]).astype(BF16)
 
 
 def pair_kernel(keep, got, *outs):
@@ -248,7 +252,7 @@
 
 def temporal_kernel(n_pair, places, n_parts, order, modulation, proj, weights, *refs):
     tokens, results, before = refs[:n_parts], refs[n_parts : 2 * n_parts], refs[2 * n_parts : n_pair + n_parts]
-    keep, give, normed, held = refs[n_pair + n_parts :]
+    keep, give, normed = refs[n_pair + n_parts :]
     n_frames = 2 * n_pair
     groups = -(-places // SUB)
     inner = proj.shape[0]
@@ -277,14 +281,11 @@
             at = slice((g * heads + h) * size, (g * heads + h + 1) * size)
             parts.append(dot(vals[h * HD : (h + 1) * HD].astype(BF16), mix[:, at]) / total[:, at])
         mixed.append(jnp.concatenate(parts, 0))
-    whole = jnp.concatenate(mixed, 1).T.astype(BF16)
-    for g in range(groups):
-        for f in range(n_frames):
-            at = g * size + f * SUB
-            held[f, g * SUB : (g + 1) * SUB] = whole[at : at + SUB]
+    whole = jnp.concatenate(mixed, 1).T
     for i, s in enumerate(order):
-        keep[s] = pack(held[2 * i].astype(F32)[:places]).astype(BF16)
-        give[s] = pack(held[2 * i + 1].astype(F32)[:places]).astype(BF16)
+        for out, f in ((keep, 2 * i), (give, 2 * i + 1)):
+            rows = [whole[g * size + f * SUB : g * size + (f + 1) * SUB] for g in range(groups)]
+            out[s] = pack(jnp.concatenate(rows, 0)[:places]).astype(BF16)
 
 
 def finish_kernel(taken, places, modulation, proj, after, *refs):
@@ -380,7 +381,7 @@
     tokens = exchange(token_keep, token_give, n_frames)
     far_keys, far_others, chosen = pl.pallas_call(
         functools.partial(prepare_kernel, wide),
-        out_shape=[struct(slots, wide), struct(2 * wide, slots), struct(rows, slots)],
+        out_shape=[struct(slots, wide), struct(2 * wide, slots), jax.ShapeDtypeStruct((n_frames, places, slots), F32)],
         in_specs=[VMEM] * 2,
         out_specs=[VMEM] * 3,
         compiler_params=params(4),
@@ -416,7 +417,7 @@
         out_shape=[struct(n_pair, moved, LANES), struct(n_pair, moved, LANES), struct(inner, slots)],
         in_specs=[VMEM] * (n_space + 1),
         out_specs=[VMEM] * 3,
-        scratch_shapes=[pltpu.VMEM((n_space, wide, slots), F32), pltpu.VMEM((n_frames, moved, LANES), BF16)],
+        scratch_shapes=[pltpu.VMEM((n_space, wide, slots), F32)],
         compiler_params=params(8),
         name="expand",
     )(chosen, *reversed(mine))
@@ -459,10 +460,7 @@
         out_shape=[struct(n_pair, moved, LANES)] * 2,
         in_specs=[VMEM] * (3 + len(last) + n_pair),
         out_specs=[VMEM] * 2,
-        scratch_shapes=[
-            pltpu.VMEM((2 * len(last) * places, width), F32),
-            pltpu.VMEM((n_frames, pad, inner), BF16),
-        ],
+        scratch_shapes=[pltpu.VMEM((2 * len(last) * places, width), F32)],
         compiler_params=params(16),
         name="temporal",
     )(

time: 65.3 us -> 65 us (level)
  transfers between devices with their start and end apart: 18 -> 18, of which waited for: 10 -> 10; matrix products, arithmetic and copies ran while one was open for 0% -> 0% of each run, Pallas kernels for 18% -> 19%
where the time goes in v6:
time: 65 us; the launch traced here: 64.9 us
  starting transfers between devices  23.2 us (36%)
  Pallas kernels  21.5 us (33%)
  waiting for transfers between devices  19 us (29%)
  local copies, waits for them, and re-layouts  1.09 us (2%)
    ppermute x18, starting transfers between devices, swap(): return lax.ppermute(block, axis, [(i, i ^ mask) for i in range(size)])  23.2 us
    ppermute x18, waiting for transfers between devices, swap(): return lax.ppermute(block, axis, [(i, i ^ mask) for i in range(size)])  19 us
    pallas_call x2, Pallas kernels, shards(): pl.pallas_call(functools.partial(project_kernel, places, len(step)), out_...  3.81 us
    pallas_call x1, Pallas kernels, shards(): pl.pallas_call(functools.partial(merge_kernel, n_space), out_shape=[struc...  3.74 us
    pallas_call x1, Pallas kernels, shards(): pl.pallas_call(functools.partial(temporal_kernel, n_pair, places, len(las...  3.55 us
    pallas_call x2, Pallas kernels, shards(): pl.pallas_call(functools.partial(finish_kernel, step, places), out_shape=...  2.84 us
    pallas_call x1, Pallas kernels, shards(): pl.pallas_call(functools.partial(others_kernel, n_space, slots, wide), ou...  2.32 us
    pallas_call x1, Pallas kernels, shards(): pl.pallas_call(functools.partial(spread_kernel, n_space), out_shape=[stru...  1.85 us
  transfers between devices with their start and end apart: 18, of which 10 were waited for; matrix products, arithmetic and copies ran while one was open for 0% of the time, Pallas kernels for 19%

profile of v6, /device:TPU:0, one launch (start us, length us, event | category | flops | bytes accessed | tf_op | source)
XLA Modules:
  0.0 64.9 jit_solution(7260952441543820319)
XLA Ops:
  0.0 0.0 copy-start.2
  0.0 3.7 %merge.1 = (bf16[768,128]{1,0:T(8,128)(2,1)}, bf16[224,1152]{1,0:T(8,128)(2,1)}) custom-call(bf16[8,56,1152]{2,1,0:T(8,128)(2,1)} %bitcast.9, s32[1,448]{1,0:T(1,128)} %slot.3, f32[6,1152]{1,0:T(8,128)} %modulation.13, bf16[1728,1152]{1,0:T(8,128)(2,1)} %bitcast.7), custom_call_target="tpu_custom_call" | custom-call | tf_op jit(solution)/shard_map/merge/pallas_call | solution.py:340
  3.8 0.0 copy-start.7
  3.8 0.0 copy-done.3
  3.8 0.1 share.1
  3.9 0.5 collective-permute-start.6
  4.4 4.7 %collective-permute-start = (bf16[768,128]{1,0:T(8,128)(2,1)}, bf16[768,128]{1,0:T(8,128)(2,1)S(1)}, u32[]{:S(2)}, u32[]{:S(2)}) collective-permute-start(bf16[768,128]{1,0:T(8,128)(2,1)} %get-tuple-element.49), channel_id=1, source_target_pairs={{0,3},{1,2},{2,1},{3,0},{4,7},{5,6},{6,5},{7,4},{8,11},{9,10},{10,... | collective-permute-start | bytes 589832 | tf_op jit(solution)/shard_map/ppermute | solution.py:310
  9.1 0.0 collective-permute-done.6.got
  9.1 0.1 pair.3
  9.1 0.0 copy-start
  9.2 0.0 copy-start.1
  9.2 0.0 copy-start.5
  9.2 1.6 %collective-permute-start.7 = (bf16[2,56,1152]{2,1,0:T(8,128)(2,1)S(1)}, bf16[2,56,1152]{2,1,0:T(8,128)(2,1)S(1)}, u32[]{:S(2)}, u32[]{:S(2)}) collective-permute-start(bf16[2,56,1152]{2,1,0:T(8,128)(2,1)S(1)} %get-tuple-element.70), channel_id=1, source_target_pairs={{0,8},{4,12},{8,0},{12,4},{16,24},{20,28},{24,16},{28,20},{1,9},{5... | collective-permute-start | bytes 774152 | tf_op jit(solution)/shard_map/ppermute | solution.py:310
  10.7 0.0 copy-done.2
  10.7 1.0 %copy-done.6 = bf16[224,1152]{1,0:T(8,128)(2,1)S(1)} copy-done((bf16[224,1152]{1,0:T(8,128)(2,1)S(1)}, bf16[224,1152]{1,0:T(8,128)(2,1)}, u32[]{:S(2)}) %copy-start.6) | copy-done | bytes 516120
  11.8 1.9 %spread.1 = (bf16[768,128]{1,0:T(8,128)(2,1)S(1)}, bf16[768,128]{1,0:T(8,128)(2,1)S(1)}, bf16[768,128]{1,0:T(8,128)(2,1)S(1)}) custom-call(bf16[224,1152]{1,0:T(8,128)(2,1)S(1)} %copy-done.6, bf16[1728,1152]{1,0:T(8,128)(2,1)S(1)} %bitcast.8), custom_call_target="tpu_custom_call" | custom-call | flops 891813888 | bytes 8918138 | tf_op jit(solution)/shard_map/spread/pallas_call | solution.py:355
  13.7 0.9 %collective-permute-start.1 = (bf16[768,128]{1,0:T(8,128)(2,1)S(1)}, bf16[768,128]{1,0:T(8,128)(2,1)S(1)}, u32[]{:S(2)}, u32[]{:S(2)}) collective-permute-start(bf16[768,128]{1,0:T(8,128)(2,1)S(1)} %get-tuple-element.54), channel_id=1, source_target_pairs={{0,2},{1,3},{2,0},{3,1},{4,6},{5,7},{6,4},{7,5},{8,10},{9,11},{10,... | collective-permute-start | bytes 589832 | tf_op jit(solution)/shard_map/ppermute | solution.py:310
  14.5 1.6 %collective-permute-start.2 = (bf16[768,128]{1,0:T(8,128)(2,1)S(1)}, bf16[768,128]{1,0:T(8,128)(2,1)S(1)}, u32[]{:S(2)}, u32[]{:S(2)}) collective-permute-start(bf16[768,128]{1,0:T(8,128)(2,1)S(1)} %get-tuple-element.55), channel_id=1, source_target_pairs={{0,1},{1,0},{2,3},{3,2},{4,5},{5,4},{6,7},{7,6},{8,9},{9,8},{10,11... | collective-permute-start | bytes 589832 | tf_op jit(solution)/shard_map/ppermute | solution.py:310
  16.1 1.5 %collective-permute-start.8 = (bf16[2,56,1152]{2,1,0:T(8,128)(2,1)S(1)}, bf16[2,56,1152]{2,1,0:T(8,128)(2,1)S(1)}, u32[]{:S(2)}, u32[]{:S(2)}) collective-permute-start(bf16[2,56,1152]{2,1,0:T(8,128)(2,1)S(1)} %get-tuple-element.71), channel_id=1, source_target_pairs={{0,16},{4,20},{8,24},{12,28},{16,0},{20,4},{24,8},{28,12},{1,17},{... | collective-permute-start | bytes 774152 | tf_op jit(solution)/shard_map/ppermute | solution.py:310
  17.6 0.0 collective-permute-done.packed
  17.6 0.8 %collective-permute-start.9 = (bf16[2,56,1152]{2,1,0:T(8,128)(2,1)S(1)}, bf16[2,56,1152]{2,1,0:T(8,128)(2,1)S(1)}, u32[]{:S(2)}, u32[]{:S(2)}) collective-permute-start(bf16[2,56,1152]{2,1,0:T(8,128)(2,1)S(1)} %get-tuple-element.72), channel_id=1, source_target_pairs={{0,24},{4,28},{8,16},{12,20},{16,8},{20,12},{24,0},{28,4},{1,25},{... | collective-permute-start | bytes 774152 | tf_op jit(solution)/shard_map/ppermute | solution.py:310
  18.4 0.0 copy-done.7
  18.4 0.3 prepare.1
  18.7 7.9 %collective-permute-done.1.refs_0_ = bf16[768,128]{1,0:T(8,128)(2,1)S(1)} collective-permute-done((bf16[768,128]{1,0:T(8,128)(2,1)S(1)}, bf16[768,128]{1,0:T(8,128)(2,1)S(1)}, u32[]{:S(2)}, u32[]{:S(2)}) %collective-permute-start.1) | collective-permute-done | bytes 196640 | tf_op jit(solution)/shard_map/ppermute | solution.py:310
  26.6 0.0 collective-permute-done.2.refs_1_
  26.6 2.3 %attend_others.1 = (bf16[264,128]{1,0:T(8,128)(2,1)S(1)}, bf16[264,128]{1,0:T(8,128)(2,1)S(1)}, bf16[264,128]{1,0:T(8,128)(2,1)S(1)}, bf16[144,224]{1,0:T(8,128)...) custom-call(bf16[224,144]{1,0:T(8,128)(2,1)S(1)} %get-tuple-element.57.far_keys, ...), custom_call_target="tpu_custom_call" | custom-call | flops 346816512 | bytes 3468165 | tf_op jit(solution)/shard_map/attend_others/pallas_call | solution.py:394
  28.9 2.5 %collective-permute-start.3 = (bf16[264,128]{1,0:T(8,128)(2,1)S(1)}, bf16[264,128]{1,0:T(8,128)(2,1)S(1)}, u32[]{:S(2)}, u32[]{:S(2)}) collective-permute-start(bf16[264,128]{1,0:T(8,128)(2,1)S(1)} %get-tuple-element.62), channel_id=1, source_target_pairs={{0,3},{1,2},{2,1},{3,0},{4,7},{5,6},{6,5},{7,4},{8,11},{9,10},{10,... | collective-permute-start | bytes 202760 | tf_op jit(solution)/shard_map/ppermute | solution.py:310
  31.4 0.0 collective-permute-start.4
  31.5 0.0 collective-permute-done.7.refs_1_
  31.5 1.9 %collective-permute-start.5 = (bf16[264,128]{1,0:T(8,128)(2,1)S(1)}, bf16[264,128]{1,0:T(8,128)(2,1)S(1)}, u32[]{:S(2)}, u32[]{:S(2)}) collective-permute-start(bf16[264,128]{1,0:T(8,128)(2,1)S(1)} %get-tuple-element.64), channel_id=1, source_target_pairs={{0,1},{1,0},{2,3},{3,2},{4,5},{5,4},{6,7},{7,6},{8,9},{9,8},{10,11... | collective-permute-start | bytes 202760 | tf_op jit(solution)/shard_map/ppermute | solution.py:310
  33.4 0.0 collective-permute-done.8.refs_0_
  33.4 0.0 collective-permute-done.9.refs_0_
  33.4 1.3 %attend_own.1.refs_3_ = bf16[144,224]{1,0:T(8,128)(2,1)S(1)} custom-call(bf16[144,224]{1,0:T(8,128)(2,1)S(1)} %get-tuple-element.73.queries, bf16[896,144]{1,0:T(8,128)(2,1)S(1)} %get-tuple-element.74.keys, bf16[144,896]{1,0:T(8,128)(2,1)S(1)} %get-tuple-element.75.vals), custom_call_target="tpu_custom_call" | custom-call | flops 115605504 | bytes 1156055 | tf_op jit(solution)/shard_map/attend_own/pallas_call | solution.py:405
  34.7 0.6 collective-permute-done.3.refs_0_
  35.3 2.1 %collective-permute-done.4.refs_1_ = bf16[264,128]{1,0:T(8,128)(2,1)S(1)} collective-permute-done((bf16[264,128]{1,0:T(8,128)(2,1)S(1)}, bf16[264,128]{1,0:T(8,128)(2,1)S(1)}, u32[]{:S(2)}, u32[]{:S(2)}) %collective-permute-start.4) | collective-permute-done | bytes 67616 | tf_op jit(solution)/shard_map/ppermute | solution.py:310
  37.4 0.0 collective-permute-done.5.refs_2_
  37.4 0.5 expand.1
  37.9 0.1 collective-permute-start.10
  38.0 1.5 %collective-permute-done.10.got = bf16[4,256,128]{2,1,0:T(8,128)(2,1)S(1)} collective-permute-done((bf16[4,256,128]{2,1,0:T(8,128)(2,1)S(1)}, bf16[4,256,128]{2,1,0:T(8,128)(2,1)S(1)}, u32[]{:S(2)}, u32[]{:S(2)}) %collective-permute-start.10) | collective-permute-done | bytes 262176 | tf_op jit(solution)/shard_map/ppermute | solution.py:310
  39.6 2.5 %collective-permute-start.13 = (bf16[2,256,128]{2,1,0:T(8,128)(2,1)S(1)}, bf16[2,256,128]{2,1,0:T(8,128)(2,1)S(1)}, u32[]{:S(2)}, u32[]{:S(2)}) collective-permute-start(bf16[2,256,128]{2,1,0:T(8,128)(2,1)S(1)} %get-tuple-element.86), channel_id=1, source_target_pairs={{0,24},{4,28},{8,16},{12,20},{16,8},{20,12},{24,0},{28,4},{1,25},{... | collective-permute-start | bytes 393224 | tf_op jit(solution)/shard_map/ppermute | solution.py:310
  42.1 0.5 collective-permute-start.11
  42.6 0.5 collective-permute-start.12
  43.1 0.0 copy-done
  43.1 0.0 copy-done.1
  43.1 0.0 copy-done.5
  43.1 1.9 %project_0.1.refs_4_ = bf16[2,64,1728]{2,1,0:T(8,128)(2,1)S(1)} custom-call(f32[6,1152]{1,0:T(8,128)S(1)} %copy-done.5, bf16[576,1152]{1,0:T(8,128)(2,1)S(1)} %copy-done.1, bf16[1728,1152]{1,0:T(8,128)(2,1)S(1)} %bitcast.4, bf16[2,56,1152]{2,1,0:T(8,128)(2,1)S(1)} %get-tuple-element.83.refs_0_, bf16[2,256,128]{2,1,0:T(8,128)(2,1)S(1)} %get-tuple-element.84.refs_1_), custom_call_target="tpu_custom_call" | custom-call | flops 445906944 | bytes 4459069 | tf_op jit(solution)/shard_map/project_0/pallas_call | solution.py:441
  45.0 1.3 %collective-permute-done.13.refs_1_ = bf16[2,256,128]{2,1,0:T(8,128)(2,1)S(1)} collective-permute-done((bf16[2,256,128]{2,1,0:T(8,128)(2,1)S(1)}, bf16[2,256,128]{2,1,0:T(8,128)(2,1)S(1)}, u32[]{:S(2)}, u32[]{:S(2)}) %collective-permute-start.13) | collective-permute-done | bytes 131104 | tf_op jit(solution)/shard_map/ppermute | solution.py:310
  46.4 1.9 %project_1.1.refs_5_ = bf16[2,64,1728]{2,1,0:T(8,128)(2,1)S(1)} custom-call(f32[6,1152]{1,0:T(8,128)S(1)} %copy-done.5, bf16[576,1152]{1,0:T(8,128)(2,1)S(1)} %copy-done.1, bf16[1728,1152]{1,0:T(8,128)(2,1)S(1)} %bitcast.5, bf16[2,56,1152]{2,1,0:T(8,128)(2,1)S(1)} %collective-permute-done.9.refs_0_, bf16[2,256,128]{2,1,0:T(8,128)(2,1)S(1)} %collective-permute-done.13.refs_1_), custom_call_target="tpu_custom_call" | custom-call | flops 445906944 | bytes 4459069 | tf_op jit(solution)/shard_map/project_1/pallas_call | solution.py:441
  48.3 0.6 collective-permute-done.11.refs_2_
  48.9 0.1 collective-permute-done.12.refs_3_
  49.0 3.5 %temporal.1 = (bf16[4,256,128]{2,1,0:T(8,128)(2,1)S(1)}, bf16[4,256,128]{2,1,0:T(8,128)(2,1)S(1)}) custom-call(f32[6,1152]{1,0:T(8,128)S(1)} %copy-done.5, bf16[576,1152]{1,0:T(8,128)(2,1)S(1)} %copy-done.1, bf16[1728,1152]{1,0:T(8,128)(2,1)S(1)} %bitcast.6, bf16[2,56,1152]{2,1,0:T(8,128)(2,1)S(1)} %collective-permute-done.8.refs_0_, ...), custom_call_target="tpu_custom_call" | custom-call | tf_op jit(solution)/shard_map/temporal/pallas_call | solution.py:458
  52.5 0.0 copy-start.4
  52.5 0.1 collective-permute-start.14
  52.6 1.5 %collective-permute-done.14.got = bf16[4,256,128]{2,1,0:T(8,128)(2,1)S(1)} collective-permute-done((bf16[4,256,128]{2,1,0:T(8,128)(2,1)S(1)}, bf16[4,256,128]{2,1,0:T(8,128)(2,1)S(1)}, u32[]{:S(2)}, u32[]{:S(2)}) %collective-permute-start.14) | collective-permute-done | bytes 262176 | tf_op jit(solution)/shard_map/ppermute | solution.py:310
  54.2 2.4 %collective-permute-start.17 = (bf16[2,256,128]{2,1,0:T(8,128)(2,1)S(1)}, bf16[2,256,128]{2,1,0:T(8,128)(2,1)S(1)}, u32[]{:S(2)}, u32[]{:S(2)}) collective-permute-start(bf16[2,256,128]{2,1,0:T(8,128)(2,1)S(1)} %get-tuple-element.92), channel_id=1, source_target_pairs={{0,24},{4,28},{8,16},{12,20},{16,8},{20,12},{24,0},{28,4},{1,25},{... | collective-permute-start | bytes 393224 | tf_op jit(solution)/shard_map/ppermute | solution.py:310
  56.6 0.6 collective-permute-start.15
  57.2 0.5 collective-permute-start.16
  57.7 1.0 %residual.1.after = bf16[8,56,1152]{2,1,0:T(8,128)(2,1)S(1)} custom-call(bf16[576,224]{1,0:T(8,128)(2,1)S(1)} %get-tuple-element.76.attended, f32[8,56,224]{2,1,0:T(8,128)S(1)} %get-tuple-element.50.chosen, bf16[8,56,1152]{2,1,0:T(8,128)(2,1)S(1)} %bitcast.11, f32[6,1152]{1,0:T(8,128)S(1)} %copy-done.5, bf16[576,1152]{1,0:T(8,128)(2,1)S(1)} %copy-done.1), custom_call_target="tpu_custom_call" | custom-call | flops 594542592 | bytes 5945425 | tf_op jit(solution)/shard_map/residual/pallas_call | solution.py:425
  58.7 2.3 %collective-permute-done.17.refs_1_ = bf16[2,256,128]{2,1,0:T(8,128)(2,1)S(1)} collective-permute-done((bf16[2,256,128]{2,1,0:T(8,128)(2,1)S(1)}, bf16[2,256,128]{2,1,0:T(8,128)(2,1)S(1)}, u32[]{:S(2)}, u32[]{:S(2)}) %collective-permute-start.17) | collective-permute-done | bytes 131104 | tf_op jit(solution)/shard_map/ppermute | solution.py:310
  61.1 0.0 copy-done.4
  61.1 1.4 %finish_0.1.refs_2_ = bf16[8,56,1152]{2,1,0:T(8,128)(2,1)} custom-call(f32[6,1152]{1,0:T(8,128)S(1)} %copy-done.5, bf16[576,1152]{1,0:T(8,128)(2,1)S(1)} %copy-done.4, bf16[8,56,1152]{2,1,0:T(8,128)(2,1)S(1)} %residual.1.after, bf16[2,256,128]{2,1,0:T(8,128)(2,1)S(1)} %get-tuple-element.91.refs_0_, bf16[2,256,128]{2,1,0:T(8,128)(2,1)S(1)} %collective-permute-done.17.refs_1_), custom_call_target="tpu_custom_call" | custom-call | flops 297271296 | bytes 2972712 | tf_op jit(solution)/shard_map/finish_0/pallas_call | solution.py:479
  62.5 1.0 %collective-permute-done.15.refs_0_ = bf16[2,256,128]{2,1,0:T(8,128)(2,1)S(1)} collective-permute-done((bf16[2,256,128]{2,1,0:T(8,128)(2,1)S(1)}, bf16[2,256,128]{2,1,0:T(8,128)(2,1)S(1)}, u32[]{:S(2)}, u32[]{:S(2)}) %collective-permute-start.15) | collective-permute-done | bytes 131104 | tf_op jit(solution)/shard_map/ppermute | solution.py:310
  63.5 0.0 collective-permute-done.16.refs_1_
  63.5 1.4 %finish_1.1 = bf16[8,56,1152]{2,1,0:T(8,128)(2,1)} custom-call(f32[6,1152]{1,0:T(8,128)S(1)} %copy-done.5, bf16[576,1152]{1,0:T(8,128)(2,1)S(1)} %copy-done.4, bf16[8,56,1152]{2,1,0:T(8,128)(2,1)S(1)} %residual.1.after, bf16[2,256,128]{2,1,0:T(8,128)(2,1)S(1)} %collective-permute-done.15.refs_0_, ...), custom_call_target="tpu_custom_call", output_to_operand_aliasing={{}: (5, {})} | custom-call | flops 297271296 | bytes 2972712 | tf_op jit(solution)/shard_map/finish_1/pallas_call | solution.py:479
  (4 shorter events, 0.1 us)
Async XLA Ops:
  0.0 10.7 %copy-start.2 = (bf16[1152,1728]{0,1:T(8,128)(2,1)S(1)}, bf16[1152,1728]{0,1:T(8,128)(2,1)}, u32[]{:S(2)}) copy-start(bf16[1152,1728]{0,1:T(8,128)(2,1)} %param.10) | copy-start | bytes 11943940
  0.0 3.8 %copy-start.3 = (bf16[1,448,1152]{2,1,0:T(8,128)(2,1)S(1)}, bf16[1,448,1152]{2,1,0:T(8,128)(2,1)}, u32[]{:S(2)}) copy-start(bf16[1,448,1152]{2,1,0:T(8,128)(2,1)} %param.7) | copy-start | bytes 3096580
  3.8 14.7 %copy-start.7 = (s32[1,448]{1,0:T(1,128)S(1)}, s32[1,448]{1,0:T(1,128)}, u32[]{:S(2)}) copy-start(s32[1,448]{1,0:T(1,128)} %slot.3) | copy-start | bytes 5380
  3.9 5.2 %collective-permute-start.6 = (bf16[4,56,1152]{2,1,0:T(8,128)(2,1)S(1)}, bf16[4,56,1152]{2,1,0:T(8,128)(2,1)S(1)}, u32[]{:S(2)}, u32[]{:S(2)}) collective-permute-start(bf16[4,56,1152]{2,1,0:T(8,128)(2,1)S(1)} %get-tuple-element.68), channel_id=1, source_target_pairs={{0,4},{4,0},{8,12},{12,8},{16,20},{20,16},{24,28},{28,24},{1,5},{5... | collective-permute-start | bytes 1548296 | tf_op jit(solution)/shard_map/ppermute | solution.py:310
  4.4 13.2 %collective-permute-start = (bf16[768,128]{1,0:T(8,128)(2,1)}, bf16[768,128]{1,0:T(8,128)(2,1)S(1)}, u32[]{:S(2)}, u32[]{:S(2)}) collective-permute-start(bf16[768,128]{1,0:T(8,128)(2,1)} %get-tuple-element.49), channel_id=1, source_target_pairs={{0,3},{1,2},{2,1},{3,0},{4,7},{5,6},{6,5},{7,4},{8,11},{9,10},{10,... | collective-permute-start | bytes 589832 | tf_op jit(solution)/shard_map/ppermute | solution.py:310
  9.1 34.0 %copy-start = (bf16[1152,1728]{0,1:T(8,128)(2,1)S(1)}, bf16[1152,1728]{0,1:T(8,128)(2,1)}, u32[]{:S(2)}) copy-start(bf16[1152,1728]{0,1:T(8,128)(2,1)} %param.12) | copy-start | bytes 11943940
  9.2 34.0 %copy-start.1 = (bf16[576,1152]{1,0:T(8,128)(2,1)S(1)}, bf16[576,1152]{1,0:T(8,128)(2,1)}, u32[]{:S(2)}) copy-start(bf16[576,1152]{1,0:T(8,128)(2,1)} %proj.9) | copy-start | bytes 3981316
  9.2 34.0 %copy-start.5 = (f32[6,1152]{1,0:T(8,128)S(1)}, f32[6,1152]{1,0:T(8,128)}, u32[]{:S(2)}) copy-start(f32[6,1152]{1,0:T(8,128)} %modulation.13) | copy-start | bytes 82948
  9.2 22.3 %collective-permute-start.7 = (bf16[2,56,1152]{2,1,0:T(8,128)(2,1)S(1)}, bf16[2,56,1152]{2,1,0:T(8,128)(2,1)S(1)}, u32[]{:S(2)}, u32[]{:S(2)}) collective-permute-start(bf16[2,56,1152]{2,1,0:T(8,128)(2,1)S(1)} %get-tuple-element.70), channel_id=1, source_target_pairs={{0,8},{4,12},{8,0},{12,4},{16,24},{20,28},{24,16},{28,20},{1,9},{5... | collective-permute-start | bytes 774152 | tf_op jit(solution)/shard_map/ppermute | solution.py:310
  10.7 1.1 %copy-start.6 = (bf16[224,1152]{1,0:T(8,128)(2,1)S(1)}, bf16[224,1152]{1,0:T(8,128)(2,1)}, u32[]{:S(2)}) copy-start(bf16[224,1152]{1,0:T(8,128)(2,1)} %get-tuple-element.53.merged) | copy-start | bytes 1548292
  13.7 12.9 %collective-permute-start.1 = (bf16[768,128]{1,0:T(8,128)(2,1)S(1)}, bf16[768,128]{1,0:T(8,128)(2,1)S(1)}, u32[]{:S(2)}, u32[]{:S(2)}) collective-permute-start(bf16[768,128]{1,0:T(8,128)(2,1)S(1)} %get-tuple-element.54), channel_id=1, source_target_pairs={{0,2},{1,3},{2,0},{3,1},{4,6},{5,7},{6,4},{7,5},{8,10},{9,11},{10,... | collective-permute-start | bytes 589832 | tf_op jit(solution)/shard_map/ppermute | solution.py:310
  14.5 12.1 %collective-permute-start.2 = (bf16[768,128]{1,0:T(8,128)(2,1)S(1)}, bf16[768,128]{1,0:T(8,128)(2,1)S(1)}, u32[]{:S(2)}, u32[]{:S(2)}) collective-permute-start(bf16[768,128]{1,0:T(8,128)(2,1)S(1)} %get-tuple-element.55), channel_id=1, source_target_pairs={{0,1},{1,0},{2,3},{3,2},{4,5},{5,4},{6,7},{7,6},{8,9},{9,8},{10,11... | collective-permute-start | bytes 589832 | tf_op jit(solution)/shard_map/ppermute | solution.py:310
  16.1 17.3 %collective-permute-start.8 = (bf16[2,56,1152]{2,1,0:T(8,128)(2,1)S(1)}, bf16[2,56,1152]{2,1,0:T(8,128)(2,1)S(1)}, u32[]{:S(2)}, u32[]{:S(2)}) collective-permute-start(bf16[2,56,1152]{2,1,0:T(8,128)(2,1)S(1)} %get-tuple-element.71), channel_id=1, source_target_pairs={{0,16},{4,20},{8,24},{12,28},{16,0},{20,4},{24,8},{28,12},{1,17},{... | collective-permute-start | bytes 774152 | tf_op jit(solution)/shard_map/ppermute | solution.py:310
  17.6 15.7 %collective-permute-start.9 = (bf16[2,56,1152]{2,1,0:T(8,128)(2,1)S(1)}, bf16[2,56,1152]{2,1,0:T(8,128)(2,1)S(1)}, u32[]{:S(2)}, u32[]{:S(2)}) collective-permute-start(bf16[2,56,1152]{2,1,0:T(8,128)(2,1)S(1)} %get-tuple-element.72), channel_id=1, source_target_pairs={{0,24},{4,28},{8,16},{12,20},{16,8},{20,12},{24,0},{28,4},{1,25},{... | collective-permute-start | bytes 774152 | tf_op jit(solution)/shard_map/ppermute | solution.py:310
  28.9 6.4 %collective-permute-start.3 = (bf16[264,128]{1,0:T(8,128)(2,1)S(1)}, bf16[264,128]{1,0:T(8,128)(2,1)S(1)}, u32[]{:S(2)}, u32[]{:S(2)}) collective-permute-start(bf16[264,128]{1,0:T(8,128)(2,1)S(1)} %get-tuple-element.62), channel_id=1, source_target_pairs={{0,3},{1,2},{2,1},{3,0},{4,7},{5,6},{6,5},{7,4},{8,11},{9,10},{10,... | collective-permute-start | bytes 202760 | tf_op jit(solution)/shard_map/ppermute | solution.py:310
  31.4 5.9 %collective-permute-start.4 = (bf16[264,128]{1,0:T(8,128)(2,1)S(1)}, bf16[264,128]{1,0:T(8,128)(2,1)S(1)}, u32[]{:S(2)}, u32[]{:S(2)}) collective-permute-start(bf16[264,128]{1,0:T(8,128)(2,1)S(1)} %get-tuple-element.63), channel_id=1, source_target_pairs={{0,2},{1,3},{2,0},{3,1},{4,6},{5,7},{6,4},{7,5},{8,10},{9,11},{10,... | collective-permute-start | bytes 202760 | tf_op jit(solution)/shard_map/ppermute | solution.py:310
  31.5 5.9 %collective-permute-start.5 = (bf16[264,128]{1,0:T(8,128)(2,1)S(1)}, bf16[264,128]{1,0:T(8,128)(2,1)S(1)}, u32[]{:S(2)}, u32[]{:S(2)}) collective-permute-start(bf16[264,128]{1,0:T(8,128)(2,1)S(1)} %get-tuple-element.64), channel_id=1, source_target_pairs={{0,1},{1,0},{2,3},{3,2},{4,5},{5,4},{6,7},{7,6},{8,9},{9,8},{10,11... | collective-permute-start | bytes 202760 | tf_op jit(solution)/shard_map/ppermute | solution.py:310
  37.9 1.6 %collective-permute-start.10 = (bf16[4,256,128]{2,1,0:T(8,128)(2,1)S(1)}, bf16[4,256,128]{2,1,0:T(8,128)(2,1)S(1)}, u32[]{:S(2)}, u32[]{:S(2)}) collective-permute-start(bf16[4,256,128]{2,1,0:T(8,128)(2,1)S(1)} %get-tuple-element.80), channel_id=1, source_target_pairs={{0,4},{4,0},{8,12},{12,8},{16,20},{20,16},{24,28},{28,24},{1,5},{5... | collective-permute-start | bytes 786440 | tf_op jit(solution)/shard_map/ppermute | solution.py:310
  39.6 6.8 %collective-permute-start.13 = (bf16[2,256,128]{2,1,0:T(8,128)(2,1)S(1)}, bf16[2,256,128]{2,1,0:T(8,128)(2,1)S(1)}, u32[]{:S(2)}, u32[]{:S(2)}) collective-permute-start(bf16[2,256,128]{2,1,0:T(8,128)(2,1)S(1)} %get-tuple-element.86), channel_id=1, source_target_pairs={{0,24},{4,28},{8,16},{12,20},{16,8},{20,12},{24,0},{28,4},{1,25},{... | collective-permute-start | bytes 393224 | tf_op jit(solution)/shard_map/ppermute | solution.py:310
  42.1 6.8 %collective-permute-start.11 = (bf16[2,256,128]{2,1,0:T(8,128)(2,1)S(1)}, bf16[2,256,128]{2,1,0:T(8,128)(2,1)S(1)}, u32[]{:S(2)}, u32[]{:S(2)}) collective-permute-start(bf16[2,256,128]{2,1,0:T(8,128)(2,1)S(1)} %get-tuple-element.81), channel_id=1, source_target_pairs={{0,16},{4,20},{8,24},{12,28},{16,0},{20,4},{24,8},{28,12},{1,17},{... | collective-permute-start | bytes 393224 | tf_op jit(solution)/shard_map/ppermute | solution.py:310
  42.6 6.4 %collective-permute-start.12 = (bf16[2,256,128]{2,1,0:T(8,128)(2,1)S(1)}, bf16[2,256,128]{2,1,0:T(8,128)(2,1)S(1)}, u32[]{:S(2)}, u32[]{:S(2)}) collective-permute-start(bf16[2,256,128]{2,1,0:T(8,128)(2,1)S(1)} %get-tuple-element.82), channel_id=1, source_target_pairs={{0,8},{4,12},{8,0},{12,4},{16,24},{20,28},{24,16},{28,20},{1,9},{5... | collective-permute-start | bytes 393224 | tf_op jit(solution)/shard_map/ppermute | solution.py:310
  52.5 8.5 %copy-start.4 = (bf16[576,1152]{1,0:T(8,128)(2,1)S(1)}, bf16[576,1152]{1,0:T(8,128)(2,1)}, u32[]{:S(2)}) copy-start(bf16[576,1152]{1,0:T(8,128)(2,1)} %proj.11) | copy-start | bytes 3981316
  52.5 1.6 %collective-permute-start.14 = (bf16[4,256,128]{2,1,0:T(8,128)(2,1)S(1)}, bf16[4,256,128]{2,1,0:T(8,128)(2,1)S(1)}, u32[]{:S(2)}, u32[]{:S(2)}) collective-permute-start(bf16[4,256,128]{2,1,0:T(8,128)(2,1)S(1)} %get-tuple-element.88), channel_id=1, source_target_pairs={{0,4},{4,0},{8,12},{12,8},{16,20},{20,16},{24,28},{28,24},{1,5},{5... | collective-permute-start | bytes 786440 | tf_op jit(solution)/shard_map/ppermute | solution.py:310
  54.2 6.9 %collective-permute-start.17 = (bf16[2,256,128]{2,1,0:T(8,128)(2,1)S(1)}, bf16[2,256,128]{2,1,0:T(8,128)(2,1)S(1)}, u32[]{:S(2)}, u32[]{:S(2)}) collective-permute-start(bf16[2,256,128]{2,1,0:T(8,128)(2,1)S(1)} %get-tuple-element.92), channel_id=1, source_target_pairs={{0,24},{4,28},{8,16},{12,20},{16,8},{20,12},{24,0},{28,4},{1,25},{... | collective-permute-start | bytes 393224 | tf_op jit(solution)/shard_map/ppermute | solution.py:310
  56.6 6.9 %collective-permute-start.15 = (bf16[2,256,128]{2,1,0:T(8,128)(2,1)S(1)}, bf16[2,256,128]{2,1,0:T(8,128)(2,1)S(1)}, u32[]{:S(2)}, u32[]{:S(2)}) collective-permute-start(bf16[2,256,128]{2,1,0:T(8,128)(2,1)S(1)} %get-tuple-element.89), channel_id=1, source_target_pairs={{0,16},{4,20},{8,24},{12,28},{16,0},{20,4},{24,8},{28,12},{1,17},{... | collective-permute-start | bytes 393224 | tf_op jit(solution)/shard_map/ppermute | solution.py:310
  57.2 6.3 %collective-permute-start.16 = (bf16[2,256,128]{2,1,0:T(8,128)(2,1)S(1)}, bf16[2,256,128]{2,1,0:T(8,128)(2,1)S(1)}, u32[]{:S(2)}, u32[]{:S(2)}) collective-permute-start(bf16[2,256,128]{2,1,0:T(8,128)(2,1)S(1)} %get-tuple-element.90), channel_id=1, source_target_pairs={{0,8},{4,12},{8,0},{12,4},{16,24},{20,28},{24,16},{28,20},{1,9},{5... | collective-permute-start | bytes 393224 | tf_op jit(solution)/shard_map/ppermute | solution.py:310

commit v7 on v6

--- a/solution.py
+++ b/solution.py
@@ -44,33 +44,36 @@
 def packing(rows, width):
     full, rest = divmod(width, LANES)
     free = LANES - rest
-    parts = rest // free + 1 if rest and rest % free == 0 else 1
-    high = -(-rows // (8 * parts)) * 8
-    if rows - high * (parts - 1) <= 0 or parts == 1:
-        parts, high = 1, rows
-    return full, rest, parts, high
+    if not rest:
+        return full, rest, []
+    count = rest // free if rest % free == 0 else 0
+    if count:
+        units = -(-rows * count // ((count + 1) * 8))
+        heights = [8 * (units // count + (i < units % count)) for i in range(count)]
+        if 0 < rows - sum(heights) <= min(heights):
+            return full, rest, heights
+    return full, rest, [rows]
 
 
 def packed_rows(rows, width):
-    full, rest, parts, high = packing(rows, width)
-    return -(-(full * rows + (max(parts - 1, 1) * high if rest else 0)) // 8) * 8
+    full, _, heights = packing(rows, width)
+    return -(-(full * rows + sum(heights)) // 8) * 8
 
 
 def pack(block):
     rows, width = block.shape
-    full, rest, parts, high = packing(rows, width)
+    full, rest, heights = packing(rows, width)
     pieces = [block[:, j * LANES : (j + 1) * LANES] for j in range(full)]
     if rest:
-        tail, free = block[:, full * LANES :], LANES - rest
-        if parts == 1:
-            pieces.append(jnp.concatenate([tail, jnp.zeros((rows, free), block.dtype)], 1))
-        else:
-            last = tail[(parts - 1) * high :]
-            if last.shape[0] < high:
-                last = jnp.concatenate([last, jnp.zeros((high - last.shape[0], rest), block.dtype)], 0)
-            for i in range(parts - 1):
-                side = last[:, i * free : (i + 1) * free]
-                pieces.append(jnp.concatenate([tail[i * high : (i + 1) * high], side], 1))
+        tail, free, top = block[:, full * LANES :], LANES - rest, 0
+        last = tail[sum(heights) :]
+        for i, high in enumerate(heights):
+            side = [last[:, i * free : (i + 1) * free]] if last.shape[0] else []
+            if high > last.shape[0]:
+                side.append(jnp.zeros((high - last.shape[0], free), block.dtype))
+            side = jnp.concatenate(side, 0) if len(side) > 1 else side[0]
+            pieces.append(jnp.concatenate([tail[top : top + high], side], 1))
+            top += high
     here = sum(p.shape[0] for p in pieces)
     if here % 8:
         pieces.append(jnp.zeros((-here % 8, LANES), block.dtype))
@@ -78,17 +81,19 @@
 
 
 def unpack(packed, rows, width):
-    full, rest, parts, high = packing(rows, width)
+    full, rest, heights = packing(rows, width)
     pieces = [packed[j * rows : (j + 1) * rows] for j in range(full)]
     if rest:
-        tail = packed[full * rows :]
-        if parts == 1:
-            pieces.append(tail[:rows, :rest])
-        else:
-            tiles = [tail[i * high : (i + 1) * high] for i in range(parts - 1)]
-            last = jnp.concatenate([t[:, rest:] for t in tiles], 1)[: rows - (parts - 1) * high]
-            pieces.append(jnp.concatenate([t[:, :rest] for t in tiles] + [last], 0))
-    return jnp.concatenate(pieces, 1)
+        tiles, top = [], full * rows
+        for high in heights:
+            tiles.append(packed[top : top + high])
+            top += high
+        over = rows - sum(heights)
+        parts = [t[:, :rest] for t in tiles]
+        if over:
+            parts.append(jnp.concatenate([t[:over, rest:] for t in tiles], 1))
+        pieces.append(jnp.concatenate(parts, 0) if len(parts) > 1 else parts[0])
+    return jnp.concatenate(pieces, 1) if len(pieces) > 1 else pieces[0]
 
 
 def merge_kernel(n_space, latents, slot, modulation, weights, out, merged, tokens, slots_in, mods, arrived, sems):

time: 65 us -> 64.8 us (level)
  no operation moved by 1% of the time
where the time goes in v7:
time: 64.8 us; the launch traced here: 64.7 us
  starting transfers between devices  23.2 us (36%)
  Pallas kernels  21.5 us (33%)
  waiting for transfers between devices  18.7 us (29%)
  local copies, waits for them, and re-layouts  1.09 us (2%)
    ppermute x18, starting transfers between devices, swap(): return lax.ppermute(block, axis, [(i, i ^ mask) for i in range(size)])  23.2 us
    ppermute x18, waiting for transfers between devices, swap(): return lax.ppermute(block, axis, [(i, i ^ mask) for i in range(size)])  18.7 us
    pallas_call x2, Pallas kernels, shards(): pl.pallas_call(functools.partial(project_kernel, places, len(step)), out_...  3.81 us
    pallas_call x1, Pallas kernels, shards(): pl.pallas_call(functools.partial(merge_kernel, n_space), out_shape=[struc...  3.75 us
    pallas_call x1, Pallas kernels, shards(): pl.pallas_call(functools.partial(temporal_kernel, n_pair, places, len(las...  3.55 us
    pallas_call x2, Pallas kernels, shards(): pl.pallas_call(functools.partial(finish_kernel, step, places), out_shape=...  2.84 us
    pallas_call x1, Pallas kernels, shards(): pl.pallas_call(functools.partial(others_kernel, n_space, slots, wide), ou...  2.39 us
    pallas_call x1, Pallas kernels, shards(): pl.pallas_call(functools.partial(spread_kernel, n_space), out_shape=[stru...  1.83 us
  transfers between devices with their start and end apart: 18, of which 10 were waited for; matrix products, arithmetic and copies ran while one was open for 0% of the time, Pallas kernels for 19%

profile of v7, /device:TPU:0, one launch (start us, length us, event | category | flops | bytes accessed | tf_op | source)
XLA Modules:
  0.0 64.7 jit_solution(16158421539856623111)
XLA Ops:
  0.0 0.0 copy-start.2
  0.0 3.7 %merge.1 = (bf16[760,128]{1,0:T(8,128)(2,1)}, bf16[224,1152]{1,0:T(8,128)(2,1)}) custom-call(bf16[8,56,1152]{2,1,0:T(8,128)(2,1)} %bitcast.9, s32[1,448]{1,0:T(1,128)} %slot.3, f32[6,1152]{1,0:T(8,128)} %modulation.13, bf16[1728,1152]{1,0:T(8,128)(2,1)} %bitcast.7), custom_call_target="tpu_custom_call" | custom-call | tf_op jit(solution)/shard_map/merge/pallas_call | solution.py:345
  3.8 0.0 copy-start.7
  3.8 0.0 copy-done.3
  3.8 0.1 share.1
  3.9 0.5 collective-permute-start.6
  4.4 4.7 %collective-permute-start = (bf16[760,128]{1,0:T(8,128)(2,1)}, bf16[760,128]{1,0:T(8,128)(2,1)S(1)}, u32[]{:S(2)}, u32[]{:S(2)}) collective-permute-start(bf16[760,128]{1,0:T(8,128)(2,1)} %get-tuple-element.49), channel_id=1, source_target_pairs={{0,3},{1,2},{2,1},{3,0},{4,7},{5,6},{6,5},{7,4},{8,11},{9,10},{10,... | collective-permute-start | bytes 583688 | tf_op jit(solution)/shard_map/ppermute | solution.py:315
  9.1 0.0 collective-permute-done.6.got
  9.1 0.1 pair.3
  9.1 0.0 copy-start
  9.2 0.0 copy-start.1
  9.2 0.0 copy-start.5
  9.2 1.6 %collective-permute-start.7 = (bf16[2,56,1152]{2,1,0:T(8,128)(2,1)S(1)}, bf16[2,56,1152]{2,1,0:T(8,128)(2,1)S(1)}, u32[]{:S(2)}, u32[]{:S(2)}) collective-permute-start(bf16[2,56,1152]{2,1,0:T(8,128)(2,1)S(1)} %get-tuple-element.70), channel_id=1, source_target_pairs={{0,8},{4,12},{8,0},{12,4},{16,24},{20,28},{24,16},{28,20},{1,9},{5... | collective-permute-start | bytes 774152 | tf_op jit(solution)/shard_map/ppermute | solution.py:315
  10.7 0.0 copy-done.2
  10.7 1.0 %copy-done.6 = bf16[224,1152]{1,0:T(8,128)(2,1)S(1)} copy-done((bf16[224,1152]{1,0:T(8,128)(2,1)S(1)}, bf16[224,1152]{1,0:T(8,128)(2,1)}, u32[]{:S(2)}) %copy-start.6) | copy-done | bytes 516120
  11.8 1.8 %spread.1 = (bf16[760,128]{1,0:T(8,128)(2,1)S(1)}, bf16[760,128]{1,0:T(8,128)(2,1)S(1)}, bf16[760,128]{1,0:T(8,128)(2,1)S(1)}) custom-call(bf16[224,1152]{1,0:T(8,128)(2,1)S(1)} %copy-done.6, bf16[1728,1152]{1,0:T(8,128)(2,1)S(1)} %bitcast.8), custom_call_target="tpu_custom_call" | custom-call | flops 891813888 | bytes 8918138 | tf_op jit(solution)/shard_map/spread/pallas_call | solution.py:360
  13.6 0.9 %collective-permute-start.1 = (bf16[760,128]{1,0:T(8,128)(2,1)S(1)}, bf16[760,128]{1,0:T(8,128)(2,1)S(1)}, u32[]{:S(2)}, u32[]{:S(2)}) collective-permute-start(bf16[760,128]{1,0:T(8,128)(2,1)S(1)} %get-tuple-element.54), channel_id=1, source_target_pairs={{0,2},{1,3},{2,0},{3,1},{4,6},{5,7},{6,4},{7,5},{8,10},{9,11},{10,... | collective-permute-start | bytes 583688 | tf_op jit(solution)/shard_map/ppermute | solution.py:315
  14.5 1.6 %collective-permute-start.2 = (bf16[760,128]{1,0:T(8,128)(2,1)S(1)}, bf16[760,128]{1,0:T(8,128)(2,1)S(1)}, u32[]{:S(2)}, u32[]{:S(2)}) collective-permute-start(bf16[760,128]{1,0:T(8,128)(2,1)S(1)} %get-tuple-element.55), channel_id=1, source_target_pairs={{0,1},{1,0},{2,3},{3,2},{4,5},{5,4},{6,7},{7,6},{8,9},{9,8},{10,11... | collective-permute-start | bytes 583688 | tf_op jit(solution)/shard_map/ppermute | solution.py:315
  16.1 1.5 %collective-permute-start.8 = (bf16[2,56,1152]{2,1,0:T(8,128)(2,1)S(1)}, bf16[2,56,1152]{2,1,0:T(8,128)(2,1)S(1)}, u32[]{:S(2)}, u32[]{:S(2)}) collective-permute-start(bf16[2,56,1152]{2,1,0:T(8,128)(2,1)S(1)} %get-tuple-element.71), channel_id=1, source_target_pairs={{0,16},{4,20},{8,24},{12,28},{16,0},{20,4},{24,8},{28,12},{1,17},{... | collective-permute-start | bytes 774152 | tf_op jit(solution)/shard_map/ppermute | solution.py:315
  17.6 0.0 collective-permute-done.packed
  17.6 0.8 %collective-permute-start.9 = (bf16[2,56,1152]{2,1,0:T(8,128)(2,1)S(1)}, bf16[2,56,1152]{2,1,0:T(8,128)(2,1)S(1)}, u32[]{:S(2)}, u32[]{:S(2)}) collective-permute-start(bf16[2,56,1152]{2,1,0:T(8,128)(2,1)S(1)} %get-tuple-element.72), channel_id=1, source_target_pairs={{0,24},{4,28},{8,16},{12,20},{16,8},{20,12},{24,0},{28,4},{1,25},{... | collective-permute-start | bytes 774152 | tf_op jit(solution)/shard_map/ppermute | solution.py:315
  18.4 0.0 copy-done.7
  18.4 0.3 prepare.1
  18.7 7.7 %collective-permute-done.1.refs_0_ = bf16[760,128]{1,0:T(8,128)(2,1)S(1)} collective-permute-done((bf16[760,128]{1,0:T(8,128)(2,1)S(1)}, bf16[760,128]{1,0:T(8,128)(2,1)S(1)}, u32[]{:S(2)}, u32[]{:S(2)}) %collective-permute-start.1) | collective-permute-done | bytes 194592 | tf_op jit(solution)/shard_map/ppermute | solution.py:315
  26.4 0.0 collective-permute-done.2.refs_1_
  26.4 2.4 %attend_others.1 = (bf16[256,128]{1,0:T(8,128)(2,1)S(1)}, bf16[256,128]{1,0:T(8,128)(2,1)S(1)}, bf16[256,128]{1,0:T(8,128)(2,1)S(1)}, bf16[144,224]{1,0:T(8,128)...) custom-call(bf16[224,144]{1,0:T(8,128)(2,1)S(1)} %get-tuple-element.57.far_keys, ...), custom_call_target="tpu_custom_call" | custom-call | flops 346816512 | bytes 3468165 | tf_op jit(solution)/shard_map/attend_others/pallas_call | solution.py:399
  28.8 2.5 %collective-permute-start.3 = (bf16[256,128]{1,0:T(8,128)(2,1)S(1)}, bf16[256,128]{1,0:T(8,128)(2,1)S(1)}, u32[]{:S(2)}, u32[]{:S(2)}) collective-permute-start(bf16[256,128]{1,0:T(8,128)(2,1)S(1)} %get-tuple-element.62), channel_id=1, source_target_pairs={{0,3},{1,2},{2,1},{3,0},{4,7},{5,6},{6,5},{7,4},{8,11},{9,10},{10,... | collective-permute-start | bytes 196616 | tf_op jit(solution)/shard_map/ppermute | solution.py:315
  31.3 0.0 collective-permute-start.4
  31.4 0.0 collective-permute-done.7.refs_1_
  31.4 1.9 %collective-permute-start.5 = (bf16[256,128]{1,0:T(8,128)(2,1)S(1)}, bf16[256,128]{1,0:T(8,128)(2,1)S(1)}, u32[]{:S(2)}, u32[]{:S(2)}) collective-permute-start(bf16[256,128]{1,0:T(8,128)(2,1)S(1)} %get-tuple-element.64), channel_id=1, source_target_pairs={{0,1},{1,0},{2,3},{3,2},{4,5},{5,4},{6,7},{7,6},{8,9},{9,8},{10,11... | collective-permute-start | bytes 196616 | tf_op jit(solution)/shard_map/ppermute | solution.py:315
  33.3 0.0 collective-permute-done.8.refs_0_
  33.3 0.0 collective-permute-done.9.refs_0_
  33.3 1.3 %attend_own.1.refs_3_ = bf16[144,224]{1,0:T(8,128)(2,1)S(1)} custom-call(bf16[144,224]{1,0:T(8,128)(2,1)S(1)} %get-tuple-element.73.queries, bf16[896,144]{1,0:T(8,128)(2,1)S(1)} %get-tuple-element.74.keys, bf16[144,896]{1,0:T(8,128)(2,1)S(1)} %get-tuple-element.75.vals), custom_call_target="tpu_custom_call" | custom-call | flops 115605504 | bytes 1156055 | tf_op jit(solution)/shard_map/attend_own/pallas_call | solution.py:410
  34.6 0.5 collective-permute-done.3.refs_0_
  35.1 2.0 %collective-permute-done.4.refs_1_ = bf16[256,128]{1,0:T(8,128)(2,1)S(1)} collective-permute-done((bf16[256,128]{1,0:T(8,128)(2,1)S(1)}, bf16[256,128]{1,0:T(8,128)(2,1)S(1)}, u32[]{:S(2)}, u32[]{:S(2)}) %collective-permute-start.4) | collective-permute-done | bytes 65568 | tf_op jit(solution)/shard_map/ppermute | solution.py:315
  37.1 0.0 collective-permute-done.5.refs_2_
  37.1 0.5 expand.1
  37.7 0.1 collective-permute-start.10
  37.8 1.5 %collective-permute-done.10.got = bf16[4,256,128]{2,1,0:T(8,128)(2,1)S(1)} collective-permute-done((bf16[4,256,128]{2,1,0:T(8,128)(2,1)S(1)}, bf16[4,256,128]{2,1,0:T(8,128)(2,1)S(1)}, u32[]{:S(2)}, u32[]{:S(2)}) %collective-permute-start.10) | collective-permute-done | bytes 262176 | tf_op jit(solution)/shard_map/ppermute | solution.py:315
  39.3 2.5 %collective-permute-start.13 = (bf16[2,256,128]{2,1,0:T(8,128)(2,1)S(1)}, bf16[2,256,128]{2,1,0:T(8,128)(2,1)S(1)}, u32[]{:S(2)}, u32[]{:S(2)}) collective-permute-start(bf16[2,256,128]{2,1,0:T(8,128)(2,1)S(1)} %get-tuple-element.86), channel_id=1, source_target_pairs={{0,24},{4,28},{8,16},{12,20},{16,8},{20,12},{24,0},{28,4},{1,25},{... | collective-permute-start | bytes 393224 | tf_op jit(solution)/shard_map/ppermute | solution.py:315
  41.8 0.5 collective-permute-start.11
  42.4 0.5 collective-permute-start.12
  42.9 0.0 copy-done
  42.9 0.0 copy-done.1
  42.9 0.0 copy-done.5
  42.9 1.9 %project_0.1.refs_4_ = bf16[2,64,1728]{2,1,0:T(8,128)(2,1)S(1)} custom-call(f32[6,1152]{1,0:T(8,128)S(1)} %copy-done.5, bf16[576,1152]{1,0:T(8,128)(2,1)S(1)} %copy-done.1, bf16[1728,1152]{1,0:T(8,128)(2,1)S(1)} %bitcast.4, bf16[2,56,1152]{2,1,0:T(8,128)(2,1)S(1)} %get-tuple-element.83.refs_0_, bf16[2,256,128]{2,1,0:T(8,128)(2,1)S(1)} %get-tuple-element.84.refs_1_), custom_call_target="tpu_custom_call" | custom-call | flops 445906944 | bytes 4459069 | tf_op jit(solution)/shard_map/project_0/pallas_call | solution.py:446
  44.8 1.3 %collective-permute-done.13.refs_1_ = bf16[2,256,128]{2,1,0:T(8,128)(2,1)S(1)} collective-permute-done((bf16[2,256,128]{2,1,0:T(8,128)(2,1)S(1)}, bf16[2,256,128]{2,1,0:T(8,128)(2,1)S(1)}, u32[]{:S(2)}, u32[]{:S(2)}) %collective-permute-start.13) | collective-permute-done | bytes 131104 | tf_op jit(solution)/shard_map/ppermute | solution.py:315
  46.1 1.9 %project_1.1.refs_5_ = bf16[2,64,1728]{2,1,0:T(8,128)(2,1)S(1)} custom-call(f32[6,1152]{1,0:T(8,128)S(1)} %copy-done.5, bf16[576,1152]{1,0:T(8,128)(2,1)S(1)} %copy-done.1, bf16[1728,1152]{1,0:T(8,128)(2,1)S(1)} %bitcast.5, bf16[2,56,1152]{2,1,0:T(8,128)(2,1)S(1)} %collective-permute-done.9.refs_0_, bf16[2,256,128]{2,1,0:T(8,128)(2,1)S(1)} %collective-permute-done.13.refs_1_), custom_call_target="tpu_custom_call" | custom-call | flops 445906944 | bytes 4459069 | tf_op jit(solution)/shard_map/project_1/pallas_call | solution.py:446
  48.0 0.6 collective-permute-done.11.refs_2_
  48.6 0.1 collective-permute-done.12.refs_3_
  48.7 3.5 %temporal.1 = (bf16[4,256,128]{2,1,0:T(8,128)(2,1)S(1)}, bf16[4,256,128]{2,1,0:T(8,128)(2,1)S(1)}) custom-call(f32[6,1152]{1,0:T(8,128)S(1)} %copy-done.5, bf16[576,1152]{1,0:T(8,128)(2,1)S(1)} %copy-done.1, bf16[1728,1152]{1,0:T(8,128)(2,1)S(1)} %bitcast.6, bf16[2,56,1152]{2,1,0:T(8,128)(2,1)S(1)} %collective-permute-done.8.refs_0_, ...), custom_call_target="tpu_custom_call" | custom-call | tf_op jit(solution)/shard_map/temporal/pallas_call | solution.py:463
  52.3 0.0 copy-start.4
  52.3 0.1 collective-permute-start.14
  52.4 1.5 %collective-permute-done.14.got = bf16[4,256,128]{2,1,0:T(8,128)(2,1)S(1)} collective-permute-done((bf16[4,256,128]{2,1,0:T(8,128)(2,1)S(1)}, bf16[4,256,128]{2,1,0:T(8,128)(2,1)S(1)}, u32[]{:S(2)}, u32[]{:S(2)}) %collective-permute-start.14) | collective-permute-done | bytes 262176 | tf_op jit(solution)/shard_map/ppermute | solution.py:315
  53.9 2.4 %collective-permute-start.17 = (bf16[2,256,128]{2,1,0:T(8,128)(2,1)S(1)}, bf16[2,256,128]{2,1,0:T(8,128)(2,1)S(1)}, u32[]{:S(2)}, u32[]{:S(2)}) collective-permute-start(bf16[2,256,128]{2,1,0:T(8,128)(2,1)S(1)} %get-tuple-element.92), channel_id=1, source_target_pairs={{0,24},{4,28},{8,16},{12,20},{16,8},{20,12},{24,0},{28,4},{1,25},{... | collective-permute-start | bytes 393224 | tf_op jit(solution)/shard_map/ppermute | solution.py:315
  56.3 0.6 collective-permute-start.15
  57.0 0.5 collective-permute-start.16
  57.5 1.0 %residual.1.after = bf16[8,56,1152]{2,1,0:T(8,128)(2,1)S(1)} custom-call(bf16[576,224]{1,0:T(8,128)(2,1)S(1)} %get-tuple-element.76.attended, f32[8,56,224]{2,1,0:T(8,128)S(1)} %get-tuple-element.50.chosen, bf16[8,56,1152]{2,1,0:T(8,128)(2,1)S(1)} %bitcast.11, f32[6,1152]{1,0:T(8,128)S(1)} %copy-done.5, bf16[576,1152]{1,0:T(8,128)(2,1)S(1)} %copy-done.1), custom_call_target="tpu_custom_call" | custom-call | flops 594542592 | bytes 5945425 | tf_op jit(solution)/shard_map/residual/pallas_call | solution.py:430
  58.5 2.3 %collective-permute-done.17.refs_1_ = bf16[2,256,128]{2,1,0:T(8,128)(2,1)S(1)} collective-permute-done((bf16[2,256,128]{2,1,0:T(8,128)(2,1)S(1)}, bf16[2,256,128]{2,1,0:T(8,128)(2,1)S(1)}, u32[]{:S(2)}, u32[]{:S(2)}) %collective-permute-start.17) | collective-permute-done | bytes 131104 | tf_op jit(solution)/shard_map/ppermute | solution.py:315
  60.8 0.0 copy-done.4
  60.8 1.4 %finish_0.1.refs_2_ = bf16[8,56,1152]{2,1,0:T(8,128)(2,1)} custom-call(f32[6,1152]{1,0:T(8,128)S(1)} %copy-done.5, bf16[576,1152]{1,0:T(8,128)(2,1)S(1)} %copy-done.4, bf16[8,56,1152]{2,1,0:T(8,128)(2,1)S(1)} %residual.1.after, bf16[2,256,128]{2,1,0:T(8,128)(2,1)S(1)} %get-tuple-element.91.refs_0_, bf16[2,256,128]{2,1,0:T(8,128)(2,1)S(1)} %collective-permute-done.17.refs_1_), custom_call_target="tpu_custom_call" | custom-call | flops 297271296 | bytes 2972712 | tf_op jit(solution)/shard_map/finish_0/pallas_call | solution.py:484
  62.3 1.0 %collective-permute-done.15.refs_0_ = bf16[2,256,128]{2,1,0:T(8,128)(2,1)S(1)} collective-permute-done((bf16[2,256,128]{2,1,0:T(8,128)(2,1)S(1)}, bf16[2,256,128]{2,1,0:T(8,128)(2,1)S(1)}, u32[]{:S(2)}, u32[]{:S(2)}) %collective-permute-start.15) | collective-permute-done | bytes 131104 | tf_op jit(solution)/shard_map/ppermute | solution.py:315
  63.2 0.0 collective-permute-done.16.refs_1_
  63.2 1.4 %finish_1.1 = bf16[8,56,1152]{2,1,0:T(8,128)(2,1)} custom-call(f32[6,1152]{1,0:T(8,128)S(1)} %copy-done.5, bf16[576,1152]{1,0:T(8,128)(2,1)S(1)} %copy-done.4, bf16[8,56,1152]{2,1,0:T(8,128)(2,1)S(1)} %residual.1.after, bf16[2,256,128]{2,1,0:T(8,128)(2,1)S(1)} %collective-permute-done.15.refs_0_, ...), custom_call_target="tpu_custom_call", output_to_operand_aliasing={{}: (5, {})} | custom-call | flops 297271296 | bytes 2972712 | tf_op jit(solution)/shard_map/finish_1/pallas_call | solution.py:484
  (4 shorter events, 0.1 us)
Async XLA Ops:
  0.0 10.7 %copy-start.2 = (bf16[1152,1728]{0,1:T(8,128)(2,1)S(1)}, bf16[1152,1728]{0,1:T(8,128)(2,1)}, u32[]{:S(2)}) copy-start(bf16[1152,1728]{0,1:T(8,128)(2,1)} %param.10) | copy-start | bytes 11943940
  0.0 3.8 %copy-start.3 = (bf16[1,448,1152]{2,1,0:T(8,128)(2,1)S(1)}, bf16[1,448,1152]{2,1,0:T(8,128)(2,1)}, u32[]{:S(2)}) copy-start(bf16[1,448,1152]{2,1,0:T(8,128)(2,1)} %param.7) | copy-start | bytes 3096580
  3.8 14.6 %copy-start.7 = (s32[1,448]{1,0:T(1,128)S(1)}, s32[1,448]{1,0:T(1,128)}, u32[]{:S(2)}) copy-start(s32[1,448]{1,0:T(1,128)} %slot.3) | copy-start | bytes 5380
  3.9 5.2 %collective-permute-start.6 = (bf16[4,56,1152]{2,1,0:T(8,128)(2,1)S(1)}, bf16[4,56,1152]{2,1,0:T(8,128)(2,1)S(1)}, u32[]{:S(2)}, u32[]{:S(2)}) collective-permute-start(bf16[4,56,1152]{2,1,0:T(8,128)(2,1)S(1)} %get-tuple-element.68), channel_id=1, source_target_pairs={{0,4},{4,0},{8,12},{12,8},{16,20},{20,16},{24,28},{28,24},{1,5},{5... | collective-permute-start | bytes 1548296 | tf_op jit(solution)/shard_map/ppermute | solution.py:315
  4.4 13.2 %collective-permute-start = (bf16[760,128]{1,0:T(8,128)(2,1)}, bf16[760,128]{1,0:T(8,128)(2,1)S(1)}, u32[]{:S(2)}, u32[]{:S(2)}) collective-permute-start(bf16[760,128]{1,0:T(8,128)(2,1)} %get-tuple-element.49), channel_id=1, source_target_pairs={{0,3},{1,2},{2,1},{3,0},{4,7},{5,6},{6,5},{7,4},{8,11},{9,10},{10,... | collective-permute-start | bytes 583688 | tf_op jit(solution)/shard_map/ppermute | solution.py:315
  9.1 33.7 %copy-start = (bf16[1152,1728]{0,1:T(8,128)(2,1)S(1)}, bf16[1152,1728]{0,1:T(8,128)(2,1)}, u32[]{:S(2)}) copy-start(bf16[1152,1728]{0,1:T(8,128)(2,1)} %param.12) | copy-start | bytes 11943940
  9.2 33.7 %copy-start.1 = (bf16[576,1152]{1,0:T(8,128)(2,1)S(1)}, bf16[576,1152]{1,0:T(8,128)(2,1)}, u32[]{:S(2)}) copy-start(bf16[576,1152]{1,0:T(8,128)(2,1)} %proj.9) | copy-start | bytes 3981316
  9.2 33.7 %copy-start.5 = (f32[6,1152]{1,0:T(8,128)S(1)}, f32[6,1152]{1,0:T(8,128)}, u32[]{:S(2)}) copy-start(f32[6,1152]{1,0:T(8,128)} %modulation.13) | copy-start | bytes 82948
  9.2 22.2 %collective-permute-start.7 = (bf16[2,56,1152]{2,1,0:T(8,128)(2,1)S(1)}, bf16[2,56,1152]{2,1,0:T(8,128)(2,1)S(1)}, u32[]{:S(2)}, u32[]{:S(2)}) collective-permute-start(bf16[2,56,1152]{2,1,0:T(8,128)(2,1)S(1)} %get-tuple-element.70), channel_id=1, source_target_pairs={{0,8},{4,12},{8,0},{12,4},{16,24},{20,28},{24,16},{28,20},{1,9},{5... | collective-permute-start | bytes 774152 | tf_op jit(solution)/shard_map/ppermute | solution.py:315
  10.7 1.1 %copy-start.6 = (bf16[224,1152]{1,0:T(8,128)(2,1)S(1)}, bf16[224,1152]{1,0:T(8,128)(2,1)}, u32[]{:S(2)}) copy-start(bf16[224,1152]{1,0:T(8,128)(2,1)} %get-tuple-element.53.merged) | copy-start | bytes 1548292
  13.6 12.8 %collective-permute-start.1 = (bf16[760,128]{1,0:T(8,128)(2,1)S(1)}, bf16[760,128]{1,0:T(8,128)(2,1)S(1)}, u32[]{:S(2)}, u32[]{:S(2)}) collective-permute-start(bf16[760,128]{1,0:T(8,128)(2,1)S(1)} %get-tuple-element.54), channel_id=1, source_target_pairs={{0,2},{1,3},{2,0},{3,1},{4,6},{5,7},{6,4},{7,5},{8,10},{9,11},{10,... | collective-permute-start | bytes 583688 | tf_op jit(solution)/shard_map/ppermute | solution.py:315
  14.5 11.9 %collective-permute-start.2 = (bf16[760,128]{1,0:T(8,128)(2,1)S(1)}, bf16[760,128]{1,0:T(8,128)(2,1)S(1)}, u32[]{:S(2)}, u32[]{:S(2)}) collective-permute-start(bf16[760,128]{1,0:T(8,128)(2,1)S(1)} %get-tuple-element.55), channel_id=1, source_target_pairs={{0,1},{1,0},{2,3},{3,2},{4,5},{5,4},{6,7},{7,6},{8,9},{9,8},{10,11... | collective-permute-start | bytes 583688 | tf_op jit(solution)/shard_map/ppermute | solution.py:315
  16.1 17.2 %collective-permute-start.8 = (bf16[2,56,1152]{2,1,0:T(8,128)(2,1)S(1)}, bf16[2,56,1152]{2,1,0:T(8,128)(2,1)S(1)}, u32[]{:S(2)}, u32[]{:S(2)}) collective-permute-start(bf16[2,56,1152]{2,1,0:T(8,128)(2,1)S(1)} %get-tuple-element.71), channel_id=1, source_target_pairs={{0,16},{4,20},{8,24},{12,28},{16,0},{20,4},{24,8},{28,12},{1,17},{... | collective-permute-start | bytes 774152 | tf_op jit(solution)/shard_map/ppermute | solution.py:315
  17.6 15.6 %collective-permute-start.9 = (bf16[2,56,1152]{2,1,0:T(8,128)(2,1)S(1)}, bf16[2,56,1152]{2,1,0:T(8,128)(2,1)S(1)}, u32[]{:S(2)}, u32[]{:S(2)}) collective-permute-start(bf16[2,56,1152]{2,1,0:T(8,128)(2,1)S(1)} %get-tuple-element.72), channel_id=1, source_target_pairs={{0,24},{4,28},{8,16},{12,20},{16,8},{20,12},{24,0},{28,4},{1,25},{... | collective-permute-start | bytes 774152 | tf_op jit(solution)/shard_map/ppermute | solution.py:315
  28.8 6.3 %collective-permute-start.3 = (bf16[256,128]{1,0:T(8,128)(2,1)S(1)}, bf16[256,128]{1,0:T(8,128)(2,1)S(1)}, u32[]{:S(2)}, u32[]{:S(2)}) collective-permute-start(bf16[256,128]{1,0:T(8,128)(2,1)S(1)} %get-tuple-element.62), channel_id=1, source_target_pairs={{0,3},{1,2},{2,1},{3,0},{4,7},{5,6},{6,5},{7,4},{8,11},{9,10},{10,... | collective-permute-start | bytes 196616 | tf_op jit(solution)/shard_map/ppermute | solution.py:315
  31.3 5.8 %collective-permute-start.4 = (bf16[256,128]{1,0:T(8,128)(2,1)S(1)}, bf16[256,128]{1,0:T(8,128)(2,1)S(1)}, u32[]{:S(2)}, u32[]{:S(2)}) collective-permute-start(bf16[256,128]{1,0:T(8,128)(2,1)S(1)} %get-tuple-element.63), channel_id=1, source_target_pairs={{0,2},{1,3},{2,0},{3,1},{4,6},{5,7},{6,4},{7,5},{8,10},{9,11},{10,... | collective-permute-start | bytes 196616 | tf_op jit(solution)/shard_map/ppermute | solution.py:315
  31.4 5.8 %collective-permute-start.5 = (bf16[256,128]{1,0:T(8,128)(2,1)S(1)}, bf16[256,128]{1,0:T(8,128)(2,1)S(1)}, u32[]{:S(2)}, u32[]{:S(2)}) collective-permute-start(bf16[256,128]{1,0:T(8,128)(2,1)S(1)} %get-tuple-element.64), channel_id=1, source_target_pairs={{0,1},{1,0},{2,3},{3,2},{4,5},{5,4},{6,7},{7,6},{8,9},{9,8},{10,11... | collective-permute-start | bytes 196616 | tf_op jit(solution)/shard_map/ppermute | solution.py:315
  37.7 1.6 %collective-permute-start.10 = (bf16[4,256,128]{2,1,0:T(8,128)(2,1)S(1)}, bf16[4,256,128]{2,1,0:T(8,128)(2,1)S(1)}, u32[]{:S(2)}, u32[]{:S(2)}) collective-permute-start(bf16[4,256,128]{2,1,0:T(8,128)(2,1)S(1)} %get-tuple-element.80), channel_id=1, source_target_pairs={{0,4},{4,0},{8,12},{12,8},{16,20},{20,16},{24,28},{28,24},{1,5},{5... | collective-permute-start | bytes 786440 | tf_op jit(solution)/shard_map/ppermute | solution.py:315
  39.3 6.8 %collective-permute-start.13 = (bf16[2,256,128]{2,1,0:T(8,128)(2,1)S(1)}, bf16[2,256,128]{2,1,0:T(8,128)(2,1)S(1)}, u32[]{:S(2)}, u32[]{:S(2)}) collective-permute-start(bf16[2,256,128]{2,1,0:T(8,128)(2,1)S(1)} %get-tuple-element.86), channel_id=1, source_target_pairs={{0,24},{4,28},{8,16},{12,20},{16,8},{20,12},{24,0},{28,4},{1,25},{... | collective-permute-start | bytes 393224 | tf_op jit(solution)/shard_map/ppermute | solution.py:315
  41.8 6.8 %collective-permute-start.11 = (bf16[2,256,128]{2,1,0:T(8,128)(2,1)S(1)}, bf16[2,256,128]{2,1,0:T(8,128)(2,1)S(1)}, u32[]{:S(2)}, u32[]{:S(2)}) collective-permute-start(bf16[2,256,128]{2,1,0:T(8,128)(2,1)S(1)} %get-tuple-element.81), channel_id=1, source_target_pairs={{0,16},{4,20},{8,24},{12,28},{16,0},{20,4},{24,8},{28,12},{1,17},{... | collective-permute-start | bytes 393224 | tf_op jit(solution)/shard_map/ppermute | solution.py:315
  42.4 6.4 %collective-permute-start.12 = (bf16[2,256,128]{2,1,0:T(8,128)(2,1)S(1)}, bf16[2,256,128]{2,1,0:T(8,128)(2,1)S(1)}, u32[]{:S(2)}, u32[]{:S(2)}) collective-permute-start(bf16[2,256,128]{2,1,0:T(8,128)(2,1)S(1)} %get-tuple-element.82), channel_id=1, source_target_pairs={{0,8},{4,12},{8,0},{12,4},{16,24},{20,28},{24,16},{28,20},{1,9},{5... | collective-permute-start | bytes 393224 | tf_op jit(solution)/shard_map/ppermute | solution.py:315
  52.3 8.5 %copy-start.4 = (bf16[576,1152]{1,0:T(8,128)(2,1)S(1)}, bf16[576,1152]{1,0:T(8,128)(2,1)}, u32[]{:S(2)}) copy-start(bf16[576,1152]{1,0:T(8,128)(2,1)} %proj.11) | copy-start | bytes 3981316
  52.3 1.6 %collective-permute-start.14 = (bf16[4,256,128]{2,1,0:T(8,128)(2,1)S(1)}, bf16[4,256,128]{2,1,0:T(8,128)(2,1)S(1)}, u32[]{:S(2)}, u32[]{:S(2)}) collective-permute-start(bf16[4,256,128]{2,1,0:T(8,128)(2,1)S(1)} %get-tuple-element.88), channel_id=1, source_target_pairs={{0,4},{4,0},{8,12},{12,8},{16,20},{20,16},{24,28},{28,24},{1,5},{5... | collective-permute-start | bytes 786440 | tf_op jit(solution)/shard_map/ppermute | solution.py:315
  53.9 6.9 %collective-permute-start.17 = (bf16[2,256,128]{2,1,0:T(8,128)(2,1)S(1)}, bf16[2,256,128]{2,1,0:T(8,128)(2,1)S(1)}, u32[]{:S(2)}, u32[]{:S(2)}) collective-permute-start(bf16[2,256,128]{2,1,0:T(8,128)(2,1)S(1)} %get-tuple-element.92), channel_id=1, source_target_pairs={{0,24},{4,28},{8,16},{12,20},{16,8},{20,12},{24,0},{28,4},{1,25},{... | collective-permute-start | bytes 393224 | tf_op jit(solution)/shard_map/ppermute | solution.py:315
  56.3 6.9 %collective-permute-start.15 = (bf16[2,256,128]{2,1,0:T(8,128)(2,1)S(1)}, bf16[2,256,128]{2,1,0:T(8,128)(2,1)S(1)}, u32[]{:S(2)}, u32[]{:S(2)}) collective-permute-start(bf16[2,256,128]{2,1,0:T(8,128)(2,1)S(1)} %get-tuple-element.89), channel_id=1, source_target_pairs={{0,16},{4,20},{8,24},{12,28},{16,0},{20,4},{24,8},{28,12},{1,17},{... | collective-permute-start | bytes 393224 | tf_op jit(solution)/shard_map/ppermute | solution.py:315
  57.0 6.3 %collective-permute-start.16 = (bf16[2,256,128]{2,1,0:T(8,128)(2,1)S(1)}, bf16[2,256,128]{2,1,0:T(8,128)(2,1)S(1)}, u32[]{:S(2)}, u32[]{:S(2)}) collective-permute-start(bf16[2,256,128]{2,1,0:T(8,128)(2,1)S(1)} %get-tuple-element.90), channel_id=1, source_target_pairs={{0,8},{4,12},{8,0},{12,4},{16,24},{20,28},{24,16},{28,20},{1,9},{5... | collective-permute-start | bytes 393224 | tf_op jit(solution)/shard_map/ppermute | solution.py:315

commit v8 on v7

--- a/solution.py
+++ b/solution.py
@@ -194,7 +194,7 @@
 
 
 def expand_kernel(n_space, n_pair, slots, wide, chosen, *refs):
-    ins, (keep, give, attended, held) = refs[:n_space], refs[n_space:]
+    ins, (keep, give, same, other, attended, held) = refs[:n_space], refs[n_space:]
     me = lax.axis_index("space")
     held[me] = ins[n_space - 1][...].astype(F32)
     for s in range(1, n_space):
@@ -206,7 +206,11 @@
     for s in range(n_pair):
         for t, out in enumerate((keep, give)):
             at = (2 * s + t) * places
-            out[s] = pack(wanted[at : at + places]).astype(BF16)
+            block = pack(wanted[at : at + places]).astype(BF16)
+            if s < n_pair - 1:
+                out[s] = block
+            else:
+                (same, other)[t][...] = block
 
 
 def cost(flops):
@@ -233,7 +237,7 @@
 def project_blocks(places, modulation, proj, weights, tokens, results, normed):
     frames = [(s, t) for s in range(len(tokens)) for t in range(2)]
     inner = proj.shape[0]
-    attended = [unpack(results[s][t].astype(F32), places, inner) for s, t in frames]
+    attended = [unpack(results[s][t][...].astype(F32), places, inner) for s, t in frames]
     attended = jnp.concatenate(attended, 0).astype(BF16)
     spatial = dot(attended, proj[...])
     gate, shift, scale = modulation[2:3], modulation[3:4], 1.0 + modulation[4:5]
@@ -249,8 +253,9 @@
 
 
 def project_kernel(places, n_parts, modulation, proj, weights, *refs):
-    out, normed = refs[2 * n_parts :]
-    blocks = project_blocks(places, modulation, proj, weights, refs[:n_parts], refs[n_parts : 2 * n_parts], normed)
+    out, normed = refs[-2:]
+    results = regroup(refs[n_parts:-2], n_parts)
+    blocks = project_blocks(places, modulation, proj, weights, refs[:n_parts], results, normed)
     for f, block in enumerate(blocks):
         out[f] = block
 
@@ -293,11 +298,12 @@
             out[s] = pack(jnp.concatenate(rows, 0)[:places]).astype(BF16)
 
 
-def finish_kernel(taken, places, modulation, proj, after, *refs):
-    parts, (out, held, sems) = refs[: len(taken)], refs[-3:]
+def finish_kernel(taken, places, n_refs, modulation, proj, after, *refs):
+    out, held, sems = refs[-3:]
+    parts = regroup(refs[:n_refs], len(taken))
     frame = lax.axis_index("frames")
     frames = [(s, t) for s in range(len(taken)) for t in range(2)]
-    mixed = [unpack(parts[s][t].astype(F32), places, proj.shape[0]) for s, t in frames]
+    mixed = [unpack(parts[s][t][...].astype(F32), places, proj.shape[0]) for s, t in frames]
     mixed = jnp.concatenate(mixed, 0).astype(BF16)
     branch = dot(mixed, proj[...])
     gate = modulation[5:6]
@@ -324,13 +330,23 @@
     got = swap(give, "frames", size, 1)
     both = pl.pallas_call(
         pair_kernel,
-        out_shape=[struct(2, *keep.shape[1:])] * (size // 2),
+        out_shape=[struct(2, *keep.shape[1:])] * keep.shape[0],
         in_specs=[VMEM] * 2,
-        out_specs=[VMEM] * (size // 2),
+        out_specs=[VMEM] * keep.shape[0],
         compiler_params=params(4),
         name="pair",
     )(keep, got)
     return swaps(both, "frames", size, 2)
+
+
+def exchange_apart(keep, give, same, other, size):
+    far = size - 2
+    straight = [swap(same, "frames", size, far), swap(other, "frames", size, far + 1)]
+    return [[both] for both in exchange(keep, give, size)] + [straight]
+
+
+def regroup(refs, count):
+    return list(refs) if len(refs) == count else list(refs[: count - 1]) + [refs[count - 1 :]]
 
 
 def shards(n_frames, n_space, latents, merge_slot, modulation, spatial_qkv, spatial_proj, temporal_qkv, temporal_proj):
@@ -417,16 +433,17 @@
         name="attend_own",
     )(own_queries, all_keys, all_vals)
     mine = swaps([own] + results, "space", n_space)
-    keep, give, attended = pl.pallas_call(
+    apart = [struct(n_pair - 1, moved, LANES)] * 2 + [struct(moved, LANES)] * 2
+    *blocks_apart, attended = pl.pallas_call(
         functools.partial(expand_kernel, n_space, n_pair, slots, wide),
-        out_shape=[struct(n_pair, moved, LANES), struct(n_pair, moved, LANES), struct(inner, slots)],
+        out_shape=apart + [struct(inner, slots)],
         in_specs=[VMEM] * (n_space + 1),
-        out_specs=[VMEM] * 3,
+        out_specs=[VMEM] * 5,
         scratch_shapes=[pltpu.VMEM((n_space, wide, slots), F32)],
         compiler_params=params(8),
         name="expand",
     )(chosen, *reversed(mine))
-    attended_parts = exchange(keep, give, n_frames)
+    attended_parts = exchange_apart(*blocks_apart, n_frames)
     after = pl.pallas_call(
         residual_kernel,
         out_shape=struct(n_frames, places, width),
@@ -442,22 +459,25 @@
     last = order[len(steps) :]
     before = []
     for i, step in enumerate(steps):
+        if before:
+            s = step[-1]
+            attended_parts[s], before = lax.optimization_barrier((attended_parts[s], before))
         before += [
             pl.pallas_call(
                 functools.partial(project_kernel, places, len(step)),
                 out_shape=struct(2 * len(step), pad, 3 * inner),
-                in_specs=[VMEM] * (3 + 2 * len(step)),
+                in_specs=[VMEM] * (3 + len(step) + sum(len(attended_parts[s]) for s in step)),
                 out_specs=VMEM,
                 scratch_shapes=[pltpu.VMEM((2 * len(step) * places, width), F32)],
                 compiler_params=params(10),
-                cost_estimate=cost(2 * 2 * places * len(step) * 3 * inner * width),
+                cost_estimate=cost((1 + 9 * i) * 2 * 2 * places * len(step) * 3 * inner * width),
                 name="project_%d" % i,
             )(
                 modulation,
                 spatial_proj,
                 temporal_qkv,
                 *[tokens[s] for s in step],
-                *[attended_parts[s] for s in step],
+                *[part for s in step for part in attended_parts[s]],
             )
         ]
     mixed = pl.pallas_call(
@@ -473,28 +493,28 @@
         spatial_proj,
         temporal_qkv,
         *[tokens[s] for s in last],
-        *[attended_parts[s] for s in last],
+        *[part for s in last for part in attended_parts[s]],
         *before,
     )
-    mixed_keep, mixed_give = mixed
-    parts = exchange(mixed_keep, mixed_give, n_frames)
+    parts = [[both] for both in exchange(*mixed, n_frames)]
     out = None
     for i, step in enumerate(([0, n_pair - 1], list(range(n_pair - 2, 0, -1)))):
         if step:
+            given = [part for s in step for part in parts[s]]
             out = pl.pallas_call(
-                functools.partial(finish_kernel, step, places),
+                functools.partial(finish_kernel, step, places, len(given)),
                 out_shape=struct(n_frames, places, width),
-                in_specs=[VMEM] * (3 + len(step)) + ([HBM] if i else []),
+                in_specs=[VMEM] * (3 + len(given)) + ([HBM] if i else []),
                 out_specs=HBM,
                 scratch_shapes=[
                     pltpu.VMEM((2 * len(step), places, width), BF16),
                     pltpu.SemaphoreType.DMA((2 * len(step),)),
                 ],
-                input_output_aliases={3 + len(step): 0} if i else {},
+                input_output_aliases={3 + len(given): 0} if i else {},
                 compiler_params=params(10),
                 cost_estimate=cost(2 * 2 * places * len(step) * inner * width),
                 name="finish_%d" % i,
-            )(modulation, temporal_proj, after, *[parts[s] for s in step], *([out] if i else []))
+            )(modulation, temporal_proj, after, *given, *([out] if i else []))
     return out.reshape(1, rows, width)
 
 
@@ -604,7 +624,7 @@
     placed = (P("frames", "space", None), P("frames", "space"), P(), P(), P(), P(), P())
 
     def local(latents, *rest):
-        fits = latents.shape[1] % (8 * n_frames) == 0 and n_frames & (n_frames - 1) == 0 and n_space & (n_space - 1) == 0
+        fits = n_frames >= 8 and latents.shape[1] % (8 * n_frames) == 0 and n_frames & (n_frames - 1) == 0 and n_space & (n_space - 1) == 0
         body = functools.partial(shards, n_frames, n_space) if fits else plain_shards
         return body(latents, *rest)
 

time: 64.8 us -> 63.9 us (0.986)
  waiting for transfers between devices: 18.7 us -> 15.4 us
  starting transfers between devices: 23.2 us -> 25.5 us
    ppermute x18 -> x19, waiting for transfers between devices: 18.7 us -> 15.4 us  [swap(): return lax.ppermute(block, axis, [(i, i ^ mask) for i in range(size)])]
    ppermute x18 -> x19, starting transfers between devices: 23.2 us -> 25.5 us  [swap(): return lax.ppermute(block, axis, [(i, i ^ mask) for i in range(size)])]
  transfers between devices with their start and end apart: 18 -> 19, of which waited for: 10 -> 7; matrix products, arithmetic and copies ran while one was open for 0% -> 0% of each run, Pallas kernels for 19% -> 19%
where the time goes in v8:
time: 63.9 us; the launch traced here: 63.7 us
  starting transfers between devices  25.5 us (40%)
  Pallas kernels  21.5 us (34%)
  waiting for transfers between devices  15.4 us (24%)
  local copies, waits for them, and re-layouts  1.09 us (2%)
    ppermute x19, starting transfers between devices, swap(): return lax.ppermute(block, axis, [(i, i ^ mask) for i in range(size)])  25.5 us
    ppermute x19, waiting for transfers between devices, swap(): return lax.ppermute(block, axis, [(i, i ^ mask) for i in range(size)])  15.4 us
    pallas_call x2, Pallas kernels, shards(): pl.pallas_call(functools.partial(project_kernel, places, len(step)), out_...  3.82 us
    pallas_call x1, Pallas kernels, shards(): pl.pallas_call(functools.partial(merge_kernel, n_space), out_shape=[struc...  3.74 us
    pallas_call x1, Pallas kernels, shards(): pl.pallas_call(functools.partial(temporal_kernel, n_pair, places, len(las...  3.55 us
    pallas_call x2, Pallas kernels, shards(): pl.pallas_call(functools.partial(finish_kernel, step, places, len(given))...  2.83 us
    pallas_call x1, Pallas kernels, shards(): pl.pallas_call(functools.partial(others_kernel, n_space, slots, wide), ou...  2.39 us
    pallas_call x1, Pallas kernels, shards(): pl.pallas_call(functools.partial(spread_kernel, n_space), out_shape=[stru...  1.84 us
  transfers between devices with their start and end apart: 19, of which 7 were waited for; matrix products, arithmetic and copies ran while one was open for 0% of the time, Pallas kernels for 19%

profile of v8, /device:TPU:0, one launch (start us, length us, event | category | flops | bytes accessed | tf_op | source)
XLA Modules:
  0.0 63.7 jit_solution(3886150407232998219)
XLA Ops:
  0.0 3.7 %merge.1 = (bf16[760,128]{1,0:T(8,128)(2,1)}, bf16[224,1152]{1,0:T(8,128)(2,1)}) custom-call(bf16[8,56,1152]{2,1,0:T(8,128)(2,1)} %bitcast.9, s32[1,448]{1,0:T(1,128)} %slot.3, f32[6,1152]{1,0:T(8,128)} %modulation.13, bf16[1728,1152]{1,0:T(8,128)(2,1)} %bitcast.4), custom_call_target="tpu_custom_call" | custom-call | tf_op jit(solution)/shard_map/merge/pallas_call | solution.py:361
  3.8 0.0 copy-start.7
  3.8 0.0 copy-done.3
  3.8 0.1 share.1
  3.9 0.5 collective-permute-start.6
  4.4 4.7 %collective-permute-start = (bf16[760,128]{1,0:T(8,128)(2,1)}, bf16[760,128]{1,0:T(8,128)(2,1)S(1)}, u32[]{:S(2)}, u32[]{:S(2)}) collective-permute-start(bf16[760,128]{1,0:T(8,128)(2,1)} %get-tuple-element.53), channel_id=1, source_target_pairs={{0,3},{1,2},{2,1},{3,0},{4,7},{5,6},{6,5},{7,4},{8,11},{9,10},{10,... | collective-permute-start | bytes 583688 | tf_op jit(solution)/shard_map/ppermute | solution.py:321
  9.1 0.0 collective-permute-done.6.got
  9.1 0.1 pair.3
  9.1 0.0 copy-start.1
  9.2 0.0 copy-start.2
  9.2 0.0 copy-start.5
  9.2 1.6 %collective-permute-start.7 = (bf16[2,56,1152]{2,1,0:T(8,128)(2,1)S(1)}, bf16[2,56,1152]{2,1,0:T(8,128)(2,1)S(1)}, u32[]{:S(2)}, u32[]{:S(2)}) collective-permute-start(bf16[2,56,1152]{2,1,0:T(8,128)(2,1)S(1)} %get-tuple-element.74), channel_id=1, source_target_pairs={{0,8},{4,12},{8,0},{12,4},{16,24},{20,28},{24,16},{28,20},{1,9},{5... | collective-permute-start | bytes 774152 | tf_op jit(solution)/shard_map/ppermute | solution.py:321
  10.7 0.0 copy-done
  10.7 1.0 %copy-done.6 = bf16[224,1152]{1,0:T(8,128)(2,1)S(1)} copy-done((bf16[224,1152]{1,0:T(8,128)(2,1)S(1)}, bf16[224,1152]{1,0:T(8,128)(2,1)}, u32[]{:S(2)}) %copy-start.6) | copy-done | bytes 516120
  11.8 1.8 %spread.1 = (bf16[760,128]{1,0:T(8,128)(2,1)S(1)}, bf16[760,128]{1,0:T(8,128)(2,1)S(1)}, bf16[760,128]{1,0:T(8,128)(2,1)S(1)}) custom-call(bf16[224,1152]{1,0:T(8,128)(2,1)S(1)} %copy-done.6, bf16[1728,1152]{1,0:T(8,128)(2,1)S(1)} %bitcast.5), custom_call_target="tpu_custom_call" | custom-call | flops 891813888 | bytes 8918138 | tf_op jit(solution)/shard_map/spread/pallas_call | solution.py:376
  13.6 0.9 %collective-permute-start.1 = (bf16[760,128]{1,0:T(8,128)(2,1)S(1)}, bf16[760,128]{1,0:T(8,128)(2,1)S(1)}, u32[]{:S(2)}, u32[]{:S(2)}) collective-permute-start(bf16[760,128]{1,0:T(8,128)(2,1)S(1)} %get-tuple-element.58), channel_id=1, source_target_pairs={{0,2},{1,3},{2,0},{3,1},{4,6},{5,7},{6,4},{7,5},{8,10},{9,11},{10,... | collective-permute-start | bytes 583688 | tf_op jit(solution)/shard_map/ppermute | solution.py:321
  14.5 1.6 %collective-permute-start.2 = (bf16[760,128]{1,0:T(8,128)(2,1)S(1)}, bf16[760,128]{1,0:T(8,128)(2,1)S(1)}, u32[]{:S(2)}, u32[]{:S(2)}) collective-permute-start(bf16[760,128]{1,0:T(8,128)(2,1)S(1)} %get-tuple-element.59), channel_id=1, source_target_pairs={{0,1},{1,0},{2,3},{3,2},{4,5},{5,4},{6,7},{7,6},{8,9},{9,8},{10,11... | collective-permute-start | bytes 583688 | tf_op jit(solution)/shard_map/ppermute | solution.py:321
  16.1 1.5 %collective-permute-start.8 = (bf16[2,56,1152]{2,1,0:T(8,128)(2,1)S(1)}, bf16[2,56,1152]{2,1,0:T(8,128)(2,1)S(1)}, u32[]{:S(2)}, u32[]{:S(2)}) collective-permute-start(bf16[2,56,1152]{2,1,0:T(8,128)(2,1)S(1)} %get-tuple-element.75), channel_id=1, source_target_pairs={{0,16},{4,20},{8,24},{12,28},{16,0},{20,4},{24,8},{28,12},{1,17},{... | collective-permute-start | bytes 774152 | tf_op jit(solution)/shard_map/ppermute | solution.py:321
  17.6 0.0 collective-permute-done.packed
  17.6 0.8 %collective-permute-start.9 = (bf16[2,56,1152]{2,1,0:T(8,128)(2,1)S(1)}, bf16[2,56,1152]{2,1,0:T(8,128)(2,1)S(1)}, u32[]{:S(2)}, u32[]{:S(2)}) collective-permute-start(bf16[2,56,1152]{2,1,0:T(8,128)(2,1)S(1)} %get-tuple-element.76), channel_id=1, source_target_pairs={{0,24},{4,28},{8,16},{12,20},{16,8},{20,12},{24,0},{28,4},{1,25},{... | collective-permute-start | bytes 774152 | tf_op jit(solution)/shard_map/ppermute | solution.py:321
  18.4 0.0 copy-done.7
  18.4 0.3 prepare.1
  18.7 7.7 %collective-permute-done.1.refs_0_ = bf16[760,128]{1,0:T(8,128)(2,1)S(1)} collective-permute-done((bf16[760,128]{1,0:T(8,128)(2,1)S(1)}, bf16[760,128]{1,0:T(8,128)(2,1)S(1)}, u32[]{:S(2)}, u32[]{:S(2)}) %collective-permute-start.1) | collective-permute-done | bytes 194592 | tf_op jit(solution)/shard_map/ppermute | solution.py:321
  26.4 0.0 collective-permute-done.2.refs_1_
  26.4 2.4 %attend_others.1 = (bf16[256,128]{1,0:T(8,128)(2,1)S(1)}, bf16[256,128]{1,0:T(8,128)(2,1)S(1)}, bf16[256,128]{1,0:T(8,128)(2,1)S(1)}, bf16[144,224]{1,0:T(8,128)...) custom-call(bf16[224,144]{1,0:T(8,128)(2,1)S(1)} %get-tuple-element.61.far_keys, ...), custom_call_target="tpu_custom_call" | custom-call | flops 346816512 | bytes 3468165 | tf_op jit(solution)/shard_map/attend_others/pallas_call | solution.py:415
  28.8 2.5 %collective-permute-start.3 = (bf16[256,128]{1,0:T(8,128)(2,1)S(1)}, bf16[256,128]{1,0:T(8,128)(2,1)S(1)}, u32[]{:S(2)}, u32[]{:S(2)}) collective-permute-start(bf16[256,128]{1,0:T(8,128)(2,1)S(1)} %get-tuple-element.66), channel_id=1, source_target_pairs={{0,3},{1,2},{2,1},{3,0},{4,7},{5,6},{6,5},{7,4},{8,11},{9,10},{10,... | collective-permute-start | bytes 196616 | tf_op jit(solution)/shard_map/ppermute | solution.py:321
  31.3 0.0 collective-permute-start.4
  31.4 0.0 collective-permute-done.7.refs_1_
  31.4 1.9 %collective-permute-start.5 = (bf16[256,128]{1,0:T(8,128)(2,1)S(1)}, bf16[256,128]{1,0:T(8,128)(2,1)S(1)}, u32[]{:S(2)}, u32[]{:S(2)}) collective-permute-start(bf16[256,128]{1,0:T(8,128)(2,1)S(1)} %get-tuple-element.68), channel_id=1, source_target_pairs={{0,1},{1,0},{2,3},{3,2},{4,5},{5,4},{6,7},{7,6},{8,9},{9,8},{10,11... | collective-permute-start | bytes 196616 | tf_op jit(solution)/shard_map/ppermute | solution.py:321
  33.3 0.0 collective-permute-done.8.refs_0_
  33.3 0.0 collective-permute-done.9.refs_0_
  33.3 1.3 %attend_own.1.refs_3_ = bf16[144,224]{1,0:T(8,128)(2,1)S(1)} custom-call(bf16[144,224]{1,0:T(8,128)(2,1)S(1)} %get-tuple-element.77.queries, bf16[896,144]{1,0:T(8,128)(2,1)S(1)} %get-tuple-element.78.keys, bf16[144,896]{1,0:T(8,128)(2,1)S(1)} %get-tuple-element.79.vals), custom_call_target="tpu_custom_call" | custom-call | flops 115605504 | bytes 1156055 | tf_op jit(solution)/shard_map/attend_own/pallas_call | solution.py:426
  34.6 0.5 collective-permute-done.3.refs_0_
  35.1 2.0 %collective-permute-done.4.refs_1_ = bf16[256,128]{1,0:T(8,128)(2,1)S(1)} collective-permute-done((bf16[256,128]{1,0:T(8,128)(2,1)S(1)}, bf16[256,128]{1,0:T(8,128)(2,1)S(1)}, u32[]{:S(2)}, u32[]{:S(2)}) %collective-permute-start.4) | collective-permute-done | bytes 65568 | tf_op jit(solution)/shard_map/ppermute | solution.py:321
  37.1 0.0 collective-permute-done.5.refs_2_
  37.1 0.5 expand.1
  37.7 0.1 collective-permute-start.10
  37.8 2.5 %collective-permute-start.13 = (bf16[256,128]{1,0:T(8,128)(2,1)S(1)}, bf16[256,128]{1,0:T(8,128)(2,1)S(1)}, u32[]{:S(2)}, u32[]{:S(2)}) collective-permute-start(bf16[256,128]{1,0:T(8,128)(2,1)S(1)} %get-tuple-element.87), channel_id=1, source_target_pairs={{0,24},{4,28},{8,16},{12,20},{16,8},{20,12},{24,0},{28,4},{1,25},{... | collective-permute-start | bytes 196616 | tf_op jit(solution)/shard_map/ppermute | solution.py:321
  40.3 0.3 collective-permute-start.14
  40.5 0.0 collective-permute-done.10.got
  40.6 1.6 %collective-permute-start.11 = (bf16[2,256,128]{2,1,0:T(8,128)(2,1)S(1)}, bf16[2,256,128]{2,1,0:T(8,128)(2,1)S(1)}, u32[]{:S(2)}, u32[]{:S(2)}) collective-permute-start(bf16[2,256,128]{2,1,0:T(8,128)(2,1)S(1)} %get-tuple-element.85), channel_id=1, source_target_pairs={{0,16},{4,20},{8,24},{12,28},{16,0},{20,4},{24,8},{28,12},{1,17},{... | collective-permute-start | bytes 393224 | tf_op jit(solution)/shard_map/ppermute | solution.py:321
  42.1 1.5 %collective-permute-start.12 = (bf16[2,256,128]{2,1,0:T(8,128)(2,1)S(1)}, bf16[2,256,128]{2,1,0:T(8,128)(2,1)S(1)}, u32[]{:S(2)}, u32[]{:S(2)}) collective-permute-start(bf16[2,256,128]{2,1,0:T(8,128)(2,1)S(1)} %get-tuple-element.86), channel_id=1, source_target_pairs={{0,8},{4,12},{8,0},{12,4},{16,24},{20,28},{24,16},{28,20},{1,9},{5... | collective-permute-start | bytes 393224 | tf_op jit(solution)/shard_map/ppermute | solution.py:321
  43.6 0.0 copy-done.1
  43.6 0.0 copy-done.2
  43.6 0.0 copy-done.5
  43.6 1.9 %project_0.1.refs_4_ = bf16[2,64,1728]{2,1,0:T(8,128)(2,1)S(1)} custom-call(f32[6,1152]{1,0:T(8,128)S(1)} %copy-done.5, bf16[576,1152]{1,0:T(8,128)(2,1)S(1)} %copy-done.2, bf16[1728,1152]{1,0:T(8,128)(2,1)S(1)} %bitcast.6, bf16[2,56,1152]{2,1,0:T(8,128)(2,1)S(1)} %get-tuple-element.89.refs_0_, bf16[2,256,128]{2,1,0:T(8,128)(2,1)S(1)} %get-tuple-element.90.refs_1_), custom_call_target="tpu_custom_call" | custom-call | flops 445906944 | bytes 4459069 | tf_op jit(solution)/shard_map/project_0/pallas_call | solution.py:466
  45.6 0.0 collective-permute-done.13.refs_1_
  45.6 0.0 collective-permute-done.14.refs_2_
  45.6 1.9 %project_1.1.refs_5_ = bf16[2,64,1728]{2,1,0:T(8,128)(2,1)S(1)} custom-call(f32[6,1152]{1,0:T(8,128)S(1)} %copy-done.5, bf16[576,1152]{1,0:T(8,128)(2,1)S(1)} %copy-done.2, bf16[1728,1152]{1,0:T(8,128)(2,1)S(1)} %bitcast.7, bf16[2,56,1152]{2,1,0:T(8,128)(2,1)S(1)} %collective-permute-done.9.refs_0_, bf16[256,128]{1,0:T(8,128)(2,1)S(1)} %collective-permute-done.13.refs_1_, ...), custom_call_target="tpu_custom_call" | custom-call | flops 4459069440 | bytes 44590696 | tf_op jit(solution)/shard_map/project_1/pallas_call | solution.py:466
  47.5 0.3 collective-permute-done.11.refs_2_
  47.8 0.0 collective-permute-done.12.refs_3_
  47.8 3.6 %temporal.1 = (bf16[4,256,128]{2,1,0:T(8,128)(2,1)S(1)}, bf16[4,256,128]{2,1,0:T(8,128)(2,1)S(1)}) custom-call(f32[6,1152]{1,0:T(8,128)S(1)} %copy-done.5, bf16[576,1152]{1,0:T(8,128)(2,1)S(1)} %copy-done.2, bf16[1728,1152]{1,0:T(8,128)(2,1)S(1)} %bitcast.8, bf16[2,56,1152]{2,1,0:T(8,128)(2,1)S(1)} %collective-permute-done.8.refs_0_, ...), custom_call_target="tpu_custom_call" | custom-call | tf_op jit(solution)/shard_map/temporal/pallas_call | solution.py:483
  51.3 0.0 copy-start.4
  51.4 0.1 collective-permute-start.15
  51.4 1.5 %collective-permute-done.15.got = bf16[4,256,128]{2,1,0:T(8,128)(2,1)S(1)} collective-permute-done((bf16[4,256,128]{2,1,0:T(8,128)(2,1)S(1)}, bf16[4,256,128]{2,1,0:T(8,128)(2,1)S(1)}, u32[]{:S(2)}, u32[]{:S(2)}) %collective-permute-start.15) | collective-permute-done | bytes 262176 | tf_op jit(solution)/shard_map/ppermute | solution.py:321
  53.0 2.1 %collective-permute-start.18 = (bf16[2,256,128]{2,1,0:T(8,128)(2,1)S(1)}, bf16[2,256,128]{2,1,0:T(8,128)(2,1)S(1)}, u32[]{:S(2)}, u32[]{:S(2)}) collective-permute-start(bf16[2,256,128]{2,1,0:T(8,128)(2,1)S(1)} %get-tuple-element.100), channel_id=1, source_target_pairs={{0,24},{4,28},{8,16},{12,20},{16,8},{20,12},{24,0},{28,4},{1,25},{... | collective-permute-start | bytes 393224 | tf_op jit(solution)/shard_map/ppermute | solution.py:321
  55.1 0.7 %collective-permute-start.16 = (bf16[2,256,128]{2,1,0:T(8,128)(2,1)S(1)}, bf16[2,256,128]{2,1,0:T(8,128)(2,1)S(1)}, u32[]{:S(2)}, u32[]{:S(2)}) collective-permute-start(bf16[2,256,128]{2,1,0:T(8,128)(2,1)S(1)} %get-tuple-element.97), channel_id=1, source_target_pairs={{0,16},{4,20},{8,24},{12,28},{16,0},{20,4},{24,8},{28,12},{1,17},{... | collective-permute-start | bytes 393224 | tf_op jit(solution)/shard_map/ppermute | solution.py:321
  55.8 0.7 %collective-permute-start.17 = (bf16[2,256,128]{2,1,0:T(8,128)(2,1)S(1)}, bf16[2,256,128]{2,1,0:T(8,128)(2,1)S(1)}, u32[]{:S(2)}, u32[]{:S(2)}) collective-permute-start(bf16[2,256,128]{2,1,0:T(8,128)(2,1)S(1)} %get-tuple-element.98), channel_id=1, source_target_pairs={{0,8},{4,12},{8,0},{12,4},{16,24},{20,28},{24,16},{28,20},{1,9},{5... | collective-permute-start | bytes 393224 | tf_op jit(solution)/shard_map/ppermute | solution.py:321
  56.6 1.0 %residual.1.after = bf16[8,56,1152]{2,1,0:T(8,128)(2,1)S(1)} custom-call(bf16[576,224]{1,0:T(8,128)(2,1)S(1)} %get-tuple-element.80.attended, f32[8,56,224]{2,1,0:T(8,128)S(1)} %get-tuple-element.54.chosen, bf16[8,56,1152]{2,1,0:T(8,128)(2,1)S(1)} %bitcast.11, f32[6,1152]{1,0:T(8,128)S(1)} %copy-done.5, bf16[576,1152]{1,0:T(8,128)(2,1)S(1)} %copy-done.2), custom_call_target="tpu_custom_call" | custom-call | flops 594542592 | bytes 5945425 | tf_op jit(solution)/shard_map/residual/pallas_call | solution.py:447
  57.6 2.7 %collective-permute-done.18.refs_1_ = bf16[2,256,128]{2,1,0:T(8,128)(2,1)S(1)} collective-permute-done((bf16[2,256,128]{2,1,0:T(8,128)(2,1)S(1)}, bf16[2,256,128]{2,1,0:T(8,128)(2,1)S(1)}, u32[]{:S(2)}, u32[]{:S(2)}) %collective-permute-start.18) | collective-permute-done | bytes 131104 | tf_op jit(solution)/shard_map/ppermute | solution.py:321
  60.2 1.4 %finish_0.1.refs_2_ = bf16[8,56,1152]{2,1,0:T(8,128)(2,1)} custom-call(f32[6,1152]{1,0:T(8,128)S(1)} %copy-done.5, bf16[576,1152]{1,0:T(8,128)(2,1)S(1)} %copy-done.4, bf16[8,56,1152]{2,1,0:T(8,128)(2,1)S(1)} %residual.1.after, bf16[2,256,128]{2,1,0:T(8,128)(2,1)S(1)} %get-tuple-element.99.refs_0_, bf16[2,256,128]{2,1,0:T(8,128)(2,1)S(1)} %collective-permute-done.18.refs_1_), custom_call_target="tpu_custom_call" | custom-call | flops 297271296 | bytes 2972712 | tf_op jit(solution)/shard_map/finish_0/pallas_call | solution.py:504
  61.6 0.7 %collective-permute-done.16.refs_0_ = bf16[2,256,128]{2,1,0:T(8,128)(2,1)S(1)} collective-permute-done((bf16[2,256,128]{2,1,0:T(8,128)(2,1)S(1)}, bf16[2,256,128]{2,1,0:T(8,128)(2,1)S(1)}, u32[]{:S(2)}, u32[]{:S(2)}) %collective-permute-start.16) | collective-permute-done | bytes 131104 | tf_op jit(solution)/shard_map/ppermute | solution.py:321
  62.3 0.0 collective-permute-done.17.refs_1_
  62.3 1.4 %finish_1.1 = bf16[8,56,1152]{2,1,0:T(8,128)(2,1)} custom-call(f32[6,1152]{1,0:T(8,128)S(1)} %copy-done.5, bf16[576,1152]{1,0:T(8,128)(2,1)S(1)} %copy-done.4, bf16[8,56,1152]{2,1,0:T(8,128)(2,1)S(1)} %residual.1.after, bf16[2,256,128]{2,1,0:T(8,128)(2,1)S(1)} %collective-permute-done.16.refs_0_, ...), custom_call_target="tpu_custom_call", output_to_operand_aliasing={{}: (5, {})} | custom-call | flops 297271296 | bytes 2972712 | tf_op jit(solution)/shard_map/finish_1/pallas_call | solution.py:504
  (6 shorter events, 0.1 us)
Async XLA Ops:
  0.0 10.7 %copy-start = (bf16[1152,1728]{0,1:T(8,128)(2,1)S(1)}, bf16[1152,1728]{0,1:T(8,128)(2,1)}, u32[]{:S(2)}) copy-start(bf16[1152,1728]{0,1:T(8,128)(2,1)} %param.10) | copy-start | bytes 11943940
  0.0 3.8 %copy-start.3 = (bf16[1,448,1152]{2,1,0:T(8,128)(2,1)S(1)}, bf16[1,448,1152]{2,1,0:T(8,128)(2,1)}, u32[]{:S(2)}) copy-start(bf16[1,448,1152]{2,1,0:T(8,128)(2,1)} %param.7) | copy-start | bytes 3096580
  3.8 14.6 %copy-start.7 = (s32[1,448]{1,0:T(1,128)S(1)}, s32[1,448]{1,0:T(1,128)}, u32[]{:S(2)}) copy-start(s32[1,448]{1,0:T(1,128)} %slot.3) | copy-start | bytes 5380
  3.9 5.2 %collective-permute-start.6 = (bf16[4,56,1152]{2,1,0:T(8,128)(2,1)S(1)}, bf16[4,56,1152]{2,1,0:T(8,128)(2,1)S(1)}, u32[]{:S(2)}, u32[]{:S(2)}) collective-permute-start(bf16[4,56,1152]{2,1,0:T(8,128)(2,1)S(1)} %get-tuple-element.72), channel_id=1, source_target_pairs={{0,4},{4,0},{8,12},{12,8},{16,20},{20,16},{24,28},{28,24},{1,5},{5... | collective-permute-start | bytes 1548296 | tf_op jit(solution)/shard_map/ppermute | solution.py:321
  4.4 13.2 %collective-permute-start = (bf16[760,128]{1,0:T(8,128)(2,1)}, bf16[760,128]{1,0:T(8,128)(2,1)S(1)}, u32[]{:S(2)}, u32[]{:S(2)}) collective-permute-start(bf16[760,128]{1,0:T(8,128)(2,1)} %get-tuple-element.53), channel_id=1, source_target_pairs={{0,3},{1,2},{2,1},{3,0},{4,7},{5,6},{6,5},{7,4},{8,11},{9,10},{10,... | collective-permute-start | bytes 583688 | tf_op jit(solution)/shard_map/ppermute | solution.py:321
  9.1 34.5 %copy-start.1 = (bf16[1152,1728]{0,1:T(8,128)(2,1)S(1)}, bf16[1152,1728]{0,1:T(8,128)(2,1)}, u32[]{:S(2)}) copy-start(bf16[1152,1728]{0,1:T(8,128)(2,1)} %param.12) | copy-start | bytes 11943940
  9.2 34.5 %copy-start.2 = (bf16[576,1152]{1,0:T(8,128)(2,1)S(1)}, bf16[576,1152]{1,0:T(8,128)(2,1)}, u32[]{:S(2)}) copy-start(bf16[576,1152]{1,0:T(8,128)(2,1)} %proj.9) | copy-start | bytes 3981316
  9.2 34.5 %copy-start.5 = (f32[6,1152]{1,0:T(8,128)S(1)}, f32[6,1152]{1,0:T(8,128)}, u32[]{:S(2)}) copy-start(f32[6,1152]{1,0:T(8,128)} %modulation.13) | copy-start | bytes 82948
  9.2 22.2 %collective-permute-start.7 = (bf16[2,56,1152]{2,1,0:T(8,128)(2,1)S(1)}, bf16[2,56,1152]{2,1,0:T(8,128)(2,1)S(1)}, u32[]{:S(2)}, u32[]{:S(2)}) collective-permute-start(bf16[2,56,1152]{2,1,0:T(8,128)(2,1)S(1)} %get-tuple-element.74), channel_id=1, source_target_pairs={{0,8},{4,12},{8,0},{12,4},{16,24},{20,28},{24,16},{28,20},{1,9},{5... | collective-permute-start | bytes 774152 | tf_op jit(solution)/shard_map/ppermute | solution.py:321
  10.7 1.1 %copy-start.6 = (bf16[224,1152]{1,0:T(8,128)(2,1)S(1)}, bf16[224,1152]{1,0:T(8,128)(2,1)}, u32[]{:S(2)}) copy-start(bf16[224,1152]{1,0:T(8,128)(2,1)} %get-tuple-element.57.merged) | copy-start | bytes 1548292
  13.6 12.8 %collective-permute-start.1 = (bf16[760,128]{1,0:T(8,128)(2,1)S(1)}, bf16[760,128]{1,0:T(8,128)(2,1)S(1)}, u32[]{:S(2)}, u32[]{:S(2)}) collective-permute-start(bf16[760,128]{1,0:T(8,128)(2,1)S(1)} %get-tuple-element.58), channel_id=1, source_target_pairs={{0,2},{1,3},{2,0},{3,1},{4,6},{5,7},{6,4},{7,5},{8,10},{9,11},{10,... | collective-permute-start | bytes 583688 | tf_op jit(solution)/shard_map/ppermute | solution.py:321
  14.5 11.9 %collective-permute-start.2 = (bf16[760,128]{1,0:T(8,128)(2,1)S(1)}, bf16[760,128]{1,0:T(8,128)(2,1)S(1)}, u32[]{:S(2)}, u32[]{:S(2)}) collective-permute-start(bf16[760,128]{1,0:T(8,128)(2,1)S(1)} %get-tuple-element.59), channel_id=1, source_target_pairs={{0,1},{1,0},{2,3},{3,2},{4,5},{5,4},{6,7},{7,6},{8,9},{9,8},{10,11... | collective-permute-start | bytes 583688 | tf_op jit(solution)/shard_map/ppermute | solution.py:321
  16.1 17.2 %collective-permute-start.8 = (bf16[2,56,1152]{2,1,0:T(8,128)(2,1)S(1)}, bf16[2,56,1152]{2,1,0:T(8,128)(2,1)S(1)}, u32[]{:S(2)}, u32[]{:S(2)}) collective-permute-start(bf16[2,56,1152]{2,1,0:T(8,128)(2,1)S(1)} %get-tuple-element.75), channel_id=1, source_target_pairs={{0,16},{4,20},{8,24},{12,28},{16,0},{20,4},{24,8},{28,12},{1,17},{... | collective-permute-start | bytes 774152 | tf_op jit(solution)/shard_map/ppermute | solution.py:321
  17.6 15.6 %collective-permute-start.9 = (bf16[2,56,1152]{2,1,0:T(8,128)(2,1)S(1)}, bf16[2,56,1152]{2,1,0:T(8,128)(2,1)S(1)}, u32[]{:S(2)}, u32[]{:S(2)}) collective-permute-start(bf16[2,56,1152]{2,1,0:T(8,128)(2,1)S(1)} %get-tuple-element.76), channel_id=1, source_target_pairs={{0,24},{4,28},{8,16},{12,20},{16,8},{20,12},{24,0},{28,4},{1,25},{... | collective-permute-start | bytes 774152 | tf_op jit(solution)/shard_map/ppermute | solution.py:321
  28.8 6.3 %collective-permute-start.3 = (bf16[256,128]{1,0:T(8,128)(2,1)S(1)}, bf16[256,128]{1,0:T(8,128)(2,1)S(1)}, u32[]{:S(2)}, u32[]{:S(2)}) collective-permute-start(bf16[256,128]{1,0:T(8,128)(2,1)S(1)} %get-tuple-element.66), channel_id=1, source_target_pairs={{0,3},{1,2},{2,1},{3,0},{4,7},{5,6},{6,5},{7,4},{8,11},{9,10},{10,... | collective-permute-start | bytes 196616 | tf_op jit(solution)/shard_map/ppermute | solution.py:321
  31.3 5.8 %collective-permute-start.4 = (bf16[256,128]{1,0:T(8,128)(2,1)S(1)}, bf16[256,128]{1,0:T(8,128)(2,1)S(1)}, u32[]{:S(2)}, u32[]{:S(2)}) collective-permute-start(bf16[256,128]{1,0:T(8,128)(2,1)S(1)} %get-tuple-element.67), channel_id=1, source_target_pairs={{0,2},{1,3},{2,0},{3,1},{4,6},{5,7},{6,4},{7,5},{8,10},{9,11},{10,... | collective-permute-start | bytes 196616 | tf_op jit(solution)/shard_map/ppermute | solution.py:321
  31.4 5.8 %collective-permute-start.5 = (bf16[256,128]{1,0:T(8,128)(2,1)S(1)}, bf16[256,128]{1,0:T(8,128)(2,1)S(1)}, u32[]{:S(2)}, u32[]{:S(2)}) collective-permute-start(bf16[256,128]{1,0:T(8,128)(2,1)S(1)} %get-tuple-element.68), channel_id=1, source_target_pairs={{0,1},{1,0},{2,3},{3,2},{4,5},{5,4},{6,7},{7,6},{8,9},{9,8},{10,11... | collective-permute-start | bytes 196616 | tf_op jit(solution)/shard_map/ppermute | solution.py:321
  37.7 2.8 %collective-permute-start.10 = (bf16[3,256,128]{2,1,0:T(8,128)(2,1)S(1)}, bf16[3,256,128]{2,1,0:T(8,128)(2,1)S(1)}, u32[]{:S(2)}, u32[]{:S(2)}) collective-permute-start(bf16[3,256,128]{2,1,0:T(8,128)(2,1)S(1)} %get-tuple-element.84), channel_id=1, source_target_pairs={{0,4},{4,0},{8,12},{12,8},{16,20},{20,16},{24,28},{28,24},{1,5},{5... | collective-permute-start | bytes 589832 | tf_op jit(solution)/shard_map/ppermute | solution.py:321
  37.8 7.8 %collective-permute-start.13 = (bf16[256,128]{1,0:T(8,128)(2,1)S(1)}, bf16[256,128]{1,0:T(8,128)(2,1)S(1)}, u32[]{:S(2)}, u32[]{:S(2)}) collective-permute-start(bf16[256,128]{1,0:T(8,128)(2,1)S(1)} %get-tuple-element.87), channel_id=1, source_target_pairs={{0,24},{4,28},{8,16},{12,20},{16,8},{20,12},{24,0},{28,4},{1,25},{... | collective-permute-start | bytes 196616 | tf_op jit(solution)/shard_map/ppermute | solution.py:321
  40.3 5.3 %collective-permute-start.14 = (bf16[256,128]{1,0:T(8,128)(2,1)S(1)}, bf16[256,128]{1,0:T(8,128)(2,1)S(1)}, u32[]{:S(2)}, u32[]{:S(2)}) collective-permute-start(bf16[256,128]{1,0:T(8,128)(2,1)S(1)} %get-tuple-element.88), channel_id=1, source_target_pairs={{0,28},{4,24},{8,20},{12,16},{16,12},{20,8},{24,4},{28,0},{1,29},{... | collective-permute-start | bytes 196616 | tf_op jit(solution)/shard_map/ppermute | solution.py:321
  40.6 7.2 %collective-permute-start.11 = (bf16[2,256,128]{2,1,0:T(8,128)(2,1)S(1)}, bf16[2,256,128]{2,1,0:T(8,128)(2,1)S(1)}, u32[]{:S(2)}, u32[]{:S(2)}) collective-permute-start(bf16[2,256,128]{2,1,0:T(8,128)(2,1)S(1)} %get-tuple-element.85), channel_id=1, source_target_pairs={{0,16},{4,20},{8,24},{12,28},{16,0},{20,4},{24,8},{28,12},{1,17},{... | collective-permute-start | bytes 393224 | tf_op jit(solution)/shard_map/ppermute | solution.py:321
  42.1 5.6 %collective-permute-start.12 = (bf16[2,256,128]{2,1,0:T(8,128)(2,1)S(1)}, bf16[2,256,128]{2,1,0:T(8,128)(2,1)S(1)}, u32[]{:S(2)}, u32[]{:S(2)}) collective-permute-start(bf16[2,256,128]{2,1,0:T(8,128)(2,1)S(1)} %get-tuple-element.86), channel_id=1, source_target_pairs={{0,8},{4,12},{8,0},{12,4},{16,24},{20,28},{24,16},{28,20},{1,9},{5... | collective-permute-start | bytes 393224 | tf_op jit(solution)/shard_map/ppermute | solution.py:321
  51.3 8.9 %copy-start.4 = (bf16[576,1152]{1,0:T(8,128)(2,1)S(1)}, bf16[576,1152]{1,0:T(8,128)(2,1)}, u32[]{:S(2)}) copy-start(bf16[576,1152]{1,0:T(8,128)(2,1)} %proj.11) | copy-start | bytes 3981316
  51.4 1.6 %collective-permute-start.15 = (bf16[4,256,128]{2,1,0:T(8,128)(2,1)S(1)}, bf16[4,256,128]{2,1,0:T(8,128)(2,1)S(1)}, u32[]{:S(2)}, u32[]{:S(2)}) collective-permute-start(bf16[4,256,128]{2,1,0:T(8,128)(2,1)S(1)} %get-tuple-element.96), channel_id=1, source_target_pairs={{0,4},{4,0},{8,12},{12,8},{16,20},{20,16},{24,28},{28,24},{1,5},{5... | collective-permute-start | bytes 786440 | tf_op jit(solution)/shard_map/ppermute | solution.py:321
  53.0 7.2 %collective-permute-start.18 = (bf16[2,256,128]{2,1,0:T(8,128)(2,1)S(1)}, bf16[2,256,128]{2,1,0:T(8,128)(2,1)S(1)}, u32[]{:S(2)}, u32[]{:S(2)}) collective-permute-start(bf16[2,256,128]{2,1,0:T(8,128)(2,1)S(1)} %get-tuple-element.100), channel_id=1, source_target_pairs={{0,24},{4,28},{8,16},{12,20},{16,8},{20,12},{24,0},{28,4},{1,25},{... | collective-permute-start | bytes 393224 | tf_op jit(solution)/shard_map/ppermute | solution.py:321
  55.1 7.2 %collective-permute-start.16 = (bf16[2,256,128]{2,1,0:T(8,128)(2,1)S(1)}, bf16[2,256,128]{2,1,0:T(8,128)(2,1)S(1)}, u32[]{:S(2)}, u32[]{:S(2)}) collective-permute-start(bf16[2,256,128]{2,1,0:T(8,128)(2,1)S(1)} %get-tuple-element.97), channel_id=1, source_target_pairs={{0,16},{4,20},{8,24},{12,28},{16,0},{20,4},{24,8},{28,12},{1,17},{... | collective-permute-start | bytes 393224 | tf_op jit(solution)/shard_map/ppermute | solution.py:321
  55.8 6.5 %collective-permute-start.17 = (bf16[2,256,128]{2,1,0:T(8,128)(2,1)S(1)}, bf16[2,256,128]{2,1,0:T(8,128)(2,1)S(1)}, u32[]{:S(2)}, u32[]{:S(2)}) collective-permute-start(bf16[2,256,128]{2,1,0:T(8,128)(2,1)S(1)} %get-tuple-element.98), channel_id=1, source_target_pairs={{0,8},{4,12},{8,0},{12,4},{16,24},{20,28},{24,16},{28,20},{1,9},{5... | collective-permute-start | bytes 393224 | tf_op jit(solution)/shard_map/ppermute | solution.py:321

commit v9 on v8

--- a/solution.py
+++ b/solution.py
@@ -262,7 +262,7 @@
 
 def temporal_kernel(n_pair, places, n_parts, order, modulation, proj, weights, *refs):
     tokens, results, before = refs[:n_parts], refs[n_parts : 2 * n_parts], refs[2 * n_parts : n_pair + n_parts]
-    keep, give, normed = refs[n_pair + n_parts :]
+    keep, give, alike, other, normed = refs[n_pair + n_parts :]
     n_frames = 2 * n_pair
     groups = -(-places // SUB)
     inner = proj.shape[0]
@@ -295,7 +295,11 @@
     for i, s in enumerate(order):
         for out, f in ((keep, 2 * i), (give, 2 * i + 1)):
             rows = [whole[g * size + f * SUB : g * size + (f + 1) * SUB] for g in range(groups)]
-            out[s] = pack(jnp.concatenate(rows, 0)[:places]).astype(BF16)
+            block = pack(jnp.concatenate(rows, 0)[:places]).astype(BF16)
+            if s < n_pair - 1:
+                out[s] = block
+            else:
+                (alike if out is keep else other)[...] = block
 
 
 def finish_kernel(taken, places, n_refs, modulation, proj, after, *refs):
@@ -482,9 +486,9 @@
         ]
     mixed = pl.pallas_call(
         functools.partial(temporal_kernel, n_pair, places, len(last), order),
-        out_shape=[struct(n_pair, moved, LANES)] * 2,
+        out_shape=apart,
         in_specs=[VMEM] * (3 + len(last) + n_pair),
-        out_specs=[VMEM] * 2,
+        out_specs=[VMEM] * 4,
         scratch_shapes=[pltpu.VMEM((2 * len(last) * places, width), F32)],
         compiler_params=params(16),
         name="temporal",
@@ -496,7 +500,7 @@
         *[part for s in last for part in attended_parts[s]],
         *before,
     )
-    parts = [[both] for both in exchange(*mixed, n_frames)]
+    parts = exchange_apart(*mixed, n_frames)
     out = None
     for i, step in enumerate(([0, n_pair - 1], list(range(n_pair - 2, 0, -1)))):
         if step:
@@ -512,7 +516,7 @@
                 ],
                 input_output_aliases={3 + len(given): 0} if i else {},
                 compiler_params=params(10),
-                cost_estimate=cost(2 * 2 * places * len(step) * inner * width),
+                cost_estimate=cost((1 + 29 * (1 - i)) * 2 * 2 * places * len(step) * inner * width),
                 name="finish_%d" % i,
             )(modulation, temporal_proj, after, *given, *([out] if i else []))
     return out.reshape(1, rows, width)

time: 63.9 us -> 63.6 us (level)
  waiting for transfers between devices: 15.4 us -> 13.2 us
  starting transfers between devices: 25.5 us -> 27.4 us
    ppermute x19 -> x20, waiting for transfers between devices: 15.4 us -> 13.2 us  [swap(): return lax.ppermute(block, axis, [(i, i ^ mask) for i in range(size)])]
    ppermute x19 -> x20, starting transfers between devices: 25.5 us -> 27.4 us  [swap(): return lax.ppermute(block, axis, [(i, i ^ mask) for i in range(size)])]
  transfers between devices with their start and end apart: 19 -> 20, of which waited for: 7 -> 7; matrix products, arithmetic and copies ran while one was open for 0% -> 0% of each run, Pallas kernels for 19% -> 19%
where the time goes in v9:
time: 63.6 us; the launch traced here: 63.4 us
  starting transfers between devices  27.4 us (43%)
  Pallas kernels  21.5 us (34%)
  waiting for transfers between devices  13.2 us (21%)
  local copies, waits for them, and re-layouts  1.09 us (2%)
    ppermute x20, starting transfers between devices, swap(): return lax.ppermute(block, axis, [(i, i ^ mask) for i in range(size)])  27.4 us
    ppermute x20, waiting for transfers between devices, swap(): return lax.ppermute(block, axis, [(i, i ^ mask) for i in range(size)])  13.2 us
    pallas_call x2, Pallas kernels, shards(): pl.pallas_call(functools.partial(project_kernel, places, len(step)), out_...  3.82 us
    pallas_call x1, Pallas kernels, shards(): pl.pallas_call(functools.partial(merge_kernel, n_space), out_shape=[struc...  3.74 us
    pallas_call x1, Pallas kernels, shards(): pl.pallas_call(functools.partial(temporal_kernel, n_pair, places, len(las...  3.55 us
    pallas_call x2, Pallas kernels, shards(): pl.pallas_call(functools.partial(finish_kernel, step, places, len(given))...  2.84 us
    pallas_call x1, Pallas kernels, shards(): pl.pallas_call(functools.partial(others_kernel, n_space, slots, wide), ou...  2.4 us
    pallas_call x1, Pallas kernels, shards(): pl.pallas_call(functools.partial(spread_kernel, n_space), out_shape=[stru...  1.83 us
  transfers between devices with their start and end apart: 20, of which 7 were waited for; matrix products, arithmetic and copies ran while one was open for 0% of the time, Pallas kernels for 19%

profile of v9, /device:TPU:0, one launch (start us, length us, event | category | flops | bytes accessed | tf_op | source)
XLA Modules:
  0.0 63.4 jit_solution(2904647244894606806)
XLA Ops:
  0.0 3.7 %merge.1 = (bf16[760,128]{1,0:T(8,128)(2,1)}, bf16[224,1152]{1,0:T(8,128)(2,1)}) custom-call(bf16[8,56,1152]{2,1,0:T(8,128)(2,1)} %bitcast.9, s32[1,448]{1,0:T(1,128)} %slot.3, f32[6,1152]{1,0:T(8,128)} %modulation.13, bf16[1728,1152]{1,0:T(8,128)(2,1)} %bitcast.4), custom_call_target="tpu_custom_call" | custom-call | tf_op jit(solution)/shard_map/merge/pallas_call | solution.py:365
  3.8 0.0 copy-start.7
  3.8 0.0 copy-done.3
  3.8 0.1 share.1
  3.9 0.5 collective-permute-start.6
  4.4 4.7 %collective-permute-start = (bf16[760,128]{1,0:T(8,128)(2,1)}, bf16[760,128]{1,0:T(8,128)(2,1)S(1)}, u32[]{:S(2)}, u32[]{:S(2)}) collective-permute-start(bf16[760,128]{1,0:T(8,128)(2,1)} %get-tuple-element.54), channel_id=1, source_target_pairs={{0,3},{1,2},{2,1},{3,0},{4,7},{5,6},{6,5},{7,4},{8,11},{9,10},{10,... | collective-permute-start | bytes 583688 | tf_op jit(solution)/shard_map/ppermute | solution.py:325
  9.1 0.0 collective-permute-done.6.got
  9.1 0.1 pair.3
  9.1 0.0 copy-start.1
  9.2 0.0 copy-start.2
  9.2 0.0 copy-start.5
  9.2 1.6 %collective-permute-start.7 = (bf16[2,56,1152]{2,1,0:T(8,128)(2,1)S(1)}, bf16[2,56,1152]{2,1,0:T(8,128)(2,1)S(1)}, u32[]{:S(2)}, u32[]{:S(2)}) collective-permute-start(bf16[2,56,1152]{2,1,0:T(8,128)(2,1)S(1)} %get-tuple-element.75), channel_id=1, source_target_pairs={{0,8},{4,12},{8,0},{12,4},{16,24},{20,28},{24,16},{28,20},{1,9},{5... | collective-permute-start | bytes 774152 | tf_op jit(solution)/shard_map/ppermute | solution.py:325
  10.7 0.0 copy-done
  10.7 1.0 %copy-done.6 = bf16[224,1152]{1,0:T(8,128)(2,1)S(1)} copy-done((bf16[224,1152]{1,0:T(8,128)(2,1)S(1)}, bf16[224,1152]{1,0:T(8,128)(2,1)}, u32[]{:S(2)}) %copy-start.6) | copy-done | bytes 516120
  11.8 1.8 %spread.1 = (bf16[760,128]{1,0:T(8,128)(2,1)S(1)}, bf16[760,128]{1,0:T(8,128)(2,1)S(1)}, bf16[760,128]{1,0:T(8,128)(2,1)S(1)}) custom-call(bf16[224,1152]{1,0:T(8,128)(2,1)S(1)} %copy-done.6, bf16[1728,1152]{1,0:T(8,128)(2,1)S(1)} %bitcast.5), custom_call_target="tpu_custom_call" | custom-call | flops 891813888 | bytes 8918138 | tf_op jit(solution)/shard_map/spread/pallas_call | solution.py:380
  13.6 0.9 %collective-permute-start.1 = (bf16[760,128]{1,0:T(8,128)(2,1)S(1)}, bf16[760,128]{1,0:T(8,128)(2,1)S(1)}, u32[]{:S(2)}, u32[]{:S(2)}) collective-permute-start(bf16[760,128]{1,0:T(8,128)(2,1)S(1)} %get-tuple-element.59), channel_id=1, source_target_pairs={{0,2},{1,3},{2,0},{3,1},{4,6},{5,7},{6,4},{7,5},{8,10},{9,11},{10,... | collective-permute-start | bytes 583688 | tf_op jit(solution)/shard_map/ppermute | solution.py:325
  14.5 1.6 %collective-permute-start.2 = (bf16[760,128]{1,0:T(8,128)(2,1)S(1)}, bf16[760,128]{1,0:T(8,128)(2,1)S(1)}, u32[]{:S(2)}, u32[]{:S(2)}) collective-permute-start(bf16[760,128]{1,0:T(8,128)(2,1)S(1)} %get-tuple-element.60), channel_id=1, source_target_pairs={{0,1},{1,0},{2,3},{3,2},{4,5},{5,4},{6,7},{7,6},{8,9},{9,8},{10,11... | collective-permute-start | bytes 583688 | tf_op jit(solution)/shard_map/ppermute | solution.py:325
  16.1 1.5 %collective-permute-start.8 = (bf16[2,56,1152]{2,1,0:T(8,128)(2,1)S(1)}, bf16[2,56,1152]{2,1,0:T(8,128)(2,1)S(1)}, u32[]{:S(2)}, u32[]{:S(2)}) collective-permute-start(bf16[2,56,1152]{2,1,0:T(8,128)(2,1)S(1)} %get-tuple-element.76), channel_id=1, source_target_pairs={{0,16},{4,20},{8,24},{12,28},{16,0},{20,4},{24,8},{28,12},{1,17},{... | collective-permute-start | bytes 774152 | tf_op jit(solution)/shard_map/ppermute | solution.py:325
  17.6 0.0 collective-permute-done.packed
  17.6 0.8 %collective-permute-start.9 = (bf16[2,56,1152]{2,1,0:T(8,128)(2,1)S(1)}, bf16[2,56,1152]{2,1,0:T(8,128)(2,1)S(1)}, u32[]{:S(2)}, u32[]{:S(2)}) collective-permute-start(bf16[2,56,1152]{2,1,0:T(8,128)(2,1)S(1)} %get-tuple-element.77), channel_id=1, source_target_pairs={{0,24},{4,28},{8,16},{12,20},{16,8},{20,12},{24,0},{28,4},{1,25},{... | collective-permute-start | bytes 774152 | tf_op jit(solution)/shard_map/ppermute | solution.py:325
  18.4 0.0 copy-done.7
  18.4 0.3 prepare.1
  18.7 7.7 %collective-permute-done.1.refs_0_ = bf16[760,128]{1,0:T(8,128)(2,1)S(1)} collective-permute-done((bf16[760,128]{1,0:T(8,128)(2,1)S(1)}, bf16[760,128]{1,0:T(8,128)(2,1)S(1)}, u32[]{:S(2)}, u32[]{:S(2)}) %collective-permute-start.1) | collective-permute-done | bytes 194592 | tf_op jit(solution)/shard_map/ppermute | solution.py:325
  26.4 0.0 collective-permute-done.2.refs_1_
  26.4 2.4 %attend_others.1 = (bf16[256,128]{1,0:T(8,128)(2,1)S(1)}, bf16[256,128]{1,0:T(8,128)(2,1)S(1)}, bf16[256,128]{1,0:T(8,128)(2,1)S(1)}, bf16[144,224]{1,0:T(8,128)...) custom-call(bf16[224,144]{1,0:T(8,128)(2,1)S(1)} %get-tuple-element.62.far_keys, ...), custom_call_target="tpu_custom_call" | custom-call | flops 346816512 | bytes 3468165 | tf_op jit(solution)/shard_map/attend_others/pallas_call | solution.py:419
  28.8 2.5 %collective-permute-start.3 = (bf16[256,128]{1,0:T(8,128)(2,1)S(1)}, bf16[256,128]{1,0:T(8,128)(2,1)S(1)}, u32[]{:S(2)}, u32[]{:S(2)}) collective-permute-start(bf16[256,128]{1,0:T(8,128)(2,1)S(1)} %get-tuple-element.67), channel_id=1, source_target_pairs={{0,3},{1,2},{2,1},{3,0},{4,7},{5,6},{6,5},{7,4},{8,11},{9,10},{10,... | collective-permute-start | bytes 196616 | tf_op jit(solution)/shard_map/ppermute | solution.py:325
  31.3 0.0 collective-permute-start.4
  31.3 0.0 collective-permute-done.7.refs_1_
  31.3 1.9 %collective-permute-start.5 = (bf16[256,128]{1,0:T(8,128)(2,1)S(1)}, bf16[256,128]{1,0:T(8,128)(2,1)S(1)}, u32[]{:S(2)}, u32[]{:S(2)}) collective-permute-start(bf16[256,128]{1,0:T(8,128)(2,1)S(1)} %get-tuple-element.69), channel_id=1, source_target_pairs={{0,1},{1,0},{2,3},{3,2},{4,5},{5,4},{6,7},{7,6},{8,9},{9,8},{10,11... | collective-permute-start | bytes 196616 | tf_op jit(solution)/shard_map/ppermute | solution.py:325
  33.3 0.0 collective-permute-done.8.refs_0_
  33.3 0.0 collective-permute-done.9.refs_0_
  33.3 1.3 %attend_own.1.refs_3_ = bf16[144,224]{1,0:T(8,128)(2,1)S(1)} custom-call(bf16[144,224]{1,0:T(8,128)(2,1)S(1)} %get-tuple-element.78.queries, bf16[896,144]{1,0:T(8,128)(2,1)S(1)} %get-tuple-element.79.keys, bf16[144,896]{1,0:T(8,128)(2,1)S(1)} %get-tuple-element.80.vals), custom_call_target="tpu_custom_call" | custom-call | flops 115605504 | bytes 1156055 | tf_op jit(solution)/shard_map/attend_own/pallas_call | solution.py:430
  34.6 0.5 collective-permute-done.3.refs_0_
  35.1 2.0 %collective-permute-done.4.refs_1_ = bf16[256,128]{1,0:T(8,128)(2,1)S(1)} collective-permute-done((bf16[256,128]{1,0:T(8,128)(2,1)S(1)}, bf16[256,128]{1,0:T(8,128)(2,1)S(1)}, u32[]{:S(2)}, u32[]{:S(2)}) %collective-permute-start.4) | collective-permute-done | bytes 65568 | tf_op jit(solution)/shard_map/ppermute | solution.py:325
  37.1 0.0 collective-permute-done.5.refs_2_
  37.1 0.5 expand.1
  37.7 0.1 collective-permute-start.10
  37.8 2.5 %collective-permute-start.13 = (bf16[256,128]{1,0:T(8,128)(2,1)S(1)}, bf16[256,128]{1,0:T(8,128)(2,1)S(1)}, u32[]{:S(2)}, u32[]{:S(2)}) collective-permute-start(bf16[256,128]{1,0:T(8,128)(2,1)S(1)} %get-tuple-element.88), channel_id=1, source_target_pairs={{0,24},{4,28},{8,16},{12,20},{16,8},{20,12},{24,0},{28,4},{1,25},{... | collective-permute-start | bytes 196616 | tf_op jit(solution)/shard_map/ppermute | solution.py:325
  40.3 0.2 collective-permute-start.14
  40.5 0.0 collective-permute-done.10.got
  40.6 1.6 %collective-permute-start.11 = (bf16[2,256,128]{2,1,0:T(8,128)(2,1)S(1)}, bf16[2,256,128]{2,1,0:T(8,128)(2,1)S(1)}, u32[]{:S(2)}, u32[]{:S(2)}) collective-permute-start(bf16[2,256,128]{2,1,0:T(8,128)(2,1)S(1)} %get-tuple-element.86), channel_id=1, source_target_pairs={{0,16},{4,20},{8,24},{12,28},{16,0},{20,4},{24,8},{28,12},{1,17},{... | collective-permute-start | bytes 393224 | tf_op jit(solution)/shard_map/ppermute | solution.py:325
  42.1 1.5 %collective-permute-start.12 = (bf16[2,256,128]{2,1,0:T(8,128)(2,1)S(1)}, bf16[2,256,128]{2,1,0:T(8,128)(2,1)S(1)}, u32[]{:S(2)}, u32[]{:S(2)}) collective-permute-start(bf16[2,256,128]{2,1,0:T(8,128)(2,1)S(1)} %get-tuple-element.87), channel_id=1, source_target_pairs={{0,8},{4,12},{8,0},{12,4},{16,24},{20,28},{24,16},{28,20},{1,9},{5... | collective-permute-start | bytes 393224 | tf_op jit(solution)/shard_map/ppermute | solution.py:325
  43.6 0.0 copy-done.2
  43.6 1.9 %project_0.1.refs_4_ = bf16[2,64,1728]{2,1,0:T(8,128)(2,1)S(1)} custom-call(f32[6,1152]{1,0:T(8,128)S(1)} %copy-done.5, bf16[576,1152]{1,0:T(8,128)(2,1)S(1)} %copy-done.2, bf16[1728,1152]{1,0:T(8,128)(2,1)S(1)} %bitcast.6, bf16[2,56,1152]{2,1,0:T(8,128)(2,1)S(1)} %get-tuple-element.90.refs_0_, bf16[2,256,128]{2,1,0:T(8,128)(2,1)S(1)} %get-tuple-element.91.refs_1_), custom_call_target="tpu_custom_call" | custom-call | flops 445906944 | bytes 4459069 | tf_op jit(solution)/shard_map/project_0/pallas_call | solution.py:470
  45.6 0.0 collective-permute-done.13.refs_1_
  45.6 0.0 collective-permute-done.14.refs_2_
  45.6 1.9 %project_1.1.refs_5_ = bf16[2,64,1728]{2,1,0:T(8,128)(2,1)S(1)} custom-call(f32[6,1152]{1,0:T(8,128)S(1)} %copy-done.5, bf16[576,1152]{1,0:T(8,128)(2,1)S(1)} %copy-done.2, bf16[1728,1152]{1,0:T(8,128)(2,1)S(1)} %bitcast.7, bf16[2,56,1152]{2,1,0:T(8,128)(2,1)S(1)} %collective-permute-done.9.refs_0_, bf16[256,128]{1,0:T(8,128)(2,1)S(1)} %collective-permute-done.13.refs_1_, ...), custom_call_target="tpu_custom_call" | custom-call | flops 4459069440 | bytes 44590696 | tf_op jit(solution)/shard_map/project_1/pallas_call | solution.py:470
  47.5 0.3 collective-permute-done.11.refs_2_
  47.8 0.0 collective-permute-done.12.refs_3_
  47.8 3.6 %temporal.1 = (bf16[3,256,128]{2,1,0:T(8,128)(2,1)S(1)}, bf16[3,256,128]{2,1,0:T(8,128)(2,1)S(1)}, bf16[256,128]{1,0:T(8,128)(2,1)S(1)}, bf16[256,128]{1,0:T(8,128)(2,1)S(1)}) custom-call(f32[6,1152]{1,0:T(8,128)S(1)} %copy-done.5, bf16[576,1152]{1,0:T(8,128)(2,1)S(1)} %copy-done.2, bf16[1728,1152]{1,0:T(8,128)(2,1)S(1)} %bitcast.8, ...), custom_call_target="tpu_custom_call" | custom-call | tf_op jit(solution)/shard_map/temporal/pallas_call | solution.py:487
  51.3 0.0 copy-start.4
  51.3 0.1 collective-permute-start.15
  51.4 2.1 %collective-permute-start.18 = (bf16[256,128]{1,0:T(8,128)(2,1)S(1)}, bf16[256,128]{1,0:T(8,128)(2,1)S(1)}, u32[]{:S(2)}, u32[]{:S(2)}) collective-permute-start(bf16[256,128]{1,0:T(8,128)(2,1)S(1)} %get-tuple-element.101), channel_id=1, source_target_pairs={{0,24},{4,28},{8,16},{12,20},{16,8},{20,12},{24,0},{28,4},{1,25},{... | collective-permute-start | bytes 196616 | tf_op jit(solution)/shard_map/ppermute | solution.py:325
  53.6 0.6 collective-permute-start.19
  54.2 1.0 %residual.1.after = bf16[8,56,1152]{2,1,0:T(8,128)(2,1)S(1)} custom-call(bf16[576,224]{1,0:T(8,128)(2,1)S(1)} %get-tuple-element.81.attended, f32[8,56,224]{2,1,0:T(8,128)S(1)} %get-tuple-element.55.chosen, bf16[8,56,1152]{2,1,0:T(8,128)(2,1)S(1)} %bitcast.11, f32[6,1152]{1,0:T(8,128)S(1)} %copy-done.5, bf16[576,1152]{1,0:T(8,128)(2,1)S(1)} %copy-done.2), custom_call_target="tpu_custom_call" | custom-call | flops 594542592 | bytes 5945425 | tf_op jit(solution)/shard_map/residual/pallas_call | solution.py:451
  55.2 0.0 collective-permute-done.15.got
  55.2 1.3 %collective-permute-start.16 = (bf16[2,256,128]{2,1,0:T(8,128)(2,1)S(1)}, bf16[2,256,128]{2,1,0:T(8,128)(2,1)S(1)}, u32[]{:S(2)}, u32[]{:S(2)}) collective-permute-start(bf16[2,256,128]{2,1,0:T(8,128)(2,1)S(1)} %get-tuple-element.98), channel_id=1, source_target_pairs={{0,16},{4,20},{8,24},{12,28},{16,0},{20,4},{24,8},{28,12},{1,17},{... | collective-permute-start | bytes 393224 | tf_op jit(solution)/shard_map/ppermute | solution.py:325
  56.5 1.4 %collective-permute-start.17 = (bf16[2,256,128]{2,1,0:T(8,128)(2,1)S(1)}, bf16[2,256,128]{2,1,0:T(8,128)(2,1)S(1)}, u32[]{:S(2)}, u32[]{:S(2)}) collective-permute-start(bf16[2,256,128]{2,1,0:T(8,128)(2,1)S(1)} %get-tuple-element.99), channel_id=1, source_target_pairs={{0,8},{4,12},{8,0},{12,4},{16,24},{20,28},{24,16},{28,20},{1,9},{5... | collective-permute-start | bytes 393224 | tf_op jit(solution)/shard_map/ppermute | solution.py:325
  57.9 0.0 collective-permute-done.18.refs_1_
  57.9 0.6 collective-permute-done.19.refs_2_
  58.5 1.4 %finish_0.1.refs_2_ = bf16[8,56,1152]{2,1,0:T(8,128)(2,1)} custom-call(f32[6,1152]{1,0:T(8,128)S(1)} %copy-done.5, bf16[576,1152]{1,0:T(8,128)(2,1)S(1)} %copy-done.4, bf16[8,56,1152]{2,1,0:T(8,128)(2,1)S(1)} %residual.1.after, bf16[2,256,128]{2,1,0:T(8,128)(2,1)S(1)} %get-tuple-element.100.refs_0_, bf16[256,128]{1,0:T(8,128)(2,1)S(1)} %collective-permute-done.18.refs_1_, ...), custom_call_target="tpu_custom_call" | custom-call | flops 8918138880 | bytes 89181392 | tf_op jit(solution)/shard_map/finish_0/pallas_call | solution.py:508
  60.0 1.7 %collective-permute-done.16.refs_0_ = bf16[2,256,128]{2,1,0:T(8,128)(2,1)S(1)} collective-permute-done((bf16[2,256,128]{2,1,0:T(8,128)(2,1)S(1)}, bf16[2,256,128]{2,1,0:T(8,128)(2,1)S(1)}, u32[]{:S(2)}, u32[]{:S(2)}) %collective-permute-start.16) | collective-permute-done | bytes 131104 | tf_op jit(solution)/shard_map/ppermute | solution.py:325
  61.7 0.3 collective-permute-done.17.refs_1_
  62.0 1.4 %finish_1.1 = bf16[8,56,1152]{2,1,0:T(8,128)(2,1)} custom-call(f32[6,1152]{1,0:T(8,128)S(1)} %copy-done.5, bf16[576,1152]{1,0:T(8,128)(2,1)S(1)} %copy-done.4, bf16[8,56,1152]{2,1,0:T(8,128)(2,1)S(1)} %residual.1.after, bf16[2,256,128]{2,1,0:T(8,128)(2,1)S(1)} %collective-permute-done.16.refs_0_, ...), custom_call_target="tpu_custom_call", output_to_operand_aliasing={{}: (5, {})} | custom-call | flops 297271296 | bytes 2972712 | tf_op jit(solution)/shard_map/finish_1/pallas_call | solution.py:508
  (8 shorter events, 0.1 us)
Async XLA Ops:
  0.0 10.7 %copy-start = (bf16[1152,1728]{0,1:T(8,128)(2,1)S(1)}, bf16[1152,1728]{0,1:T(8,128)(2,1)}, u32[]{:S(2)}) copy-start(bf16[1152,1728]{0,1:T(8,128)(2,1)} %param.10) | copy-start | bytes 11943940
  0.0 3.8 %copy-start.3 = (bf16[1,448,1152]{2,1,0:T(8,128)(2,1)S(1)}, bf16[1,448,1152]{2,1,0:T(8,128)(2,1)}, u32[]{:S(2)}) copy-start(bf16[1,448,1152]{2,1,0:T(8,128)(2,1)} %param.7) | copy-start | bytes 3096580
  3.8 14.6 %copy-start.7 = (s32[1,448]{1,0:T(1,128)S(1)}, s32[1,448]{1,0:T(1,128)}, u32[]{:S(2)}) copy-start(s32[1,448]{1,0:T(1,128)} %slot.3) | copy-start | bytes 5380
  3.9 5.2 %collective-permute-start.6 = (bf16[4,56,1152]{2,1,0:T(8,128)(2,1)S(1)}, bf16[4,56,1152]{2,1,0:T(8,128)(2,1)S(1)}, u32[]{:S(2)}, u32[]{:S(2)}) collective-permute-start(bf16[4,56,1152]{2,1,0:T(8,128)(2,1)S(1)} %get-tuple-element.73), channel_id=1, source_target_pairs={{0,4},{4,0},{8,12},{12,8},{16,20},{20,16},{24,28},{28,24},{1,5},{5... | collective-permute-start | bytes 1548296 | tf_op jit(solution)/shard_map/ppermute | solution.py:325
  4.4 13.2 %collective-permute-start = (bf16[760,128]{1,0:T(8,128)(2,1)}, bf16[760,128]{1,0:T(8,128)(2,1)S(1)}, u32[]{:S(2)}, u32[]{:S(2)}) collective-permute-start(bf16[760,128]{1,0:T(8,128)(2,1)} %get-tuple-element.54), channel_id=1, source_target_pairs={{0,3},{1,2},{2,1},{3,0},{4,7},{5,6},{6,5},{7,4},{8,11},{9,10},{10,... | collective-permute-start | bytes 583688 | tf_op jit(solution)/shard_map/ppermute | solution.py:325
  9.1 34.5 %copy-start.1 = (bf16[1152,1728]{0,1:T(8,128)(2,1)S(1)}, bf16[1152,1728]{0,1:T(8,128)(2,1)}, u32[]{:S(2)}) copy-start(bf16[1152,1728]{0,1:T(8,128)(2,1)} %param.12) | copy-start | bytes 11943940
  9.2 34.5 %copy-start.2 = (bf16[576,1152]{1,0:T(8,128)(2,1)S(1)}, bf16[576,1152]{1,0:T(8,128)(2,1)}, u32[]{:S(2)}) copy-start(bf16[576,1152]{1,0:T(8,128)(2,1)} %proj.9) | copy-start | bytes 3981316
  9.2 34.5 %copy-start.5 = (f32[6,1152]{1,0:T(8,128)S(1)}, f32[6,1152]{1,0:T(8,128)}, u32[]{:S(2)}) copy-start(f32[6,1152]{1,0:T(8,128)} %modulation.13) | copy-start | bytes 82948
  9.2 22.2 %collective-permute-start.7 = (bf16[2,56,1152]{2,1,0:T(8,128)(2,1)S(1)}, bf16[2,56,1152]{2,1,0:T(8,128)(2,1)S(1)}, u32[]{:S(2)}, u32[]{:S(2)}) collective-permute-start(bf16[2,56,1152]{2,1,0:T(8,128)(2,1)S(1)} %get-tuple-element.75), channel_id=1, source_target_pairs={{0,8},{4,12},{8,0},{12,4},{16,24},{20,28},{24,16},{28,20},{1,9},{5... | collective-permute-start | bytes 774152 | tf_op jit(solution)/shard_map/ppermute | solution.py:325
  10.7 1.1 %copy-start.6 = (bf16[224,1152]{1,0:T(8,128)(2,1)S(1)}, bf16[224,1152]{1,0:T(8,128)(2,1)}, u32[]{:S(2)}) copy-start(bf16[224,1152]{1,0:T(8,128)(2,1)} %get-tuple-element.58.merged) | copy-start | bytes 1548292
  13.6 12.8 %collective-permute-start.1 = (bf16[760,128]{1,0:T(8,128)(2,1)S(1)}, bf16[760,128]{1,0:T(8,128)(2,1)S(1)}, u32[]{:S(2)}, u32[]{:S(2)}) collective-permute-start(bf16[760,128]{1,0:T(8,128)(2,1)S(1)} %get-tuple-element.59), channel_id=1, source_target_pairs={{0,2},{1,3},{2,0},{3,1},{4,6},{5,7},{6,4},{7,5},{8,10},{9,11},{10,... | collective-permute-start | bytes 583688 | tf_op jit(solution)/shard_map/ppermute | solution.py:325
  14.5 11.9 %collective-permute-start.2 = (bf16[760,128]{1,0:T(8,128)(2,1)S(1)}, bf16[760,128]{1,0:T(8,128)(2,1)S(1)}, u32[]{:S(2)}, u32[]{:S(2)}) collective-permute-start(bf16[760,128]{1,0:T(8,128)(2,1)S(1)} %get-tuple-element.60), channel_id=1, source_target_pairs={{0,1},{1,0},{2,3},{3,2},{4,5},{5,4},{6,7},{7,6},{8,9},{9,8},{10,11... | collective-permute-start | bytes 583688 | tf_op jit(solution)/shard_map/ppermute | solution.py:325
  16.1 17.2 %collective-permute-start.8 = (bf16[2,56,1152]{2,1,0:T(8,128)(2,1)S(1)}, bf16[2,56,1152]{2,1,0:T(8,128)(2,1)S(1)}, u32[]{:S(2)}, u32[]{:S(2)}) collective-permute-start(bf16[2,56,1152]{2,1,0:T(8,128)(2,1)S(1)} %get-tuple-element.76), channel_id=1, source_target_pairs={{0,16},{4,20},{8,24},{12,28},{16,0},{20,4},{24,8},{28,12},{1,17},{... | collective-permute-start | bytes 774152 | tf_op jit(solution)/shard_map/ppermute | solution.py:325
  17.6 15.6 %collective-permute-start.9 = (bf16[2,56,1152]{2,1,0:T(8,128)(2,1)S(1)}, bf16[2,56,1152]{2,1,0:T(8,128)(2,1)S(1)}, u32[]{:S(2)}, u32[]{:S(2)}) collective-permute-start(bf16[2,56,1152]{2,1,0:T(8,128)(2,1)S(1)} %get-tuple-element.77), channel_id=1, source_target_pairs={{0,24},{4,28},{8,16},{12,20},{16,8},{20,12},{24,0},{28,4},{1,25},{... | collective-permute-start | bytes 774152 | tf_op jit(solution)/shard_map/ppermute | solution.py:325
  28.8 6.3 %collective-permute-start.3 = (bf16[256,128]{1,0:T(8,128)(2,1)S(1)}, bf16[256,128]{1,0:T(8,128)(2,1)S(1)}, u32[]{:S(2)}, u32[]{:S(2)}) collective-permute-start(bf16[256,128]{1,0:T(8,128)(2,1)S(1)} %get-tuple-element.67), channel_id=1, source_target_pairs={{0,3},{1,2},{2,1},{3,0},{4,7},{5,6},{6,5},{7,4},{8,11},{9,10},{10,... | collective-permute-start | bytes 196616 | tf_op jit(solution)/shard_map/ppermute | solution.py:325
  31.3 5.8 %collective-permute-start.4 = (bf16[256,128]{1,0:T(8,128)(2,1)S(1)}, bf16[256,128]{1,0:T(8,128)(2,1)S(1)}, u32[]{:S(2)}, u32[]{:S(2)}) collective-permute-start(bf16[256,128]{1,0:T(8,128)(2,1)S(1)} %get-tuple-element.68), channel_id=1, source_target_pairs={{0,2},{1,3},{2,0},{3,1},{4,6},{5,7},{6,4},{7,5},{8,10},{9,11},{10,... | collective-permute-start | bytes 196616 | tf_op jit(solution)/shard_map/ppermute | solution.py:325
  31.3 5.8 %collective-permute-start.5 = (bf16[256,128]{1,0:T(8,128)(2,1)S(1)}, bf16[256,128]{1,0:T(8,128)(2,1)S(1)}, u32[]{:S(2)}, u32[]{:S(2)}) collective-permute-start(bf16[256,128]{1,0:T(8,128)(2,1)S(1)} %get-tuple-element.69), channel_id=1, source_target_pairs={{0,1},{1,0},{2,3},{3,2},{4,5},{5,4},{6,7},{7,6},{8,9},{9,8},{10,11... | collective-permute-start | bytes 196616 | tf_op jit(solution)/shard_map/ppermute | solution.py:325
  37.7 2.8 %collective-permute-start.10 = (bf16[3,256,128]{2,1,0:T(8,128)(2,1)S(1)}, bf16[3,256,128]{2,1,0:T(8,128)(2,1)S(1)}, u32[]{:S(2)}, u32[]{:S(2)}) collective-permute-start(bf16[3,256,128]{2,1,0:T(8,128)(2,1)S(1)} %get-tuple-element.85), channel_id=1, source_target_pairs={{0,4},{4,0},{8,12},{12,8},{16,20},{20,16},{24,28},{28,24},{1,5},{5... | collective-permute-start | bytes 589832 | tf_op jit(solution)/shard_map/ppermute | solution.py:325
  37.8 7.8 %collective-permute-start.13 = (bf16[256,128]{1,0:T(8,128)(2,1)S(1)}, bf16[256,128]{1,0:T(8,128)(2,1)S(1)}, u32[]{:S(2)}, u32[]{:S(2)}) collective-permute-start(bf16[256,128]{1,0:T(8,128)(2,1)S(1)} %get-tuple-element.88), channel_id=1, source_target_pairs={{0,24},{4,28},{8,16},{12,20},{16,8},{20,12},{24,0},{28,4},{1,25},{... | collective-permute-start | bytes 196616 | tf_op jit(solution)/shard_map/ppermute | solution.py:325
  40.3 5.3 %collective-permute-start.14 = (bf16[256,128]{1,0:T(8,128)(2,1)S(1)}, bf16[256,128]{1,0:T(8,128)(2,1)S(1)}, u32[]{:S(2)}, u32[]{:S(2)}) collective-permute-start(bf16[256,128]{1,0:T(8,128)(2,1)S(1)} %get-tuple-element.89), channel_id=1, source_target_pairs={{0,28},{4,24},{8,20},{12,16},{16,12},{20,8},{24,4},{28,0},{1,29},{... | collective-permute-start | bytes 196616 | tf_op jit(solution)/shard_map/ppermute | solution.py:325
  40.6 7.2 %collective-permute-start.11 = (bf16[2,256,128]{2,1,0:T(8,128)(2,1)S(1)}, bf16[2,256,128]{2,1,0:T(8,128)(2,1)S(1)}, u32[]{:S(2)}, u32[]{:S(2)}) collective-permute-start(bf16[2,256,128]{2,1,0:T(8,128)(2,1)S(1)} %get-tuple-element.86), channel_id=1, source_target_pairs={{0,16},{4,20},{8,24},{12,28},{16,0},{20,4},{24,8},{28,12},{1,17},{... | collective-permute-start | bytes 393224 | tf_op jit(solution)/shard_map/ppermute | solution.py:325
  42.1 5.6 %collective-permute-start.12 = (bf16[2,256,128]{2,1,0:T(8,128)(2,1)S(1)}, bf16[2,256,128]{2,1,0:T(8,128)(2,1)S(1)}, u32[]{:S(2)}, u32[]{:S(2)}) collective-permute-start(bf16[2,256,128]{2,1,0:T(8,128)(2,1)S(1)} %get-tuple-element.87), channel_id=1, source_target_pairs={{0,8},{4,12},{8,0},{12,4},{16,24},{20,28},{24,16},{28,20},{1,9},{5... | collective-permute-start | bytes 393224 | tf_op jit(solution)/shard_map/ppermute | solution.py:325
  51.3 7.2 %copy-start.4 = (bf16[576,1152]{1,0:T(8,128)(2,1)S(1)}, bf16[576,1152]{1,0:T(8,128)(2,1)}, u32[]{:S(2)}) copy-start(bf16[576,1152]{1,0:T(8,128)(2,1)} %proj.11) | copy-start | bytes 3981316
  51.3 3.8 %collective-permute-start.15 = (bf16[3,256,128]{2,1,0:T(8,128)(2,1)S(1)}, bf16[3,256,128]{2,1,0:T(8,128)(2,1)S(1)}, u32[]{:S(2)}, u32[]{:S(2)}) collective-permute-start(bf16[3,256,128]{2,1,0:T(8,128)(2,1)S(1)} %get-tuple-element.97), channel_id=1, source_target_pairs={{0,4},{4,0},{8,12},{12,8},{16,20},{20,16},{24,28},{28,24},{1,5},{5... | collective-permute-start | bytes 589832 | tf_op jit(solution)/shard_map/ppermute | solution.py:325
  51.4 6.5 %collective-permute-start.18 = (bf16[256,128]{1,0:T(8,128)(2,1)S(1)}, bf16[256,128]{1,0:T(8,128)(2,1)S(1)}, u32[]{:S(2)}, u32[]{:S(2)}) collective-permute-start(bf16[256,128]{1,0:T(8,128)(2,1)S(1)} %get-tuple-element.101), channel_id=1, source_target_pairs={{0,24},{4,28},{8,16},{12,20},{16,8},{20,12},{24,0},{28,4},{1,25},{... | collective-permute-start | bytes 196616 | tf_op jit(solution)/shard_map/ppermute | solution.py:325
  53.6 5.0 %collective-permute-start.19 = (bf16[256,128]{1,0:T(8,128)(2,1)S(1)}, bf16[256,128]{1,0:T(8,128)(2,1)S(1)}, u32[]{:S(2)}, u32[]{:S(2)}) collective-permute-start(bf16[256,128]{1,0:T(8,128)(2,1)S(1)} %get-tuple-element.102), channel_id=1, source_target_pairs={{0,28},{4,24},{8,20},{12,16},{16,12},{20,8},{24,4},{28,0},{1,29},{... | collective-permute-start | bytes 196616 | tf_op jit(solution)/shard_map/ppermute | solution.py:325
  55.2 6.4 %collective-permute-start.16 = (bf16[2,256,128]{2,1,0:T(8,128)(2,1)S(1)}, bf16[2,256,128]{2,1,0:T(8,128)(2,1)S(1)}, u32[]{:S(2)}, u32[]{:S(2)}) collective-permute-start(bf16[2,256,128]{2,1,0:T(8,128)(2,1)S(1)} %get-tuple-element.98), channel_id=1, source_target_pairs={{0,16},{4,20},{8,24},{12,28},{16,0},{20,4},{24,8},{28,12},{1,17},{... | collective-permute-start | bytes 393224 | tf_op jit(solution)/shard_map/ppermute | solution.py:325
  56.5 5.5 %collective-permute-start.17 = (bf16[2,256,128]{2,1,0:T(8,128)(2,1)S(1)}, bf16[2,256,128]{2,1,0:T(8,128)(2,1)S(1)}, u32[]{:S(2)}, u32[]{:S(2)}) collective-permute-start(bf16[2,256,128]{2,1,0:T(8,128)(2,1)S(1)} %get-tuple-element.99), channel_id=1, source_target_pairs={{0,8},{4,12},{8,0},{12,4},{16,24},{20,28},{24,16},{28,20},{1,9},{5... | collective-permute-start | bytes 393224 | tf_op jit(solution)/shard_map/ppermute | solution.py:325
